TPU v7x, 32 devices: a whole 2x2x4 slice. The times are simulated.
32 devices in a mesh: band: 16 (over z, y, x), lev: 2 (over core).
Axes of the slice: x: 2, y: 2, z: 4, core: 2. Of those that a mesh axis runs over, the one named last changes fastest.
Arguments:
- spectra: bfloat16 [2, 64, 320, 641], P(None, 'lev', 'band'), may hold values from -0.15625 to 0.15625
- legendre: bfloat16 [8, 16, 320, 641], P('lev', None, 'band'), may hold values from -0.25 to 0.25
- pairing: int32 [320], P('band'), may hold values from 0 to 319, each once
- eta_shift: bfloat16 [16, 128, 2816], P('lev', 'band'), may hold values from -4 to 4
- cells: int32 [3, 16, 128, 2816], P(None, 'lev', 'band'), may hold values from -1 to 2815, as said below
Outputs:
- advected: bfloat16 [2, 16, 128, 2816], P(None, 'lev', 'band')
- displacement: float32 [2, 16, 128, 2816], P(None, 'lev', 'band')
Inputs may be any that keep to these rules, and one draw needn't show every extreme that they name: cells[0] is the arrival row or the row before it, cells[1] the arrival longitude or the one before it (cyclically), cells[2] the arrival level or the one before it.
All inputs are finite; a program needn't handle non-finite values.
Results may differ from a plain program's by a relative error of at most 0.0076.
Values may be sent and summed in bfloat16 or wider, within the bound.
No kernel may reach another device: no remote copies, remote signals or barrier semaphores. Data moves between devices by JAX's collectives and lax.ppermute only.
A program may use at most 192 MiB of HBM per device.

v0:
```python
import math

import jax
import jax.numpy as jnp
from jax import lax
from jax.sharding import PartitionSpec as P

M = 640
ITERS = 2


COURANT = 0.8


def with_halo(array, sides, width):
    for axis, dim in sides:
        size, length = (lax.axis_size(axis), array.shape[dim])
        up = [(i, (i + 1) % size) for i in range(size - 1)]
        down = [(j, i) for i, j in up]
        last = lax.slice_in_dim(array, length - width, length, axis=dim)
        first = lax.slice_in_dim(array, 0, width, axis=dim)
        before = lax.ppermute(last, axis, up)
        after = lax.ppermute(first, axis, down)
        array = jnp.concatenate([before, array, after], axis=dim)
    return array


def cubic_weights(fraction):
    return (
        -fraction * (fraction - 1.0) * (fraction - 2.0) / 6.0,
        (fraction + 1.0) * (fraction - 1.0) * (fraction - 2.0) / 2.0,
        -(fraction + 1.0) * fraction * (fraction - 2.0) / 2.0,
        (fraction + 1.0) * fraction * (fraction - 1.0) / 6.0,
    )


def tap_weights(shift, offset):
    fraction = jnp.clip(-shift - offset.astype(jnp.float32), -0.5, 1.5)
    first, second, third, fourth = cubic_weights(fraction)
    nothing = jnp.zeros_like(fraction)
    at_arrival = offset == 0
    return (
        jnp.where(at_arrival, nothing, first),
        jnp.where(at_arrival, first, second),
        jnp.where(at_arrival, second, third),
        jnp.where(at_arrival, third, fourth),
        jnp.where(at_arrival, fourth, nothing),
    )


def rolled_copies(padded):
    return [jnp.roll(padded, 2 - lon_step, axis=3) for lon_step in range(5)]


def interpolate(copies, field_ids, level_taps, row_taps, lon_taps):
    level_count = level_taps[0].shape[0]
    row_count = level_taps[0].shape[1]
    totals = [jnp.zeros(level_taps[0].shape, jnp.float32) for field_id in field_ids]
    for level_step in range(5):
        for row_step in range(5):
            outer = level_taps[level_step] * row_taps[row_step]
            for position in range(len(field_ids)):
                inner = jnp.zeros(outer.shape, jnp.float32)
                for lon_step in range(5):
                    block = copies[lon_step][
                        level_step : level_step + level_count,
                        field_ids[position],
                        row_step : row_step + row_count,
                        :,
                    ]
                    inner = inner + lon_taps[lon_step] * block.astype(jnp.float32)
                totals[position] = totals[position] + outer * inner
    return totals


def departure(
    fields,
    wind_copies,
    tracer_copies,
    wind_ids,
    tracer_ids,
    eta_shift,
    row_offset,
    lon_offset,
    level_offset,
):
    east = fields[:, 0].astype(jnp.float32)
    north = fields[:, 1].astype(jnp.float32)
    level_taps = tap_weights(eta_shift.astype(jnp.float32), level_offset)
    shift_row = COURANT * north
    shift_lon = COURANT * east
    for sweep in range(ITERS):
        row_taps = tap_weights(shift_row, row_offset)
        lon_taps = tap_weights(shift_lon, lon_offset)
        east_found, north_found = interpolate(wind_copies, wind_ids, level_taps, row_taps, lon_taps)
        shift_row = 0.5 * COURANT * (north + north_found)
        shift_lon = 0.5 * COURANT * (east + east_found)
    row_taps = tap_weights(shift_row, row_offset)
    lon_taps = tap_weights(shift_lon, lon_offset)
    heat, moisture = interpolate(tracer_copies, tracer_ids, level_taps, row_taps, lon_taps)
    return (jnp.stack([heat, moisture]).astype(jnp.bfloat16), jnp.stack([shift_row, shift_lon]))


def split_halves(spectra, pairing):
    width = spectra.shape[-1]
    columns = lax.broadcasted_iota(jnp.int32, (pairing.shape[0], width), 1)
    first_part = columns < (width - 1 - pairing)[:, None]
    nothing = jnp.zeros((), spectra.dtype)
    return jnp.stack(
        [jnp.where(first_part, spectra, nothing), jnp.where(first_part, nothing, spectra)]
    )


def synthesis(pair_ids, lon_ids, lon_total):
    orders = jnp.stack([pair_ids, M - 1 - pair_ids])
    phase = (orders[:, :, None] * lon_ids[None, None, :] % lon_total).astype(jnp.float32) * (
        2.0 * math.pi / lon_total
    )
    weight = jnp.where(orders == 0, 1.0, 2.0).astype(jnp.float32)[:, :, None]
    return jnp.stack([weight * jnp.cos(phase), -weight * jnp.sin(phase)]).astype(jnp.bfloat16)


def legendre_rows(table, halves):
    return jnp.einsum(
        "scpk,hrfpk->cpsfhr", table, halves, preferred_element_type=jnp.float32
    ).astype(jnp.bfloat16)


def per_device(spectra, legendre, pairing, eta_shift, cells):
    grid_shape = eta_shift.shape
    row_count = grid_shape[1]
    halves = split_halves(spectra, pairing)
    result = legendre_rows(lax.all_gather(legendre, "lev", axis=0, tiled=True), halves)
    local_sums = result.reshape(result.shape[0], result.shape[1], -1)
    spectral = lax.all_to_all(local_sums, "band", split_axis=0, concat_axis=1, tiled=True)
    all_pairs = lax.all_gather(pairing, "band", axis=0, tiled=True)
    field_count = 4 * grid_shape[0]
    spectral = spectral.reshape(all_pairs.shape[0], row_count, field_count, 2, 2)
    lon_total = grid_shape[2]
    lon_half = lon_total // 2
    pieces = []
    for lon_part in range(2):
        lon_block = lon_part * lon_half + jnp.arange(lon_half, dtype=jnp.int32)
        basis = synthesis(all_pairs, lon_block, lon_total)
        pieces.append(
            jnp.einsum(
                "psfhr,rhpj->fsj", spectral, basis, preferred_element_type=jnp.float32
            ).astype(jnp.bfloat16)
        )
    grid = jnp.concatenate(pieces, axis=2)
    fields = grid.reshape(grid_shape[0], 4, grid_shape[1], lon_total)
    level_ids = lax.axis_index("lev") * grid_shape[0] + lax.broadcasted_iota(
        jnp.int32, grid_shape, 0
    )
    row_ids = lax.axis_index("band") * grid_shape[1] + lax.broadcasted_iota(
        jnp.int32, grid_shape, 1
    )
    lon_ids = lax.broadcasted_iota(jnp.int32, grid_shape, 2)
    row_offset = cells[0] - row_ids
    lon_offset = (cells[1] - lon_ids + 2) % lon_total - 2
    level_offset = cells[2] - level_ids
    padded = with_halo(fields, (("band", 2), ("lev", 0)), 2)
    wind_copies = rolled_copies(padded)
    tracer_ids = (2, 3)
    return departure(
        fields,
        wind_copies,
        wind_copies,
        (0, 1),
        tracer_ids,
        eta_shift,
        row_offset,
        lon_offset,
        level_offset,
    )


def solution(mesh):
    return jax.shard_map(
        per_device,
        mesh=mesh,
        in_specs=(
            P(None, "lev", "band", None),
            P("lev", None, "band", None),
            P("band"),
            P("lev", "band", None),
            P(None, "lev", "band", None),
        ),
        out_specs=(P(None, "lev", "band", None), P(None, "lev", "band", None)),
        check_vma=False,
    )
```

profile of v0, /device:TPU:9, one launch (start us, length us, event | category | flops | bytes accessed | tf_op | source)
XLA Modules:
  0.0 1063.2 jit_solution(13383224726284624088)
XLA Ops:
  7.2 3.1 copy.39
  12.0 9.8 all-reduce
  22.0 4.2 select_bitcast_fusion.1
  26.2 1.3 fusion.712
  27.5 1.0 subtract_clamp_fusion.4
  28.5 7.9 convert_bitcast_fusion
  36.4 10.2 copy.40
  46.6 5.6 copy.41
  52.2 4.5 all-to-all-start
  56.8 32.8 %multiply_convert_fusion.1 = (bf16[1,2,320,1408]{3,2,0,1:T(8,128)(2,1)}, bf16[1,2,320,1408]{3,2,0,1:T(8,128)(2,1)}, bf16[1,2,320,1408]{3,2,0,1:T(8,128)(2,1)}, bf16[1,2,320,1408]{3,2,0,1:T(8,128)(2,1)}) fusion(s32[1408]{0:T(1024)S(1)} %iota_add_fusion, s32[2,320]{1,0:T(2,128)S(1)} %pad_add_fusion, f32[2,320]{1,0:T(2,128)S(1)} %get-tuple-element.288, ...), kind=kLoop, calls=%fused_computation.469 | loop fusion | flops 23429120 | bytes 7222272 | tf_op jit(solution)/shard_map/convert.504
  89.6 4.9 copy.42
  94.5 7.1 reshape.1137
  101.7 3.4 fusion.25
  105.1 1.2 fusion.24
  106.3 1.2 pad_maximum_fusion
  107.5 3.7 reshape.1138
  111.2 3.3 constant_dynamic-update-slice_fusion.1
  114.5 1.1 copy-done.4
  116.1 3.1 collective-permute-start
  119.2 1.4 fusion.1026
  120.6 4.0 collective-permute-start.1
  124.6 1.5 collective-permute-done
  126.3 2.0 copy_dynamic-update-slice_fusion.2
  128.3 3.3 collective-permute-done.1
  132.2 9.4 collective-permute-start.3
  141.6 1.3 collective-permute-start.2
  142.9 1.0 constant_dynamic-update-slice_fusion
  143.9 2.3 fusion.1454
  146.9 2.0 fusion.1557
  148.9 4.4 fusion.1555
  154.5 2.4 fusion.1209
  156.8 2.2 fusion.1210
  159.0 2.5 pad.10
  161.5 2.5 pad.8
  164.0 2.3 fusion.1110
  166.3 2.2 fusion.1111
  168.5 2.2 fusion.1207
  170.7 2.1 fusion.1108
  172.8 2.5 fusion.1208
  175.3 2.5 fusion.1109
  177.8 2.4 fusion.1218
  180.2 2.5 fusion.1119
  182.7 2.4 fusion.1227
  185.0 2.4 fusion.1128
  187.4 2.2 fusion.1236
  189.6 2.2 fusion.1137
  191.9 2.2 fusion.1245
  194.1 2.2 fusion.1146
  196.3 2.5 fusion.1331
  198.8 1.9 fusion.1254
  200.6 1.2 fusion.1155
  201.8 6.9 fusion.58
  208.7 6.9 fusion.59
  215.6 8.8 fusion.56
  224.4 9.0 fusion.57
  233.4 171.8 %subtract_clamp_fusion.2 = (f32[8,8,2816]{2,1,0:T(8,128)}, pred[8,8,2816]{2,1,0:T(8,128)(4,1)}, f32[8,8,2816]{2,1,0:T(8,128)}, f32[8,8,2816]{2,1,0:T(8,128)}, f3...) fusion(s32[8,8,2816]{2,1,0:T(8,128)} %fusion.712, ...), kind=kLoop, calls=%fused_computation.2279 | loop fusion | flops 165085184 | bytes 66703904 | tf_op jit(solution)/shard_map/jit(clip)/min | solution.py:38
  405.3 227.2 %fusion.1022 = (f32[8,8,2816]{2,1,0:T(8,128)}, f32[8,8,2816]{2,1,0:T(8,128)}) fusion(pred[8,8,2816]{2,1,0:T(8,128)(4,1)} %get-tuple-element.269, f32[8,8,2816]{2,1,0:T(8,128)} %get-tuple-element.4, bf16[8,1,8,2816]{3,2,0,1:T(8,128)(2,1)} %get-tuple-element.73, bf16[8,1,8,2816]{3,2,0,1:T(8,128)(2,1)} %get-tuple-element.64, ...), kind=kLoop, calls=%fused_computation.2286 | loop fusion | flops 232308736 | bytes 41451552 | tf_op jit(solution)/shard_map/mul | solution.py:96
  632.5 140.2 %fusion.1023 = f32[8,8,2816]{2,1,0:T(8,128)S(1)} fusion(pred[8,8,2816]{2,1,0:T(8,128)(4,1)} %get-tuple-element.269, f32[8,8,2816]{2,1,0:T(8,128)} %get-tuple-element.4, bf16[8,1,8,2816]{3,2,0,1:T(8,128)(2,1)} %get-tuple-element.62, bf16[8,1,8,2816]{3,2,0,1:T(8,128)(2,1)} %get-tuple-element.61, bf16[8,1,8,2816]{3,2,0,1:T(8,128)(2,1)} %get-tuple-element.60, ...), kind=kLoop, calls=%fused_computation.2287 | loop fusion | flops 120750080 | bytes 39649280 | tf_op jit(solution)/shard_map/mul | solution.py:97
  772.7 1.3 pad_maximum_fusion.1
  774.0 8.8 fusion.60
  782.8 8.8 fusion.66
  791.6 5.1 fusion.72
  796.7 144.4 %fusion.1470 = bf16[1,8,8,2816]{3,2,1,0:T(8,128)(2,1)} fusion(bf16[8,1,8,2816]{3,2,0,1:T(8,128)(2,1)} %get-tuple-element.166, bf16[8,1,8,2816]{3,2,0,1:T(8,128)(2,1)} %get-tuple-element.157, bf16[8,1,8,2816]{3,1,2,0:T(2,128)(2,1)} %get-tuple-element.257, bf16[12,4,12,2]{3,2,0,1:T(8,128)(2,1)} %get-tuple-element.220, ...), kind=kLoop, calls=%fused_computation.2843 | loop fusion | flops 125255680 | bytes 46889888 | tf_op jit(solution)/shard_map/stack | solution.py:101
  941.2 113.9 %fusion.1469 = bf16[1,8,8,2816]{3,2,1,0:T(8,128)(2,1)S(1)} fusion(bf16[12,4,12,2]{3,2,0,1:T(8,128)(2,1)S(1)} %get-tuple-element.221, bf16[12,4,12,2814]{3,2,0,1:T(8,128)(2,1)S(1)} %bitcast.2752, bf16[12,4,12,1]{3,2,0,1:T(8,128)(2,1)S(1)} %get-tuple-element.225, bf16[12,4,12,2815]{3,2,0,1:T(8,128)(2,1)S(1)} %bitcast.2750, ...), kind=kLoop, calls=%fused_computation.2842 | loop fusion | flops 120029184 | bytes 54817440 | tf_op jit(solution)/shard_map/stack | solution.py:101
  (80 shorter events, 5.1 us)
Async XLA Ops:
  7.2 3.2 copy-start.15
  7.2 4.6 copy-start.14
  7.2 21.3 %all-gather.2.cloned.1.call-start = ((), (), s32[]{:S(2)}) async-start(), calls=%async_computation.1 | async-start | bytes 5898240 | tf_op jit(solution)/shard_map/all_gather | solution.py:133
  10.3 15.9 %copy-start.5 = (s32[3,8,8,2816]{3,2,1,0:T(8,128)S(1)}, s32[3,8,8,2816]{3,2,1,0:T(8,128)}, u32[]{:S(2)}) copy-start(s32[3,8,8,2816]{3,2,1,0:T(8,128)} %param.9) | copy-start | bytes 6488068
  10.3 17.2 %copy-start.13 = (bf16[8,8,2816]{2,1,0:T(8,128)(2,1)S(1)}, bf16[8,8,2816]{2,1,0:T(8,128)(2,1)}, u32[]{:S(2)}) copy-start(bf16[8,8,2816]{2,1,0:T(8,128)(2,1)} %param.8) | copy-start | bytes 1081348
  52.2 37.4 %all-to-all-start = ((bf16[16,20,1024]{2,1,0:T(8,128)(2,1)}), bf16[16,20,1024]{2,1,0:T(8,128)(2,1)S(1)}, u32[]{:S(2)}, u32[]{:S(2)}) async-start(bf16[16,20,1024]{2,1,0:T(8,128)(2,1)} %copy.41), calls=%async_computation | async-start | bytes 1572864 | tf_op jit(solution)/shard_map/all_to_all | solution.py:135
  101.7 3.4 copy-start.10
  101.7 3.4 copy-start.11
  114.5 1.1 copy-start.4
  116.1 10.0 collective-permute-start
  120.6 11.0 %collective-permute-start.1 = (bf16[8,4,2,2816]{3,2,0,1:T(2,128)(2,1)S(1)}, bf16[8,4,2,2816]{3,2,0,1:T(2,128)(2,1)S(1)}, u32[]{:S(2)}, u32[]{:S(2)}) collective-permute-start(bf16[8,4,2,2816]{3,2,0,1:T(2,128)(2,1)S(1)} %get-tuple-element.280), channel_id=1, source_target_pairs={{2,0},{4,2},{6,4},{8,6},{10,8},{12,10},{14,12},{16,14},{18,16},{20... | collective-permute-start | bytes 1081352 | tf_op jit(solution)/shard_map/ppermute | solution.py:23
  126.1 20.1 %copy-start.9 = (bf16[8,4,2,2816]{3,2,0,1:T(2,128)(2,1)}, bf16[8,4,2,2816]{3,2,0,1:T(2,128)(2,1)S(1)}, u32[]{:S(2)}) copy-start(bf16[8,4,2,2816]{3,2,0,1:T(2,128)(2,1)S(1)} %collective-permute-done) | copy-start | bytes 1081348
  132.2 14.7 %collective-permute-start.3 = (bf16[2,4,12,2816]{3,1,2,0:T(4,128)(2,1)S(1)}, bf16[2,4,12,2816]{3,1,2,0:T(4,128)(2,1)S(1)}, u32[]{:S(2)}, u32[]{:S(2)}) collective-permute-start(bf16[2,4,12,2816]{3,1,2,0:T(4,128)(2,1)S(1)} %get-tuple-element.272), channel_id=1, source_target_pairs={{1,0},{3,2},{5,4},{7,6},{9,8},{11,10},{13,12},{15,14},{17,16},{19,... | collective-permute-start | bytes 1622024 | tf_op jit(solution)/shard_map/ppermute | solution.py:23
  141.6 4.6 collective-permute-start.2
  146.8 2.1 copy-start.3
  148.9 49.8 %copy-start = (bf16[12,4,12,2815]{3,2,0,1:T(8,128)(2,1)}, bf16[12,4,12,2815]{3,2,0,1:T(8,128)(2,1)S(1)}, u32[]{:S(2)}) copy-start(bf16[12,4,12,2815]{3,2,0,1:T(8,128)(2,1)S(1)} %get-tuple-element.227) | copy-start | bytes 9728644
  148.9 49.8 %copy-start.2 = (bf16[12,4,12,2815]{3,2,0,1:T(8,128)(2,1)}, bf16[12,4,12,2815]{3,2,0,1:T(8,128)(2,1)S(1)}, u32[]{:S(2)}) copy-start(bf16[12,4,12,2815]{3,2,0,1:T(8,128)(2,1)S(1)} %get-tuple-element.226) | copy-start | bytes 9728644
  153.4 47.2 %copy-start.1 = (bf16[12,4,12,2814]{3,2,0,1:T(8,128)(2,1)}, bf16[12,4,12,2814]{3,2,0,1:T(8,128)(2,1)S(1)}, u32[]{:S(2)}) copy-start(bf16[12,4,12,2814]{3,2,0,1:T(8,128)(2,1)S(1)} %get-tuple-element.223) | copy-start | bytes 9725188
  154.5 478.0 %copy-start.6 = (bf16[12,4,12,1]{3,2,0,1:T(8,128)(2,1)}, bf16[12,4,12,1]{3,2,0,1:T(8,128)(2,1)S(1)}, u32[]{:S(2)}) copy-start(bf16[12,4,12,1]{3,2,0,1:T(8,128)(2,1)S(1)} %get-tuple-element.224) | copy-start | bytes 3460
  632.5 140.2 %copy-start.7 = (f32[8,8,2816]{2,1,0:T(8,128)S(1)}, f32[8,8,2816]{2,1,0:T(8,128)}, u32[]{:S(2)}) copy-start(f32[8,8,2816]{2,1,0:T(8,128)} %get-tuple-element.2) | copy-start | bytes 2162692
  772.7 10.1 copy-start.8
  774.0 22.6 %slice-start.4 = ((s8[4325376]{0:T(1024)(128)(4,1)}), s8[4194304]{0:T(1024)(128)(4,1)S(1)}, s32[]{:S(2)}) async-start(s8[4325376]{0:T(1024)(128)(4,1)} %bitcast.2753), calls=%async_computation.6 | async-start | bytes 8388608
  782.8 13.9 %slice-start.5 = ((s8[4325376]{0:T(1024)(128)(4,1)}), s8[131072]{0:T(1024)(128)(4,1)S(1)}, s32[]{:S(2)}) async-start(s8[4325376]{0:T(1024)(128)(4,1)} %bitcast.2753), calls=%async_computation.7 | async-start | bytes 262144
  791.6 149.6 %slice-start = ((s8[4325376]{0:T(1024)(128)(4,1)}), s8[4194304]{0:T(1024)(128)(4,1)S(1)}, s32[]{:S(2)}) async-start(s8[4325376]{0:T(1024)(128)(4,1)} %bitcast.2749), calls=%async_computation.2 | async-start | bytes 8388608
  791.6 149.6 %slice-start.2 = ((s8[4325376]{0:T(1024)(128)(4,1)}), s8[4194304]{0:T(1024)(128)(4,1)S(1)}, s32[]{:S(2)}) async-start(s8[4325376]{0:T(1024)(128)(4,1)} %bitcast.2751), calls=%async_computation.4 | async-start | bytes 8388608
  791.6 149.6 %slice-start.6 = ((s8[4325376]{0:T(1024)(128)(4,1)}), s8[131072]{0:T(1024)(128)(4,1)S(1)}, s32[]{:S(2)}) async-start(s8[4325376]{0:T(1024)(128)(4,1)} %bitcast.2755), calls=%async_computation.8 | async-start | bytes 262144
  796.7 144.5 %slice-start.1 = ((s8[4325376]{0:T(1024)(128)(4,1)}), s8[131072]{0:T(1024)(128)(4,1)S(1)}, s32[]{:S(2)}) async-start(s8[4325376]{0:T(1024)(128)(4,1)} %bitcast.2749), calls=%async_computation.3 | async-start | bytes 262144
  796.7 144.5 %slice-start.3 = ((s8[4325376]{0:T(1024)(128)(4,1)}), s8[131072]{0:T(1024)(128)(4,1)S(1)}, s32[]{:S(2)}) async-start(s8[4325376]{0:T(1024)(128)(4,1)} %bitcast.2751), calls=%async_computation.5 | async-start | bytes 262144
  796.7 144.5 %slice-start.7 = ((s8[4325376]{0:T(1024)(128)(4,1)}), s8[4194304]{0:T(1024)(128)(4,1)S(1)}, s32[]{:S(2)}) async-start(s8[4325376]{0:T(1024)(128)(4,1)} %bitcast.2755), calls=%async_computation.9 | async-start | bytes 8388608
  941.2 114.0 %copy-start.12 = (bf16[1,8,8,2816]{3,2,1,0:T(8,128)(2,1)S(1)}, bf16[1,8,8,2816]{3,2,1,0:T(8,128)(2,1)}, u32[]{:S(2)}) copy-start(bf16[1,8,8,2816]{3,2,1,0:T(8,128)(2,1)} %fusion.1470) | copy-start | bytes 1081348
Sparse Core Ops, SparseCore 0:
  10.5 15.1 all-gather.1
where the time goes:
time: 1070 us; the launch traced here: 1060 us
  other arithmetic  941 us (88%)
  local copies, waits for them, and re-layouts  57.4 us (5%)
  starting transfers between devices  22.3 us (2%)
  between operations  15.6 us (1%)
  matrix products  12.4 us (1%)
    another operation x3, other arithmetic, departure(): jnp.stack([heat, moisture]).astype(jnp.bfloat16)  259 us
    mul x1, other arithmetic, departure(): shift_row = 0.5 * COURANT * (north + north_found)  227 us
    min x2, other arithmetic, tap_weights(): fraction = jnp.clip(-shift - offset.astype(jnp.float32), -0.5, 1.5)  173 us
    mul x1, other arithmetic, departure(): shift_lon = 0.5 * COURANT * (east + east_found)  140 us
    concatenate x8, other arithmetic, with_halo(): array = jnp.concatenate([before, array, after], axis=dim)  56.5 us
    concatenate x19, other arithmetic, rolled_copies(): return [jnp.roll(padded, 2 - lon_step, axis=3) for lon_step in range(5)]  42.3 us
    another operation x1, other arithmetic  32.8 us
  transfers between devices with their start and end apart: 6, of which 2 were waited for; matrix products, arithmetic and copies ran while one was open for 4% of the time, Pallas kernels for 0%

commit v1 on v0

v1 whole, which is shorter than its diff:
```python
import functools
import math

import jax
import jax.numpy as jnp
from jax import lax
from jax.experimental import pallas as pl
from jax.experimental.pallas import tpu as pltpu
from jax.sharding import PartitionSpec as P

M = 640
ITERS = 2


COURANT = 0.8


HALO = 2
LANES = 128


def slot_weights(place, here, low, high, sixth):
    z = jnp.minimum(jnp.maximum(place, low), high)
    square = z * z
    less = square - 1.0
    outer = less * z * sixth
    triple = 3.0 * outer
    half = 0.5 * z
    half_square = 0.5 * square
    return (
        half_square - half - jnp.where(here, outer, triple),
        triple - less,
        half_square + half - jnp.where(here, triple, outer),
        outer,
    )


def bounds(here):
    return (
        jnp.where(here, -0.5, -1.5),
        jnp.where(here, 1.5, 0.5),
        jnp.where(here, 1.0 / 6.0, -1.0 / 6.0),
    )


def weighted(weights, values):
    return (weights[0] * values[0] + weights[1] * values[1]) + (
        weights[2] * values[2] + weights[3] * values[3]
    )


def shifted_lanes(before, here, after, lane):
    return (
        jnp.where(lane < 2, pltpu.roll(before, 2, 1), pltpu.roll(here, 2, 1)),
        jnp.where(lane < 1, pltpu.roll(before, 1, 1), pltpu.roll(here, 1, 1)),
        here,
        jnp.where(lane < LANES - 1, pltpu.roll(here, LANES - 1, 1), pltpu.roll(after, LANES - 1, 1)),
        jnp.where(lane < LANES - 2, pltpu.roll(here, LANES - 2, 1), pltpu.roll(after, LANES - 2, 1)),
    )


def fill(chunk, chunk_total, center_ref, edge_ref, scratch):
    slabs, field_count, rows, _ = center_ref.shape
    before = jnp.where(chunk == 0, chunk_total - 1, chunk - 1)
    after = jnp.where(chunk == chunk_total - 1, 0, chunk + 1)
    starts = [pl.multiple_of(c * LANES, LANES) for c in (before, chunk, after)]
    lane = lax.broadcasted_iota(jnp.int32, (rows, LANES), 1)
    edge_lane = lax.broadcasted_iota(jnp.int32, (2 * HALO, LANES), 1)

    def slab_step(slab, carry):
        for field in range(field_count):
            blocks = [center_ref[slab, field, :, pl.ds(s, LANES)] for s in starts]
            for step, moved in enumerate(shifted_lanes(*blocks, lane)):
                scratch[field, slab, step, rows : 2 * rows, :] = moved
            edges = [edge_ref[slab, field, :, pl.ds(s, LANES)] for s in starts]
            for step, moved in enumerate(shifted_lanes(*edges, edge_lane)):
                scratch[field, slab, step, rows - 2 * HALO : rows, :] = moved
                scratch[field, slab, step, 2 * rows : 2 * rows + 2 * HALO, :] = moved
        return carry

    lax.fori_loop(0, slabs, slab_step, 0)


def level_sums(scratch, field, k, zero, rows, weights, level_here, row_here, lon_here):
    def load(a, b, c):
        return scratch[field, k + HALO + a, c + HALO, pl.ds(zero + (rows + b), rows), :]

    def slab_slots(a):
        out = {}
        for c in (-1, 0, 1):
            for b in (-1, 0, 1):
                out[b, c] = load(a, b, c)
            out[2, c] = jnp.where(row_here, load(a, 2, c), load(a, -2, c))
        for b in (-1, 0, 1):
            out[b, 2] = jnp.where(lon_here, load(a, b, 2), load(a, b, -2))
        out[2, 2] = jnp.where(
            row_here,
            jnp.where(lon_here, load(a, 2, 2), load(a, 2, -2)),
            jnp.where(lon_here, load(a, -2, 2), load(a, -2, -2)),
        )
        return out

    slabs = [slab_slots(a) for a in (-1, 0, 1, 2, -2)]
    return {
        key: weighted(
            weights,
            (
                slabs[0][key],
                slabs[1][key],
                slabs[2][key],
                jnp.where(level_here, slabs[3][key], slabs[4][key]),
            ),
        )
        for key in slabs[0]
    }


def across(sums, row_weights, lon_weights):
    slots = (-1, 0, 1, 2)
    return weighted(
        lon_weights, [weighted(row_weights, [sums[b, c] for b in slots]) for c in slots]
    )


def at_arrival(base_ref, cells_ref, k, chunk, lanes):
    shape = cells_ref.shape[2:3] + (LANES,)
    level_here = cells_ref[2, k, :, lanes] == base_ref[0] + k
    row_here = cells_ref[0, k, :, lanes] == base_ref[1] + lax.broadcasted_iota(jnp.int32, shape, 0)
    lon_here = cells_ref[1, k, :, lanes] == chunk * LANES + lax.broadcasted_iota(
        jnp.int32, shape, 1
    )
    return level_here, row_here, lon_here


def wind_kernel(chunk_total, base_ref, center_ref, edge_ref, eta_ref, cells_ref, out_ref, scratch):
    levels, rows, width = eta_ref.shape
    zero = base_ref[2]

    def chunk_step(part, carry):
        chunk = pl.program_id(0) * (width // LANES) + part
        lanes = pl.ds(pl.multiple_of(part * LANES, LANES), LANES)
        fill(chunk, chunk_total, center_ref, edge_ref, scratch)

        def level_step(k, inner):
            level_here, row_here, lon_here = at_arrival(base_ref, cells_ref, k, chunk, lanes)
            weights = slot_weights(
                -eta_ref[k, :, lanes].astype(jnp.float32), level_here, *bounds(level_here)
            )
            sums = [
                level_sums(
                    scratch, field, k, zero, rows, weights, level_here, row_here, lon_here
                )
                for field in range(2)
            ]
            east = scratch[0, k + HALO, HALO, rows : 2 * rows, :]
            north = scratch[1, k + HALO, HALO, rows : 2 * rows, :]
            row_bounds, lon_bounds = bounds(row_here), bounds(lon_here)
            shift_row = COURANT * north
            shift_lon = COURANT * east
            for sweep in range(ITERS):
                row_weights = slot_weights(-shift_row, row_here, *row_bounds)
                lon_weights = slot_weights(-shift_lon, lon_here, *lon_bounds)
                east_found = across(sums[0], row_weights, lon_weights)
                north_found = across(sums[1], row_weights, lon_weights)
                shift_row = 0.5 * COURANT * (north + north_found)
                shift_lon = 0.5 * COURANT * (east + east_found)
            out_ref[0, k, :, lanes] = shift_row
            out_ref[1, k, :, lanes] = shift_lon
            return inner

        lax.fori_loop(0, levels, level_step, 0)
        return carry

    lax.fori_loop(0, width // LANES, chunk_step, 0)


def tracer_kernel(
    chunk_total, base_ref, center_ref, edge_ref, eta_ref, cells_ref, shift_ref, out_ref, scratch
):
    levels, rows, width = eta_ref.shape
    zero = base_ref[2]

    def chunk_step(part, carry):
        chunk = pl.program_id(0) * (width // LANES) + part
        lanes = pl.ds(pl.multiple_of(part * LANES, LANES), LANES)
        fill(chunk, chunk_total, center_ref, edge_ref, scratch)

        def level_step(k, inner):
            level_here, row_here, lon_here = at_arrival(base_ref, cells_ref, k, chunk, lanes)
            weights = slot_weights(
                -eta_ref[k, :, lanes].astype(jnp.float32), level_here, *bounds(level_here)
            )
            row_weights = slot_weights(-shift_ref[0, k, :, lanes], row_here, *bounds(row_here))
            lon_weights = slot_weights(-shift_ref[1, k, :, lanes], lon_here, *bounds(lon_here))
            for field in range(2):
                sums = level_sums(
                    scratch, field, k, zero, rows, weights, level_here, row_here, lon_here
                )
                found = across(sums, row_weights, lon_weights)
                out_ref[field, k, :, lanes] = found.astype(out_ref.dtype)
            return inner

        lax.fori_loop(0, levels, level_step, 0)
        return carry

    lax.fori_loop(0, width // LANES, chunk_step, 0)


def interpolation_call(kernel, base, center, edge, eta_shift, cells, extra, out_dtype):
    levels, rows, lon_total = eta_shift.shape
    chunk_total = lon_total // LANES
    parts = 2 if chunk_total % 2 == 0 else 1
    width = lon_total // parts
    whole = lambda array: pl.BlockSpec(array.shape, lambda i: (0,) * array.ndim)
    pair = pl.BlockSpec((2, levels, rows, width), lambda i: (0, 0, 0, i))
    points = levels * rows * lon_total
    return pl.pallas_call(
        functools.partial(kernel, chunk_total),
        grid=(parts,),
        out_shape=jax.ShapeDtypeStruct((2, levels, rows, lon_total), out_dtype),
        in_specs=[
            pl.BlockSpec(memory_space=pltpu.SMEM),
            whole(center),
            whole(edge),
            pl.BlockSpec((levels, rows, width), lambda i: (0, 0, i)),
            pl.BlockSpec((3, levels, rows, width), lambda i: (0, 0, 0, i)),
        ]
        + [pair] * len(extra),
        out_specs=pair,
        scratch_shapes=[pltpu.VMEM((2, levels + 2 * HALO, 5, 3 * rows, LANES), jnp.float32)],
        compiler_params=pltpu.CompilerParams(vmem_limit_bytes=48 * 1024 * 1024),
        cost_estimate=pl.CostEstimate(
            flops=points * 500, bytes_accessed=points * 40, transcendentals=0
        ),
    )(base, center, edge, eta_shift, cells, *extra)

def row_edges(fields):
    size = lax.axis_size("band")
    up = [(i, (i + 1) % size) for i in range(size - 1)]
    down = [(j, i) for i, j in up]
    rows = fields.shape[2]
    before = lax.ppermute(fields[:, :, rows - HALO :], "band", up)
    after = lax.ppermute(fields[:, :, :HALO], "band", down)
    return jnp.concatenate([after, before], axis=2)


def level_edges(array):
    size, count = (lax.axis_size("lev"), array.shape[0])
    last, first = (array[count - HALO :], array[:HALO])
    if size == 2:
        at_top = lax.axis_index("lev") == 0
        found = lax.ppermute(jnp.where(at_top, last, first), "lev", [(0, 1), (1, 0)])
        nothing = jnp.zeros_like(found)
        return jnp.where(at_top, nothing, found), jnp.where(at_top, found, nothing)
    up = [(i, i + 1) for i in range(size - 1)]
    down = [(j, i) for i, j in up]
    return lax.ppermute(last, "lev", up), lax.ppermute(first, "lev", down)


def with_edges(fields):
    rows = fields.shape[2]
    edge = row_edges(fields)
    before, after = level_edges(jnp.concatenate([fields, edge], axis=2))
    center = jnp.concatenate([before[:, :, :rows], fields, after[:, :, :rows]], axis=0)
    edge = jnp.concatenate([before[:, :, rows:], edge, after[:, :, rows:]], axis=0)
    return center.astype(jnp.float32), edge.astype(jnp.float32)


def split_halves(spectra, pairing):
    width = spectra.shape[-1]
    columns = lax.broadcasted_iota(jnp.int32, (pairing.shape[0], width), 1)
    first_part = columns < (width - 1 - pairing)[:, None]
    nothing = jnp.zeros((), spectra.dtype)
    return jnp.stack(
        [jnp.where(first_part, spectra, nothing), jnp.where(first_part, nothing, spectra)]
    )


def synthesis(pair_ids, lon_ids, lon_total):
    orders = jnp.stack([pair_ids, M - 1 - pair_ids])
    phase = (orders[:, :, None] * lon_ids[None, None, :] % lon_total).astype(jnp.float32) * (
        2.0 * math.pi / lon_total
    )
    weight = jnp.where(orders == 0, 1.0, 2.0).astype(jnp.float32)[:, :, None]
    return jnp.stack([weight * jnp.cos(phase), -weight * jnp.sin(phase)]).astype(jnp.bfloat16)


def legendre_rows(table, halves):
    return jnp.einsum(
        "scpk,hrfpk->cpsfhr", table, halves, preferred_element_type=jnp.float32
    ).astype(jnp.bfloat16)


def per_device(spectra, legendre, pairing, eta_shift, cells):
    grid_shape = eta_shift.shape
    row_count = grid_shape[1]
    halves = split_halves(spectra, pairing)
    result = legendre_rows(lax.all_gather(legendre, "lev", axis=0, tiled=True), halves)
    local_sums = result.reshape(result.shape[0], result.shape[1], -1)
    spectral = lax.all_to_all(local_sums, "band", split_axis=0, concat_axis=1, tiled=True)
    all_pairs = lax.all_gather(pairing, "band", axis=0, tiled=True)
    field_count = 4 * grid_shape[0]
    spectral = spectral.reshape(all_pairs.shape[0], row_count, field_count, 2, 2)
    lon_total = grid_shape[2]
    lon_half = lon_total // 2
    pieces = []
    for lon_part in range(2):
        lon_block = lon_part * lon_half + jnp.arange(lon_half, dtype=jnp.int32)
        basis = synthesis(all_pairs, lon_block, lon_total)
        pieces.append(
            jnp.einsum(
                "psfhr,rhpj->fsj", spectral, basis, preferred_element_type=jnp.float32
            ).astype(jnp.bfloat16)
        )
    grid = jnp.concatenate(pieces, axis=2)
    fields = grid.reshape(grid_shape[0], 4, grid_shape[1], lon_total)
    base = jnp.stack(
        [
            lax.axis_index("lev") * grid_shape[0],
            lax.axis_index("band") * grid_shape[1],
            jnp.int32(0),
        ]
    ).astype(jnp.int32)
    winds = with_edges(fields[:, :2])
    tracers = with_edges(fields[:, 2:])
    displacement = interpolation_call(
        wind_kernel, base, *winds, eta_shift, cells, (), jnp.float32
    )
    advected = interpolation_call(
        tracer_kernel, base, *tracers, eta_shift, cells, (displacement,), jnp.bfloat16
    )
    return advected, displacement


def solution(mesh):
    return jax.shard_map(
        per_device,
        mesh=mesh,
        in_specs=(
            P(None, "lev", "band", None),
            P("lev", None, "band", None),
            P("band"),
            P("lev", "band", None),
            P(None, "lev", "band", None),
        ),
        out_specs=(P(None, "lev", "band", None), P(None, "lev", "band", None)),
        check_vma=False,
    )
```

time: 1070 us -> 233 us (0.22)
  other arithmetic: 941 us -> 37 us
  Pallas kernels: 0 us -> 94 us
  local copies, waits for them, and re-layouts: 57.4 us -> 35.2 us
    mul x2 -> x0, other arithmetic: 367 us -> none  [the longest x1 227 us: departure(): shift_row = 0.5 * COURANT * (north + north_found)]
    another operation x5 -> x2, other arithmetic: 293 us -> 32.8 us  [the longest x3 259 us: departure(): jnp.stack([heat, moisture]).astype(jnp.bfloat16)]
    min x2 -> x0, other arithmetic: 173 us -> none  [tap_weights(): fraction = jnp.clip(-shift - offset.astype(jnp.float32), -0.5, 1.5)]
    concatenate x27 -> x0, other arithmetic: 98.8 us -> none  [the longest x8 56.5 us: with_halo(): array = jnp.concatenate([before, array, after], axis=dim)]
    pallas_call x0 -> x2, Pallas kernels: none -> 94 us  [interpolation_call(): pl.pallas_call(functools.partial(kernel, chunk_total), grid=(parts,), out...]
  transfers between devices with their start and end apart: 6 -> 8, of which waited for: 2 -> 3; matrix products, arithmetic and copies ran while one was open for 4% -> 16% of each run, Pallas kernels for 0% -> 0%
where the time goes in v1:
time: 233 us; the launch traced here: 232 us
  Pallas kernels  94 us (40%)
  other arithmetic  37 us (16%)
  local copies, waits for them, and re-layouts  35.2 us (15%)
  starting transfers between devices  24.4 us (10%)
  between operations  15 us (6%)
  matrix products  10.9 us (5%)
  blocking collectives  9.84 us (4%)
  waiting for transfers between devices  5.21 us (2%)
    pallas_call x2, Pallas kernels, interpolation_call(): pl.pallas_call(functools.partial(kernel, chunk_total), grid=(parts,), out...  94 us
    another operation x1, other arithmetic  32.8 us
    unnamed x1, blocking collectives  9.84 us
    convert_element_type x1, local copies, waits for them, and re-layouts, legendre_rows(): return jnp.einsum('scpk,hrfpk->cpsfhr', table, halves, preferred_element_...  9.55 us
    ppermute x2, starting transfers between devices, row_edges(): after = lax.ppermute(fields[:, :, :HALO], 'band', down)  7.71 us
    reshape x1, local copies, waits for them, and re-layouts, per_device(): spectral.reshape(all_pairs.shape[0], row_count, field_count, 2, 2)  7.13 us
    unnamed x18, local copies, waits for them, and re-layouts  6.52 us
    all_to_all x1, starting transfers between devices, per_device(): lax.all_to_all(local_sums, 'band', split_axis=0, concat_axis=1, tiled=True)  6.42 us
  transfers between devices with their start and end apart: 8, of which 3 were waited for; matrix products, arithmetic and copies ran while one was open for 16% of the time, Pallas kernels for 0%

profile of v1, /device:TPU:9, one launch (start us, length us, event | category | flops | bytes accessed | tf_op | source)
XLA Modules:
  0.0 231.5 jit_solution(491805094510602911)
XLA Ops:
  7.2 0.0 all-gather.2.cloned.1.call-start
  7.2 3.1 %copy.23 = bf16[4,16,20,641]{3,1,0,2:T(8,128)(2,1)} copy(bf16[4,16,20,641]{3,1,2,0:T(8,128)(2,1)} %param.6) | data formatting | bytes 3281920 | tf_op args[1]
  10.3 0.0 copy-start.6
  10.3 0.0 copy-start.5
  10.3 0.0 copy-start.3
  10.3 0.0 all-gather.2.cloned.1.call-update
  10.3 0.6 copy-done.6
  10.9 0.6 dynamic-slice
  12.2 0.0 copy-done.5
  12.2 0.2 dynamic-update-slice
  12.4 9.8 %all-reduce = s32[320]{0:T(512)S(1)} all-reduce(s32[320]{0:T(512)S(1)} %dynamic-update-slice), channel_id=1, replica_groups=mesh['band'=16,'lev'=2] {'band'}, use_global_device_ids=true, to_apply=%add | all-reduce | flops 320 | bytes 2560
  22.3 0.1 iota_compare_fusion
  22.4 0.0 copy-done.3
  22.4 2.2 select_bitcast_fusion.1
  24.6 1.0 all-gather.2.cloned.1.call-done
  25.6 6.4 %convert_bitcast_fusion = bf16[16,20,8,32,2,2]{3,0,2,5,4,1:T(8,128)(2,1)S(1)} fusion(bf16[8,16,20,641]{3,1,0,2:T(8,128)(2,1)} %all-gather.2.cloned.1.call-done, bf16[1,2,32,20,641]{4,2,1,0,3:T(8,128)(2,1)} %get-tuple-element.3, bf16[1,2,32,20,641]{4,2,1,0,3:T(8,128)(2,1)} %get-tuple-element.2), kind=kOutput, calls=%fused_computation.33 | convolution fusion | flops 426977280 | bytes 7219200 | tf_op jit(solution)/shard_map/scpk,hrfpk->cpsfhr/dot_general | solution.py:289
  32.0 9.5 %copy.24 = bf16[16,20,8,32,2,2]{1,0,5,4,3,2:T(8,128)(2,1)} copy(bf16[16,20,8,32,2,2]{3,0,2,5,4,1:T(8,128)(2,1)S(1)} %convert_bitcast_fusion) | data formatting | bytes 1310720 | tf_op jit(solution)/shard_map/convert_element_type | solution.py:291
  41.6 5.6 %copy.25 = bf16[16,20,1024]{2,1,0:T(8,128)(2,1)} copy(bf16[16,20,1024]{1,0,2:T(8,128)(2,1)} %bitcast.71) | data formatting | bytes 1310720 | tf_op jit(solution)/shard_map/reshape | solution.py:299
  47.2 6.4 %all-to-all-start = ((bf16[16,20,1024]{2,1,0:T(8,128)(2,1)}), bf16[16,20,1024]{2,1,0:T(8,128)(2,1)S(1)}, u32[]{:S(2)}, u32[]{:S(2)}) async-start(bf16[16,20,1024]{2,1,0:T(8,128)(2,1)} %copy.25), calls=%async_computation | async-start | bytes 1572864 | tf_op jit(solution)/shard_map/all_to_all | solution.py:300
  53.6 0.1 pad_add_fusion.1.base_ref
  53.7 32.8 %multiply_convert_fusion.1 = (bf16[1,2,320,1408]{3,2,0,1:T(8,128)(2,1)}, bf16[1,2,320,1408]{3,2,0,1:T(8,128)(2,1)}, bf16[1,2,320,1408]{3,2,0,1:T(8,128)(2,1)S(1)}, bf16[1,2,320,1408]{3,2,0,1:T(8,128)(2,1)}) fusion(s32[1408]{0:T(1024)S(1)} %iota_add_fusion, s32[2,320]{1,0:T(2,128)S(1)} %pad_add_fusion, f32[2,320]{1,0:T(2,128)S(1)} %get-tuple-element.18, ...), kind=kLoop, calls=%fused_computation.20 | loop fusion | flops 23429120 | bytes 7222272 | tf_op jit(solution)/shard_map/convert
  86.5 0.0 all-to-all-done
  86.5 4.9 %copy.26 = bf16[16,20,1024]{1,0,2:T(8,128)(2,1)} copy(bf16[16,20,1024]{2,1,0:T(8,128)(2,1)S(1)} %all-to-all-done) | data formatting | bytes 1310720 | tf_op jit(solution)/shard_map/all_to_all | solution.py:300
  91.4 7.1 %reshape.137 = bf16[320,8,32,2,2]{0,4,3,2,1:T(2,128)(2,1)S(1)} reshape(bf16[16,20,1024]{1,0,2:T(8,128)(2,1)} %copy.26) | data formatting | bytes 1310720 | tf_op jit(solution)/shard_map/reshape | solution.py:303
  98.5 0.0 copy-start.4
  98.5 3.3 %fusion.24 = bf16[32,8,1408]{2,0,1:T(8,128)(2,1)S(1)} fusion(bf16[1,2,320,1408]{3,2,0,1:T(8,128)(2,1)} %get-tuple-element.15, bf16[1,2,320,1408]{3,2,0,1:T(8,128)(2,1)} %get-tuple-element.14, bf16[320,8,32,2,2]{0,4,3,2,1:T(2,128)(2,1)S(1)} %reshape.137), kind=kOutput, calls=%fused_computation.36 | convolution fusion | flops 930316288 | bytes 4980736 | tf_op jit(solution)/shard_map/psfhr,rhpj->fsj/dot_general | solution.py:311
  101.9 0.0 copy-done.4
  101.9 1.2 fusion.25
  103.1 0.1 pad_maximum_fusion
  103.2 0.8 copy.29
  104.0 0.5 fusion.37
  104.5 4.0 %collective-permute-start.3 = (bf16[8,2,2,2816]{3,2,1,0:T(2,128)(2,1)S(1)}, bf16[8,2,2,2816]{3,2,1,0:T(2,128)(2,1)S(1)}, u32[]{:S(2)}, u32[]{:S(2)}) collective-permute-start(bf16[8,2,2,2816]{3,2,1,0:T(2,128)(2,1)S(1)} %get-tuple-element.6), channel_id=1, source_target_pairs={{2,0},{4,2},{6,4},{8,6},{10,8},{12,10},{14,12},{16,14},{18,16},{20... | collective-permute-start | bytes 540680 | tf_op jit(solution)/shard_map/ppermute | solution.py:243
  108.5 1.9 collective-permute-start.4
  110.4 0.1 fusion.36
  110.5 3.4 %collective-permute-start.1 = (bf16[8,2,2,2816]{3,2,1,0:T(2,128)(2,1)S(1)}, bf16[8,2,2,2816]{3,2,1,0:T(2,128)(2,1)S(1)}, u32[]{:S(2)}, u32[]{:S(2)}) collective-permute-start(bf16[8,2,2,2816]{3,2,1,0:T(2,128)(2,1)S(1)} %get-tuple-element.8), channel_id=1, source_target_pairs={{0,2},{2,4},{4,6},{6,8},{8,10},{10,12},{12,14},{14,16},{16,18},{18... | collective-permute-start | bytes 540680 | tf_op jit(solution)/shard_map/ppermute | solution.py:242
  113.9 3.7 %collective-permute-start = (bf16[8,2,2,2816]{3,2,1,0:T(2,128)(2,1)S(1)}, bf16[8,2,2,2816]{3,2,1,0:T(2,128)(2,1)S(1)}, u32[]{:S(2)}, u32[]{:S(2)}) collective-permute-start(bf16[8,2,2,2816]{3,2,1,0:T(2,128)(2,1)S(1)} %get-tuple-element.9), channel_id=1, source_target_pairs={{2,0},{4,2},{6,4},{8,6},{10,8},{12,10},{14,12},{16,14},{18,16},{20... | collective-permute-start | bytes 540680 | tf_op jit(solution)/shard_map/ppermute | solution.py:243
  117.6 0.0 collective-permute-done.3
  117.6 0.0 collective-permute-done.4
  117.6 0.2 fusion.30
  117.9 3.6 %collective-permute-start.5 = (bf16[2,2,12,2816]{3,2,1,0:T(8,128)(2,1)S(1)}, bf16[2,2,12,2816]{3,2,1,0:T(8,128)(2,1)S(1)}, u32[]{:S(2)}, u32[]{:S(2)}) collective-permute-start(bf16[2,2,12,2816]{3,2,1,0:T(8,128)(2,1)S(1)} %fusion.30), channel_id=1, source_target_pairs={{0,1},{1,0},{2,3},{3,2},{4,5},{5,4},{6,7},{7,6},{8,9},{9,8},{10,11... | collective-permute-start | bytes 811016 | tf_op jit(solution)/shard_map/ppermute | solution.py:252
  121.5 3.0 %collective-permute-done.1 = bf16[8,2,2,2816]{3,2,1,0:T(2,128)(2,1)S(1)} collective-permute-done((bf16[8,2,2,2816]{3,2,1,0:T(2,128)(2,1)S(1)}, bf16[8,2,2,2816]{3,2,1,0:T(2,128)(2,1)S(1)}, u32[]{:S(2)}, u32[]{:S(2)}) %collective-permute-start.1) | collective-permute-done | bytes 180256 | tf_op jit(solution)/shard_map/ppermute | solution.py:242
  124.6 0.0 collective-permute-done
  124.6 0.2 fusion.31
  124.8 1.3 collective-permute-start.2
  126.1 0.0 collective-permute-done.5
  126.1 0.1 broadcast_select_fusion.1
  126.2 1.1 collective-permute-done.2
  127.4 0.1 broadcast_select_fusion.3
  127.5 0.2 maximum_convert_fusion.center_ref
  127.7 0.0 copy-start
  127.7 0.0 copy-start.2
  127.7 0.2 maximum_convert_fusion.1.center_ref
  127.9 0.4 maximum_convert_fusion.3.edge_ref
  128.3 1.0 copy-done
  129.3 0.0 copy-done.2
  129.3 49.0 %shard_map.68.shift_ref = f32[2,8,8,2816]{3,2,1,0:T(8,128)} custom-call(s32[3]{0:T(128)S(1)} %pad_add_fusion.1.base_ref, f32[12,2,8,2816]{3,2,1,0:T(8,128)S(1)} %maximum_convert_fusion.1.center_ref, f32[12,2,4,2816]{3,2,1,0:T(4,128)S(1)} %maximum_convert_fusion.3.edge_ref, bf16[8,8,2816]{2,1,0:T(8,128)(2,1)S(1)} %copy-done.2, s32[3,8,8,2816]{3,2,1,0:T(8,128)S(1)} %copy-done), custom_call_target="tpu_custom_call" | custom-call | flops 90112000 | bytes 7208960 | tf_op jit(solution)/shard_map/pallas_call | solution.py:217
  178.3 0.0 copy-start.1
  178.3 0.4 maximum_convert_fusion.2.edge_ref
  178.7 1.0 copy-done.1
  179.7 45.0 %shard_map.69 = bf16[2,8,8,2816]{3,2,1,0:T(8,128)(2,1)} custom-call(s32[3]{0:T(128)S(1)} %pad_add_fusion.1.base_ref, f32[12,2,8,2816]{3,2,1,0:T(8,128)S(1)} %maximum_convert_fusion.center_ref, f32[12,2,4,2816]{3,2,1,0:T(4,128)S(1)} %maximum_convert_fusion.2.edge_ref, bf16[8,8,2816]{2,1,0:T(8,128)(2,1)S(1)} %copy-done.2, s32[3,8,8,2816]{3,2,1,0:T(8,128)} %cells_ref.3, ...), custom_call_target="tpu_custom_call" | custom-call | flops 90112000 | bytes 7208960 | tf_op jit(solution)/shard_map/pallas_call | solution.py:217
  (16 shorter events, 0.2 us)
Async XLA Ops:
  7.2 18.5 %all-gather.2.cloned.1.call-start = ((), (), s32[]{:S(2)}) async-start(), calls=%async_computation.1 | async-start | bytes 5898240 | tf_op jit(solution)/shard_map/all_gather | solution.py:298
  10.3 0.7 copy-start.6
  10.3 1.9 copy-start.5
  10.3 12.1 %copy-start.3 = (bf16[2,32,20,641]{3,1,2,0:T(8,128)(2,1)S(1)}, bf16[2,32,20,641]{3,1,2,0:T(8,128)(2,1)}, u32[]{:S(2)}) copy-start(bf16[2,32,20,641]{3,1,2,0:T(8,128)(2,1)} %param.5) | copy-start | bytes 4922884
  47.2 39.3 %all-to-all-start = ((bf16[16,20,1024]{2,1,0:T(8,128)(2,1)}), bf16[16,20,1024]{2,1,0:T(8,128)(2,1)S(1)}, u32[]{:S(2)}, u32[]{:S(2)}) async-start(bf16[16,20,1024]{2,1,0:T(8,128)(2,1)} %copy.25), calls=%async_computation | async-start | bytes 1572864 | tf_op jit(solution)/shard_map/all_to_all | solution.py:300
  98.5 3.4 %copy-start.4 = (bf16[1,2,320,1408]{3,2,0,1:T(8,128)(2,1)S(1)}, bf16[1,2,320,1408]{3,2,0,1:T(8,128)(2,1)}, u32[]{:S(2)}) copy-start(bf16[1,2,320,1408]{3,2,0,1:T(8,128)(2,1)} %get-tuple-element.17) | copy-start | bytes 5406724
  104.5 13.1 %collective-permute-start.3 = (bf16[8,2,2,2816]{3,2,1,0:T(2,128)(2,1)S(1)}, bf16[8,2,2,2816]{3,2,1,0:T(2,128)(2,1)S(1)}, u32[]{:S(2)}, u32[]{:S(2)}) collective-permute-start(bf16[8,2,2,2816]{3,2,1,0:T(2,128)(2,1)S(1)} %get-tuple-element.6), channel_id=1, source_target_pairs={{2,0},{4,2},{6,4},{8,6},{10,8},{12,10},{14,12},{16,14},{18,16},{20... | collective-permute-start | bytes 540680 | tf_op jit(solution)/shard_map/ppermute | solution.py:243
  108.5 9.1 %collective-permute-start.4 = (bf16[8,2,2,2816]{3,2,1,0:T(2,128)(2,1)S(1)}, bf16[8,2,2,2816]{3,2,1,0:T(2,128)(2,1)S(1)}, u32[]{:S(2)}, u32[]{:S(2)}) collective-permute-start(bf16[8,2,2,2816]{3,2,1,0:T(2,128)(2,1)S(1)} %get-tuple-element.7), channel_id=1, source_target_pairs={{0,2},{2,4},{4,6},{6,8},{8,10},{10,12},{12,14},{14,16},{16,18},{18... | collective-permute-start | bytes 540680 | tf_op jit(solution)/shard_map/ppermute | solution.py:242
  110.5 14.0 %collective-permute-start.1 = (bf16[8,2,2,2816]{3,2,1,0:T(2,128)(2,1)S(1)}, bf16[8,2,2,2816]{3,2,1,0:T(2,128)(2,1)S(1)}, u32[]{:S(2)}, u32[]{:S(2)}) collective-permute-start(bf16[8,2,2,2816]{3,2,1,0:T(2,128)(2,1)S(1)} %get-tuple-element.8), channel_id=1, source_target_pairs={{0,2},{2,4},{4,6},{6,8},{8,10},{10,12},{12,14},{14,16},{16,18},{18... | collective-permute-start | bytes 540680 | tf_op jit(solution)/shard_map/ppermute | solution.py:242
  113.9 10.7 %collective-permute-start = (bf16[8,2,2,2816]{3,2,1,0:T(2,128)(2,1)S(1)}, bf16[8,2,2,2816]{3,2,1,0:T(2,128)(2,1)S(1)}, u32[]{:S(2)}, u32[]{:S(2)}) collective-permute-start(bf16[8,2,2,2816]{3,2,1,0:T(2,128)(2,1)S(1)} %get-tuple-element.9), channel_id=1, source_target_pairs={{2,0},{4,2},{6,4},{8,6},{10,8},{12,10},{14,12},{16,14},{18,16},{20... | collective-permute-start | bytes 540680 | tf_op jit(solution)/shard_map/ppermute | solution.py:243
  117.9 8.2 %collective-permute-start.5 = (bf16[2,2,12,2816]{3,2,1,0:T(8,128)(2,1)S(1)}, bf16[2,2,12,2816]{3,2,1,0:T(8,128)(2,1)S(1)}, u32[]{:S(2)}, u32[]{:S(2)}) collective-permute-start(bf16[2,2,12,2816]{3,2,1,0:T(8,128)(2,1)S(1)} %fusion.30), channel_id=1, source_target_pairs={{0,1},{1,0},{2,3},{3,2},{4,5},{5,4},{6,7},{7,6},{8,9},{9,8},{10,11... | collective-permute-start | bytes 811016 | tf_op jit(solution)/shard_map/ppermute | solution.py:252
  124.8 2.6 %collective-permute-start.2 = (bf16[2,2,12,2816]{3,2,1,0:T(8,128)(2,1)S(1)}, bf16[2,2,12,2816]{3,2,1,0:T(8,128)(2,1)S(1)}, u32[]{:S(2)}, u32[]{:S(2)}) collective-permute-start(bf16[2,2,12,2816]{3,2,1,0:T(8,128)(2,1)S(1)} %fusion.31), channel_id=1, source_target_pairs={{0,1},{1,0},{2,3},{3,2},{4,5},{5,4},{6,7},{7,6},{8,9},{9,8},{10,11... | collective-permute-start | bytes 811016 | tf_op jit(solution)/shard_map/ppermute | solution.py:252
  127.7 1.6 copy-start
  127.7 1.6 copy-start.2
  178.3 1.4 copy-start.1
Sparse Core Ops, SparseCore 0:
  10.4 15.1 all-gather.1

commit v2 on v1

--- a/solution.py
+++ b/solution.py
@@ -66,59 +66,52 @@
     starts = [pl.multiple_of(c * LANES, LANES) for c in (before, chunk, after)]
     lane = lax.broadcasted_iota(jnp.int32, (rows, LANES), 1)
     edge_lane = lax.broadcasted_iota(jnp.int32, (2 * HALO, LANES), 1)
+    tall = 3 * rows
 
     def slab_step(slab, carry):
+        first = pl.multiple_of(slab * (5 * tall), 8)
         for field in range(field_count):
             blocks = [center_ref[slab, field, :, pl.ds(s, LANES)] for s in starts]
             for step, moved in enumerate(shifted_lanes(*blocks, lane)):
-                scratch[field, slab, step, rows : 2 * rows, :] = moved
+                scratch[field, pl.ds(first + (step * tall + rows), rows), :] = moved
             edges = [edge_ref[slab, field, :, pl.ds(s, LANES)] for s in starts]
             for step, moved in enumerate(shifted_lanes(*edges, edge_lane)):
-                scratch[field, slab, step, rows - 2 * HALO : rows, :] = moved
-                scratch[field, slab, step, 2 * rows : 2 * rows + 2 * HALO, :] = moved
+                top = first + (step * tall + rows - 2 * HALO)
+                scratch[field, pl.ds(top, 2 * HALO), :] = moved
+                scratch[field, pl.ds(first + (step * tall + 2 * rows), 2 * HALO), :] = moved
         return carry
 
     lax.fori_loop(0, slabs, slab_step, 0)
 
 
-def level_sums(scratch, field, k, zero, rows, weights, level_here, row_here, lon_here):
+def level_sum(scratch, field, base, rows, slot, weights, level_here, row_here, lon_here):
+    tall = 3 * rows
+
     def load(a, b, c):
-        return scratch[field, k + HALO + a, c + HALO, pl.ds(zero + (rows + b), rows), :]
-
-    def slab_slots(a):
-        out = {}
-        for c in (-1, 0, 1):
-            for b in (-1, 0, 1):
-                out[b, c] = load(a, b, c)
-            out[2, c] = jnp.where(row_here, load(a, 2, c), load(a, -2, c))
-        for b in (-1, 0, 1):
-            out[b, 2] = jnp.where(lon_here, load(a, b, 2), load(a, b, -2))
-        out[2, 2] = jnp.where(
-            row_here,
-            jnp.where(lon_here, load(a, 2, 2), load(a, 2, -2)),
-            jnp.where(lon_here, load(a, -2, 2), load(a, -2, -2)),
-        )
-        return out
-
-    slabs = [slab_slots(a) for a in (-1, 0, 1, 2, -2)]
-    return {
-        key: weighted(
-            weights,
-            (
-                slabs[0][key],
-                slabs[1][key],
-                slabs[2][key],
-                jnp.where(level_here, slabs[3][key], slabs[4][key]),
-            ),
-        )
-        for key in slabs[0]
-    }
+        offset = ((a + HALO) * 5 + c + HALO) * tall + rows + b
+        return scratch[field, pl.ds(base + offset, rows), :]
+
+    def pick_lon(a, b):
+        if slot[1] == 2:
+            return jnp.where(lon_here, load(a, b, 2), load(a, b, -2))
+        return load(a, b, slot[1])
+
+    def pick(a):
+        if slot[0] == 2:
+            return jnp.where(row_here, pick_lon(a, 2), pick_lon(a, -2))
+        return pick_lon(a, slot[0])
+
+    total = weights[0] * pick(-1) + weights[1] * pick(0)
+    total = total + weights[2] * pick(1)
+    return total + weights[3] * jnp.where(level_here, pick(2), pick(-2))
+
+
+SLOTS = (-1, 0, 1, 2)
 
 
 def across(sums, row_weights, lon_weights):
-    slots = (-1, 0, 1, 2)
     return weighted(
-        lon_weights, [weighted(row_weights, [sums[b, c] for b in slots]) for c in slots]
+        lon_weights, [weighted(row_weights, [sums(b, c) for b in SLOTS]) for c in SLOTS]
     )
 
 
@@ -134,7 +127,6 @@
 
 def wind_kernel(chunk_total, base_ref, center_ref, edge_ref, eta_ref, cells_ref, out_ref, scratch):
     levels, rows, width = eta_ref.shape
-    zero = base_ref[2]
 
     def chunk_step(part, carry):
         chunk = pl.program_id(0) * (width // LANES) + part
@@ -146,22 +138,28 @@
             weights = slot_weights(
                 -eta_ref[k, :, lanes].astype(jnp.float32), level_here, *bounds(level_here)
             )
+            base = k * (15 * rows)
             sums = [
-                level_sums(
-                    scratch, field, k, zero, rows, weights, level_here, row_here, lon_here
-                )
+                {
+                    (b, c): level_sum(
+                        scratch, field, base, rows, (b, c), weights, level_here, row_here, lon_here
+                    )
+                    for c in SLOTS
+                    for b in SLOTS
+                }
                 for field in range(2)
             ]
-            east = scratch[0, k + HALO, HALO, rows : 2 * rows, :]
-            north = scratch[1, k + HALO, HALO, rows : 2 * rows, :]
+            middle = (HALO * 5 + HALO) * 3 * rows + rows
+            east = scratch[0, pl.ds(base + middle, rows), :]
+            north = scratch[1, pl.ds(base + middle, rows), :]
             row_bounds, lon_bounds = bounds(row_here), bounds(lon_here)
             shift_row = COURANT * north
             shift_lon = COURANT * east
             for sweep in range(ITERS):
                 row_weights = slot_weights(-shift_row, row_here, *row_bounds)
                 lon_weights = slot_weights(-shift_lon, lon_here, *lon_bounds)
-                east_found = across(sums[0], row_weights, lon_weights)
-                north_found = across(sums[1], row_weights, lon_weights)
+                east_found = across(lambda b, c: sums[0][b, c], row_weights, lon_weights)
+                north_found = across(lambda b, c: sums[1][b, c], row_weights, lon_weights)
                 shift_row = 0.5 * COURANT * (north + north_found)
                 shift_lon = 0.5 * COURANT * (east + east_found)
             out_ref[0, k, :, lanes] = shift_row
@@ -178,7 +176,6 @@
     chunk_total, base_ref, center_ref, edge_ref, eta_ref, cells_ref, shift_ref, out_ref, scratch
 ):
     levels, rows, width = eta_ref.shape
-    zero = base_ref[2]
 
     def chunk_step(part, carry):
         chunk = pl.program_id(0) * (width // LANES) + part
@@ -192,10 +189,14 @@
             )
             row_weights = slot_weights(-shift_ref[0, k, :, lanes], row_here, *bounds(row_here))
             lon_weights = slot_weights(-shift_ref[1, k, :, lanes], lon_here, *bounds(lon_here))
+            base = k * (15 * rows)
             for field in range(2):
-                sums = level_sums(
-                    scratch, field, k, zero, rows, weights, level_here, row_here, lon_here
-                )
+
+                def sums(b, c, field=field):
+                    return level_sum(
+                        scratch, field, base, rows, (b, c), weights, level_here, row_here, lon_here
+                    )
+
                 found = across(sums, row_weights, lon_weights)
                 out_ref[field, k, :, lanes] = found.astype(out_ref.dtype)
             return inner
@@ -227,7 +228,7 @@
         ]
         + [pair] * len(extra),
         out_specs=pair,
-        scratch_shapes=[pltpu.VMEM((2, levels + 2 * HALO, 5, 3 * rows, LANES), jnp.float32)],
+        scratch_shapes=[pltpu.VMEM((2, (levels + 2 * HALO) * 15 * rows, LANES), jnp.float32)],
         compiler_params=pltpu.CompilerParams(vmem_limit_bytes=48 * 1024 * 1024),
         cost_estimate=pl.CostEstimate(
             flops=points * 500, bytes_accessed=points * 40, transcendentals=0
@@ -318,7 +319,6 @@
         [
             lax.axis_index("lev") * grid_shape[0],
             lax.axis_index("band") * grid_shape[1],
-            jnp.int32(0),
         ]
     ).astype(jnp.int32)
     winds = with_edges(fields[:, :2])

time: 233 us -> 230 us (0.987)
  Pallas kernels: 94 us -> 90.4 us
    pallas_call x2, Pallas kernels: 94 us -> 90.4 us  [interpolation_call(): pl.pallas_call(functools.partial(kernel, chunk_total), grid=(parts,), out...]
where the time goes in v2:
time: 230 us; the launch traced here: 228 us
  Pallas kernels  90.4 us (39%)
  other arithmetic  37 us (16%)
  local copies, waits for them, and re-layouts  35.2 us (15%)
  starting transfers between devices  24.4 us (11%)
  between operations  15 us (7%)
  matrix products  10.9 us (5%)
  blocking collectives  9.84 us (4%)
  waiting for transfers between devices  5.19 us (2%)
    pallas_call x2, Pallas kernels, interpolation_call(): pl.pallas_call(functools.partial(kernel, chunk_total), grid=(parts,), out...  90.4 us
    another operation x1, other arithmetic  32.8 us
    unnamed x1, blocking collectives  9.84 us
    convert_element_type x1, local copies, waits for them, and re-layouts, legendre_rows(): return jnp.einsum('scpk,hrfpk->cpsfhr', table, halves, preferred_element_...  9.55 us
    ppermute x2, starting transfers between devices, row_edges(): after = lax.ppermute(fields[:, :, :HALO], 'band', down)  7.76 us
    reshape x1, local copies, waits for them, and re-layouts, per_device(): spectral.reshape(all_pairs.shape[0], row_count, field_count, 2, 2)  7.13 us
    unnamed x18, local copies, waits for them, and re-layouts  6.52 us
    all_to_all x1, starting transfers between devices, per_device(): lax.all_to_all(local_sums, 'band', split_axis=0, concat_axis=1, tiled=True)  6.42 us
  transfers between devices with their start and end apart: 8, of which 3 were waited for; matrix products, arithmetic and copies ran while one was open for 16% of the time, Pallas kernels for 0%

profile of v2, /device:TPU:9, one launch (start us, length us, event | category | flops | bytes accessed | tf_op | source)
XLA Modules:
  0.0 228.0 jit_solution(1015266266031190916)
XLA Ops:
  7.2 0.0 all-gather.2.cloned.1.call-start
  7.2 3.1 %copy.23 = bf16[4,16,20,641]{3,1,0,2:T(8,128)(2,1)} copy(bf16[4,16,20,641]{3,1,2,0:T(8,128)(2,1)} %param.6) | data formatting | bytes 3281920 | tf_op args[1]
  10.3 0.0 copy-start.6
  10.3 0.0 copy-start.5
  10.3 0.0 copy-start.3
  10.3 0.0 all-gather.2.cloned.1.call-update
  10.3 0.6 copy-done.6
  10.9 0.6 dynamic-slice
  12.2 0.0 copy-done.5
  12.2 0.2 dynamic-update-slice
  12.4 9.8 %all-reduce = s32[320]{0:T(512)S(1)} all-reduce(s32[320]{0:T(512)S(1)} %dynamic-update-slice), channel_id=1, replica_groups=mesh['band'=16,'lev'=2] {'band'}, use_global_device_ids=true, to_apply=%add | all-reduce | flops 320 | bytes 2560
  22.3 0.1 iota_compare_fusion
  22.4 0.0 copy-done.3
  22.4 2.2 select_bitcast_fusion.1
  24.6 1.0 all-gather.2.cloned.1.call-done
  25.6 6.4 %convert_bitcast_fusion = bf16[16,20,8,32,2,2]{3,0,2,5,4,1:T(8,128)(2,1)S(1)} fusion(bf16[8,16,20,641]{3,1,0,2:T(8,128)(2,1)} %all-gather.2.cloned.1.call-done, bf16[1,2,32,20,641]{4,2,1,0,3:T(8,128)(2,1)} %get-tuple-element.3, bf16[1,2,32,20,641]{4,2,1,0,3:T(8,128)(2,1)} %get-tuple-element.2), kind=kOutput, calls=%fused_computation.33 | convolution fusion | flops 426977280 | bytes 7219200 | tf_op jit(solution)/shard_map/scpk,hrfpk->cpsfhr/dot_general | solution.py:290
  32.0 9.5 %copy.24 = bf16[16,20,8,32,2,2]{1,0,5,4,3,2:T(8,128)(2,1)} copy(bf16[16,20,8,32,2,2]{3,0,2,5,4,1:T(8,128)(2,1)S(1)} %convert_bitcast_fusion) | data formatting | bytes 1310720 | tf_op jit(solution)/shard_map/convert_element_type | solution.py:292
  41.6 5.6 %copy.25 = bf16[16,20,1024]{2,1,0:T(8,128)(2,1)} copy(bf16[16,20,1024]{1,0,2:T(8,128)(2,1)} %bitcast.71) | data formatting | bytes 1310720 | tf_op jit(solution)/shard_map/reshape | solution.py:300
  47.2 6.4 %all-to-all-start = ((bf16[16,20,1024]{2,1,0:T(8,128)(2,1)}), bf16[16,20,1024]{2,1,0:T(8,128)(2,1)S(1)}, u32[]{:S(2)}, u32[]{:S(2)}) async-start(bf16[16,20,1024]{2,1,0:T(8,128)(2,1)} %copy.25), calls=%async_computation | async-start | bytes 1572864 | tf_op jit(solution)/shard_map/all_to_all | solution.py:301
  53.6 0.1 pad_add_fusion.1.base_ref
  53.7 32.8 %multiply_convert_fusion.1 = (bf16[1,2,320,1408]{3,2,0,1:T(8,128)(2,1)}, bf16[1,2,320,1408]{3,2,0,1:T(8,128)(2,1)}, bf16[1,2,320,1408]{3,2,0,1:T(8,128)(2,1)S(1)}, bf16[1,2,320,1408]{3,2,0,1:T(8,128)(2,1)}) fusion(s32[1408]{0:T(1024)S(1)} %iota_add_fusion, s32[2,320]{1,0:T(2,128)S(1)} %pad_add_fusion, f32[2,320]{1,0:T(2,128)S(1)} %get-tuple-element.18, ...), kind=kLoop, calls=%fused_computation.20 | loop fusion | flops 23429120 | bytes 7222272 | tf_op jit(solution)/shard_map/convert
  86.5 0.0 all-to-all-done
  86.5 4.9 %copy.26 = bf16[16,20,1024]{1,0,2:T(8,128)(2,1)} copy(bf16[16,20,1024]{2,1,0:T(8,128)(2,1)S(1)} %all-to-all-done) | data formatting | bytes 1310720 | tf_op jit(solution)/shard_map/all_to_all | solution.py:301
  91.4 7.1 %reshape.137 = bf16[320,8,32,2,2]{0,4,3,2,1:T(2,128)(2,1)S(1)} reshape(bf16[16,20,1024]{1,0,2:T(8,128)(2,1)} %copy.26) | data formatting | bytes 1310720 | tf_op jit(solution)/shard_map/reshape | solution.py:304
  98.5 0.0 copy-start.4
  98.5 3.3 %fusion.24 = bf16[32,8,1408]{2,0,1:T(8,128)(2,1)S(1)} fusion(bf16[1,2,320,1408]{3,2,0,1:T(8,128)(2,1)} %get-tuple-element.15, bf16[1,2,320,1408]{3,2,0,1:T(8,128)(2,1)} %get-tuple-element.14, bf16[320,8,32,2,2]{0,4,3,2,1:T(2,128)(2,1)S(1)} %reshape.137), kind=kOutput, calls=%fused_computation.36 | convolution fusion | flops 930316288 | bytes 4980736 | tf_op jit(solution)/shard_map/psfhr,rhpj->fsj/dot_general | solution.py:312
  101.9 0.0 copy-done.4
  101.9 1.2 fusion.25
  103.1 0.1 pad_maximum_fusion
  103.2 0.8 copy.29
  104.0 0.5 fusion.37
  104.5 4.0 %collective-permute-start.3 = (bf16[8,2,2,2816]{3,2,1,0:T(2,128)(2,1)S(1)}, bf16[8,2,2,2816]{3,2,1,0:T(2,128)(2,1)S(1)}, u32[]{:S(2)}, u32[]{:S(2)}) collective-permute-start(bf16[8,2,2,2816]{3,2,1,0:T(2,128)(2,1)S(1)} %get-tuple-element.6), channel_id=1, source_target_pairs={{2,0},{4,2},{6,4},{8,6},{10,8},{12,10},{14,12},{16,14},{18,16},{20... | collective-permute-start | bytes 540680 | tf_op jit(solution)/shard_map/ppermute | solution.py:244
  108.5 1.9 collective-permute-start.4
  110.4 0.1 fusion.36
  110.6 3.3 %collective-permute-start.1 = (bf16[8,2,2,2816]{3,2,1,0:T(2,128)(2,1)S(1)}, bf16[8,2,2,2816]{3,2,1,0:T(2,128)(2,1)S(1)}, u32[]{:S(2)}, u32[]{:S(2)}) collective-permute-start(bf16[8,2,2,2816]{3,2,1,0:T(2,128)(2,1)S(1)} %get-tuple-element.8), channel_id=1, source_target_pairs={{0,2},{2,4},{4,6},{6,8},{8,10},{10,12},{12,14},{14,16},{16,18},{18... | collective-permute-start | bytes 540680 | tf_op jit(solution)/shard_map/ppermute | solution.py:243
  113.9 3.7 %collective-permute-start = (bf16[8,2,2,2816]{3,2,1,0:T(2,128)(2,1)S(1)}, bf16[8,2,2,2816]{3,2,1,0:T(2,128)(2,1)S(1)}, u32[]{:S(2)}, u32[]{:S(2)}) collective-permute-start(bf16[8,2,2,2816]{3,2,1,0:T(2,128)(2,1)S(1)} %get-tuple-element.9), channel_id=1, source_target_pairs={{2,0},{4,2},{6,4},{8,6},{10,8},{12,10},{14,12},{16,14},{18,16},{20... | collective-permute-start | bytes 540680 | tf_op jit(solution)/shard_map/ppermute | solution.py:244
  117.6 0.0 collective-permute-done.3
  117.7 0.0 collective-permute-done.4
  117.7 0.2 fusion.30
  117.9 3.6 %collective-permute-start.5 = (bf16[2,2,12,2816]{3,2,1,0:T(8,128)(2,1)S(1)}, bf16[2,2,12,2816]{3,2,1,0:T(8,128)(2,1)S(1)}, u32[]{:S(2)}, u32[]{:S(2)}) collective-permute-start(bf16[2,2,12,2816]{3,2,1,0:T(8,128)(2,1)S(1)} %fusion.30), channel_id=1, source_target_pairs={{0,1},{1,0},{2,3},{3,2},{4,5},{5,4},{6,7},{7,6},{8,9},{9,8},{10,11... | collective-permute-start | bytes 811016 | tf_op jit(solution)/shard_map/ppermute | solution.py:253
  121.6 3.0 %collective-permute-done.1 = bf16[8,2,2,2816]{3,2,1,0:T(2,128)(2,1)S(1)} collective-permute-done((bf16[8,2,2,2816]{3,2,1,0:T(2,128)(2,1)S(1)}, bf16[8,2,2,2816]{3,2,1,0:T(2,128)(2,1)S(1)}, u32[]{:S(2)}, u32[]{:S(2)}) %collective-permute-start.1) | collective-permute-done | bytes 180256 | tf_op jit(solution)/shard_map/ppermute | solution.py:243
  124.6 0.0 collective-permute-done
  124.6 0.2 fusion.31
  124.8 1.2 collective-permute-start.2
  126.0 0.0 collective-permute-done.5
  126.1 0.1 broadcast_select_fusion.1
  126.2 1.1 collective-permute-done.2
  127.4 0.1 broadcast_select_fusion.3
  127.5 0.2 maximum_convert_fusion.center_ref
  127.7 0.0 copy-start
  127.7 0.0 copy-start.2
  127.7 0.2 maximum_convert_fusion.1.center_ref
  127.9 0.4 maximum_convert_fusion.3.edge_ref
  128.3 1.0 copy-done
  129.3 0.0 copy-done.2
  129.3 47.3 %shard_map.68.shift_ref = f32[2,8,8,2816]{3,2,1,0:T(8,128)} custom-call(s32[2]{0:T(128)S(1)} %pad_add_fusion.1.base_ref, f32[12,2,8,2816]{3,2,1,0:T(8,128)S(1)} %maximum_convert_fusion.1.center_ref, f32[12,2,4,2816]{3,2,1,0:T(4,128)S(1)} %maximum_convert_fusion.3.edge_ref, bf16[8,8,2816]{2,1,0:T(8,128)(2,1)S(1)} %copy-done.2, s32[3,8,8,2816]{3,2,1,0:T(8,128)S(1)} %copy-done), custom_call_target="tpu_custom_call" | custom-call | flops 90112000 | bytes 7208960 | tf_op jit(solution)/shard_map/pallas_call | solution.py:218
  176.6 0.0 copy-start.1
  176.6 0.4 maximum_convert_fusion.2.edge_ref
  177.0 1.0 copy-done.1
  178.0 43.1 %shard_map.69 = bf16[2,8,8,2816]{3,2,1,0:T(8,128)(2,1)} custom-call(s32[2]{0:T(128)S(1)} %pad_add_fusion.1.base_ref, f32[12,2,8,2816]{3,2,1,0:T(8,128)S(1)} %maximum_convert_fusion.center_ref, f32[12,2,4,2816]{3,2,1,0:T(4,128)S(1)} %maximum_convert_fusion.2.edge_ref, bf16[8,8,2816]{2,1,0:T(8,128)(2,1)S(1)} %copy-done.2, s32[3,8,8,2816]{3,2,1,0:T(8,128)} %cells_ref.3, ...), custom_call_target="tpu_custom_call" | custom-call | flops 90112000 | bytes 7208960 | tf_op jit(solution)/shard_map/pallas_call | solution.py:218
  (16 shorter events, 0.2 us)
Async XLA Ops:
  7.2 18.5 %all-gather.2.cloned.1.call-start = ((), (), s32[]{:S(2)}) async-start(), calls=%async_computation.1 | async-start | bytes 5898240 | tf_op jit(solution)/shard_map/all_gather | solution.py:299
  10.3 0.7 copy-start.6
  10.3 1.9 copy-start.5
  10.3 12.1 %copy-start.3 = (bf16[2,32,20,641]{3,1,2,0:T(8,128)(2,1)S(1)}, bf16[2,32,20,641]{3,1,2,0:T(8,128)(2,1)}, u32[]{:S(2)}) copy-start(bf16[2,32,20,641]{3,1,2,0:T(8,128)(2,1)} %param.5) | copy-start | bytes 4922884
  47.2 39.3 %all-to-all-start = ((bf16[16,20,1024]{2,1,0:T(8,128)(2,1)}), bf16[16,20,1024]{2,1,0:T(8,128)(2,1)S(1)}, u32[]{:S(2)}, u32[]{:S(2)}) async-start(bf16[16,20,1024]{2,1,0:T(8,128)(2,1)} %copy.25), calls=%async_computation | async-start | bytes 1572864 | tf_op jit(solution)/shard_map/all_to_all | solution.py:301
  98.5 3.4 %copy-start.4 = (bf16[1,2,320,1408]{3,2,0,1:T(8,128)(2,1)S(1)}, bf16[1,2,320,1408]{3,2,0,1:T(8,128)(2,1)}, u32[]{:S(2)}) copy-start(bf16[1,2,320,1408]{3,2,0,1:T(8,128)(2,1)} %get-tuple-element.17) | copy-start | bytes 5406724
  104.5 13.2 %collective-permute-start.3 = (bf16[8,2,2,2816]{3,2,1,0:T(2,128)(2,1)S(1)}, bf16[8,2,2,2816]{3,2,1,0:T(2,128)(2,1)S(1)}, u32[]{:S(2)}, u32[]{:S(2)}) collective-permute-start(bf16[8,2,2,2816]{3,2,1,0:T(2,128)(2,1)S(1)} %get-tuple-element.6), channel_id=1, source_target_pairs={{2,0},{4,2},{6,4},{8,6},{10,8},{12,10},{14,12},{16,14},{18,16},{20... | collective-permute-start | bytes 540680 | tf_op jit(solution)/shard_map/ppermute | solution.py:244
  108.5 9.1 %collective-permute-start.4 = (bf16[8,2,2,2816]{3,2,1,0:T(2,128)(2,1)S(1)}, bf16[8,2,2,2816]{3,2,1,0:T(2,128)(2,1)S(1)}, u32[]{:S(2)}, u32[]{:S(2)}) collective-permute-start(bf16[8,2,2,2816]{3,2,1,0:T(2,128)(2,1)S(1)} %get-tuple-element.7), channel_id=1, source_target_pairs={{0,2},{2,4},{4,6},{6,8},{8,10},{10,12},{12,14},{14,16},{16,18},{18... | collective-permute-start | bytes 540680 | tf_op jit(solution)/shard_map/ppermute | solution.py:243
  110.6 14.0 %collective-permute-start.1 = (bf16[8,2,2,2816]{3,2,1,0:T(2,128)(2,1)S(1)}, bf16[8,2,2,2816]{3,2,1,0:T(2,128)(2,1)S(1)}, u32[]{:S(2)}, u32[]{:S(2)}) collective-permute-start(bf16[8,2,2,2816]{3,2,1,0:T(2,128)(2,1)S(1)} %get-tuple-element.8), channel_id=1, source_target_pairs={{0,2},{2,4},{4,6},{6,8},{8,10},{10,12},{12,14},{14,16},{16,18},{18... | collective-permute-start | bytes 540680 | tf_op jit(solution)/shard_map/ppermute | solution.py:243
  113.9 10.7 %collective-permute-start = (bf16[8,2,2,2816]{3,2,1,0:T(2,128)(2,1)S(1)}, bf16[8,2,2,2816]{3,2,1,0:T(2,128)(2,1)S(1)}, u32[]{:S(2)}, u32[]{:S(2)}) collective-permute-start(bf16[8,2,2,2816]{3,2,1,0:T(2,128)(2,1)S(1)} %get-tuple-element.9), channel_id=1, source_target_pairs={{2,0},{4,2},{6,4},{8,6},{10,8},{12,10},{14,12},{16,14},{18,16},{20... | collective-permute-start | bytes 540680 | tf_op jit(solution)/shard_map/ppermute | solution.py:244
  117.9 8.1 %collective-permute-start.5 = (bf16[2,2,12,2816]{3,2,1,0:T(8,128)(2,1)S(1)}, bf16[2,2,12,2816]{3,2,1,0:T(8,128)(2,1)S(1)}, u32[]{:S(2)}, u32[]{:S(2)}) collective-permute-start(bf16[2,2,12,2816]{3,2,1,0:T(8,128)(2,1)S(1)} %fusion.30), channel_id=1, source_target_pairs={{0,1},{1,0},{2,3},{3,2},{4,5},{5,4},{6,7},{7,6},{8,9},{9,8},{10,11... | collective-permute-start | bytes 811016 | tf_op jit(solution)/shard_map/ppermute | solution.py:253
  124.8 2.5 %collective-permute-start.2 = (bf16[2,2,12,2816]{3,2,1,0:T(8,128)(2,1)S(1)}, bf16[2,2,12,2816]{3,2,1,0:T(8,128)(2,1)S(1)}, u32[]{:S(2)}, u32[]{:S(2)}) collective-permute-start(bf16[2,2,12,2816]{3,2,1,0:T(8,128)(2,1)S(1)} %fusion.31), channel_id=1, source_target_pairs={{0,1},{1,0},{2,3},{3,2},{4,5},{5,4},{6,7},{7,6},{8,9},{9,8},{10,11... | collective-permute-start | bytes 811016 | tf_op jit(solution)/shard_map/ppermute | solution.py:253
  127.7 1.6 copy-start
  127.7 1.6 copy-start.2
  176.6 1.4 copy-start.1
Sparse Core Ops, SparseCore 0:
  10.4 15.1 all-gather.1

commit v3 on v2

v3 whole, which is shorter than its diff:
```python
import functools
import math

import jax
import jax.numpy as jnp
import numpy as np
from jax import lax
from jax.experimental import pallas as pl
from jax.experimental.pallas import tpu as pltpu
from jax.sharding import PartitionSpec as P

ITERS = 2


COURANT = 0.8
HALO = 2
LANES = 128
ROWS = 8
SLOTS = (-1, 0, 1, 2)


def slot_weights(place, here, low, high, sixth):
    z = jnp.minimum(jnp.maximum(place, low), high)
    square = z * z
    less = square - 1.0
    outer = less * z * sixth
    triple = 3.0 * outer
    half = 0.5 * z
    half_square = 0.5 * square
    return (
        half_square - half - jnp.where(here, outer, triple),
        triple - less,
        half_square + half - jnp.where(here, triple, outer),
        outer,
    )


def bounds(here):
    return (
        jnp.where(here, -0.5, -1.5),
        jnp.where(here, 1.5, 0.5),
        jnp.where(here, 1.0 / 6.0, -1.0 / 6.0),
    )


def weighted(weights, values):
    return (weights[0] * values[0] + weights[1] * values[1]) + (
        weights[2] * values[2] + weights[3] * values[3]
    )


def shifted_lanes(before, here, after, lane):
    return (
        jnp.where(lane < 2, pltpu.roll(before, 2, 1), pltpu.roll(here, 2, 1)),
        jnp.where(lane < 1, pltpu.roll(before, 1, 1), pltpu.roll(here, 1, 1)),
        here,
        jnp.where(lane < LANES - 1, pltpu.roll(here, LANES - 1, 1), pltpu.roll(after, LANES - 1, 1)),
        jnp.where(lane < LANES - 2, pltpu.roll(here, LANES - 2, 1), pltpu.roll(after, LANES - 2, 1)),
    )


def fill(slab, chunk, chunk_total, center_ref, edge_ref, scratch):
    field_count, _, rows, _ = center_ref.shape
    before = jnp.where(chunk == 0, chunk_total - 1, chunk - 1)
    after = jnp.where(chunk == chunk_total - 1, 0, chunk + 1)
    starts = [pl.multiple_of(c * LANES, LANES) for c in (before, chunk, after)]
    lane = lax.broadcasted_iota(jnp.int32, (rows, LANES), 1)
    edge_lane = lax.broadcasted_iota(jnp.int32, (2 * HALO, LANES), 1)
    tall = 3 * rows
    first = pl.multiple_of(slab * (5 * tall), 8)
    for field in range(field_count):
        blocks = [center_ref[field, slab, :, pl.ds(s, LANES)] for s in starts]
        for step, moved in enumerate(shifted_lanes(*blocks, lane)):
            scratch[field, pl.ds(first + (step * tall + rows), rows), :] = moved
        edges = [edge_ref[field, slab, :, pl.ds(s, LANES)] for s in starts]
        for step, moved in enumerate(shifted_lanes(*edges, edge_lane)):
            top = first + (step * tall + rows - 2 * HALO)
            scratch[field, pl.ds(top, 2 * HALO), :] = moved
            scratch[field, pl.ds(first + (step * tall + 2 * rows), 2 * HALO), :] = moved


def level_sums(scratch, field, base, rows, slot, points):
    tall = 3 * rows
    loaded = {}

    def load(a, b, c):
        if (a, b, c) not in loaded:
            offset = ((a + HALO) * 5 + c + HALO) * tall + rows + b
            loaded[a, b, c] = scratch[field, pl.ds(base + offset, rows), :]
        return loaded[a, b, c]

    def one(step, weights, level_here, row_here, lon_here):
        def pick_lon(a, b):
            if slot[1] == 2:
                return jnp.where(lon_here, load(a + step, b, 2), load(a + step, b, -2))
            return load(a + step, b, slot[1])

        def pick(a):
            if slot[0] == 2:
                return jnp.where(row_here, pick_lon(a, 2), pick_lon(a, -2))
            return pick_lon(a, slot[0])

        total = weights[0] * pick(-1) + weights[1] * pick(0)
        total = total + weights[2] * pick(1)
        return total + weights[3] * jnp.where(level_here, pick(2), pick(-2))

    return [one(step, *point) for step, point in enumerate(points)]


def across(sums, row_weights, lon_weights):
    return weighted(
        lon_weights, [weighted(row_weights, [sums[b, c] for b in SLOTS]) for c in SLOTS]
    )


def arrival(base_ref, eta_ref, cells_ref, k, chunk, lanes):
    shape = (cells_ref.shape[2], LANES)
    level_here = cells_ref[2, k, :, lanes] == base_ref[0] + k
    row_here = cells_ref[0, k, :, lanes] == base_ref[1] + lax.broadcasted_iota(jnp.int32, shape, 0)
    lon_here = cells_ref[1, k, :, lanes] == chunk * LANES + lax.broadcasted_iota(
        jnp.int32, shape, 1
    )
    weights = slot_weights(
        -eta_ref[k, :, lanes].astype(jnp.float32), level_here, *bounds(level_here)
    )
    return weights, level_here, row_here, lon_here


def wind_levels(base, lanes, k, points, scratch, out_ref):
    rows = out_ref.shape[2]
    for step, point in enumerate(points):
        here = base + step * (15 * rows)
        sums = [
            {
                (b, c): level_sums(scratch, field, here, rows, (b, c), [point])[0]
                for c in SLOTS
                for b in SLOTS
            }
            for field in range(2)
        ]
        middle = (HALO * 5 + HALO) * 3 * rows + rows
        east = scratch[0, pl.ds(here + middle, rows), :]
        north = scratch[1, pl.ds(here + middle, rows), :]
        _, _, row_here, lon_here = point
        row_bounds, lon_bounds = bounds(row_here), bounds(lon_here)
        shift_row = COURANT * north
        shift_lon = COURANT * east
        for sweep in range(ITERS):
            row_weights = slot_weights(-shift_row, row_here, *row_bounds)
            lon_weights = slot_weights(-shift_lon, lon_here, *lon_bounds)
            east_found = across(sums[0], row_weights, lon_weights)
            north_found = across(sums[1], row_weights, lon_weights)
            shift_row = 0.5 * COURANT * (north + north_found)
            shift_lon = 0.5 * COURANT * (east + east_found)
        out_ref[0, k + step, :, lanes] = shift_row
        out_ref[1, k + step, :, lanes] = shift_lon


def tracer_levels(shift_ref, base, lanes, k, points, scratch, out_ref):
    rows = out_ref.shape[2]
    row_weights = []
    lon_weights = []
    for step, (_, _, row_here, lon_here) in enumerate(points):
        row_weights.append(
            slot_weights(-shift_ref[0, k + step, :, lanes], row_here, *bounds(row_here))
        )
        lon_weights.append(
            slot_weights(-shift_ref[1, k + step, :, lanes], lon_here, *bounds(lon_here))
        )
    for field in range(2):
        totals = [None] * len(points)
        for c, lon_slot in enumerate(SLOTS):
            columns = [None] * len(points)
            for b, row_slot in enumerate(SLOTS):
                found = level_sums(scratch, field, base, rows, (row_slot, lon_slot), points)
                for step, value in enumerate(found):
                    term = row_weights[step][b] * value
                    columns[step] = term if b == 0 else columns[step] + term
            for step, column in enumerate(columns):
                term = lon_weights[step][c] * column
                totals[step] = term if c == 0 else totals[step] + term
        for step, total in enumerate(totals):
            out_ref[field, k + step, :, lanes] = total.astype(out_ref.dtype)


def interpolation_kernel(
    levels_body, base_ref, center_ref, edge_ref, eta_ref, cells_ref, *others
):
    extra, (out_ref, even_scratch, odd_scratch) = others[:-3], others[-3:]
    levels, rows, lon_total = eta_ref.shape
    chunk_total = lon_total // LANES
    slabs = levels + 2 * HALO
    together = 2 if levels % 2 == 0 and slabs % (levels // 2) == 0 else 1
    steps = levels // together
    per_step = -(-slabs // steps)
    source = (center_ref, edge_ref)

    def first_fill(slab, carry):
        fill(slab, 0, chunk_total, *source, even_scratch)
        return carry

    lax.fori_loop(0, slabs, first_fill, 0)

    def one_chunk(chunk, scratch, other):
        lanes = pl.ds(pl.multiple_of(chunk * LANES, LANES), LANES)
        following = jnp.where(chunk == chunk_total - 1, 0, chunk + 1)

        def level_step(step, carry):
            k = step * together
            for n in range(per_step):
                slab = jnp.minimum(step * per_step + n, slabs - 1)
                fill(slab, following, chunk_total, *source, other)
            points = [
                arrival(base_ref, eta_ref, cells_ref, k + n, chunk, lanes) for n in range(together)
            ]
            levels_body(*extra, k * (15 * rows), lanes, k, points, scratch, out_ref)
            return carry

        lax.fori_loop(0, steps, level_step, 0)

    def chunk_pair(pair, carry):
        one_chunk(2 * pair, even_scratch, odd_scratch)
        one_chunk(2 * pair + 1, odd_scratch, even_scratch)
        return carry

    lax.fori_loop(0, chunk_total // 2, chunk_pair, 0)


def interpolation_call(levels_body, base, center, edge, eta_shift, cells, extra, out_dtype):
    levels, rows, lon_total = eta_shift.shape
    points = levels * rows * lon_total
    scratch = pltpu.VMEM((2, (levels + 2 * HALO) * 15 * rows, LANES), jnp.float32)
    in_vmem = pl.BlockSpec(memory_space=pltpu.VMEM)
    return pl.pallas_call(
        functools.partial(interpolation_kernel, levels_body),
        out_shape=jax.ShapeDtypeStruct((2, levels, rows, lon_total), out_dtype),
        in_specs=[pl.BlockSpec(memory_space=pltpu.SMEM)] + [in_vmem] * (4 + len(extra)),
        out_specs=in_vmem,
        scratch_shapes=[scratch, scratch],
        compiler_params=pltpu.CompilerParams(vmem_limit_bytes=32 * 1024 * 1024),
        cost_estimate=pl.CostEstimate(
            flops=points * 500, bytes_accessed=points * 40, transcendentals=0
        ),
    )(base, center, edge, eta_shift, cells, *extra)


def row_edges(fields):
    size = lax.axis_size("band")
    up = [(i, (i + 1) % size) for i in range(size - 1)]
    down = [(j, i) for i, j in up]
    rows = fields.shape[2]
    before = lax.ppermute(fields[:, :, rows - HALO :].astype(jnp.bfloat16), "band", up)
    after = lax.ppermute(fields[:, :, :HALO].astype(jnp.bfloat16), "band", down)
    return jnp.concatenate([after, before], axis=2)


def level_edges(array):
    size, count = (lax.axis_size("lev"), array.shape[1])
    last, first = (array[:, count - HALO :], array[:, :HALO])
    if size == 2:
        at_top = lax.axis_index("lev") == 0
        found = lax.ppermute(jnp.where(at_top, last, first), "lev", [(0, 1), (1, 0)])
        nothing = jnp.zeros_like(found)
        return jnp.where(at_top, nothing, found), jnp.where(at_top, found, nothing)
    up = [(i, i + 1) for i in range(size - 1)]
    down = [(j, i) for i, j in up]
    return lax.ppermute(last, "lev", up), lax.ppermute(first, "lev", down)


def with_edges(fields):
    rows = fields.shape[2]
    edge = row_edges(fields)
    both = jnp.concatenate([fields.astype(jnp.bfloat16), edge], axis=2)
    before, after = level_edges(both)
    center = jnp.concatenate(
        [
            before[:, :, :rows].astype(jnp.float32),
            fields,
            after[:, :, :rows].astype(jnp.float32),
        ],
        axis=1,
    )
    edge = jnp.concatenate([before[:, :, rows:], edge, after[:, :, rows:]], axis=1)
    return center, edge.astype(jnp.float32)


def up_to(value, step):
    return -(-value // step) * step


def legendre_kernel(pairing_ref, spectra_ref, table_ref, out_ref, columns, rows_here):
    _, level_fields, pairs, degrees = spectra_ref.shape
    bands = table_ref.shape[1]
    levels = level_fields // 4
    order = degrees - 1
    padded = columns.shape[1] // (2 * level_fields)
    blocks = columns.shape[0]
    full = degrees // LANES
    columns[blocks - 1] = jnp.zeros(columns.shape[1:], jnp.float32)
    rows_here[blocks - 1] = jnp.zeros(rows_here.shape[1:], jnp.float32)

    def spread(block, target, position):
        first = pl.multiple_of(position * padded, 8)
        for t in range(full):
            piece = block[:, t * LANES : (t + 1) * LANES].astype(jnp.float32)
            target[t, pl.ds(first, pairs), :] = piece
        rest = degrees - full * LANES
        if rest:
            piece = block[:, full * LANES :].astype(jnp.float32)
            target[full, pl.ds(first, pairs), :rest] = piece

    def spectra_step(level, carry):
        for part in range(2):
            for field in range(4):
                position = part * level_fields + field * levels + level
                spread(spectra_ref[part, 4 * level + field], columns, position)
        return carry

    def table_step(band, carry):
        for row in range(ROWS):
            spread(table_ref[row, band], rows_here, band * ROWS + row)
        return carry

    lax.fori_loop(0, levels, spectra_step, 0)
    lax.fori_loop(0, bands, table_step, 0)
    count = 2 * level_fields
    width = out_ref.shape[3]
    if width > 2 * count:
        out_ref[...] = jnp.zeros(out_ref.shape, out_ref.dtype)

    def pair_step(p, carry):
        edge = order - pairing_ref[p]
        left = []
        first_half = []
        second_half = []
        for t in range(blocks):
            left.append(rows_here[t, pl.ds(p, bands * ROWS, stride=padded), :].astype(jnp.bfloat16))
            block = columns[t, pl.ds(p, count, stride=padded), :]
            lane = lax.broadcasted_iota(jnp.int32, block.shape, 1) + t * LANES
            zero = jnp.zeros_like(block)
            first_half.append(jnp.where(lane < edge, block, zero).astype(jnp.bfloat16))
            second_half.append(jnp.where(lane < edge, zero, block).astype(jnp.bfloat16))
        halves = jnp.concatenate(
            [jnp.concatenate(first_half, axis=1), jnp.concatenate(second_half, axis=1)], axis=0
        )
        sums = lax.dot_general(
            jnp.concatenate(left, axis=1),
            halves,
            (((1,), (1,)), ((), ())),
            preferred_element_type=jnp.float32,
        )
        sums = sums.astype(jnp.bfloat16).reshape(bands, ROWS, 2 * count)
        out_ref[:, p, :, : 2 * count] = sums
        return carry

    lax.fori_loop(0, pairs, pair_step, 0)


def legendre_call(pairing, spectra, table):
    _, level_fields, pairs, degrees = spectra.shape
    bands = table.shape[1]
    padded = up_to(pairs, 8)
    blocks = up_to(degrees, LANES) // LANES
    width = up_to(4 * level_fields, LANES)
    in_vmem = pl.BlockSpec(memory_space=pltpu.VMEM)
    return pl.pallas_call(
        legendre_kernel,
        out_shape=jax.ShapeDtypeStruct((bands, pairs, ROWS, width), jnp.bfloat16),
        in_specs=[pl.BlockSpec(memory_space=pltpu.SMEM), in_vmem, in_vmem],
        out_specs=in_vmem,
        scratch_shapes=[
            pltpu.VMEM((blocks, 2 * level_fields * padded, LANES), jnp.float32),
            pltpu.VMEM((blocks, ROWS * bands * padded, LANES), jnp.float32),
        ],
        compiler_params=pltpu.CompilerParams(vmem_limit_bytes=48 * 1024 * 1024),
        cost_estimate=pl.CostEstimate(
            flops=2 * ROWS * bands * 4 * level_fields * pairs * degrees,
            bytes_accessed=8_000_000,
            transcendentals=0,
        ),
    )(pairing, spectra, table)


def fourier_table(pair_total, padded, lon_total):
    order_total = 2 * pair_total
    half = pair_total // 2
    low = 2 * np.arange(half)
    high = low + 1
    even = np.concatenate([low, order_total - 1 - high])
    odd = np.concatenate([order_total - 1 - low, high])
    lon = np.arange(lon_total // 2)
    table = np.zeros((2, 2, padded, lon_total // 2), np.float32)
    for parity, orders in enumerate((even, odd)):
        phase = (orders[:, None] * lon[None, :]) % lon_total * (2.0 * math.pi / lon_total)
        weight = np.where(orders == 0, 1.0, 2.0)[:, None]
        table[parity, 0, :pair_total] = weight * np.cos(phase)
        table[parity, 1, :pair_total] = -weight * np.sin(phase)
    return table.reshape(2, 2 * padded, lon_total // 2).astype(jnp.bfloat16)


def fourier_kernel(level_fields, sums_ref, place_ref, table_ref, wind_ref, tracer_ref, flat, lhs):
    pair_total, rows, width = sums_ref.shape
    padded = place_ref.shape[0]
    blocks = padded // LANES
    flat[...] = sums_ref[...].astype(jnp.float32).reshape(pair_total * rows, width)
    low = lax.broadcasted_iota(jnp.int32, (level_fields, padded), 1) < pair_total // 2
    for row in range(rows):
        here = flat[pl.ds(row, pair_total, stride=rows), :].astype(jnp.bfloat16)
        ordered = jnp.dot(place_ref[...], here, preferred_element_type=jnp.float32).T
        for part in range(2):
            start = part * level_fields
            straight = ordered[start : start + level_fields]
            start = start + 2 * level_fields
            crossed = ordered[start : start + level_fields]
            both = (jnp.where(low, straight, crossed), jnp.where(low, crossed, straight))
            for parity in range(2):
                for t in range(blocks):
                    lhs[parity, part * blocks + t, pl.ds(row, level_fields, stride=rows), :] = both[
                        parity
                    ][:, t * LANES : (t + 1) * LANES]
    half = table_ref.shape[2]
    group = level_fields * rows // 2
    for number, out_ref in enumerate((wind_ref, tracer_ref)):
        found = []
        for parity in range(2):
            left = jnp.concatenate(
                [
                    lhs[parity, t, number * group : (number + 1) * group, :].astype(jnp.bfloat16)
                    for t in range(2 * blocks)
                ],
                axis=1,
            )
            found.append(jnp.dot(left, table_ref[parity], preferred_element_type=jnp.float32))
        shape = out_ref.shape[:3] + (half,)
        for part, value in enumerate((found[0] + found[1], found[0] - found[1])):
            value = value.astype(jnp.bfloat16).astype(jnp.float32).reshape(shape)
            out_ref[:, :, :, part * half : (part + 1) * half] = value


def fourier_call(sums, place, lon_total, level_fields):
    pair_total, rows, width = sums.shape
    padded = place.shape[0]
    table = jnp.asarray(fourier_table(pair_total, padded, lon_total))
    shape = jax.ShapeDtypeStruct((2, level_fields // 4, rows, lon_total), jnp.float32)
    in_vmem = pl.BlockSpec(memory_space=pltpu.VMEM)
    return pl.pallas_call(
        functools.partial(fourier_kernel, level_fields),
        out_shape=(shape, shape),
        in_specs=[in_vmem, in_vmem, in_vmem],
        out_specs=(in_vmem, in_vmem),
        scratch_shapes=[
            pltpu.VMEM((pair_total * rows, width), jnp.float32),
            pltpu.VMEM((2, 2 * padded // LANES, level_fields * rows, LANES), jnp.float32),
        ],
        compiler_params=pltpu.CompilerParams(vmem_limit_bytes=48 * 1024 * 1024),
        cost_estimate=pl.CostEstimate(
            flops=4 * level_fields * rows * padded * lon_total,
            bytes_accessed=8_000_000,
            transcendentals=0,
        ),
    )(sums, place, table)


def pair_places(pairing, padded):
    count = pairing.shape[0]
    row = jnp.pad(pairing, (0, up_to(count, LANES) - count))
    tile = jnp.broadcast_to(row[None, None, :], (1, 8) + row.shape)
    orders = lax.all_gather(tile, "band", axis=0, tiled=True)[:, 0, :count].reshape(-1)
    half = orders.shape[0] // 2
    place = orders // 2 + jnp.where(orders % 2 == 0, 0, half)
    return place[None, :] == lax.broadcasted_iota(jnp.int32, (padded, orders.shape[0]), 0)


def per_device(spectra, legendre, pairing, eta_shift, cells):
    levels, rows, lon_total = eta_shift.shape
    pair_total = pairing.shape[0] * lax.axis_size("band")
    place = pair_places(pairing, up_to(pair_total, LANES)).astype(jnp.bfloat16)
    table = lax.all_gather(legendre, "lev", axis=0, tiled=True)
    sums = legendre_call(pairing, spectra, table)
    sums = lax.all_to_all(sums, "band", split_axis=0, concat_axis=0, tiled=True)
    sums = sums.reshape((pair_total,) + sums.shape[2:])
    winds, tracers = fourier_call(sums, place, lon_total, 4 * levels)
    base = jnp.stack([lax.axis_index("lev") * levels, lax.axis_index("band") * rows])
    base = base.astype(jnp.int32)
    displacement = interpolation_call(
        wind_levels, base, *with_edges(winds), eta_shift, cells, (), jnp.float32
    )
    advected = interpolation_call(
        tracer_levels,
        base,
        *with_edges(tracers),
        eta_shift,
        cells,
        (displacement,),
        jnp.bfloat16,
    )
    return advected, displacement


def solution(mesh):
    return jax.shard_map(
        per_device,
        mesh=mesh,
        in_specs=(
            P(None, "lev", "band", None),
            P("lev", None, "band", None),
            P("band"),
            P("lev", "band", None),
            P(None, "lev", "band", None),
        ),
        out_specs=(P(None, "lev", "band", None), P(None, "lev", "band", None)),
        check_vma=False,
    )
```

time: 230 us -> 179 us (0.78)
  other arithmetic: 37 us -> 2.07 us
  Pallas kernels: 90.4 us -> 64.8 us
  local copies, waits for them, and re-layouts: 35.2 us -> 11.2 us
  blocking collectives: 9.84 us -> 32.1 us
  starting transfers between devices: 24.4 us -> 37 us
  matrix products: 10.9 us -> 0 us
  waiting for transfers between devices: 5.19 us -> 16 us
    another operation x4 -> x1, other arithmetic: 35 us -> 0.08 us  [per_device(): jnp.stack([lax.axis_index('lev') * levels, lax.axis_index('band') * rows])]
    all_gather x0 -> x1, blocking collectives: none -> 32.1 us  [pair_places(): lax.all_gather(tile, 'band', axis=0, tiled=True)[:, 0, :count].reshape(-1)]
    pallas_call x2 -> x4, Pallas kernels: 90.4 us -> 64.8 us  [the longest x2 50.2 us: interpolation_call(): pl.pallas_call(functools.partial(interpolation_kernel, levels_body), out_...]
    all_gather x1, waiting for transfers between devices: 1.02 us -> 14.2 us  [per_device(): table = lax.all_gather(legendre, 'lev', axis=0, tiled=True)]
    reshape x2 -> x0, local copies, waits for them, and re-layouts: 12.7 us -> none  [the longest x1 7.13 us: per_device(): spectral.reshape(all_pairs.shape[0], row_count, field_count, 2, 2)]
    dot_general x3 -> x0, matrix products: 10.9 us -> none  [the longest x1 6.38 us: legendre_rows(): jnp.einsum('scpk,hrfpk->cpsfhr', table, halves, preferred_element_type=jn...]
    ppermute x2, starting transfers between devices: 4.89 us -> 15.7 us  [level_edges(): lax.ppermute(jnp.where(at_top, last, first), 'lev', [(0, 1), (1, 0)])]
    unnamed x1 -> x0, blocking collectives: 9.84 us -> none
  transfers between devices with their start and end apart: 8 -> 8, of which waited for: 3 -> 2; matrix products, arithmetic and copies ran while one was open for 16% -> 2% of each run, Pallas kernels for 0% -> 0%
where the time goes in v3:
time: 179 us; the launch traced here: 177 us
  Pallas kernels  64.8 us (36%)
  starting transfers between devices  37 us (21%)
  blocking collectives  32.1 us (18%)
  waiting for transfers between devices  16 us (9%)
  between operations  14.3 us (8%)
  local copies, waits for them, and re-layouts  11.2 us (6%)
  other arithmetic  2.07 us (1%)
    pallas_call x2, Pallas kernels, interpolation_call(): pl.pallas_call(functools.partial(interpolation_kernel, levels_body), out_...  50.2 us
    all_gather x1, blocking collectives, pair_places(): lax.all_gather(tile, 'band', axis=0, tiled=True)[:, 0, :count].reshape(-1)  32.1 us
    ppermute x2, starting transfers between devices, level_edges(): lax.ppermute(jnp.where(at_top, last, first), 'lev', [(0, 1), (1, 0)])  15.7 us
    all_gather x1, waiting for transfers between devices, per_device(): table = lax.all_gather(legendre, 'lev', axis=0, tiled=True)  14.2 us
    ppermute x2, starting transfers between devices, row_edges(): after = lax.ppermute(fields[:, :, :HALO].astype(jnp.bfloat16), 'band', down)  11 us
    pallas_call x1, Pallas kernels, legendre_call(): pl.pallas_call(legendre_kernel, out_shape=jax.ShapeDtypeStruct((bands, pa...  9.94 us
    all_to_all x1, starting transfers between devices, per_device(): sums = lax.all_to_all(sums, 'band', split_axis=0, concat_axis=0, tiled=True)  6.41 us
    all_gather x1, local copies, waits for them, and re-layouts, per_device(): table = lax.all_gather(legendre, 'lev', axis=0, tiled=True)  5.81 us
  transfers between devices with their start and end apart: 8, of which 2 were waited for; matrix products, arithmetic and copies ran while one was open for 2% of the time, Pallas kernels for 0%

profile of v3, /device:TPU:9, one launch (start us, length us, event | category | flops | bytes accessed | tf_op | source)
XLA Modules:
  0.0 177.3 jit_solution(7244924676934944287)
XLA Ops:
  7.2 0.0 all-gather.4.cloned.1.call-start
  7.2 0.7 all-gather.4.cloned.1.call-update
  7.9 2.6 %copy.10.spectra_ref = bf16[2,32,20,641]{3,2,1,0:T(8,128)(2,1)S(1)} copy(bf16[2,32,20,641]{3,1,2,0:T(8,128)(2,1)} %param.6) | data formatting | bytes 3281920 | tf_op args[0]
  10.5 0.0 copy-start.3
  10.6 14.2 %all-gather.4.cloned.1.call-done = bf16[8,16,20,641]{3,1,2,0:T(8,128)(2,1)} async-done(((bf16[4,16,20,641]{3,1,2,0:T(8,128)(2,1)}), bf16[8,16,20,641]{3,1,2,0:T(8,128)(2,1)}) %all-gather.4.cloned.1.call-update) | async-done | bytes 3281936 | tf_op jit(solution)/shard_map/all_gather | solution.py:478
  24.7 5.8 %copy.11.table_ref = bf16[8,16,20,641]{3,2,1,0:T(8,128)(2,1)} copy(bf16[8,16,20,641]{3,1,2,0:T(8,128)(2,1)} %all-gather.4.cloned.1.call-done) | data formatting | bytes 6563840 | tf_op jit(solution)/shard_map/all_gather | solution.py:478
  30.6 0.0 copy-done.3
  30.6 9.9 %shard_map.77 = bf16[16,20,8,128]{3,2,1,0:T(8,128)(2,1)} custom-call(s32[20]{0:T(128)S(1)} %copy-done.3, bf16[2,32,20,641]{3,2,1,0:T(8,128)(2,1)S(1)} %copy.10.spectra_ref, bf16[8,16,20,641]{3,2,1,0:T(8,128)(2,1)} %copy.11.table_ref), custom_call_target="tpu_custom_call" | custom-call | flops 420085760 | bytes 8000000 | tf_op jit(solution)/shard_map/pallas_call | solution.py:366
  40.5 6.4 %all-to-all-start = ((bf16[16,20,8,128]{3,2,1,0:T(8,128)(2,1)}), bf16[16,20,8,128]{3,2,1,0:T(8,128)(2,1)S(1)}, u32[]{:S(2)}, u32[]{:S(2)}) async-start(bf16[16,20,8,128]{3,2,1,0:T(8,128)(2,1)} %shard_map.77), calls=%async_computation | async-start | bytes 1310720 | tf_op jit(solution)/shard_map/all_to_all | solution.py:480
  46.9 32.1 %all-gather.1 = s32[16,1,128]{2,1,0:T(1,128)S(1)} all-gather(s32[1,1,128]{2,1,0:T(1,128)S(1)} %pad_bitcast_fusion), channel_id=3, replica_groups=mesh['band'=16,'lev'=2] {'band'}, dimensions={0}, use_global_device_ids=true | all-gather | bytes 8704 | tf_op jit(solution)/shard_map/all_gather | solution.py:468
  79.0 0.1 reshape_squeeze.3
  79.1 0.1 pad_add_fusion.base_ref
  79.2 0.1 fusion.place_ref
  79.3 0.0 all-to-all-done
  79.3 4.7 %shard_map.78 = (f32[2,8,8,2816]{3,2,1,0:T(8,128)S(1)}, f32[2,8,8,2816]{3,2,1,0:T(8,128)S(1)}) custom-call(bf16[320,8,128]{2,1,0:T(8,128)(2,1)S(1)} %bitcast.7, bf16[384,320]{1,0:T(8,128)(2,1)S(1)} %fusion.place_ref, bf16[2,768,1408]{2,1,0:T(8,128)(2,1)} %constant.44.clone.table_ref), custom_call_target="tpu_custom_call" | custom-call | flops 1107296256 | bytes 8000000 | tf_op jit(solution)/shard_map/pallas_call | solution.py:446
  83.9 0.1 convert_element_type.36
  84.0 0.2 fusion.7
  84.3 5.9 %collective-permute-start.3 = (bf16[2,8,2,2816]{3,2,1,0:T(2,128)(2,1)S(1)}, bf16[2,8,2,2816]{3,2,1,0:T(2,128)(2,1)S(1)}, u32[]{:S(2)}, u32[]{:S(2)}) collective-permute-start(bf16[2,8,2,2816]{3,2,1,0:T(2,128)(2,1)S(1)} %get-tuple-element.6), channel_id=1, source_target_pairs={{2,0},{4,2},{6,4},{8,6},{10,8},{12,10},{14,12},{16,14},{18,16},{20... | collective-permute-start | bytes 540680 | tf_op jit(solution)/shard_map/ppermute | solution.py:253
  90.1 1.9 %collective-permute-start.4 = (bf16[2,8,2,2816]{3,2,1,0:T(2,128)(2,1)S(1)}, bf16[2,8,2,2816]{3,2,1,0:T(2,128)(2,1)S(1)}, u32[]{:S(2)}, u32[]{:S(2)}) collective-permute-start(bf16[2,8,2,2816]{3,2,1,0:T(2,128)(2,1)S(1)} %get-tuple-element.7), channel_id=1, source_target_pairs={{0,2},{2,4},{4,6},{6,8},{8,10},{10,12},{12,14},{14,16},{16,18},{18... | collective-permute-start | bytes 540680 | tf_op jit(solution)/shard_map/ppermute | solution.py:252
  92.1 0.1 convert_element_type.32
  92.2 0.2 fusion.8
  92.4 5.2 %collective-permute-start = (bf16[2,8,2,2816]{3,2,1,0:T(2,128)(2,1)S(1)}, bf16[2,8,2,2816]{3,2,1,0:T(2,128)(2,1)S(1)}, u32[]{:S(2)}, u32[]{:S(2)}) collective-permute-start(bf16[2,8,2,2816]{3,2,1,0:T(2,128)(2,1)S(1)} %get-tuple-element.8), channel_id=1, source_target_pairs={{2,0},{4,2},{6,4},{8,6},{10,8},{12,10},{14,12},{16,14},{18,16},{20... | collective-permute-start | bytes 540680 | tf_op jit(solution)/shard_map/ppermute | solution.py:253
  97.6 1.9 %collective-permute-start.1 = (bf16[2,8,2,2816]{3,2,1,0:T(2,128)(2,1)S(1)}, bf16[2,8,2,2816]{3,2,1,0:T(2,128)(2,1)S(1)}, u32[]{:S(2)}, u32[]{:S(2)}) collective-permute-start(bf16[2,8,2,2816]{3,2,1,0:T(2,128)(2,1)S(1)} %get-tuple-element.9), channel_id=1, source_target_pairs={{0,2},{2,4},{4,6},{6,8},{8,10},{10,12},{12,14},{14,16},{16,18},{18... | collective-permute-start | bytes 540680 | tf_op jit(solution)/shard_map/ppermute | solution.py:252
  99.5 0.0 collective-permute-done.3
  99.5 0.0 collective-permute-done.4
  99.5 0.2 fusion.1
  99.8 8.9 %collective-permute-start.5 = (bf16[2,2,12,2816]{3,2,1,0:T(8,128)(2,1)S(1)}, bf16[2,2,12,2816]{3,2,1,0:T(8,128)(2,1)S(1)}, u32[]{:S(2)}, u32[]{:S(2)}) collective-permute-start(bf16[2,2,12,2816]{3,2,1,0:T(8,128)(2,1)S(1)} %fusion.1), channel_id=1, source_target_pairs={{0,1},{1,0},{2,3},{3,2},{4,5},{5,4},{6,7},{7,6},{8,9},{9,8},{10,11... | collective-permute-start | bytes 811016 | tf_op jit(solution)/shard_map/ppermute | solution.py:262
  108.6 0.0 collective-permute-done
  108.6 0.0 collective-permute-done.1
  108.6 0.2 fusion.2
  108.9 6.8 %collective-permute-start.2 = (bf16[2,2,12,2816]{3,2,1,0:T(8,128)(2,1)S(1)}, bf16[2,2,12,2816]{3,2,1,0:T(8,128)(2,1)S(1)}, u32[]{:S(2)}, u32[]{:S(2)}) collective-permute-start(bf16[2,2,12,2816]{3,2,1,0:T(8,128)(2,1)S(1)} %fusion.2), channel_id=1, source_target_pairs={{0,1},{1,0},{2,3},{3,2},{4,5},{5,4},{6,7},{7,6},{8,9},{9,8},{10,11... | collective-permute-start | bytes 811016 | tf_op jit(solution)/shard_map/ppermute | solution.py:262
  115.7 0.0 collective-permute-done.5
  115.7 0.1 broadcast_select_fusion.1
  115.7 0.1 slice_convert_fusion
  115.8 1.1 collective-permute-done.2
  117.0 0.1 broadcast_select_fusion.3
  117.0 0.1 slice_convert_fusion.2
  117.1 0.1 pad_maximum_fusion.1.center_ref
  117.3 0.0 copy-start
  117.3 0.1 pad_maximum_fusion.center_ref
  117.4 0.0 copy-start.2
  117.5 0.4 maximum_convert_fusion.1.edge_ref
  117.9 1.0 copy-done
  118.9 0.0 copy-done.2
  118.9 26.0 %shard_map.79.others_0_ = f32[2,8,8,2816]{3,2,1,0:T(8,128)} custom-call(s32[2]{0:T(128)S(1)} %pad_add_fusion.base_ref, f32[2,12,8,2816]{3,2,1,0:T(8,128)S(1)} %pad_maximum_fusion.1.center_ref, f32[2,12,4,2816]{3,2,1,0:T(4,128)S(1)} %maximum_convert_fusion.1.edge_ref, bf16[8,8,2816]{2,1,0:T(8,128)(2,1)S(1)} %copy-done.2, s32[3,8,8,2816]{3,2,1,0:T(8,128)S(1)} %copy-done), custom_call_target="tpu_custom_call" | custom-call | flops 90112000 | bytes 7208960 | tf_op jit(solution)/shard_map/pallas_call | solution.py:234
  144.9 0.0 copy-start.1
  144.9 0.4 maximum_convert_fusion.edge_ref
  145.3 1.0 copy-done.1
  146.3 24.2 %shard_map.80 = bf16[2,8,8,2816]{3,2,1,0:T(8,128)(2,1)} custom-call(s32[2]{0:T(128)S(1)} %pad_add_fusion.base_ref, f32[2,12,8,2816]{3,2,1,0:T(8,128)S(1)} %pad_maximum_fusion.center_ref, f32[2,12,4,2816]{3,2,1,0:T(4,128)S(1)} %maximum_convert_fusion.edge_ref, bf16[8,8,2816]{2,1,0:T(8,128)(2,1)S(1)} %copy-done.2, s32[3,8,8,2816]{3,2,1,0:T(8,128)S(1)} %copy-done, ...), custom_call_target="tpu_custom_call" | custom-call | flops 90112000 | bytes 7208960 | tf_op jit(solution)/shard_map/pallas_call | solution.py:234
  (6 shorter events, 0.1 us)
Async XLA Ops:
  7.2 17.6 %all-gather.4.cloned.1.call-start = ((), (), s32[]{:S(2)}) async-start(), calls=%async_computation.1 | async-start | bytes 5898240 | tf_op jit(solution)/shard_map/all_gather | solution.py:478
  10.5 20.0 %copy-start.3 = (s32[20]{0:T(128)S(1)}, s32[20]{0:T(128)}, u32[]{:S(2)}) copy-start(s32[20]{0:T(128)} %pairing_ref.1) | copy-start | bytes 244
  40.5 38.8 %all-to-all-start = ((bf16[16,20,8,128]{3,2,1,0:T(8,128)(2,1)}), bf16[16,20,8,128]{3,2,1,0:T(8,128)(2,1)S(1)}, u32[]{:S(2)}, u32[]{:S(2)}) async-start(bf16[16,20,8,128]{3,2,1,0:T(8,128)(2,1)} %shard_map.77), calls=%async_computation | async-start | bytes 1310720 | tf_op jit(solution)/shard_map/all_to_all | solution.py:480
  84.3 15.2 %collective-permute-start.3 = (bf16[2,8,2,2816]{3,2,1,0:T(2,128)(2,1)S(1)}, bf16[2,8,2,2816]{3,2,1,0:T(2,128)(2,1)S(1)}, u32[]{:S(2)}, u32[]{:S(2)}) collective-permute-start(bf16[2,8,2,2816]{3,2,1,0:T(2,128)(2,1)S(1)} %get-tuple-element.6), channel_id=1, source_target_pairs={{2,0},{4,2},{6,4},{8,6},{10,8},{12,10},{14,12},{16,14},{18,16},{20... | collective-permute-start | bytes 540680 | tf_op jit(solution)/shard_map/ppermute | solution.py:253
  90.1 9.4 %collective-permute-start.4 = (bf16[2,8,2,2816]{3,2,1,0:T(2,128)(2,1)S(1)}, bf16[2,8,2,2816]{3,2,1,0:T(2,128)(2,1)S(1)}, u32[]{:S(2)}, u32[]{:S(2)}) collective-permute-start(bf16[2,8,2,2816]{3,2,1,0:T(2,128)(2,1)S(1)} %get-tuple-element.7), channel_id=1, source_target_pairs={{0,2},{2,4},{4,6},{6,8},{8,10},{10,12},{12,14},{14,16},{16,18},{18... | collective-permute-start | bytes 540680 | tf_op jit(solution)/shard_map/ppermute | solution.py:252
  92.4 16.2 %collective-permute-start = (bf16[2,8,2,2816]{3,2,1,0:T(2,128)(2,1)S(1)}, bf16[2,8,2,2816]{3,2,1,0:T(2,128)(2,1)S(1)}, u32[]{:S(2)}, u32[]{:S(2)}) collective-permute-start(bf16[2,8,2,2816]{3,2,1,0:T(2,128)(2,1)S(1)} %get-tuple-element.8), channel_id=1, source_target_pairs={{2,0},{4,2},{6,4},{8,6},{10,8},{12,10},{14,12},{16,14},{18,16},{20... | collective-permute-start | bytes 540680 | tf_op jit(solution)/shard_map/ppermute | solution.py:253
  97.6 11.1 %collective-permute-start.1 = (bf16[2,8,2,2816]{3,2,1,0:T(2,128)(2,1)S(1)}, bf16[2,8,2,2816]{3,2,1,0:T(2,128)(2,1)S(1)}, u32[]{:S(2)}, u32[]{:S(2)}) collective-permute-start(bf16[2,8,2,2816]{3,2,1,0:T(2,128)(2,1)S(1)} %get-tuple-element.9), channel_id=1, source_target_pairs={{0,2},{2,4},{4,6},{6,8},{8,10},{10,12},{12,14},{14,16},{16,18},{18... | collective-permute-start | bytes 540680 | tf_op jit(solution)/shard_map/ppermute | solution.py:252
  99.8 15.9 %collective-permute-start.5 = (bf16[2,2,12,2816]{3,2,1,0:T(8,128)(2,1)S(1)}, bf16[2,2,12,2816]{3,2,1,0:T(8,128)(2,1)S(1)}, u32[]{:S(2)}, u32[]{:S(2)}) collective-permute-start(bf16[2,2,12,2816]{3,2,1,0:T(8,128)(2,1)S(1)} %fusion.1), channel_id=1, source_target_pairs={{0,1},{1,0},{2,3},{3,2},{4,5},{5,4},{6,7},{7,6},{8,9},{9,8},{10,11... | collective-permute-start | bytes 811016 | tf_op jit(solution)/shard_map/ppermute | solution.py:262
  108.9 8.1 %collective-permute-start.2 = (bf16[2,2,12,2816]{3,2,1,0:T(8,128)(2,1)S(1)}, bf16[2,2,12,2816]{3,2,1,0:T(8,128)(2,1)S(1)}, u32[]{:S(2)}, u32[]{:S(2)}) collective-permute-start(bf16[2,2,12,2816]{3,2,1,0:T(8,128)(2,1)S(1)} %fusion.2), channel_id=1, source_target_pairs={{0,1},{1,0},{2,3},{3,2},{4,5},{5,4},{6,7},{7,6},{8,9},{9,8},{10,11... | collective-permute-start | bytes 811016 | tf_op jit(solution)/shard_map/ppermute | solution.py:262
  117.3 1.6 copy-start
  117.4 1.5 copy-start.2
  144.9 1.4 copy-start.1
Sparse Core Ops, SparseCore 0:
  9.5 15.1 all-gather.3

commit v4 on v3

v4 whole, which is shorter than its diff:
```python
import functools
import math

import jax
import jax.numpy as jnp
import numpy as np
from jax import lax
from jax.experimental import pallas as pl
from jax.experimental.pallas import tpu as pltpu
from jax.sharding import PartitionSpec as P

ITERS = 2


COURANT = 0.8
HALO = 2
LANES = 128
ROWS = 8
SLOTS = (-1, 0, 1, 2)


def slot_weights(place, here, low, high, sixth):
    z = jnp.minimum(jnp.maximum(place, low), high)
    square = z * z
    less = square - 1.0
    outer = less * z * sixth
    triple = 3.0 * outer
    half = 0.5 * z
    half_square = 0.5 * square
    return (
        half_square - half - jnp.where(here, outer, triple),
        triple - less,
        half_square + half - jnp.where(here, triple, outer),
        outer,
    )


def bounds(here):
    return (
        jnp.where(here, -0.5, -1.5),
        jnp.where(here, 1.5, 0.5),
        jnp.where(here, 1.0 / 6.0, -1.0 / 6.0),
    )


def weighted(weights, values):
    return (weights[0] * values[0] + weights[1] * values[1]) + (
        weights[2] * values[2] + weights[3] * values[3]
    )


def shifted_lanes(before, here, after, lane):
    return (
        jnp.where(lane < 2, pltpu.roll(before, 2, 1), pltpu.roll(here, 2, 1)),
        jnp.where(lane < 1, pltpu.roll(before, 1, 1), pltpu.roll(here, 1, 1)),
        here,
        jnp.where(lane < LANES - 1, pltpu.roll(here, LANES - 1, 1), pltpu.roll(after, LANES - 1, 1)),
        jnp.where(lane < LANES - 2, pltpu.roll(here, LANES - 2, 1), pltpu.roll(after, LANES - 2, 1)),
    )


def fill_units(slab, chunk, chunk_total, center_ref, edge_ref, scratch):
    _, field_count, rows, _ = center_ref.shape
    before = jnp.where(chunk == 0, chunk_total - 1, chunk - 1)
    after = jnp.where(chunk == chunk_total - 1, 0, chunk + 1)
    starts = [pl.multiple_of(c * LANES, LANES) for c in (before, chunk, after)]
    lane = lax.broadcasted_iota(jnp.int32, (rows, LANES), 1)
    tall = 3 * rows
    first = slab * (5 * tall)

    def edge_start():
        return shifted_lanes(*[edge_ref[slab, :, pl.ds(s, LANES)] for s in starts], lane)

    def edge_finish(values):
        for step, moved in enumerate(values):
            for field, offset in ((0, rows // 2), (0, 2 * rows), (1, 0), (1, rows + rows // 2)):
                scratch[field, pl.ds(first + (step * tall + offset), rows), :] = moved

    def center_unit(field):
        def start():
            blocks = [center_ref[slab, field, :, pl.ds(s, LANES)] for s in starts]
            return shifted_lanes(*blocks, lane)

        def finish(values):
            for step, moved in enumerate(values):
                scratch[field, pl.ds(first + (step * tall + rows), rows), :] = moved

        return start, finish

    return [(edge_start, edge_finish)] + [center_unit(field) for field in range(field_count)]


class Interleave:
    def __init__(self, units, ticks):
        self.units = list(units)
        self.every = max(1, ticks // max(1, len(self.units)))
        self.count = 0
        self.pending = None

    def advance(self):
        if self.pending is not None:
            self.pending[0](self.pending[1])
            self.pending = None
        if self.units:
            start, finish = self.units.pop(0)
            self.pending = (finish, start())

    def tick(self):
        if self.count % self.every == 0:
            self.advance()
        self.count += 1

    def flush(self):
        while self.units or self.pending is not None:
            self.advance()


def level_sums(scratch, field, base, rows, slot, points):
    tall = 3 * rows
    loaded = {}

    def load(a, b, c):
        if (a, b, c) not in loaded:
            offset = ((a + HALO) * 5 + c + HALO) * tall + rows + b
            loaded[a, b, c] = scratch[field, pl.ds(base + offset, rows), :]
        return loaded[a, b, c]

    def one(step, weights, level_here, row_here, lon_here):
        def pick_lon(a, b):
            if slot[1] == 2:
                return jnp.where(lon_here, load(a + step, b, 2), load(a + step, b, -2))
            return load(a + step, b, slot[1])

        def pick(a):
            if slot[0] == 2:
                return jnp.where(row_here, pick_lon(a, 2), pick_lon(a, -2))
            return pick_lon(a, slot[0])

        total = weights[0] * pick(-1) + weights[1] * pick(0)
        total = total + weights[2] * pick(1)
        return total + weights[3] * jnp.where(level_here, pick(2), pick(-2))

    return [one(step, *point) for step, point in enumerate(points)]


def across(sums, row_weights, lon_weights):
    return weighted(
        lon_weights, [weighted(row_weights, [sums[b, c] for b in SLOTS]) for c in SLOTS]
    )


def arrival(base_ref, eta_ref, cells_ref, k, chunk, lanes):
    shape = (cells_ref.shape[2], LANES)
    level_here = cells_ref[2, k, :, lanes] == base_ref[0] + k
    row_here = cells_ref[0, k, :, lanes] == base_ref[1] + lax.broadcasted_iota(jnp.int32, shape, 0)
    lon_here = cells_ref[1, k, :, lanes] == chunk * LANES + lax.broadcasted_iota(
        jnp.int32, shape, 1
    )
    weights = slot_weights(
        -eta_ref[k, :, lanes].astype(jnp.float32), level_here, *bounds(level_here)
    )
    return weights, level_here, row_here, lon_here


def wind_levels(base, lanes, k, points, scratch, filling, out_ref):
    rows = out_ref.shape[2]
    for step, point in enumerate(points):
        here = base + step * (15 * rows)
        sums = [{}, {}]
        for field in range(2):
            for c in SLOTS:
                for b in SLOTS:
                    filling.tick()
                    found = level_sums(scratch, field, here, rows, (b, c), [point])
                    sums[field][b, c] = found[0]
        middle = (HALO * 5 + HALO) * 3 * rows + rows
        east = scratch[0, pl.ds(here + middle, rows), :]
        north = scratch[1, pl.ds(here + middle, rows), :]
        _, _, row_here, lon_here = point
        row_bounds, lon_bounds = bounds(row_here), bounds(lon_here)
        shift_row = COURANT * north
        shift_lon = COURANT * east
        for sweep in range(ITERS):
            row_weights = slot_weights(-shift_row, row_here, *row_bounds)
            lon_weights = slot_weights(-shift_lon, lon_here, *lon_bounds)
            east_found = across(sums[0], row_weights, lon_weights)
            north_found = across(sums[1], row_weights, lon_weights)
            shift_row = 0.5 * COURANT * (north + north_found)
            shift_lon = 0.5 * COURANT * (east + east_found)
        out_ref[0, k + step, :, lanes] = shift_row
        out_ref[1, k + step, :, lanes] = shift_lon


def tracer_levels(shift_ref, base, lanes, k, points, scratch, filling, out_ref):
    rows = out_ref.shape[2]
    row_weights = []
    lon_weights = []
    for step, (_, _, row_here, lon_here) in enumerate(points):
        row_weights.append(
            slot_weights(-shift_ref[0, k + step, :, lanes], row_here, *bounds(row_here))
        )
        lon_weights.append(
            slot_weights(-shift_ref[1, k + step, :, lanes], lon_here, *bounds(lon_here))
        )
    for field in range(2):
        totals = [None] * len(points)
        for c, lon_slot in enumerate(SLOTS):
            columns = [None] * len(points)
            for b, row_slot in enumerate(SLOTS):
                filling.tick()
                found = level_sums(scratch, field, base, rows, (row_slot, lon_slot), points)
                for step, value in enumerate(found):
                    term = row_weights[step][b] * value
                    columns[step] = term if b == 0 else columns[step] + term
            for step, column in enumerate(columns):
                term = lon_weights[step][c] * column
                totals[step] = term if c == 0 else totals[step] + term
        for step, total in enumerate(totals):
            out_ref[field, k + step, :, lanes] = total.astype(out_ref.dtype)


def interpolation_kernel(
    levels_body, base_ref, center_ref, edge_ref, eta_ref, cells_ref, *others
):
    extra, (out_ref, even_scratch, odd_scratch) = others[:-3], others[-3:]
    levels, rows, lon_total = eta_ref.shape
    chunk_total = lon_total // LANES
    slabs = levels + 2 * HALO
    together = 2 if levels % 2 == 0 and slabs % (levels // 2) == 0 else 1
    steps = levels // together
    per_step = -(-slabs // steps)
    source = (center_ref, edge_ref)

    def first_fill(slab, carry):
        for start, finish in fill_units(slab, 0, chunk_total, *source, even_scratch):
            finish(start())
        return carry

    lax.fori_loop(0, slabs, first_fill, 0)

    def one_chunk(chunk, scratch, other):
        lanes = pl.ds(pl.multiple_of(chunk * LANES, LANES), LANES)
        following = jnp.where(chunk == chunk_total - 1, 0, chunk + 1)

        def level_step(step, carry):
            k = step * together
            units = []
            for n in range(per_step):
                slab = jnp.minimum(step * per_step + n, slabs - 1)
                units += fill_units(slab, following, chunk_total, *source, other)
            filling = Interleave(units, 32)
            points = [
                arrival(base_ref, eta_ref, cells_ref, k + n, chunk, lanes) for n in range(together)
            ]
            levels_body(*extra, k * (15 * rows), lanes, k, points, scratch, filling, out_ref)
            filling.flush()
            return carry

        lax.fori_loop(0, steps, level_step, 0)

    def chunk_pair(pair, carry):
        one_chunk(2 * pair, even_scratch, odd_scratch)
        one_chunk(2 * pair + 1, odd_scratch, even_scratch)
        return carry

    lax.fori_loop(0, chunk_total // 2, chunk_pair, 0)


def interpolation_call(levels_body, base, center, edge, eta_shift, cells, extra, out_dtype):
    levels, rows, lon_total = eta_shift.shape
    points = levels * rows * lon_total
    scratch = pltpu.VMEM((2, (levels + 2 * HALO) * 15 * rows, LANES), jnp.float32)
    in_vmem = pl.BlockSpec(memory_space=pltpu.VMEM)
    return pl.pallas_call(
        functools.partial(interpolation_kernel, levels_body),
        out_shape=jax.ShapeDtypeStruct((2, levels, rows, lon_total), out_dtype),
        in_specs=[pl.BlockSpec(memory_space=pltpu.SMEM)] + [in_vmem] * (4 + len(extra)),
        out_specs=in_vmem,
        scratch_shapes=[scratch, scratch],
        compiler_params=pltpu.CompilerParams(vmem_limit_bytes=32 * 1024 * 1024),
        cost_estimate=pl.CostEstimate(
            flops=points * 500, bytes_accessed=points * 40, transcendentals=0
        ),
    )(base, center, edge, eta_shift, cells, *extra)


def level_edges(array):
    size, count = (lax.axis_size("lev"), array.shape[0])
    last, first = (array[count - HALO :], array[:HALO])
    if size == 2:
        at_top = lax.axis_index("lev") == 0
        found = lax.ppermute(jnp.where(at_top, last, first), "lev", [(0, 1), (1, 0)])
        nothing = jnp.zeros_like(found)
        return jnp.where(at_top, nothing, found), jnp.where(at_top, found, nothing)
    up = [(i, i + 1) for i in range(size - 1)]
    down = [(j, i) for i, j in up]
    return lax.ppermute(last, "lev", up), lax.ppermute(first, "lev", down)


def with_levels(center, edge):
    levels, field_count, rows, lon_total = center.shape
    flat = center.reshape(levels, field_count * rows, lon_total)
    sides = level_edges(jnp.concatenate([flat, edge], axis=1).astype(jnp.bfloat16))
    before, after = [side.astype(jnp.float32) for side in sides]
    cut = field_count * rows
    flat = jnp.concatenate([before[:, :cut], flat, after[:, :cut]], axis=0)
    edge = jnp.concatenate([before[:, cut:], edge, after[:, cut:]], axis=0)
    return flat.reshape((-1,) + center.shape[1:]), edge


def up_to(value, step):
    return -(-value // step) * step


TALL = ROWS + 2 * HALO
CODE = 16


def legendre_kernel(numbers_ref, codes_ref, spectra_ref, *others):
    tables, (out_ref, sums, table_tail, column_tail) = others[:-4], others[-4:]
    _, pairs, level_fields, degrees = spectra_ref.shape
    bands, block, _ = out_ref.shape
    code_row = block - CODE
    full = degrees // LANES * LANES
    count = 2 * level_fields
    own = numbers_ref[0]
    sums[...] = jnp.zeros(sums.shape, jnp.float32)
    table_tail[...] = jnp.zeros(table_tail.shape, jnp.float32)
    column_tail[...] = jnp.zeros(column_tail.shape, jnp.float32)
    codes = codes_ref[...]
    for band in range(bands):
        first = (band + 1) * block + code_row
        sums[first : first + 1, :] = jnp.right_shift(codes, 4).astype(jnp.float32)
        sums[first + 1 : first + 2, :] = (codes & 15).astype(jnp.float32)

    def pair_step(p, carry):
        edge = degrees - 1 - numbers_ref[1 + p]
        left = []
        for number, table_ref in enumerate(tables):
            for row in range(table_ref.shape[0]):
                piece = table_ref[row, p]
                left.append(piece[:, :full])
                first = (number * table_ref.shape[0] + row) * bands
                table_tail[first : first + bands, : degrees - full] = piece[:, full:].astype(
                    jnp.float32
                )
        left = jnp.concatenate(left, axis=0)
        left = jnp.concatenate([left, table_tail[...].astype(jnp.bfloat16)], axis=1)
        halves = ([], [])
        for part in range(2):
            piece = spectra_ref[part, p]
            whole = piece[:, :full].astype(jnp.float32)
            lane = lax.broadcasted_iota(jnp.int32, whole.shape, 1)
            zero = jnp.zeros_like(whole)
            halves[0].append(jnp.where(lane < edge, whole, zero).astype(jnp.bfloat16))
            halves[1].append(jnp.where(lane < edge, zero, whole).astype(jnp.bfloat16))
            first = part * level_fields
            column_tail[first : first + level_fields, : degrees - full] = piece[:, full:].astype(
                jnp.float32
            )
        tail = column_tail[...].astype(jnp.bfloat16)
        right = jnp.concatenate(
            [
                jnp.concatenate([jnp.concatenate(halves[0], axis=0), jnp.zeros_like(tail)], axis=1),
                jnp.concatenate([jnp.concatenate(halves[1], axis=0), tail], axis=1),
            ],
            axis=0,
        )
        found = lax.dot_general(
            left, right, (((1,), (1,)), ((), ())), preferred_element_type=jnp.float32
        )
        found = [found[i * bands : (i + 1) * bands] for i in range(ROWS)]

        def put(band, row, value):
            start = band * block + p * TALL + row
            sums[pl.ds(start, bands, stride=block), : 2 * count] = value

        if len(tables) == 1:
            ordered = found
            for row in range(ROWS):
                put(1, HALO + row, found[row])
        else:
            part_rows = ROWS // 2
            at_top = own == 0
            for i in range(part_rows):
                put(1, HALO + own * part_rows + i, found[i])
                put(1, HALO + (1 - own) * part_rows + i, found[part_rows + i])
            low, high = found[:part_rows], found[part_rows:]
            ordered = [jnp.where(at_top, x, y) for x, y in zip(low, high)]
            ordered += [jnp.where(at_top, y, x) for x, y in zip(low, high)]
        for i in range(HALO):
            put(0, HALO + ROWS + i, ordered[i])
            put(2, i, ordered[ROWS - HALO + i])
        return carry

    lax.fori_loop(0, pairs, pair_step, 0)
    kept = sums[block : (bands + 1) * block, :]
    out_ref[...] = kept.astype(jnp.bfloat16).reshape(out_ref.shape)


def legendre_call(pairing, spectra, tables):
    _, pairs, level_fields, degrees = spectra.shape
    bands = tables[0].shape[2]
    block = up_to(pairs * TALL, 16) + CODE
    width = up_to(4 * level_fields, LANES)
    numbers = jnp.concatenate([lax.axis_index("lev").astype(jnp.int32)[None], pairing])
    codes = jnp.pad(pairing, (0, width - pairs))[None, :]
    in_vmem = pl.BlockSpec(memory_space=pltpu.VMEM)
    return pl.pallas_call(
        legendre_kernel,
        out_shape=jax.ShapeDtypeStruct((bands, block, width), jnp.bfloat16),
        in_specs=[pl.BlockSpec(memory_space=pltpu.SMEM)] + [in_vmem] * (2 + len(tables)),
        out_specs=in_vmem,
        scratch_shapes=[
            pltpu.VMEM(((bands + 2) * block, width), jnp.float32),
            pltpu.VMEM((ROWS * bands, LANES), jnp.float32),
            pltpu.VMEM((2 * level_fields, LANES), jnp.float32),
        ],
        compiler_params=pltpu.CompilerParams(vmem_limit_bytes=32 * 1024 * 1024),
        cost_estimate=pl.CostEstimate(
            flops=2 * ROWS * bands * 4 * level_fields * pairs * degrees,
            bytes_accessed=8_000_000,
            transcendentals=0,
        ),
    )(numbers, codes, spectra, *tables)


def fourier_table(pair_total, padded, lon_total):
    order_total = 2 * pair_total
    half = pair_total // 2
    low = 2 * np.arange(half)
    high = low + 1
    even = np.concatenate([low, order_total - 1 - high])
    odd = np.concatenate([order_total - 1 - low, high])
    lon = np.arange(lon_total // 2)
    table = np.zeros((2, 2, padded, lon_total // 2), np.float32)
    for parity, orders in enumerate((even, odd)):
        phase = (orders[:, None] * lon[None, :]) % lon_total * (2.0 * math.pi / lon_total)
        weight = np.where(orders == 0, 1.0, 2.0)[:, None]
        table[parity, 0, :pair_total] = weight * np.cos(phase)
        table[parity, 1, :pair_total] = -weight * np.sin(phase)
    return table.reshape(2, 2 * padded, lon_total // 2).astype(jnp.bfloat16)


def owner_tables(bands, pairs):
    slots = np.arange(bands * pairs)
    owner = slots[:, None] // pairs == np.arange(LANES)[None, :]
    lane = slots[:, None] % pairs == np.arange(LANES)[None, :]
    return owner.astype(jnp.bfloat16), lane.astype(np.float32)


def fourier_kernel(level_fields, pairs, sums_ref, owner_ref, lane_ref, table_ref, *others):
    wind_ref, tracer_ref, wind_edge_ref, tracer_edge_ref, flat, codes, gathered, lhs = others
    bands, block, width = sums_ref.shape
    pair_total = bands * pairs
    padded = gathered.shape[0]
    blocks = padded // LANES
    code_row = block - CODE
    flat[...] = sums_ref[...].astype(jnp.float32).reshape(bands * block, width)
    gathered[pair_total:, :] = jnp.zeros((padded - pair_total, width), jnp.float32)
    codes[...] = jnp.zeros(codes.shape, jnp.float32)
    numbers = []
    for part in range(2):
        found = flat[pl.ds(code_row + part, bands, stride=block), :LANES]
        codes[part, :bands, :] = found
        numbers.append(
            jnp.dot(
                owner_ref[...],
                codes[part].astype(jnp.bfloat16),
                preferred_element_type=jnp.float32,
            )
        )
    pair_id = jnp.sum(
        (16.0 * numbers[0] + numbers[1]) * lane_ref[...], axis=1, keepdims=True
    ).astype(jnp.int32)
    place = jnp.right_shift(pair_id, 1) + (pair_id & 1) * (pair_total // 2)
    columns = lax.broadcasted_iota(jnp.int32, (pair_total, padded), 1)
    place = jnp.where(columns == place, 1.0, 0.0)
    if padded > pair_total:
        place = jnp.concatenate(
            [place, jnp.zeros((padded - pair_total, padded), jnp.float32)], axis=0
        )
    place = place.astype(jnp.bfloat16)
    low = lax.broadcasted_iota(jnp.int32, (level_fields, padded), 1) < pair_total // 2
    middle = level_fields * ROWS
    for row in range(TALL):
        for band in range(bands):
            gathered[band * pairs : (band + 1) * pairs, :] = flat[
                pl.ds(band * block + row, pairs, stride=TALL), :
            ]
        ordered = jnp.dot(
            gathered[...].T.astype(jnp.bfloat16), place, preferred_element_type=jnp.float32
        )
        if HALO <= row < HALO + ROWS:
            first, stride = row - HALO, ROWS
        else:
            first, stride = middle + (row - HALO - ROWS) % TALL, 2 * HALO
        for part in range(2):
            start = part * level_fields
            straight = ordered[start : start + level_fields]
            start = start + 2 * level_fields
            crossed = ordered[start : start + level_fields]
            both = (jnp.where(low, straight, crossed), jnp.where(low, crossed, straight))
            for parity in range(2):
                for t in range(blocks):
                    lhs[
                        parity, part * blocks + t, pl.ds(first, level_fields, stride=stride), :
                    ] = both[parity][:, t * LANES : (t + 1) * LANES]
    half = table_ref.shape[2]
    levels = level_fields // 4

    def transform(first, count):
        found = []
        for parity in range(2):
            left = jnp.concatenate(
                [
                    lhs[parity, t, first : first + count, :].astype(jnp.bfloat16)
                    for t in range(2 * blocks)
                ],
                axis=1,
            )
            found.append(jnp.dot(left, table_ref[parity], preferred_element_type=jnp.float32))
        pieces = (found[0] + found[1], found[0] - found[1])
        return [piece.astype(jnp.bfloat16).astype(jnp.float32) for piece in pieces]

    group = 2 if levels % 2 == 0 else 1
    for level in range(0, levels, group):
        pieces = transform(level * 4 * ROWS, group * 4 * ROWS)
        for part, value in enumerate(pieces):
            value = value.reshape(group, 4, ROWS, half)
            lanes = slice(part * half, (part + 1) * half)
            wind_ref[level : level + group, :, :, lanes] = value[:, :2]
            tracer_ref[level : level + group, :, :, lanes] = value[:, 2:]
    for part, value in enumerate(transform(middle, level_fields * 2 * HALO)):
        value = value.reshape(levels, 8 * HALO, half)
        lanes = slice(part * half, (part + 1) * half)
        wind_edge_ref[:, :, lanes] = value[:, : 4 * HALO]
        tracer_edge_ref[:, :, lanes] = value[:, 4 * HALO :]


def fourier_call(sums, pairs, lon_total, level_fields):
    bands, block, width = sums.shape
    pair_total = bands * pairs
    padded = up_to(pair_total, LANES)
    table = jnp.asarray(fourier_table(pair_total, padded, lon_total))
    owner, lane = [jnp.asarray(x) for x in owner_tables(bands, pairs)]
    levels = level_fields // 4
    center = jax.ShapeDtypeStruct((levels, 2, ROWS, lon_total), jnp.float32)
    edge = jax.ShapeDtypeStruct((levels, 4 * HALO, lon_total), jnp.float32)
    in_vmem = pl.BlockSpec(memory_space=pltpu.VMEM)
    return pl.pallas_call(
        functools.partial(fourier_kernel, level_fields, pairs),
        out_shape=(center, center, edge, edge),
        in_specs=[in_vmem] * 4,
        out_specs=(in_vmem,) * 4,
        scratch_shapes=[
            pltpu.VMEM((bands * block, width), jnp.float32),
            pltpu.VMEM((2, LANES, LANES), jnp.float32),
            pltpu.VMEM((padded, width), jnp.float32),
            pltpu.VMEM((2, 2 * padded // LANES, level_fields * TALL, LANES), jnp.float32),
        ],
        compiler_params=pltpu.CompilerParams(vmem_limit_bytes=40 * 1024 * 1024),
        cost_estimate=pl.CostEstimate(
            flops=4 * level_fields * TALL * padded * lon_total,
            bytes_accessed=8_000_000,
            transcendentals=0,
        ),
    )(sums, owner, lane, table)


def per_device(spectra, legendre, pairing, eta_shift, cells):
    levels, rows, lon_total = eta_shift.shape
    spectra = jnp.transpose(spectra, (0, 2, 1, 3))
    table = jnp.transpose(legendre, (0, 2, 1, 3))
    if lax.axis_size("lev") == 2:
        tables = (table, lax.ppermute(table, "lev", [(0, 1), (1, 0)]))
    else:
        tables = (lax.all_gather(table, "lev", axis=0, tiled=True),)
    sums = legendre_call(pairing, spectra, tables)
    sums = lax.all_to_all(sums, "band", split_axis=0, concat_axis=0, tiled=True)
    winds, tracers, wind_edge, tracer_edge = fourier_call(
        sums, pairing.shape[0], lon_total, 4 * levels
    )
    base = jnp.stack([lax.axis_index("lev") * levels, lax.axis_index("band") * rows])
    base = base.astype(jnp.int32)
    displacement = interpolation_call(
        wind_levels, base, *with_levels(winds, wind_edge), eta_shift, cells, (), jnp.float32
    )
    advected = interpolation_call(
        tracer_levels,
        base,
        *with_levels(tracers, tracer_edge),
        eta_shift,
        cells,
        (displacement,),
        jnp.bfloat16,
    )
    return advected, displacement


def solution(mesh):
    return jax.shard_map(
        per_device,
        mesh=mesh,
        in_specs=(
            P(None, "lev", "band", None),
            P("lev", None, "band", None),
            P("band"),
            P("lev", "band", None),
            P(None, "lev", "band", None),
        ),
        out_specs=(P(None, "lev", "band", None), P(None, "lev", "band", None)),
        check_vma=False,
    )
```

time: 179 us -> 107 us (0.60)
  blocking collectives: 32.1 us -> 0 us
  starting transfers between devices: 37 us -> 10.1 us
  between operations: 14.3 us -> 0.8 us
  waiting for transfers between devices: 16 us -> 28 us
  Pallas kernels: 64.8 us -> 57.5 us
  local copies, waits for them, and re-layouts: 11.2 us -> 8.96 us
    all_gather x1 -> x0, blocking collectives: 32.1 us -> none  [pair_places(): lax.all_gather(tile, 'band', axis=0, tiled=True)[:, 0, :count].reshape(-1)]
    all_to_all x1, waiting for transfers between devices: 0.01 us -> 24.2 us  [per_device(): sums = lax.all_to_all(sums, 'band', split_axis=0, concat_axis=0, tiled=True)]
    all_gather x1 -> x0, waiting for transfers between devices: 14.2 us -> none  [per_device(): table = lax.all_gather(legendre, 'lev', axis=0, tiled=True)]
    ppermute x4 -> x1, starting transfers between devices: 14.9 us -> 0.74 us  [per_device(): tables = (table, lax.ppermute(table, 'lev', [(0, 1), (1, 0)]))]
    ppermute x2, starting transfers between devices: 15.7 us -> 2.56 us  [level_edges(): lax.ppermute(jnp.where(at_top, last, first), 'lev', [(0, 1), (1, 0)])]
    all_gather x1 -> x0, local copies, waits for them, and re-layouts: 5.81 us -> none  [per_device(): table = lax.all_gather(legendre, 'lev', axis=0, tiled=True)]
    pallas_call x2, Pallas kernels: 50.2 us -> 45.3 us  [interpolation_call(): pl.pallas_call(functools.partial(interpolation_kernel, levels_body), out_...]
    unnamed x10 -> x16, local copies, waits for them, and re-layouts: 4.69 us -> 8.15 us
  transfers between devices with their start and end apart: 8 -> 4, of which waited for: 2 -> 4; matrix products, arithmetic and copies ran while one was open for 2% -> 2% of each run, Pallas kernels for 0% -> 0%
where the time goes in v4:
time: 107 us
  Pallas kernels  57.5 us (54%)
  waiting for transfers between devices  28 us (26%)
  starting transfers between devices  10.1 us (9%)
  local copies, waits for them, and re-layouts  8.96 us (8%)
  other arithmetic  1.75 us (2%)
    pallas_call x2, Pallas kernels, interpolation_call(): pl.pallas_call(functools.partial(interpolation_kernel, levels_body), out_...  45.3 us
    all_to_all x1, waiting for transfers between devices, per_device(): sums = lax.all_to_all(sums, 'band', split_axis=0, concat_axis=0, tiled=True)  24.2 us
    unnamed x16, local copies, waits for them, and re-layouts  8.15 us
    pallas_call x1, Pallas kernels, legendre_call(): pl.pallas_call(legendre_kernel, out_shape=jax.ShapeDtypeStruct((bands, bl...  7.49 us
    all_to_all x1, starting transfers between devices, per_device(): sums = lax.all_to_all(sums, 'band', split_axis=0, concat_axis=0, tiled=True)  6.8 us
    pallas_call x1, Pallas kernels, fourier_call(): pl.pallas_call(functools.partial(fourier_kernel, level_fields, pairs), ou...  4.76 us
    ppermute x2, starting transfers between devices, level_edges(): lax.ppermute(jnp.where(at_top, last, first), 'lev', [(0, 1), (1, 0)])  2.56 us
    ppermute x1, waiting for transfers between devices, per_device(): tables = (table, lax.ppermute(table, 'lev', [(0, 1), (1, 0)]))  2.42 us
  transfers between devices with their start and end apart: 4, of which 4 were waited for; matrix products, arithmetic and copies ran while one was open for 2% of the time, Pallas kernels for 0%

profile of v4, /device:TPU:9, one launch (start us, length us, event | category | flops | bytes accessed | tf_op | source)
XLA Modules:
  0.0 107.1 jit_solution(4772098771369989917)
XLA Ops:
  0.6 0.7 collective-permute-start
  1.4 0.7 pad_bitcast_fusion.codes_ref
  2.0 0.7 pad_add_fusion.1.numbers_ref
  2.8 2.4 %collective-permute-done.others_1_ = bf16[4,20,16,641]{3,2,1,0:T(8,128)(2,1)S(1)} collective-permute-done((bf16[4,20,16,641]{3,2,1,0:T(8,128)(2,1)}, bf16[4,20,16,641]{3,2,1,0:T(8,128)(2,1)S(1)}, u32[]{:S(2)}, u32[]{:S(2)}) %collective-permute-start) | collective-permute-done | bytes 1640992 | tf_op jit(solution)/shard_map/ppermute | solution.py:576
  5.2 0.0 copy-start.2
  5.2 1.5 %copy-done.2 = bf16[2,32,20,641]{3,1,2,0:T(8,128)(2,1)S(1)} copy-done((bf16[2,32,20,641]{3,1,2,0:T(8,128)(2,1)S(1)}, bf16[2,32,20,641]{3,1,2,0:T(8,128)(2,1)}, u32[]{:S(2)}) %copy-start.2) | copy-done | bytes 1640984
  6.7 0.0 copy-start.3
  6.7 1.5 %copy-done.3 = bf16[4,16,20,641]{3,1,2,0:T(8,128)(2,1)S(1)} copy-done((bf16[4,16,20,641]{3,1,2,0:T(8,128)(2,1)S(1)}, bf16[4,16,20,641]{3,1,2,0:T(8,128)(2,1)}, u32[]{:S(2)}) %copy-start.3) | copy-done | bytes 1640984
  8.3 7.5 %shard_map.95 = bf16[16,256,128]{2,1,0:T(8,128)(2,1)} custom-call(s32[21]{0:T(128)S(1)} %pad_add_fusion.1.numbers_ref, s32[1,128]{1,0:T(1,128)S(1)} %pad_bitcast_fusion.codes_ref, bf16[2,20,32,641]{3,2,1,0:T(8,128)(2,1)S(1)} %bitcast.19, bf16[4,20,16,641]{3,2,1,0:T(8,128)(2,1)S(1)} %bitcast.21, bf16[4,20,16,641]{3,2,1,0:T(8,128)(2,1)S(1)} %collective-permute-done.others_1_), custom_call_target="tpu_custom_call" | custom-call | flops 420085760 | bytes 8000000 | tf_op jit(solution)/shard_map/pallas_call | solution.py:409
  15.8 0.0 copy-start.6
  15.8 0.0 copy-start.7
  15.8 6.8 %all-to-all-start = ((bf16[16,256,128]{2,1,0:T(8,128)(2,1)}), bf16[16,256,128]{2,1,0:T(8,128)(2,1)S(1)}, u32[]{:S(2)}, u32[]{:S(2)}) async-start(bf16[16,256,128]{2,1,0:T(8,128)(2,1)} %shard_map.95), calls=%async_computation | async-start | bytes 2097152 | tf_op jit(solution)/shard_map/all_to_all | solution.py:580
  22.6 0.1 pad_add_fusion.base_ref
  22.6 24.2 %all-to-all-done.sums_ref = bf16[16,256,128]{2,1,0:T(8,128)(2,1)S(1)} async-done(((bf16[16,256,128]{2,1,0:T(8,128)(2,1)}), bf16[16,256,128]{2,1,0:T(8,128)(2,1)S(1)}, u32[]{:S(2)}, u32[]{:S(2)}) %all-to-all-start) | async-done | bytes 1048608 | tf_op jit(solution)/shard_map/all_to_all | solution.py:580
  46.8 0.0 copy-done.6
  46.8 0.0 copy-done.7
  46.8 0.0 copy-start.5
  46.9 2.2 %copy-done.5 = bf16[2,768,1408]{2,1,0:T(8,128)(2,1)S(1)} copy-done((bf16[2,768,1408]{2,1,0:T(8,128)(2,1)S(1)}, bf16[2,768,1408]{2,1,0:T(8,128)(2,1)}, u32[]{:S(2)}) %copy-start.5) | copy-done | bytes 4325400
  49.1 4.8 %shard_map.96 = (f32[8,2,8,2816]{3,2,1,0:T(8,128)S(1)}, f32[8,2,8,2816]{3,2,1,0:T(8,128)S(1)}, f32[8,8,2816]{2,1,0:T(8,128)S(1)}, f32[8,8,2816]{2,1,0:T(8,128)S(1)}) custom-call(bf16[16,256,128]{2,1,0:T(8,128)(2,1)S(1)} %all-to-all-done.sums_ref, bf16[320,128]{1,0:T(8,128)(2,1)S(1)} %copy-done.7, f32[320,128]{1,0:T(8,128)S(1)} %copy-done.6, ...), custom_call_target="tpu_custom_call" | custom-call | flops 1660944384 | bytes 8000000 | tf_op jit(solution)/shard_map/pallas_call | solution.py:551
  53.8 0.1 convert_bitcast_fusion
  54.0 0.1 fusion
  54.0 2.5 %collective-permute-start.2 = (bf16[2,24,2816]{2,1,0:T(8,128)(2,1)S(1)}, bf16[2,24,2816]{2,1,0:T(8,128)(2,1)S(1)}, u32[]{:S(2)}, u32[]{:S(2)}) collective-permute-start(bf16[2,24,2816]{2,1,0:T(8,128)(2,1)S(1)} %fusion), channel_id=1, source_target_pairs={{0,1},{1,0},{2,3},{3,2},{4,5},{5,4},{6,7},{7,6},{8,9},{9,8},{10,11... | collective-permute-start | bytes 811016 | tf_op jit(solution)/shard_map/ppermute | solution.py:292
  56.5 0.1 convert_bitcast_fusion.1
  56.6 0.1 fusion.1
  56.7 0.1 collective-permute-start.1
  56.8 0.9 collective-permute-done.2
  57.7 0.1 select_convert_fusion.1
  57.9 0.5 collective-permute-done.1
  58.3 0.1 select_convert_fusion.3
  58.5 0.1 pad_maximum_fusion.3.edge_ref
  58.6 0.1 pad_maximum_fusion.1.center_ref
  58.7 0.1 pad_maximum_fusion.2.edge_ref
  58.8 0.0 copy-start
  58.8 0.0 copy-start.4
  58.9 0.1 pad_maximum_fusion.center_ref
  59.0 1.4 %copy-done = s32[3,8,8,2816]{3,2,1,0:T(8,128)S(1)} copy-done((s32[3,8,8,2816]{3,2,1,0:T(8,128)S(1)}, s32[3,8,8,2816]{3,2,1,0:T(8,128)}, u32[]{:S(2)}) %copy-start) | copy-done | bytes 2162712
  60.4 0.0 copy-done.4
  60.5 22.8 %shard_map.97.others_0_ = f32[2,8,8,2816]{3,2,1,0:T(8,128)} custom-call(s32[2]{0:T(128)S(1)} %pad_add_fusion.base_ref, f32[12,2,8,2816]{3,2,1,0:T(8,128)S(1)} %pad_maximum_fusion.1.center_ref, f32[12,8,2816]{2,1,0:T(8,128)S(1)} %pad_maximum_fusion.3.edge_ref, bf16[8,8,2816]{2,1,0:T(8,128)(2,1)S(1)} %copy-done.4, s32[3,8,8,2816]{3,2,1,0:T(8,128)S(1)} %copy-done), custom_call_target="tpu_custom_call" | custom-call | flops 90112000 | bytes 7208960 | tf_op jit(solution)/shard_map/pallas_call | solution.py:274
  83.3 0.0 copy-start.1
  83.3 1.4 %copy-done.1 = f32[2,8,8,2816]{3,2,1,0:T(8,128)S(1)} copy-done((f32[2,8,8,2816]{3,2,1,0:T(8,128)S(1)}, f32[2,8,8,2816]{3,2,1,0:T(8,128)}, u32[]{:S(2)}) %copy-start.1) | copy-done | bytes 1441816
  84.7 22.4 %shard_map.98 = bf16[2,8,8,2816]{3,2,1,0:T(8,128)(2,1)} custom-call(s32[2]{0:T(128)S(1)} %pad_add_fusion.base_ref, f32[12,2,8,2816]{3,2,1,0:T(8,128)S(1)} %pad_maximum_fusion.center_ref, f32[12,8,2816]{2,1,0:T(8,128)S(1)} %pad_maximum_fusion.2.edge_ref, bf16[8,8,2816]{2,1,0:T(8,128)(2,1)S(1)} %copy-done.4, s32[3,8,8,2816]{3,2,1,0:T(8,128)S(1)} %copy-done, ...), custom_call_target="tpu_custom_call" | custom-call | flops 90112000 | bytes 7208960 | tf_op jit(solution)/shard_map/pallas_call | solution.py:274
  (8 shorter events, 0.2 us)
Async XLA Ops:
  0.6 4.6 %collective-permute-start = (bf16[4,20,16,641]{3,2,1,0:T(8,128)(2,1)}, bf16[4,20,16,641]{3,2,1,0:T(8,128)(2,1)S(1)}, u32[]{:S(2)}, u32[]{:S(2)}) collective-permute-start(bf16[4,20,16,641]{3,2,1,0:T(8,128)(2,1)} %bitcast.20), channel_id=1, source_target_pairs={{0,1},{1,0},{2,3},{3,2},{4,5},{5,4},{6,7},{7,6},{8,9},{9,8},{10,11... | collective-permute-start | bytes 4922888 | tf_op jit(solution)/shard_map/ppermute | solution.py:576
  5.2 1.5 %copy-start.2 = (bf16[2,32,20,641]{3,1,2,0:T(8,128)(2,1)S(1)}, bf16[2,32,20,641]{3,1,2,0:T(8,128)(2,1)}, u32[]{:S(2)}) copy-start(bf16[2,32,20,641]{3,1,2,0:T(8,128)(2,1)} %param.8) | copy-start | bytes 4922884
  6.7 1.5 %copy-start.3 = (bf16[4,16,20,641]{3,1,2,0:T(8,128)(2,1)S(1)}, bf16[4,16,20,641]{3,1,2,0:T(8,128)(2,1)}, u32[]{:S(2)}) copy-start(bf16[4,16,20,641]{3,1,2,0:T(8,128)(2,1)} %param.9) | copy-start | bytes 4922884
  15.8 31.1 %copy-start.6 = (f32[320,128]{1,0:T(8,128)S(1)}, f32[320,128]{1,0:T(8,128)}, u32[]{:S(2)}) copy-start(f32[320,128]{1,0:T(8,128)} %constant.22.clone.lane_ref) | copy-start | bytes 491524
  15.8 31.1 %copy-start.7 = (bf16[320,128]{1,0:T(8,128)(2,1)S(1)}, bf16[320,128]{1,0:T(8,128)(2,1)}, u32[]{:S(2)}) copy-start(bf16[320,128]{1,0:T(8,128)(2,1)} %constant.21.clone.owner_ref) | copy-start | bytes 245764
  15.8 31.1 %all-to-all-start = ((bf16[16,256,128]{2,1,0:T(8,128)(2,1)}), bf16[16,256,128]{2,1,0:T(8,128)(2,1)S(1)}, u32[]{:S(2)}, u32[]{:S(2)}) async-start(bf16[16,256,128]{2,1,0:T(8,128)(2,1)} %shard_map.95), calls=%async_computation | async-start | bytes 2097152 | tf_op jit(solution)/shard_map/all_to_all | solution.py:580
  46.8 2.2 %copy-start.5 = (bf16[2,768,1408]{2,1,0:T(8,128)(2,1)S(1)}, bf16[2,768,1408]{2,1,0:T(8,128)(2,1)}, u32[]{:S(2)}) copy-start(bf16[2,768,1408]{2,1,0:T(8,128)(2,1)} %constant.20.clone.table_ref) | copy-start | bytes 12976132
  54.0 3.7 %collective-permute-start.2 = (bf16[2,24,2816]{2,1,0:T(8,128)(2,1)S(1)}, bf16[2,24,2816]{2,1,0:T(8,128)(2,1)S(1)}, u32[]{:S(2)}, u32[]{:S(2)}) collective-permute-start(bf16[2,24,2816]{2,1,0:T(8,128)(2,1)S(1)} %fusion), channel_id=1, source_target_pairs={{0,1},{1,0},{2,3},{3,2},{4,5},{5,4},{6,7},{7,6},{8,9},{9,8},{10,11... | collective-permute-start | bytes 811016 | tf_op jit(solution)/shard_map/ppermute | solution.py:292
  56.7 1.6 %collective-permute-start.1 = (bf16[2,24,2816]{2,1,0:T(8,128)(2,1)S(1)}, bf16[2,24,2816]{2,1,0:T(8,128)(2,1)S(1)}, u32[]{:S(2)}, u32[]{:S(2)}) collective-permute-start(bf16[2,24,2816]{2,1,0:T(8,128)(2,1)S(1)} %fusion.1), channel_id=1, source_target_pairs={{0,1},{1,0},{2,3},{3,2},{4,5},{5,4},{6,7},{7,6},{8,9},{9,8},{10,11... | collective-permute-start | bytes 811016 | tf_op jit(solution)/shard_map/ppermute | solution.py:292
  58.8 1.6 %copy-start = (s32[3,8,8,2816]{3,2,1,0:T(8,128)S(1)}, s32[3,8,8,2816]{3,2,1,0:T(8,128)}, u32[]{:S(2)}) copy-start(s32[3,8,8,2816]{3,2,1,0:T(8,128)} %cells_ref.3) | copy-start | bytes 6488068
  58.8 1.6 %copy-start.4 = (bf16[8,8,2816]{2,1,0:T(8,128)(2,1)S(1)}, bf16[8,8,2816]{2,1,0:T(8,128)(2,1)}, u32[]{:S(2)}) copy-start(bf16[8,8,2816]{2,1,0:T(8,128)(2,1)} %eta_ref.3) | copy-start | bytes 1081348
  83.3 1.4 %copy-start.1 = (f32[2,8,8,2816]{3,2,1,0:T(8,128)S(1)}, f32[2,8,8,2816]{3,2,1,0:T(8,128)}, u32[]{:S(2)}) copy-start(f32[2,8,8,2816]{3,2,1,0:T(8,128)} %shard_map.97.others_0_) | copy-start | bytes 4325380

commit v5 on v4

--- a/solution.py
+++ b/solution.py
@@ -51,30 +51,33 @@
 
 def shifted_lanes(before, here, after, lane):
     return (
-        jnp.where(lane < 2, pltpu.roll(before, 2, 1), pltpu.roll(here, 2, 1)),
-        jnp.where(lane < 1, pltpu.roll(before, 1, 1), pltpu.roll(here, 1, 1)),
+        pltpu.roll(jnp.where(lane < LANES - 2, here, before), 2, 1),
+        pltpu.roll(jnp.where(lane < LANES - 1, here, before), 1, 1),
         here,
-        jnp.where(lane < LANES - 1, pltpu.roll(here, LANES - 1, 1), pltpu.roll(after, LANES - 1, 1)),
-        jnp.where(lane < LANES - 2, pltpu.roll(here, LANES - 2, 1), pltpu.roll(after, LANES - 2, 1)),
-    )
+        pltpu.roll(jnp.where(lane < 1, after, here), LANES - 1, 1),
+        pltpu.roll(jnp.where(lane < 2, after, here), LANES - 2, 1),
+    )
+
+
+STACK = 5 * ROWS
+FIELD_ROW = (ROWS, 3 * ROWS)
 
 
 def fill_units(slab, chunk, chunk_total, center_ref, edge_ref, scratch):
-    _, field_count, rows, _ = center_ref.shape
     before = jnp.where(chunk == 0, chunk_total - 1, chunk - 1)
     after = jnp.where(chunk == chunk_total - 1, 0, chunk + 1)
     starts = [pl.multiple_of(c * LANES, LANES) for c in (before, chunk, after)]
-    lane = lax.broadcasted_iota(jnp.int32, (rows, LANES), 1)
-    tall = 3 * rows
-    first = slab * (5 * tall)
+    lane = lax.broadcasted_iota(jnp.int32, (ROWS, LANES), 1)
+    first = pl.multiple_of(slab * (5 * STACK), ROWS)
 
     def edge_start():
-        return shifted_lanes(*[edge_ref[slab, :, pl.ds(s, LANES)] for s in starts], lane)
+        moved = shifted_lanes(*[edge_ref[slab, :, pl.ds(s, LANES)] for s in starts], lane)
+        return [(value, pltpu.roll(value, ROWS // 2, 0)) for value in moved]
 
     def edge_finish(values):
-        for step, moved in enumerate(values):
-            for field, offset in ((0, rows // 2), (0, 2 * rows), (1, 0), (1, rows + rows // 2)):
-                scratch[field, pl.ds(first + (step * tall + offset), rows), :] = moved
+        for step, (between, outside) in enumerate(values):
+            for offset, value in ((0, outside), (2 * ROWS, between), (4 * ROWS, outside)):
+                scratch[pl.ds(first + (step * STACK + offset), ROWS), :] = value
 
     def center_unit(field):
         def start():
@@ -83,11 +86,11 @@
 
         def finish(values):
             for step, moved in enumerate(values):
-                scratch[field, pl.ds(first + (step * tall + rows), rows), :] = moved
+                scratch[pl.ds(first + (step * STACK + FIELD_ROW[field]), ROWS), :] = moved
 
         return start, finish
 
-    return [(edge_start, edge_finish)] + [center_unit(field) for field in range(field_count)]
+    return [(edge_start, edge_finish)] + [center_unit(field) for field in range(2)]
 
 
 class Interleave:
@@ -115,14 +118,13 @@
             self.advance()
 
 
-def level_sums(scratch, field, base, rows, slot, points):
-    tall = 3 * rows
+def level_sums(scratch, field, base, slot, points):
     loaded = {}
 
     def load(a, b, c):
         if (a, b, c) not in loaded:
-            offset = ((a + HALO) * 5 + c + HALO) * tall + rows + b
-            loaded[a, b, c] = scratch[field, pl.ds(base + offset, rows), :]
+            offset = ((a + HALO) * 5 + c + HALO) * STACK + FIELD_ROW[field] + b
+            loaded[a, b, c] = scratch[pl.ds(base + offset, ROWS), :]
         return loaded[a, b, c]
 
     def one(step, weights, level_here, row_here, lon_here):
@@ -163,19 +165,19 @@
 
 
 def wind_levels(base, lanes, k, points, scratch, filling, out_ref):
-    rows = out_ref.shape[2]
+    outputs = []
     for step, point in enumerate(points):
-        here = base + step * (15 * rows)
+        here = base + step * (5 * STACK)
         sums = [{}, {}]
         for field in range(2):
             for c in SLOTS:
                 for b in SLOTS:
                     filling.tick()
-                    found = level_sums(scratch, field, here, rows, (b, c), [point])
+                    found = level_sums(scratch, field, here, (b, c), [point])
                     sums[field][b, c] = found[0]
-        middle = (HALO * 5 + HALO) * 3 * rows + rows
-        east = scratch[0, pl.ds(here + middle, rows), :]
-        north = scratch[1, pl.ds(here + middle, rows), :]
+        middle = (HALO * 5 + HALO) * STACK
+        east = scratch[pl.ds(here + (middle + FIELD_ROW[0]), ROWS), :]
+        north = scratch[pl.ds(here + (middle + FIELD_ROW[1]), ROWS), :]
         _, _, row_here, lon_here = point
         row_bounds, lon_bounds = bounds(row_here), bounds(lon_here)
         shift_row = COURANT * north
@@ -187,46 +189,55 @@
             north_found = across(sums[1], row_weights, lon_weights)
             shift_row = 0.5 * COURANT * (north + north_found)
             shift_lon = 0.5 * COURANT * (east + east_found)
-        out_ref[0, k + step, :, lanes] = shift_row
-        out_ref[1, k + step, :, lanes] = shift_lon
+        outputs.append((shift_row, shift_lon))
+    filling.flush()
+    for step, pair in enumerate(outputs):
+        for part in range(2):
+            out_ref[part, k + step, :, lanes] = pair[part]
 
 
 def tracer_levels(shift_ref, base, lanes, k, points, scratch, filling, out_ref):
-    rows = out_ref.shape[2]
-    row_weights = []
-    lon_weights = []
-    for step, (_, _, row_here, lon_here) in enumerate(points):
-        row_weights.append(
-            slot_weights(-shift_ref[0, k + step, :, lanes], row_here, *bounds(row_here))
-        )
-        lon_weights.append(
-            slot_weights(-shift_ref[1, k + step, :, lanes], lon_here, *bounds(lon_here))
-        )
-    for field in range(2):
-        totals = [None] * len(points)
-        for c, lon_slot in enumerate(SLOTS):
-            columns = [None] * len(points)
-            for b, row_slot in enumerate(SLOTS):
-                filling.tick()
-                found = level_sums(scratch, field, base, rows, (row_slot, lon_slot), points)
-                for step, value in enumerate(found):
-                    term = row_weights[step][b] * value
-                    columns[step] = term if b == 0 else columns[step] + term
-            for step, column in enumerate(columns):
-                term = lon_weights[step][c] * column
-                totals[step] = term if c == 0 else totals[step] + term
-        for step, total in enumerate(totals):
-            out_ref[field, k + step, :, lanes] = total.astype(out_ref.dtype)
+    outputs = []
+    for first in range(0, len(points), 2):
+        few = points[first : first + 2]
+        row_weights = []
+        lon_weights = []
+        for step, (_, _, row_here, lon_here) in enumerate(few):
+            place = k + first + step
+            row_weights.append(
+                slot_weights(-shift_ref[0, place, :, lanes], row_here, *bounds(row_here))
+            )
+            lon_weights.append(
+                slot_weights(-shift_ref[1, place, :, lanes], lon_here, *bounds(lon_here))
+            )
+        for field in range(2):
+            totals = [None] * len(few)
+            for c, lon_slot in enumerate(SLOTS):
+                columns = [None] * len(few)
+                for b, row_slot in enumerate(SLOTS):
+                    filling.tick()
+                    here = base + first * (5 * STACK)
+                    found = level_sums(scratch, field, here, (row_slot, lon_slot), few)
+                    for step, value in enumerate(found):
+                        term = row_weights[step][b] * value
+                        columns[step] = term if b == 0 else columns[step] + term
+                for step, column in enumerate(columns):
+                    term = lon_weights[step][c] * column
+                    totals[step] = term if c == 0 else totals[step] + term
+            outputs += [(field, first + step, total) for step, total in enumerate(totals)]
+    filling.flush()
+    for field, step, total in outputs:
+        out_ref[field, k + step, :, lanes] = total.astype(out_ref.dtype)
 
 
 def interpolation_kernel(
-    levels_body, base_ref, center_ref, edge_ref, eta_ref, cells_ref, *others
+    levels_body, slots_per_level, base_ref, center_ref, edge_ref, eta_ref, cells_ref, *others
 ):
     extra, (out_ref, even_scratch, odd_scratch) = others[:-3], others[-3:]
     levels, rows, lon_total = eta_ref.shape
     chunk_total = lon_total // LANES
     slabs = levels + 2 * HALO
-    together = 2 if levels % 2 == 0 and slabs % (levels // 2) == 0 else 1
+    together = next(n for n in (4, 2, 1) if levels % n == 0)
     steps = levels // together
     per_step = -(-slabs // steps)
     source = (center_ref, edge_ref)
@@ -248,12 +259,12 @@
             for n in range(per_step):
                 slab = jnp.minimum(step * per_step + n, slabs - 1)
                 units += fill_units(slab, following, chunk_total, *source, other)
-            filling = Interleave(units, 32)
+            filling = Interleave(units, slots_per_level * together)
             points = [
                 arrival(base_ref, eta_ref, cells_ref, k + n, chunk, lanes) for n in range(together)
             ]
-            levels_body(*extra, k * (15 * rows), lanes, k, points, scratch, filling, out_ref)
-            filling.flush()
+            base = pl.multiple_of(k * (5 * STACK), ROWS)
+            levels_body(*extra, base, lanes, k, points, scratch, filling, out_ref)
             return carry
 
         lax.fori_loop(0, steps, level_step, 0)
@@ -266,13 +277,13 @@
     lax.fori_loop(0, chunk_total // 2, chunk_pair, 0)
 
 
-def interpolation_call(levels_body, base, center, edge, eta_shift, cells, extra, out_dtype):
+def interpolation_call(levels_body, slots_per_level, base, center, edge, eta_shift, cells, extra, out_dtype):
     levels, rows, lon_total = eta_shift.shape
     points = levels * rows * lon_total
-    scratch = pltpu.VMEM((2, (levels + 2 * HALO) * 15 * rows, LANES), jnp.float32)
+    scratch = pltpu.VMEM(((levels + 2 * HALO) * 5 * STACK, LANES), jnp.float32)
     in_vmem = pl.BlockSpec(memory_space=pltpu.VMEM)
     return pl.pallas_call(
-        functools.partial(interpolation_kernel, levels_body),
+        functools.partial(interpolation_kernel, levels_body, slots_per_level),
         out_shape=jax.ShapeDtypeStruct((2, levels, rows, lon_total), out_dtype),
         in_specs=[pl.BlockSpec(memory_space=pltpu.SMEM)] + [in_vmem] * (4 + len(extra)),
         out_specs=in_vmem,
@@ -584,10 +595,11 @@
     base = jnp.stack([lax.axis_index("lev") * levels, lax.axis_index("band") * rows])
     base = base.astype(jnp.int32)
     displacement = interpolation_call(
-        wind_levels, base, *with_levels(winds, wind_edge), eta_shift, cells, (), jnp.float32
+        wind_levels, 32, base, *with_levels(winds, wind_edge), eta_shift, cells, (), jnp.float32
     )
     advected = interpolation_call(
         tracer_levels,
+        16,
         base,
         *with_levels(tracers, tracer_edge),
         eta_shift,

time: 107 us -> 108 us (level)
  no operation moved by 1% of the time
where the time goes in v5:
time: 108 us
  Pallas kernels  58.1 us (54%)
  waiting for transfers between devices  28 us (26%)
  starting transfers between devices  10.1 us (9%)
  local copies, waits for them, and re-layouts  8.96 us (8%)
  other arithmetic  1.75 us (2%)
    pallas_call x2, Pallas kernels, interpolation_call(): pl.pallas_call(functools.partial(interpolation_kernel, levels_body, slots...  45.8 us
    all_to_all x1, waiting for transfers between devices, per_device(): sums = lax.all_to_all(sums, 'band', split_axis=0, concat_axis=0, tiled=True)  24.2 us
    unnamed x16, local copies, waits for them, and re-layouts  8.15 us
    pallas_call x1, Pallas kernels, legendre_call(): pl.pallas_call(legendre_kernel, out_shape=jax.ShapeDtypeStruct((bands, bl...  7.49 us
    all_to_all x1, starting transfers between devices, per_device(): sums = lax.all_to_all(sums, 'band', split_axis=0, concat_axis=0, tiled=True)  6.8 us
    pallas_call x1, Pallas kernels, fourier_call(): pl.pallas_call(functools.partial(fourier_kernel, level_fields, pairs), ou...  4.76 us
    ppermute x2, starting transfers between devices, level_edges(): lax.ppermute(jnp.where(at_top, last, first), 'lev', [(0, 1), (1, 0)])  2.56 us
    ppermute x1, waiting for transfers between devices, per_device(): tables = (table, lax.ppermute(table, 'lev', [(0, 1), (1, 0)]))  2.42 us
  transfers between devices with their start and end apart: 4, of which 4 were waited for; matrix products, arithmetic and copies ran while one was open for 2% of the time, Pallas kernels for 0%

profile of v5, /device:TPU:9, one launch (start us, length us, event | category | flops | bytes accessed | tf_op | source)
XLA Modules:
  0.0 107.7 jit_solution(12183579443293145165)
XLA Ops:
  0.6 0.7 collective-permute-start
  1.4 0.7 pad_bitcast_fusion.codes_ref
  2.0 0.7 pad_add_fusion.1.numbers_ref
  2.8 2.4 %collective-permute-done.others_1_ = bf16[4,20,16,641]{3,2,1,0:T(8,128)(2,1)S(1)} collective-permute-done((bf16[4,20,16,641]{3,2,1,0:T(8,128)(2,1)}, bf16[4,20,16,641]{3,2,1,0:T(8,128)(2,1)S(1)}, u32[]{:S(2)}, u32[]{:S(2)}) %collective-permute-start) | collective-permute-done | bytes 1640992 | tf_op jit(solution)/shard_map/ppermute | solution.py:587
  5.2 0.0 copy-start.2
  5.2 1.5 %copy-done.2 = bf16[2,32,20,641]{3,1,2,0:T(8,128)(2,1)S(1)} copy-done((bf16[2,32,20,641]{3,1,2,0:T(8,128)(2,1)S(1)}, bf16[2,32,20,641]{3,1,2,0:T(8,128)(2,1)}, u32[]{:S(2)}) %copy-start.2) | copy-done | bytes 1640984
  6.7 0.0 copy-start.3
  6.7 1.5 %copy-done.3 = bf16[4,16,20,641]{3,1,2,0:T(8,128)(2,1)S(1)} copy-done((bf16[4,16,20,641]{3,1,2,0:T(8,128)(2,1)S(1)}, bf16[4,16,20,641]{3,1,2,0:T(8,128)(2,1)}, u32[]{:S(2)}) %copy-start.3) | copy-done | bytes 1640984
  8.3 7.5 %shard_map.95 = bf16[16,256,128]{2,1,0:T(8,128)(2,1)} custom-call(s32[21]{0:T(128)S(1)} %pad_add_fusion.1.numbers_ref, s32[1,128]{1,0:T(1,128)S(1)} %pad_bitcast_fusion.codes_ref, bf16[2,20,32,641]{3,2,1,0:T(8,128)(2,1)S(1)} %bitcast.19, bf16[4,20,16,641]{3,2,1,0:T(8,128)(2,1)S(1)} %bitcast.21, bf16[4,20,16,641]{3,2,1,0:T(8,128)(2,1)S(1)} %collective-permute-done.others_1_), custom_call_target="tpu_custom_call" | custom-call | flops 420085760 | bytes 8000000 | tf_op jit(solution)/shard_map/pallas_call | solution.py:420
  15.8 0.0 copy-start.6
  15.8 0.0 copy-start.7
  15.8 6.8 %all-to-all-start = ((bf16[16,256,128]{2,1,0:T(8,128)(2,1)}), bf16[16,256,128]{2,1,0:T(8,128)(2,1)S(1)}, u32[]{:S(2)}, u32[]{:S(2)}) async-start(bf16[16,256,128]{2,1,0:T(8,128)(2,1)} %shard_map.95), calls=%async_computation | async-start | bytes 2097152 | tf_op jit(solution)/shard_map/all_to_all | solution.py:591
  22.6 0.1 pad_add_fusion.base_ref
  22.6 24.2 %all-to-all-done.sums_ref = bf16[16,256,128]{2,1,0:T(8,128)(2,1)S(1)} async-done(((bf16[16,256,128]{2,1,0:T(8,128)(2,1)}), bf16[16,256,128]{2,1,0:T(8,128)(2,1)S(1)}, u32[]{:S(2)}, u32[]{:S(2)}) %all-to-all-start) | async-done | bytes 1048608 | tf_op jit(solution)/shard_map/all_to_all | solution.py:591
  46.8 0.0 copy-done.6
  46.8 0.0 copy-done.7
  46.8 0.0 copy-start.5
  46.9 2.2 %copy-done.5 = bf16[2,768,1408]{2,1,0:T(8,128)(2,1)S(1)} copy-done((bf16[2,768,1408]{2,1,0:T(8,128)(2,1)S(1)}, bf16[2,768,1408]{2,1,0:T(8,128)(2,1)}, u32[]{:S(2)}) %copy-start.5) | copy-done | bytes 4325400
  49.1 4.8 %shard_map.96 = (f32[8,2,8,2816]{3,2,1,0:T(8,128)S(1)}, f32[8,2,8,2816]{3,2,1,0:T(8,128)S(1)}, f32[8,8,2816]{2,1,0:T(8,128)S(1)}, f32[8,8,2816]{2,1,0:T(8,128)S(1)}) custom-call(bf16[16,256,128]{2,1,0:T(8,128)(2,1)S(1)} %all-to-all-done.sums_ref, bf16[320,128]{1,0:T(8,128)(2,1)S(1)} %copy-done.7, f32[320,128]{1,0:T(8,128)S(1)} %copy-done.6, ...), custom_call_target="tpu_custom_call" | custom-call | flops 1660944384 | bytes 8000000 | tf_op jit(solution)/shard_map/pallas_call | solution.py:562
  53.8 0.1 convert_bitcast_fusion
  54.0 0.1 fusion
  54.0 2.5 %collective-permute-start.2 = (bf16[2,24,2816]{2,1,0:T(8,128)(2,1)S(1)}, bf16[2,24,2816]{2,1,0:T(8,128)(2,1)S(1)}, u32[]{:S(2)}, u32[]{:S(2)}) collective-permute-start(bf16[2,24,2816]{2,1,0:T(8,128)(2,1)S(1)} %fusion), channel_id=1, source_target_pairs={{0,1},{1,0},{2,3},{3,2},{4,5},{5,4},{6,7},{7,6},{8,9},{9,8},{10,11... | collective-permute-start | bytes 811016 | tf_op jit(solution)/shard_map/ppermute | solution.py:303
  56.5 0.1 convert_bitcast_fusion.1
  56.6 0.1 fusion.1
  56.7 0.1 collective-permute-start.1
  56.8 0.9 collective-permute-done.2
  57.7 0.1 select_convert_fusion.1
  57.9 0.5 collective-permute-done.1
  58.3 0.1 select_convert_fusion.3
  58.5 0.1 pad_maximum_fusion.3.edge_ref
  58.6 0.1 pad_maximum_fusion.1.center_ref
  58.7 0.1 pad_maximum_fusion.2.edge_ref
  58.8 0.0 copy-start
  58.8 0.0 copy-start.4
  58.9 0.1 pad_maximum_fusion.center_ref
  59.0 1.4 %copy-done = s32[3,8,8,2816]{3,2,1,0:T(8,128)S(1)} copy-done((s32[3,8,8,2816]{3,2,1,0:T(8,128)S(1)}, s32[3,8,8,2816]{3,2,1,0:T(8,128)}, u32[]{:S(2)}) %copy-start) | copy-done | bytes 2162712
  60.4 0.0 copy-done.4
  60.5 24.5 %shard_map.97.others_0_ = f32[2,8,8,2816]{3,2,1,0:T(8,128)} custom-call(s32[2]{0:T(128)S(1)} %pad_add_fusion.base_ref, f32[12,2,8,2816]{3,2,1,0:T(8,128)S(1)} %pad_maximum_fusion.1.center_ref, f32[12,8,2816]{2,1,0:T(8,128)S(1)} %pad_maximum_fusion.3.edge_ref, bf16[8,8,2816]{2,1,0:T(8,128)(2,1)S(1)} %copy-done.4, s32[3,8,8,2816]{3,2,1,0:T(8,128)S(1)} %copy-done), custom_call_target="tpu_custom_call" | custom-call | flops 90112000 | bytes 7208960 | tf_op jit(solution)/shard_map/pallas_call | solution.py:285
  85.0 0.0 copy-start.1
  85.0 1.4 %copy-done.1 = f32[2,8,8,2816]{3,2,1,0:T(8,128)S(1)} copy-done((f32[2,8,8,2816]{3,2,1,0:T(8,128)S(1)}, f32[2,8,8,2816]{3,2,1,0:T(8,128)}, u32[]{:S(2)}) %copy-start.1) | copy-done | bytes 1441816
  86.3 21.3 %shard_map.98 = bf16[2,8,8,2816]{3,2,1,0:T(8,128)(2,1)} custom-call(s32[2]{0:T(128)S(1)} %pad_add_fusion.base_ref, f32[12,2,8,2816]{3,2,1,0:T(8,128)S(1)} %pad_maximum_fusion.center_ref, f32[12,8,2816]{2,1,0:T(8,128)S(1)} %pad_maximum_fusion.2.edge_ref, bf16[8,8,2816]{2,1,0:T(8,128)(2,1)S(1)} %copy-done.4, s32[3,8,8,2816]{3,2,1,0:T(8,128)S(1)} %copy-done, ...), custom_call_target="tpu_custom_call" | custom-call | flops 90112000 | bytes 7208960 | tf_op jit(solution)/shard_map/pallas_call | solution.py:285
  (8 shorter events, 0.2 us)
Async XLA Ops:
  0.6 4.6 %collective-permute-start = (bf16[4,20,16,641]{3,2,1,0:T(8,128)(2,1)}, bf16[4,20,16,641]{3,2,1,0:T(8,128)(2,1)S(1)}, u32[]{:S(2)}, u32[]{:S(2)}) collective-permute-start(bf16[4,20,16,641]{3,2,1,0:T(8,128)(2,1)} %bitcast.20), channel_id=1, source_target_pairs={{0,1},{1,0},{2,3},{3,2},{4,5},{5,4},{6,7},{7,6},{8,9},{9,8},{10,11... | collective-permute-start | bytes 4922888 | tf_op jit(solution)/shard_map/ppermute | solution.py:587
  5.2 1.5 %copy-start.2 = (bf16[2,32,20,641]{3,1,2,0:T(8,128)(2,1)S(1)}, bf16[2,32,20,641]{3,1,2,0:T(8,128)(2,1)}, u32[]{:S(2)}) copy-start(bf16[2,32,20,641]{3,1,2,0:T(8,128)(2,1)} %param.8) | copy-start | bytes 4922884
  6.7 1.5 %copy-start.3 = (bf16[4,16,20,641]{3,1,2,0:T(8,128)(2,1)S(1)}, bf16[4,16,20,641]{3,1,2,0:T(8,128)(2,1)}, u32[]{:S(2)}) copy-start(bf16[4,16,20,641]{3,1,2,0:T(8,128)(2,1)} %param.9) | copy-start | bytes 4922884
  15.8 31.1 %copy-start.6 = (f32[320,128]{1,0:T(8,128)S(1)}, f32[320,128]{1,0:T(8,128)}, u32[]{:S(2)}) copy-start(f32[320,128]{1,0:T(8,128)} %constant.22.clone.lane_ref) | copy-start | bytes 491524
  15.8 31.1 %copy-start.7 = (bf16[320,128]{1,0:T(8,128)(2,1)S(1)}, bf16[320,128]{1,0:T(8,128)(2,1)}, u32[]{:S(2)}) copy-start(bf16[320,128]{1,0:T(8,128)(2,1)} %constant.21.clone.owner_ref) | copy-start | bytes 245764
  15.8 31.1 %all-to-all-start = ((bf16[16,256,128]{2,1,0:T(8,128)(2,1)}), bf16[16,256,128]{2,1,0:T(8,128)(2,1)S(1)}, u32[]{:S(2)}, u32[]{:S(2)}) async-start(bf16[16,256,128]{2,1,0:T(8,128)(2,1)} %shard_map.95), calls=%async_computation | async-start | bytes 2097152 | tf_op jit(solution)/shard_map/all_to_all | solution.py:591
  46.8 2.2 %copy-start.5 = (bf16[2,768,1408]{2,1,0:T(8,128)(2,1)S(1)}, bf16[2,768,1408]{2,1,0:T(8,128)(2,1)}, u32[]{:S(2)}) copy-start(bf16[2,768,1408]{2,1,0:T(8,128)(2,1)} %constant.20.clone.table_ref) | copy-start | bytes 12976132
  54.0 3.7 %collective-permute-start.2 = (bf16[2,24,2816]{2,1,0:T(8,128)(2,1)S(1)}, bf16[2,24,2816]{2,1,0:T(8,128)(2,1)S(1)}, u32[]{:S(2)}, u32[]{:S(2)}) collective-permute-start(bf16[2,24,2816]{2,1,0:T(8,128)(2,1)S(1)} %fusion), channel_id=1, source_target_pairs={{0,1},{1,0},{2,3},{3,2},{4,5},{5,4},{6,7},{7,6},{8,9},{9,8},{10,11... | collective-permute-start | bytes 811016 | tf_op jit(solution)/shard_map/ppermute | solution.py:303
  56.7 1.6 %collective-permute-start.1 = (bf16[2,24,2816]{2,1,0:T(8,128)(2,1)S(1)}, bf16[2,24,2816]{2,1,0:T(8,128)(2,1)S(1)}, u32[]{:S(2)}, u32[]{:S(2)}) collective-permute-start(bf16[2,24,2816]{2,1,0:T(8,128)(2,1)S(1)} %fusion.1), channel_id=1, source_target_pairs={{0,1},{1,0},{2,3},{3,2},{4,5},{5,4},{6,7},{7,6},{8,9},{9,8},{10,11... | collective-permute-start | bytes 811016 | tf_op jit(solution)/shard_map/ppermute | solution.py:303
  58.8 1.6 %copy-start = (s32[3,8,8,2816]{3,2,1,0:T(8,128)S(1)}, s32[3,8,8,2816]{3,2,1,0:T(8,128)}, u32[]{:S(2)}) copy-start(s32[3,8,8,2816]{3,2,1,0:T(8,128)} %cells_ref.3) | copy-start | bytes 6488068
  58.8 1.6 %copy-start.4 = (bf16[8,8,2816]{2,1,0:T(8,128)(2,1)S(1)}, bf16[8,8,2816]{2,1,0:T(8,128)(2,1)}, u32[]{:S(2)}) copy-start(bf16[8,8,2816]{2,1,0:T(8,128)(2,1)} %eta_ref.3) | copy-start | bytes 1081348
  85.0 1.4 %copy-start.1 = (f32[2,8,8,2816]{3,2,1,0:T(8,128)S(1)}, f32[2,8,8,2816]{3,2,1,0:T(8,128)}, u32[]{:S(2)}) copy-start(f32[2,8,8,2816]{3,2,1,0:T(8,128)} %shard_map.97.others_0_) | copy-start | bytes 4325380

commit v6 on v5

v6 whole, which is shorter than its diff:
```python
import functools
import math

import jax
import jax.numpy as jnp
import numpy as np
from jax import lax
from jax.experimental import pallas as pl
from jax.experimental.pallas import tpu as pltpu
from jax.sharding import PartitionSpec as P

ITERS = 2


COURANT = 0.8
HALO = 2
LANES = 128
ROWS = 8
SLOTS = (-1, 0, 1, 2)


def slot_weights(place, here, low, high, sixth):
    z = jnp.minimum(jnp.maximum(place, low), high)
    square = z * z
    less = square - 1.0
    outer = less * z * sixth
    triple = 3.0 * outer
    half = 0.5 * z
    half_square = 0.5 * square
    return (
        half_square - half - jnp.where(here, outer, triple),
        triple - less,
        half_square + half - jnp.where(here, triple, outer),
        outer,
    )


def bounds(here):
    return (
        jnp.where(here, -0.5, -1.5),
        jnp.where(here, 1.5, 0.5),
        jnp.where(here, 1.0 / 6.0, -1.0 / 6.0),
    )


def weighted(weights, values):
    return (weights[0] * values[0] + weights[1] * values[1]) + (
        weights[2] * values[2] + weights[3] * values[3]
    )


def shifted_lanes(before, here, after, lane):
    return (
        pltpu.roll(jnp.where(lane < LANES - 2, here, before), 2, 1),
        pltpu.roll(jnp.where(lane < LANES - 1, here, before), 1, 1),
        here,
        pltpu.roll(jnp.where(lane < 1, after, here), LANES - 1, 1),
        pltpu.roll(jnp.where(lane < 2, after, here), LANES - 2, 1),
    )


STACK = 5 * ROWS
FIELD_ROW = (ROWS, 3 * ROWS)


def fill_units(slab, chunk, chunk_total, field_ref, scratch):
    before = jnp.where(chunk == 0, chunk_total - 1, chunk - 1)
    after = jnp.where(chunk == chunk_total - 1, 0, chunk + 1)
    starts = [pl.multiple_of(c * LANES, LANES) for c in (before, chunk, after)]
    lane = lax.broadcasted_iota(jnp.int32, (ROWS, LANES), 1)
    first = pl.multiple_of(slab * (5 * STACK), ROWS)

    def edge_start():
        moved = shifted_lanes(
            *[field_ref[slab, 2 * ROWS : 3 * ROWS, pl.ds(s, LANES)] for s in starts], lane
        )
        return [(value, pltpu.roll(value, ROWS // 2, 0)) for value in moved]

    def edge_finish(values):
        for step, (between, outside) in enumerate(values):
            for offset, value in ((0, outside), (2 * ROWS, between), (4 * ROWS, outside)):
                scratch[pl.ds(first + (step * STACK + offset), ROWS), :] = value

    def center_unit(field):
        def start():
            rows = slice(field * ROWS, (field + 1) * ROWS)
            blocks = [field_ref[slab, rows, pl.ds(s, LANES)] for s in starts]
            return shifted_lanes(*blocks, lane)

        def finish(values):
            for step, moved in enumerate(values):
                scratch[pl.ds(first + (step * STACK + FIELD_ROW[field]), ROWS), :] = moved

        return start, finish

    return [(edge_start, edge_finish)] + [center_unit(field) for field in range(2)]


class Interleave:
    def __init__(self, units, ticks):
        self.units = list(units)
        self.every = max(1, ticks // max(1, len(self.units)))
        self.count = 0
        self.pending = None

    def advance(self):
        if self.pending is not None:
            self.pending[0](self.pending[1])
            self.pending = None
        if self.units:
            start, finish = self.units.pop(0)
            self.pending = (finish, start())

    def tick(self):
        if self.count % self.every == 0:
            self.advance()
        self.count += 1

    def flush(self):
        while self.units or self.pending is not None:
            self.advance()


def level_sums(scratch, field, base, slot, points):
    loaded = {}

    def load(a, b, c):
        if (a, b, c) not in loaded:
            offset = ((a + HALO) * 5 + c + HALO) * STACK + FIELD_ROW[field] + b
            loaded[a, b, c] = scratch[pl.ds(base + offset, ROWS), :]
        return loaded[a, b, c]

    def one(step, weights, level_here, row_here, lon_here):
        def pick_lon(a, b):
            if slot[1] == 2:
                return jnp.where(lon_here, load(a + step, b, 2), load(a + step, b, -2))
            return load(a + step, b, slot[1])

        def pick(a):
            if slot[0] == 2:
                return jnp.where(row_here, pick_lon(a, 2), pick_lon(a, -2))
            return pick_lon(a, slot[0])

        total = weights[0] * pick(-1) + weights[1] * pick(0)
        total = total + weights[2] * pick(1)
        return total + weights[3] * jnp.where(level_here, pick(2), pick(-2))

    return [one(step, *point) for step, point in enumerate(points)]


def across(sums, row_weights, lon_weights):
    return weighted(
        lon_weights, [weighted(row_weights, [sums[b, c] for b in SLOTS]) for c in SLOTS]
    )


def arrival(base_ref, eta_ref, cells_ref, k, chunk, lanes):
    shape = (cells_ref.shape[2], LANES)
    level_here = cells_ref[2, k, :, lanes] == base_ref[0] + k
    row_here = cells_ref[0, k, :, lanes] == base_ref[1] + lax.broadcasted_iota(jnp.int32, shape, 0)
    lon_here = cells_ref[1, k, :, lanes] == chunk * LANES + lax.broadcasted_iota(
        jnp.int32, shape, 1
    )
    weights = slot_weights(
        -eta_ref[k, :, lanes].astype(jnp.float32), level_here, *bounds(level_here)
    )
    return weights, level_here, row_here, lon_here


def wind_levels(base, lanes, k, points, scratch, filling, out_ref):
    for step, point in enumerate(points):
        here = base + step * (5 * STACK)
        sums = [{}, {}]
        for field in range(2):
            for c in SLOTS:
                for b in SLOTS:
                    filling.tick()
                    found = level_sums(scratch, field, here, (b, c), [point])
                    sums[field][b, c] = found[0]
        middle = (HALO * 5 + HALO) * STACK
        east = scratch[pl.ds(here + (middle + FIELD_ROW[0]), ROWS), :]
        north = scratch[pl.ds(here + (middle + FIELD_ROW[1]), ROWS), :]
        _, _, row_here, lon_here = point
        row_bounds, lon_bounds = bounds(row_here), bounds(lon_here)
        shift_row = COURANT * north
        shift_lon = COURANT * east
        for sweep in range(ITERS):
            row_weights = slot_weights(-shift_row, row_here, *row_bounds)
            lon_weights = slot_weights(-shift_lon, lon_here, *lon_bounds)
            east_found = across(sums[0], row_weights, lon_weights)
            north_found = across(sums[1], row_weights, lon_weights)
            shift_row = 0.5 * COURANT * (north + north_found)
            shift_lon = 0.5 * COURANT * (east + east_found)
        if step == len(points) - 1:
            filling.flush()
        out_ref[0, k + step, :, lanes] = shift_row
        out_ref[1, k + step, :, lanes] = shift_lon


def tracer_levels(shift_ref, base, lanes, k, points, scratch, filling, out_ref):
    outputs = []
    for step, point in enumerate(points):
        here = base + step * (5 * STACK)
        _, _, row_here, lon_here = point
        row_weights = slot_weights(
            -shift_ref[0, k + step, :, lanes], row_here, *bounds(row_here)
        )
        lon_weights = slot_weights(
            -shift_ref[1, k + step, :, lanes], lon_here, *bounds(lon_here)
        )
        for field in range(2):
            total = None
            for c, lon_slot in enumerate(SLOTS):
                column = None
                for b, row_slot in enumerate(SLOTS):
                    filling.tick()
                    found = level_sums(scratch, field, here, (row_slot, lon_slot), [point])[0]
                    term = row_weights[b] * found
                    column = term if b == 0 else column + term
                term = lon_weights[c] * column
                total = term if c == 0 else total + term
            outputs.append((field, step, total))
    filling.flush()
    for field, step, total in outputs:
        out_ref[field, k + step, :, lanes] = total.astype(out_ref.dtype)


def interpolation_kernel(levels_body, together, near_count, base_ref, field_ref, *others):
    nears, others = others[:near_count], others[near_count:]
    point_count = (len(others) - 6) // 2
    point_sources, others = others[:point_count], others[point_count:]
    out_ref, done_ref, full, even_scratch, odd_scratch = others[:5]
    points_here, arrivals = others[5:-1], others[-1]
    done_ref[...] = jnp.zeros(done_ref.shape, done_ref.dtype)
    copies = [
        pltpu.make_async_copy(source, target, arrivals.at[n])
        for n, (source, target) in enumerate(zip(point_sources, points_here))
    ]
    for copy in copies:
        copy.start()
    eta_ref, cells_ref = points_here[:2]
    levels, rows, lon_total = eta_ref.shape
    chunk_total = lon_total // LANES
    slabs = levels + 2 * HALO
    steps = levels // together
    per_step = -(-slabs // steps)
    full[HALO : HALO + levels] = field_ref[...]
    if near_count == 1:
        found = jnp.where(base_ref[0] == 0, levels + HALO, 0)
        full[pl.ds(found, HALO)] = nears[0][...].astype(jnp.float32)
        empty = levels + HALO - found
        full[pl.ds(empty, HALO)] = jnp.zeros((HALO,) + full.shape[1:], jnp.float32)
    else:
        full[:HALO] = nears[0][...].astype(jnp.float32)
        full[HALO + levels :] = nears[1][...].astype(jnp.float32)

    def first_fill(slab, carry):
        for start, finish in fill_units(slab, 0, chunk_total, full, even_scratch):
            finish(start())
        return carry

    lax.fori_loop(0, slabs, first_fill, 0)
    for copy in copies:
        copy.wait()

    def one_chunk(chunk, scratch, other):
        lanes = pl.ds(pl.multiple_of(chunk * LANES, LANES), LANES)
        following = jnp.where(chunk == chunk_total - 1, 0, chunk + 1)

        def level_step(step, carry):
            k = step * together
            units = []
            for n in range(per_step):
                slab = jnp.minimum(step * per_step + n, slabs - 1)
                units += fill_units(slab, following, chunk_total, full, other)
            filling = Interleave(units, 32 * together)
            points = [
                arrival(base_ref, eta_ref, cells_ref, k + n, chunk, lanes) for n in range(together)
            ]
            base = pl.multiple_of(k * (5 * STACK), ROWS)
            levels_body(
                *points_here[2:], base, lanes, k, points, scratch, filling, out_ref
            )
            return carry

        lax.fori_loop(0, steps, level_step, 0)

    def chunk_pair(pair, carry):
        one_chunk(2 * pair, even_scratch, odd_scratch)
        one_chunk(2 * pair + 1, odd_scratch, even_scratch)
        return carry

    lax.fori_loop(0, chunk_total // 2, chunk_pair, 0)


def interpolation_call(levels_body, base, fields, nears, points, out_dtype):
    levels, rows, lon_total = points[0].shape
    count = levels * rows * lon_total
    together = 2 if levels % 2 == 0 else 1
    scratch = pltpu.VMEM(((levels + 2 * HALO) * 5 * STACK, LANES), jnp.float32)
    in_vmem = pl.BlockSpec(memory_space=pltpu.VMEM)
    return pl.pallas_call(
        functools.partial(interpolation_kernel, levels_body, together, len(nears)),
        out_shape=(
            jax.ShapeDtypeStruct((2, levels, rows, lon_total), out_dtype),
            jax.ShapeDtypeStruct((ROWS, LANES), jnp.float32),
        ),
        in_specs=[pl.BlockSpec(memory_space=pltpu.SMEM)]
        + [in_vmem] * (1 + len(nears))
        + [pl.BlockSpec(memory_space=pl.ANY)] * len(points),
        out_specs=(in_vmem, in_vmem),
        scratch_shapes=[
            pltpu.VMEM((levels + 2 * HALO,) + fields.shape[1:], jnp.float32),
            scratch,
            scratch,
        ]
        + [pltpu.VMEM(x.shape, x.dtype) for x in points]
        + [pltpu.SemaphoreType.DMA((len(points),))],
        compiler_params=pltpu.CompilerParams(vmem_limit_bytes=32 * 1024 * 1024),
        cost_estimate=pl.CostEstimate(
            flops=count * 500, bytes_accessed=count * 40, transcendentals=0
        ),
    )(base, fields, *nears, *points)


def swap_levels(send):
    if lax.axis_size("lev") == 2:
        return (lax.ppermute(send[0], "lev", [(0, 1), (1, 0)]),)
    up = [(i, i + 1) for i in range(lax.axis_size("lev") - 1)]
    down = [(j, i) for i, j in up]
    return lax.ppermute(send[1], "lev", up), lax.ppermute(send[0], "lev", down)


def up_to(value, step):
    return -(-value // step) * step


TALL = ROWS + 2 * HALO
PAIRED = TALL // 2
HALF = LANES // 2


def legendre_kernel(numbers_ref, codes_ref, order_ref, spectra_ref, *others):
    tables, others = others[:-6], others[-6:]
    wind_ref, tracer_ref, wind_sums, tracer_sums, table_tail, column_tail = others
    _, group, level_fields, degrees = spectra_ref.shape
    bands, block, _ = wind_ref.shape
    full = degrees // LANES * LANES
    at_top = numbers_ref[0] == 0
    step = pl.program_id(0)

    @pl.when(step == 0)
    def _():
        wind_sums[...] = jnp.zeros(wind_sums.shape, jnp.float32)
        tracer_sums[...] = jnp.zeros(tracer_sums.shape, jnp.float32)
        table_tail[...] = jnp.zeros(table_tail.shape, jnp.float32)
        column_tail[...] = jnp.zeros(column_tail.shape, jnp.float32)
        codes = codes_ref[...]
        code_row = up_to(pl.num_programs(0) * group * PAIRED, ROWS)
        for band in range(bands):
            first = band * block + code_row
            wind_sums[pl.ds(first, 1), :] = jnp.right_shift(codes, 4).astype(jnp.float32)
            wind_sums[pl.ds(first + 1, 1), :] = (codes & 15).astype(jnp.float32)

    band_row = lax.broadcasted_iota(jnp.int32, (bands, LANES), 0)
    first_half = lax.broadcasted_iota(jnp.int32, (bands, LANES), 1) < HALF
    nothing = jnp.zeros((bands, LANES), jnp.float32)
    for p in range(group):
        slot = step * group + p
        edge = degrees - 1 - numbers_ref[1 + slot]
        left = []
        for number, table_ref in enumerate(tables):
            for row in range(table_ref.shape[0]):
                piece = table_ref[row, p]
                left.append(piece[:, :full])
                first = (number * table_ref.shape[0] + row) * bands
                table_tail[p, first : first + bands, : degrees - full] = piece[:, full:].astype(
                    jnp.float32
                )
        left = jnp.concatenate(left, axis=0)
        left = jnp.concatenate([left, table_tail[p].astype(jnp.bfloat16)], axis=1)
        halves = ([], [])
        for part in range(2):
            piece = spectra_ref[part, p]
            whole = piece[:, :full].astype(jnp.float32)
            lane = lax.broadcasted_iota(jnp.int32, whole.shape, 1)
            zero = jnp.zeros_like(whole)
            halves[0].append(jnp.where(lane < edge, whole, zero).astype(jnp.bfloat16))
            halves[1].append(jnp.where(lane < edge, zero, whole).astype(jnp.bfloat16))
            first = part * level_fields
            column_tail[p, first : first + level_fields, : degrees - full] = piece[
                :, full:
            ].astype(jnp.float32)
        tail = column_tail[p].astype(jnp.bfloat16)
        right = jnp.concatenate(
            [
                jnp.concatenate([jnp.concatenate(halves[0], axis=0), jnp.zeros_like(tail)], axis=1),
                jnp.concatenate([jnp.concatenate(halves[1], axis=0), tail], axis=1),
            ],
            axis=0,
        )
        found = lax.dot_general(
            left, right, (((1,), (1,)), ((), ())), preferred_element_type=jnp.float32
        )
        found = jnp.dot(
            found.astype(jnp.bfloat16), order_ref[...], preferred_element_type=jnp.float32
        )
        found = [found[i * bands : (i + 1) * bands] for i in range(ROWS)]
        if len(tables) == 2:
            low, high = found[: ROWS // 2], found[ROWS // 2 :]
            found = [jnp.where(at_top, x, y) for x, y in zip(low, high)]
            found += [jnp.where(at_top, y, x) for x, y in zip(low, high)]
        above = [
            jnp.where(band_row == 0, nothing, pltpu.roll(x, 1, 0)) for x in found[ROWS - HALO :]
        ]
        below = [
            jnp.where(band_row == bands - 1, nothing, pltpu.roll(x, bands - 1, 0))
            for x in found[:HALO]
        ]
        rows = above + found + below
        for i in range(PAIRED):
            low, high = rows[i], rows[PAIRED + i]
            place = pl.ds(slot * PAIRED + i, bands, stride=block)
            wind_sums[place, :] = jnp.where(first_half, low, pltpu.roll(high, HALF, 1))
            tracer_sums[place, :] = jnp.where(first_half, pltpu.roll(low, HALF, 1), high)

    @pl.when(step == pl.num_programs(0) - 1)
    def _():
        wind_ref[...] = wind_sums[...].astype(jnp.bfloat16).reshape(wind_ref.shape)
        tracer_ref[...] = tracer_sums[...].astype(jnp.bfloat16).reshape(tracer_ref.shape)


def column_order(level_fields):
    levels = level_fields // 4
    order = np.zeros((4 * level_fields, LANES), np.float32)
    for column in range(4 * level_fields):
        part, rest = divmod(column, level_fields)
        level, field = divmod(rest, 4)
        target = (field // 2) * HALF + part * 2 * levels + 2 * level + field % 2
        order[column, target] = 1.0
    return order.astype(jnp.bfloat16)


def block_rows(pairs):
    return up_to(up_to(pairs * PAIRED, ROWS) + 2, 16)


def legendre_call(pairing, spectra, tables):
    _, pairs, level_fields, degrees = spectra.shape
    bands = tables[0].shape[2]
    block = block_rows(pairs)
    group = next(n for n in (4, 5, 2, 1) if pairs % n == 0)
    numbers = jnp.concatenate([lax.axis_index("lev").astype(jnp.int32)[None], pairing])
    codes = jnp.pad(pairing, (0, LANES - pairs))[None, :]
    shape = jax.ShapeDtypeStruct((bands, block, LANES), jnp.bfloat16)
    whole = pl.BlockSpec((bands, block, LANES), lambda i: (0, 0, 0))
    by_pair = lambda array: pl.BlockSpec(
        (array.shape[0], group) + array.shape[2:], lambda i: (0, i, 0, 0)
    )
    return pl.pallas_call(
        legendre_kernel,
        grid=(pairs // group,),
        out_shape=(shape, shape),
        in_specs=[
            pl.BlockSpec(memory_space=pltpu.SMEM),
            pl.BlockSpec((1, LANES), lambda i: (0, 0)),
            pl.BlockSpec((4 * level_fields, LANES), lambda i: (0, 0)),
            by_pair(spectra),
        ]
        + [by_pair(table) for table in tables],
        out_specs=(whole, whole),
        scratch_shapes=[
            pltpu.VMEM((bands * block, LANES), jnp.float32),
            pltpu.VMEM((bands * block, LANES), jnp.float32),
            pltpu.VMEM((group, ROWS * bands, LANES), jnp.float32),
            pltpu.VMEM((group, 2 * level_fields, LANES), jnp.float32),
        ],
        compiler_params=pltpu.CompilerParams(vmem_limit_bytes=32 * 1024 * 1024),
        cost_estimate=pl.CostEstimate(
            flops=2 * ROWS * bands * 4 * level_fields * pairs * degrees,
            bytes_accessed=8_000_000,
            transcendentals=0,
        ),
    )(numbers, codes, jnp.asarray(column_order(level_fields)), spectra, *tables)


def fourier_table(pair_total, padded, lon_total):
    order_total = 2 * pair_total
    half = pair_total // 2
    low = 2 * np.arange(half)
    high = low + 1
    even = np.concatenate([low, order_total - 1 - high])
    odd = np.concatenate([order_total - 1 - low, high])
    lon = np.arange(lon_total // 2)
    table = np.zeros((2, 2, padded, lon_total // 2), np.float32)
    for parity, orders in enumerate((even, odd)):
        phase = (orders[:, None] * lon[None, :]) % lon_total * (2.0 * math.pi / lon_total)
        weight = np.where(orders == 0, 1.0, 2.0)[:, None]
        table[parity, 0, :pair_total] = weight * np.cos(phase)
        table[parity, 1, :pair_total] = -weight * np.sin(phase)
    return table.reshape(2, 2 * padded, lon_total // 2).astype(jnp.bfloat16)


def owner_tables(bands, pairs):
    slots = np.arange(bands * pairs)
    owner = slots[:, None] // pairs == np.arange(LANES)[None, :]
    lane = slots[:, None] % pairs == np.arange(LANES)[None, :]
    return owner.astype(jnp.bfloat16), lane.astype(np.float32)


def pair_places(flat, owner_ref, lane_ref, codes, bands, block, code_row, padded):
    pair_total = owner_ref.shape[0]
    codes[...] = jnp.zeros(codes.shape, jnp.float32)
    numbers = []
    for part in range(2):
        codes[part, :bands, :] = flat[pl.ds(code_row + part, bands, stride=block), :]
        numbers.append(
            jnp.dot(
                owner_ref[...],
                codes[part].astype(jnp.bfloat16),
                preferred_element_type=jnp.float32,
            )
        )
    pair_id = jnp.sum(
        (16.0 * numbers[0] + numbers[1]) * lane_ref[...], axis=1, keepdims=True
    ).astype(jnp.int32)
    place = jnp.right_shift(pair_id, 1) + (pair_id & 1) * (pair_total // 2)
    columns = lax.broadcasted_iota(jnp.int32, (pair_total, padded), 1)
    place = jnp.where(columns == place, 1.0, 0.0)
    if padded > pair_total:
        place = jnp.concatenate(
            [place, jnp.zeros((padded - pair_total, padded), jnp.float32)], axis=0
        )
    return place.astype(jnp.bfloat16)


def fourier_kernel(pairs, levels, leads, base_ref, sums_ref, table_ref, *others):
    if leads:
        owner_ref, lane_ref, field_ref, send_ref, place_ref = others[:5]
    else:
        place_ref, _, field_ref, send_ref = others[:4]
    codes, flat, gathered, lhs, table, arrival_sem = others[-6:]
    copy = pltpu.make_async_copy(table_ref, table, arrival_sem)
    copy.start()
    bands, block, width = sums_ref.shape
    pair_total = bands * pairs
    padded = gathered.shape[0]
    blocks = padded // LANES
    fields = 2 * levels
    flat[...] = sums_ref[...].astype(jnp.float32).reshape(bands * block, width)
    gathered[pair_total:, :] = jnp.zeros((padded - pair_total, width), jnp.float32)
    if leads:
        code_row = up_to(pairs * PAIRED, ROWS)
        place_ref[...] = pair_places(
            flat, owner_ref, lane_ref, codes, bands, block, code_row, padded
        )
    place = place_ref[...]
    low = lax.broadcasted_iota(jnp.int32, (fields, padded), 1) < pair_total // 2
    middle = fields * ROWS
    for i in range(PAIRED):
        for band in range(bands):
            gathered[band * pairs : (band + 1) * pairs, :] = flat[
                pl.ds(band * block + i, pairs, stride=PAIRED), :
            ]
        ordered = jnp.dot(
            gathered[...].T.astype(jnp.bfloat16), place, preferred_element_type=jnp.float32
        )
        for side in range(2):
            row = side * PAIRED + i
            if HALO <= row < HALO + ROWS:
                first, stride = row - HALO, ROWS
            else:
                first, stride = middle + (row - HALO - ROWS) % TALL, 2 * HALO
            for part in range(2):
                start = side * HALF + part * fields
                straight = ordered[start : start + fields]
                start = start + 2 * fields
                crossed = ordered[start : start + fields]
                both = (jnp.where(low, straight, crossed), jnp.where(low, crossed, straight))
                for parity in range(2):
                    for t in range(blocks):
                        lhs[parity, part * blocks + t, pl.ds(first, fields, stride=stride), :] = (
                            both[parity][:, t * LANES : (t + 1) * LANES]
                        )
    copy.wait()
    half = table.shape[2]

    def transform(first, count):
        found = []
        for parity in range(2):
            left = jnp.concatenate(
                [
                    lhs[parity, t, first : first + count, :].astype(jnp.bfloat16)
                    for t in range(2 * blocks)
                ],
                axis=1,
            )
            found.append(jnp.dot(left, table[parity], preferred_element_type=jnp.float32))
        pieces = (found[0] + found[1], found[0] - found[1])
        return [piece.astype(jnp.bfloat16).astype(jnp.float32) for piece in pieces]

    group = next(n for n in (4, 2, 1) if levels % n == 0)
    for level in range(0, levels, group):
        pieces = transform(level * 2 * ROWS, group * 2 * ROWS)
        for part, value in enumerate(pieces):
            value = value.reshape(group, 2 * ROWS, half)
            field_ref[level : level + group, : 2 * ROWS, part * half : (part + 1) * half] = value
    for part, value in enumerate(transform(middle, fields * 2 * HALO)):
        value = value.reshape(levels, 4 * HALO, half)
        field_ref[:, 2 * ROWS :, part * half : (part + 1) * half] = value
    if send_ref.shape[0] == 1:
        start = jnp.where(base_ref[0] == 0, levels - HALO, 0)
        send_ref[0] = field_ref[pl.ds(start, HALO)].astype(jnp.bfloat16)
    else:
        send_ref[0] = field_ref[:HALO].astype(jnp.bfloat16)
        send_ref[1] = field_ref[levels - HALO :].astype(jnp.bfloat16)


def fourier_call(base, sums, table, pairs, levels, lon_total, place=None, after=None):
    bands, block, width = sums.shape
    pair_total = bands * pairs
    padded = up_to(pair_total, LANES)
    leads = place is None
    sends = 1 if lax.axis_size("lev") == 2 else 2
    field_shape = (levels, 3 * ROWS, lon_total)
    out_shape = [
        jax.ShapeDtypeStruct(field_shape, jnp.float32),
        jax.ShapeDtypeStruct((sends, HALO) + field_shape[1:], jnp.bfloat16),
    ]
    extra = [place, after]
    if leads:
        out_shape.append(jax.ShapeDtypeStruct((padded, padded), jnp.bfloat16))
        extra = [jnp.asarray(x) for x in owner_tables(bands, pairs)]
    in_vmem = pl.BlockSpec(memory_space=pltpu.VMEM)
    return pl.pallas_call(
        functools.partial(fourier_kernel, pairs, levels, leads),
        out_shape=tuple(out_shape),
        in_specs=[
            pl.BlockSpec(memory_space=pltpu.SMEM),
            in_vmem,
            pl.BlockSpec(memory_space=pl.ANY),
        ]
        + [in_vmem] * 2,
        out_specs=(in_vmem,) * len(out_shape),
        scratch_shapes=[
            pltpu.VMEM((2, LANES, LANES), jnp.float32),
            pltpu.VMEM((bands * block, width), jnp.float32),
            pltpu.VMEM((padded, width), jnp.float32),
            pltpu.VMEM((2, 2 * padded // LANES, 2 * levels * TALL, LANES), jnp.float32),
            pltpu.VMEM(table.shape, table.dtype),
            pltpu.SemaphoreType.DMA,
        ],
        compiler_params=pltpu.CompilerParams(vmem_limit_bytes=32 * 1024 * 1024),
        cost_estimate=pl.CostEstimate(
            flops=2 * levels * 4 * TALL * padded * lon_total,
            bytes_accessed=8_000_000,
            transcendentals=0,
        ),
    )(base, sums, table, *extra)


def exchange(sums):
    return lax.all_to_all(sums, "band", split_axis=0, concat_axis=0, tiled=True)


def per_device(spectra, legendre, pairing, eta_shift, cells):
    levels, rows, lon_total = eta_shift.shape
    pairs = pairing.shape[0]
    spectra = jnp.transpose(spectra, (0, 2, 1, 3))
    table = jnp.transpose(legendre, (0, 2, 1, 3))
    if lax.axis_size("lev") == 2:
        tables = (table, lax.ppermute(table, "lev", [(0, 1), (1, 0)]))
    else:
        tables = (lax.all_gather(table, "lev", axis=0, tiled=True),)
    base = jnp.stack([lax.axis_index("lev") * levels, lax.axis_index("band") * rows])
    base = base.astype(jnp.int32)
    wind_sums, tracer_sums = legendre_call(pairing, spectra, tables)
    wind_sums = exchange(wind_sums)
    wind_sums, tracer_sums = lax.optimization_barrier((wind_sums, tracer_sums))
    tracer_sums = exchange(tracer_sums)
    pair_total = pairs * lax.axis_size("band")
    twiddles = jnp.asarray(fourier_table(pair_total, up_to(pair_total, LANES), lon_total))
    size = (pairs, levels, lon_total)
    winds, send, place = fourier_call(base, wind_sums, twiddles, *size)
    displacement, done = interpolation_call(
        wind_levels, base, winds, swap_levels(send), (eta_shift, cells), jnp.float32
    )
    tracers, send = fourier_call(base, tracer_sums, twiddles, *size, place, done)
    advected, _ = interpolation_call(
        tracer_levels,
        base,
        tracers,
        swap_levels(send),
        (eta_shift, cells, displacement),
        jnp.bfloat16,
    )
    return advected, displacement


def solution(mesh):
    return jax.shard_map(
        per_device,
        mesh=mesh,
        in_specs=(
            P(None, "lev", "band", None),
            P("lev", None, "band", None),
            P("band"),
            P("lev", "band", None),
            P(None, "lev", "band", None),
        ),
        out_specs=(P(None, "lev", "band", None), P(None, "lev", "band", None)),
        check_vma=False,
    )
```

time: 108 us -> 116 us (1.074)
  waiting for transfers between devices: 28 us -> 4.77 us
  blocking collectives: 0 us -> 20.1 us
  Pallas kernels: 58.1 us -> 69.7 us
  starting transfers between devices: 10.1 us -> 7.87 us
  local copies, waits for them, and re-layouts: 8.96 us -> 10.8 us
    all_to_all x1, waiting for transfers between devices: 24.2 us -> 0.01 us  [exchange(): return lax.all_to_all(sums, 'band', split_axis=0, concat_axis=0, tiled=True)]
    all_to_all x0 -> x1, blocking collectives: none -> 20.1 us  [exchange(): return lax.all_to_all(sums, 'band', split_axis=0, concat_axis=0, tiled=True)]
    pallas_call x4 -> x5, Pallas kernels: 58.1 us -> 69.7 us  [the longest x2 53.8 us: interpolation_call(): pl.pallas_call(functools.partial(interpolation_kernel, levels_body, toget...]
    all_to_all x1, starting transfers between devices: 6.8 us -> 4.63 us  [exchange(): return lax.all_to_all(sums, 'band', split_axis=0, concat_axis=0, tiled=True)]
    unnamed x16 -> x22, local copies, waits for them, and re-layouts: 8.15 us -> 10.1 us
  transfers between devices with their start and end apart: 4 -> 4, of which waited for: 4 -> 3; matrix products, arithmetic and copies ran while one was open for 2% -> 1% of each run, Pallas kernels for 0% -> 28%
where the time goes in v6:
time: 116 us; the launch traced here: 115 us
  Pallas kernels  69.7 us (60%)
  blocking collectives  20.1 us (17%)
  local copies, waits for them, and re-layouts  10.8 us (9%)
  starting transfers between devices  7.87 us (7%)
  waiting for transfers between devices  4.77 us (4%)
    pallas_call x2, Pallas kernels, interpolation_call(): pl.pallas_call(functools.partial(interpolation_kernel, levels_body, toget...  53.8 us
    all_to_all x1, blocking collectives, exchange(): return lax.all_to_all(sums, 'band', split_axis=0, concat_axis=0, tiled=True)  20.1 us
    unnamed x22, local copies, waits for them, and re-layouts  10.1 us
    pallas_call x1, Pallas kernels, legendre_call(): pl.pallas_call(legendre_kernel, grid=(pairs // group,), out_shape=(shape,...  7.99 us
    pallas_call x2, Pallas kernels, fourier_call(): pl.pallas_call(functools.partial(fourier_kernel, pairs, levels, leads), o...  7.93 us
    all_to_all x1, starting transfers between devices, exchange(): return lax.all_to_all(sums, 'band', split_axis=0, concat_axis=0, tiled=True)  4.63 us
    ppermute x2, starting transfers between devices, swap_levels(): return (lax.ppermute(send[0], 'lev', [(0, 1), (1, 0)]),)  2.49 us
    ppermute x1, waiting for transfers between devices, per_device(): tables = (table, lax.ppermute(table, 'lev', [(0, 1), (1, 0)]))  2.42 us
  transfers between devices with their start and end apart: 4, of which 3 were waited for; matrix products, arithmetic and copies ran while one was open for 1% of the time, Pallas kernels for 28%

profile of v6, /device:TPU:9, one launch (start us, length us, event | category | flops | bytes accessed | tf_op | source)
XLA Modules:
  0.0 114.7 jit_solution(14523490682639815518)
XLA Ops:
  0.6 0.7 collective-permute-start
  1.4 0.7 pad_bitcast_fusion.codes_ref
  2.0 0.7 pad_add_fusion.1.numbers_ref
  2.8 2.4 %collective-permute-done.others_1_ = bf16[4,20,16,641]{3,2,1,0:T(8,128)(2,1)S(1)} collective-permute-done((bf16[4,20,16,641]{3,2,1,0:T(8,128)(2,1)}, bf16[4,20,16,641]{3,2,1,0:T(8,128)(2,1)S(1)}, u32[]{:S(2)}, u32[]{:S(2)}) %collective-permute-start) | collective-permute-done | bytes 1640992 | tf_op jit(solution)/shard_map/ppermute | solution.py:672
  5.2 0.0 copy-start.3
  5.2 1.5 %copy-done.3 = bf16[2,32,20,641]{3,1,2,0:T(8,128)(2,1)S(1)} copy-done((bf16[2,32,20,641]{3,1,2,0:T(8,128)(2,1)S(1)}, bf16[2,32,20,641]{3,1,2,0:T(8,128)(2,1)}, u32[]{:S(2)}) %copy-start.3) | copy-done | bytes 1640984
  6.7 0.0 copy-start.4
  6.7 1.5 %copy-done.4 = bf16[4,16,20,641]{3,1,2,0:T(8,128)(2,1)S(1)} copy-done((bf16[4,16,20,641]{3,1,2,0:T(8,128)(2,1)S(1)}, bf16[4,16,20,641]{3,1,2,0:T(8,128)(2,1)}, u32[]{:S(2)}) %copy-start.4) | copy-done | bytes 1640984
  8.3 0.0 copy-start.10
  8.3 0.8 copy-done.10
  9.0 8.0 %shard_map.104 = (bf16[16,128,128]{2,1,0:T(8,128)(2,1)S(1)}, bf16[16,128,128]{2,1,0:T(8,128)(2,1)}) custom-call(s32[21]{0:T(128)S(1)} %pad_add_fusion.1.numbers_ref, s32[1,128]{1,0:T(1,128)S(1)} %pad_bitcast_fusion.codes_ref, bf16[128,128]{1,0:T(8,128)(2,1)S(1)} %copy-done.10, bf16[2,20,32,641]{3,2,1,0:T(8,128)(2,1)S(1)} %bitcast.9, ...), custom_call_target="tpu_custom_call" | custom-call | flops 420085760 | bytes 8000000 | tf_op jit(solution)/shard_map/pallas_call | solution.py:460
  17.0 20.1 %all_to_all.10.sums_ref = bf16[16,128,128]{2,1,0:T(8,128)(2,1)S(1)} all-to-all(bf16[16,128,128]{2,1,0:T(8,128)(2,1)S(1)} %get-tuple-element.14), channel_id=1, replica_groups=mesh['band'=16,'lev'=2] {'band'}, dimensions={0} | all-to-all | bytes 1048576 | tf_op jit(solution)/shard_map/all_to_all | solution.py:663
  37.1 4.6 %all-to-all-start.1 = ((bf16[16,128,128]{2,1,0:T(8,128)(2,1)}), bf16[16,128,128]{2,1,0:T(8,128)(2,1)S(1)}, u32[]{:S(2)}, u32[]{:S(2)}) async-start(bf16[16,128,128]{2,1,0:T(8,128)(2,1)} %get-tuple-element.16), calls=%async_computation.1 | async-start | bytes 1048576 | tf_op jit(solution)/shard_map/all_to_all | solution.py:663
  41.7 0.1 pad_add_fusion.base_ref
  41.8 0.0 copy-start
  41.8 2.2 %copy-done = bf16[2,768,1408]{2,1,0:T(8,128)(2,1)S(1)} copy-done((bf16[2,768,1408]{2,1,0:T(8,128)(2,1)S(1)}, bf16[2,768,1408]{2,1,0:T(8,128)(2,1)}, u32[]{:S(2)}) %copy-start) | copy-done | bytes 4325400
  44.0 0.0 copy-start.8
  44.1 0.9 copy-done.8
  45.0 0.0 copy-start.9
  45.0 0.9 copy-done.9
  45.9 0.0 copy-start.2
  45.9 0.0 copy-start.6
  45.9 4.1 %shard_map.105 = (f32[8,24,2816]{2,1,0:T(8,128)S(1)}, bf16[1,2,24,2816]{3,2,1,0:T(8,128)(2,1)S(1)}, bf16[384,384]{1,0:T(8,128)(2,1)S(1)}) custom-call(s32[2]{0:T(128)S(1)} %pad_add_fusion.base_ref, bf16[16,128,128]{2,1,0:T(8,128)(2,1)S(1)} %all_to_all.10.sums_ref, bf16[2,768,1408]{2,1,0:T(8,128)(2,1)S(1)} %copy-done, bf16[320,128]{1,0:T(8,128)(2,1)S(1)} %copy-done.9, ...), custom_call_target="tpu_custom_call" | custom-call | flops 830472192 | bytes 8000000 | tf_op jit(solution)/shard_map/pallas_call | solution.py:635
  49.9 2.1 %collective-permute-start.1 = (bf16[2,24,2816]{2,1,0:T(8,128)(2,1)S(1)}, bf16[2,24,2816]{2,1,0:T(8,128)(2,1)S(1)}, u32[]{:S(2)}, u32[]{:S(2)}) collective-permute-start(bf16[2,24,2816]{2,1,0:T(8,128)(2,1)S(1)} %bitcast.12), channel_id=1, source_target_pairs={{0,1},{1,0},{2,3},{3,2},{4,5},{5,4},{6,7},{7,6},{8,9},{9,8},{10,11... | collective-permute-start | bytes 811016 | tf_op jit(solution)/shard_map/ppermute | solution.py:328
  52.0 1.2 %collective-permute-done.1.others_0_ = bf16[2,24,2816]{2,1,0:T(8,128)(2,1)S(1)} collective-permute-done((bf16[2,24,2816]{2,1,0:T(8,128)(2,1)S(1)}, bf16[2,24,2816]{2,1,0:T(8,128)(2,1)S(1)}, u32[]{:S(2)}, u32[]{:S(2)}) %collective-permute-start.1) | collective-permute-done | bytes 270368 | tf_op jit(solution)/shard_map/ppermute | solution.py:328
  53.2 0.0 copy-done.2
  53.2 0.0 copy-done.6
  53.2 27.8 %shard_map.106 = (f32[2,8,8,2816]{3,2,1,0:T(8,128)}, f32[8,128]{1,0:T(8,128)S(1)}) custom-call(s32[2]{0:T(128)S(1)} %pad_add_fusion.base_ref, f32[8,24,2816]{2,1,0:T(8,128)S(1)} %get-tuple-element.19.field_ref, bf16[2,24,2816]{2,1,0:T(8,128)(2,1)S(1)} %collective-permute-done.1.others_0_, bf16[8,8,2816]{2,1,0:T(8,128)(2,1)S(1)} %copy-done.6, ...), custom_call_target="tpu_custom_call" | custom-call | flops 90112000 | bytes 7208960 | tf_op jit(solution)/shard_map/pallas_call | solution.py:302
  81.0 0.0 all-to-all-done.1.sums_ref
  81.0 0.0 copy-start.1
  81.0 2.2 %copy-done.1 = bf16[2,768,1408]{2,1,0:T(8,128)(2,1)S(1)} copy-done((bf16[2,768,1408]{2,1,0:T(8,128)(2,1)S(1)}, bf16[2,768,1408]{2,1,0:T(8,128)(2,1)}, u32[]{:S(2)}) %copy-start.1) | copy-done | bytes 4325400
  83.3 0.0 copy-start.5
  83.3 0.0 copy-start.7
  83.3 3.9 %shard_map.107 = (f32[8,24,2816]{2,1,0:T(8,128)S(1)}, bf16[1,2,24,2816]{3,2,1,0:T(8,128)(2,1)S(1)}) custom-call(s32[2]{0:T(128)S(1)} %pad_add_fusion.base_ref, bf16[16,128,128]{2,1,0:T(8,128)(2,1)S(1)} %all-to-all-done.1.sums_ref, bf16[2,768,1408]{2,1,0:T(8,128)(2,1)S(1)} %copy-done.1, bf16[384,384]{1,0:T(8,128)(2,1)S(1)} %get-tuple-element.18.others_0_, ...), custom_call_target="tpu_custom_call" | custom-call | flops 830472192 | bytes 8000000 | tf_op jit(solution)/shard_map/pallas_call | solution.py:635
  87.1 0.4 collective-permute-start.2
  87.6 1.2 %collective-permute-done.2.others_0_ = bf16[2,24,2816]{2,1,0:T(8,128)(2,1)S(1)} collective-permute-done((bf16[2,24,2816]{2,1,0:T(8,128)(2,1)S(1)}, bf16[2,24,2816]{2,1,0:T(8,128)(2,1)S(1)}, u32[]{:S(2)}, u32[]{:S(2)}) %collective-permute-start.2) | collective-permute-done | bytes 270368 | tf_op jit(solution)/shard_map/ppermute | solution.py:328
  88.8 0.0 copy-done.5
  88.8 0.0 copy-done.7
  88.8 26.0 %shard_map.108 = (bf16[2,8,8,2816]{3,2,1,0:T(8,128)(2,1)}, f32[8,128]{1,0:T(8,128)}) custom-call(s32[2]{0:T(128)S(1)} %pad_add_fusion.base_ref, f32[8,24,2816]{2,1,0:T(8,128)S(1)} %get-tuple-element.22.field_ref, bf16[2,24,2816]{2,1,0:T(8,128)(2,1)S(1)} %collective-permute-done.2.others_0_, bf16[8,8,2816]{2,1,0:T(8,128)(2,1)S(1)} %copy-done.7, ...), custom_call_target="tpu_custom_call" | custom-call | flops 90112000 | bytes 7208960 | tf_op jit(solution)/shard_map/pallas_call | solution.py:302
Async XLA Ops:
  0.6 4.6 %collective-permute-start = (bf16[4,20,16,641]{3,2,1,0:T(8,128)(2,1)}, bf16[4,20,16,641]{3,2,1,0:T(8,128)(2,1)S(1)}, u32[]{:S(2)}, u32[]{:S(2)}) collective-permute-start(bf16[4,20,16,641]{3,2,1,0:T(8,128)(2,1)} %bitcast.10), channel_id=1, source_target_pairs={{0,1},{1,0},{2,3},{3,2},{4,5},{5,4},{6,7},{7,6},{8,9},{9,8},{10,11... | collective-permute-start | bytes 4922888 | tf_op jit(solution)/shard_map/ppermute | solution.py:672
  5.2 1.5 %copy-start.3 = (bf16[2,32,20,641]{3,1,2,0:T(8,128)(2,1)S(1)}, bf16[2,32,20,641]{3,1,2,0:T(8,128)(2,1)}, u32[]{:S(2)}) copy-start(bf16[2,32,20,641]{3,1,2,0:T(8,128)(2,1)} %param.9) | copy-start | bytes 4922884
  6.7 1.5 %copy-start.4 = (bf16[4,16,20,641]{3,1,2,0:T(8,128)(2,1)S(1)}, bf16[4,16,20,641]{3,1,2,0:T(8,128)(2,1)}, u32[]{:S(2)}) copy-start(bf16[4,16,20,641]{3,1,2,0:T(8,128)(2,1)} %param.10) | copy-start | bytes 4922884
  8.3 0.8 copy-start.10
  37.1 43.9 %all-to-all-start.1 = ((bf16[16,128,128]{2,1,0:T(8,128)(2,1)}), bf16[16,128,128]{2,1,0:T(8,128)(2,1)S(1)}, u32[]{:S(2)}, u32[]{:S(2)}) async-start(bf16[16,128,128]{2,1,0:T(8,128)(2,1)} %get-tuple-element.16), calls=%async_computation.1 | async-start | bytes 1048576 | tf_op jit(solution)/shard_map/all_to_all | solution.py:663
  41.8 2.2 %copy-start = (bf16[2,768,1408]{2,1,0:T(8,128)(2,1)S(1)}, bf16[2,768,1408]{2,1,0:T(8,128)(2,1)}, u32[]{:S(2)}) copy-start(bf16[2,768,1408]{2,1,0:T(8,128)(2,1)} %constant.21.clone.table_ref) | copy-start | bytes 12976132
  44.0 0.9 copy-start.8
  45.0 0.9 copy-start.9
  45.9 7.3 %copy-start.2 = (s32[3,8,8,2816]{3,2,1,0:T(8,128)S(1)}, s32[3,8,8,2816]{3,2,1,0:T(8,128)}, u32[]{:S(2)}) copy-start(s32[3,8,8,2816]{3,2,1,0:T(8,128)} %others_2_.3) | copy-start | bytes 6488068
  45.9 7.3 %copy-start.6 = (bf16[8,8,2816]{2,1,0:T(8,128)(2,1)S(1)}, bf16[8,8,2816]{2,1,0:T(8,128)(2,1)}, u32[]{:S(2)}) copy-start(bf16[8,8,2816]{2,1,0:T(8,128)(2,1)} %others_1_.4) | copy-start | bytes 1081348
  49.9 3.2 %collective-permute-start.1 = (bf16[2,24,2816]{2,1,0:T(8,128)(2,1)S(1)}, bf16[2,24,2816]{2,1,0:T(8,128)(2,1)S(1)}, u32[]{:S(2)}, u32[]{:S(2)}) collective-permute-start(bf16[2,24,2816]{2,1,0:T(8,128)(2,1)S(1)} %bitcast.12), channel_id=1, source_target_pairs={{0,1},{1,0},{2,3},{3,2},{4,5},{5,4},{6,7},{7,6},{8,9},{9,8},{10,11... | collective-permute-start | bytes 811016 | tf_op jit(solution)/shard_map/ppermute | solution.py:328
  81.0 2.2 %copy-start.1 = (bf16[2,768,1408]{2,1,0:T(8,128)(2,1)S(1)}, bf16[2,768,1408]{2,1,0:T(8,128)(2,1)}, u32[]{:S(2)}) copy-start(bf16[2,768,1408]{2,1,0:T(8,128)(2,1)} %constant.21.clone.table_ref) | copy-start | bytes 12976132
  83.3 5.5 %copy-start.5 = (f32[2,8,8,2816]{3,2,1,0:T(8,128)S(1)}, f32[2,8,8,2816]{3,2,1,0:T(8,128)}, u32[]{:S(2)}) copy-start(f32[2,8,8,2816]{3,2,1,0:T(8,128)} %get-tuple-element.13.others_3_) | copy-start | bytes 4325380
  83.3 5.5 %copy-start.7 = (bf16[8,8,2816]{2,1,0:T(8,128)(2,1)S(1)}, bf16[8,8,2816]{2,1,0:T(8,128)(2,1)}, u32[]{:S(2)}) copy-start(bf16[8,8,2816]{2,1,0:T(8,128)(2,1)} %others_1_.4) | copy-start | bytes 1081348
  87.1 1.6 %collective-permute-start.2 = (bf16[2,24,2816]{2,1,0:T(8,128)(2,1)S(1)}, bf16[2,24,2816]{2,1,0:T(8,128)(2,1)S(1)}, u32[]{:S(2)}, u32[]{:S(2)}) collective-permute-start(bf16[2,24,2816]{2,1,0:T(8,128)(2,1)S(1)} %bitcast.13), channel_id=1, source_target_pairs={{0,1},{1,0},{2,3},{3,2},{4,5},{5,4},{6,7},{7,6},{8,9},{9,8},{10,11... | collective-permute-start | bytes 811016 | tf_op jit(solution)/shard_map/ppermute | solution.py:328

commit v7 on v6

--- a/solution.py
+++ b/solution.py
@@ -125,8 +125,10 @@
     loaded = {}
 
     def load(a, b, c):
+        offset = ((a + HALO) * 5 + c + HALO) * STACK + FIELD_ROW[field] + b
+        if slot == (2, 2):
+            return scratch[pl.ds(base + offset, ROWS), :]
         if (a, b, c) not in loaded:
-            offset = ((a + HALO) * 5 + c + HALO) * STACK + FIELD_ROW[field] + b
             loaded[a, b, c] = scratch[pl.ds(base + offset, ROWS), :]
         return loaded[a, b, c]
 
@@ -148,98 +150,150 @@
     return [one(step, *point) for step, point in enumerate(points)]
 
 
-def across(sums, row_weights, lon_weights):
+def across(scratch, field, base, points, row_weights, lon_weights, filling, keep=None):
+    columns = [[None] * 4 for _ in points]
+    for b, row_slot in enumerate(SLOTS):
+        for c, lon_slot in enumerate(SLOTS):
+            filling.tick()
+            found = level_sums(scratch, field, base, (row_slot, lon_slot), points)
+            for step, value in enumerate(found):
+                if keep is not None:
+                    keep[field, step, 4 * b + c] = value
+                term = row_weights[step][b] * value
+                columns[step][c] = term if b == 0 else columns[step][c] + term
+    return [weighted(weights, column) for weights, column in zip(lon_weights, columns)]
+
+
+def across_kept(keep, field, step, row_weights, lon_weights):
     return weighted(
-        lon_weights, [weighted(row_weights, [sums[b, c] for b in SLOTS]) for c in SLOTS]
-    )
-
-
-def arrival(base_ref, eta_ref, cells_ref, k, chunk, lanes):
-    shape = (cells_ref.shape[2], LANES)
-    level_here = cells_ref[2, k, :, lanes] == base_ref[0] + k
-    row_here = cells_ref[0, k, :, lanes] == base_ref[1] + lax.broadcasted_iota(jnp.int32, shape, 0)
-    lon_here = cells_ref[1, k, :, lanes] == chunk * LANES + lax.broadcasted_iota(
-        jnp.int32, shape, 1
-    )
-    weights = slot_weights(
-        -eta_ref[k, :, lanes].astype(jnp.float32), level_here, *bounds(level_here)
-    )
-    return weights, level_here, row_here, lon_here
-
-
-def wind_levels(base, lanes, k, points, scratch, filling, out_ref):
-    for step, point in enumerate(points):
-        here = base + step * (5 * STACK)
-        sums = [{}, {}]
-        for field in range(2):
-            for c in SLOTS:
-                for b in SLOTS:
-                    filling.tick()
-                    found = level_sums(scratch, field, here, (b, c), [point])
-                    sums[field][b, c] = found[0]
-        middle = (HALO * 5 + HALO) * STACK
-        east = scratch[pl.ds(here + (middle + FIELD_ROW[0]), ROWS), :]
-        north = scratch[pl.ds(here + (middle + FIELD_ROW[1]), ROWS), :]
-        _, _, row_here, lon_here = point
-        row_bounds, lon_bounds = bounds(row_here), bounds(lon_here)
-        shift_row = COURANT * north
-        shift_lon = COURANT * east
+        lon_weights,
+        [
+            weighted(row_weights, [keep[field, step, 4 * b + c] for b in range(4)])
+            for c in range(4)
+        ],
+    )
+
+
+def prepare_kernel(base_ref, after_ref, eta_ref, cells_ref, table_ref, points_ref, out_ref, sem):
+    copy = pltpu.make_async_copy(table_ref, out_ref, sem)
+    copy.start()
+    levels, rows, lon_total = eta_ref.shape
+    shape = (rows, LANES)
+    row_here = base_ref[1] + lax.broadcasted_iota(jnp.int32, shape, 0)
+    lane = lax.broadcasted_iota(jnp.int32, shape, 1)
+
+    def chunk_step(chunk, carry):
+        lanes = pl.ds(pl.multiple_of(chunk * LANES, LANES), LANES)
+        for k in range(levels):
+            level_here = cells_ref[2, k, :, lanes] == base_ref[0] + k
+            weights = slot_weights(
+                -eta_ref[k, :, lanes].astype(jnp.float32), level_here, *bounds(level_here)
+            )
+            here = (
+                level_here,
+                cells_ref[0, k, :, lanes] == row_here,
+                cells_ref[1, k, :, lanes] == chunk * LANES + lane,
+            )
+            for n, value in enumerate(weights + tuple(bounds(x)[0] for x in here)):
+                points_ref[n, k, :, lanes] = value
+        return carry
+
+    lax.fori_loop(0, lon_total // LANES, chunk_step, 0)
+    copy.wait()
+
+
+def prepare_call(base, after, eta_shift, cells, table):
+    in_vmem = pl.BlockSpec(memory_space=pltpu.VMEM)
+    return pl.pallas_call(
+        prepare_kernel,
+        out_shape=(
+            jax.ShapeDtypeStruct((7,) + eta_shift.shape, jnp.float32),
+            jax.ShapeDtypeStruct(table.shape, table.dtype),
+        ),
+        in_specs=[pl.BlockSpec(memory_space=pltpu.SMEM)]
+        + [in_vmem] * 3
+        + [pl.BlockSpec(memory_space=pl.ANY)],
+        out_specs=(in_vmem, in_vmem),
+        scratch_shapes=[pltpu.SemaphoreType.DMA],
+        compiler_params=pltpu.CompilerParams(vmem_limit_bytes=32 * 1024 * 1024),
+        cost_estimate=pl.CostEstimate(
+            flops=40 * eta_shift.size, bytes_accessed=20_000_000, transcendentals=0
+        ),
+    )(base, after, eta_shift, cells, table)
+
+
+def arrival(points_ref, k, lanes):
+    here = [points_ref[n, k, :, lanes] > -1.0 for n in range(4, 7)]
+    return tuple(points_ref[n, k, :, lanes] for n in range(4)), *here
+
+
+def both_weights(shift_row, shift_lon, point):
+    _, _, row_here, lon_here = point
+    return (
+        slot_weights(-shift_row, row_here, *bounds(row_here)),
+        slot_weights(-shift_lon, lon_here, *bounds(lon_here)),
+    )
+
+
+def wind_levels(base, lanes, k, points, scratch, keep, filling, *out_refs):
+    def arrival_wind(field, step):
+        middle = (HALO * 5 + HALO) * STACK + step * (5 * STACK) + FIELD_ROW[field]
+        return scratch[pl.ds(base + middle, ROWS), :]
+
+    count = range(len(points))
+    weights = [
+        both_weights(
+            COURANT * arrival_wind(1, step), COURANT * arrival_wind(0, step), points[step]
+        )
+        for step in count
+    ]
+    row_weights, lon_weights = zip(*weights)
+    found = [
+        across(scratch, field, base, points, row_weights, lon_weights, filling, keep)
+        for field in range(2)
+    ]
+    filling.flush()
+    for step in count:
+        east, north = arrival_wind(0, step), arrival_wind(1, step)
+        east_found, north_found = found[0][step], found[1][step]
         for sweep in range(ITERS):
-            row_weights = slot_weights(-shift_row, row_here, *row_bounds)
-            lon_weights = slot_weights(-shift_lon, lon_here, *lon_bounds)
-            east_found = across(sums[0], row_weights, lon_weights)
-            north_found = across(sums[1], row_weights, lon_weights)
             shift_row = 0.5 * COURANT * (north + north_found)
             shift_lon = 0.5 * COURANT * (east + east_found)
-        if step == len(points) - 1:
-            filling.flush()
-        out_ref[0, k + step, :, lanes] = shift_row
-        out_ref[1, k + step, :, lanes] = shift_lon
-
-
-def tracer_levels(shift_ref, base, lanes, k, points, scratch, filling, out_ref):
-    outputs = []
-    for step, point in enumerate(points):
-        here = base + step * (5 * STACK)
-        _, _, row_here, lon_here = point
-        row_weights = slot_weights(
-            -shift_ref[0, k + step, :, lanes], row_here, *bounds(row_here)
-        )
-        lon_weights = slot_weights(
-            -shift_ref[1, k + step, :, lanes], lon_here, *bounds(lon_here)
-        )
-        for field in range(2):
-            total = None
-            for c, lon_slot in enumerate(SLOTS):
-                column = None
-                for b, row_slot in enumerate(SLOTS):
-                    filling.tick()
-                    found = level_sums(scratch, field, here, (row_slot, lon_slot), [point])[0]
-                    term = row_weights[b] * found
-                    column = term if b == 0 else column + term
-                term = lon_weights[c] * column
-                total = term if c == 0 else total + term
-            outputs.append((field, step, total))
+            if sweep < ITERS - 1:
+                weights = both_weights(shift_row, shift_lon, points[step])
+                east_found = across_kept(keep, 0, step, *weights)
+                north_found = across_kept(keep, 1, step, *weights)
+        for out_ref in out_refs:
+            out_ref[0, k + step, :, lanes] = shift_row
+            out_ref[1, k + step, :, lanes] = shift_lon
+
+
+def tracer_levels(shift_ref, base, lanes, k, points, scratch, keep, filling, out_ref):
+    weights = [
+        both_weights(
+            shift_ref[0, k + step, :, lanes], shift_ref[1, k + step, :, lanes], points[step]
+        )
+        for step in range(len(points))
+    ]
+    row_weights, lon_weights = zip(*weights)
+    found = [
+        across(scratch, field, base, points, row_weights, lon_weights, filling)
+        for field in range(2)
+    ]
     filling.flush()
-    for field, step, total in outputs:
-        out_ref[field, k + step, :, lanes] = total.astype(out_ref.dtype)
-
-
-def interpolation_kernel(levels_body, together, near_count, base_ref, field_ref, *others):
+    for field in range(2):
+        for step, total in enumerate(found[field]):
+            out_ref[field, k + step, :, lanes] = total.astype(out_ref.dtype)
+
+
+def interpolation_kernel(
+    levels_body, together, near_count, out_count, base_ref, field_ref, points_ref, *others
+):
     nears, others = others[:near_count], others[near_count:]
-    point_count = (len(others) - 6) // 2
-    point_sources, others = others[:point_count], others[point_count:]
-    out_ref, done_ref, full, even_scratch, odd_scratch = others[:5]
-    points_here, arrivals = others[5:-1], others[-1]
+    full, even_scratch, odd_scratch, keep = others[-4:]
+    extra, out_refs, done_ref = others[: -5 - out_count], others[-5 - out_count : -5], others[-5]
     done_ref[...] = jnp.zeros(done_ref.shape, done_ref.dtype)
-    copies = [
-        pltpu.make_async_copy(source, target, arrivals.at[n])
-        for n, (source, target) in enumerate(zip(point_sources, points_here))
-    ]
-    for copy in copies:
-        copy.start()
-    eta_ref, cells_ref = points_here[:2]
-    levels, rows, lon_total = eta_ref.shape
+    _, levels, rows, lon_total = points_ref.shape
     chunk_total = lon_total // LANES
     slabs = levels + 2 * HALO
     steps = levels // together
@@ -260,8 +314,6 @@
         return carry
 
     lax.fori_loop(0, slabs, first_fill, 0)
-    for copy in copies:
-        copy.wait()
 
     def one_chunk(chunk, scratch, other):
         lanes = pl.ds(pl.multiple_of(chunk * LANES, LANES), LANES)
@@ -273,13 +325,11 @@
             for n in range(per_step):
                 slab = jnp.minimum(step * per_step + n, slabs - 1)
                 units += fill_units(slab, following, chunk_total, full, other)
-            filling = Interleave(units, 32 * together)
-            points = [
-                arrival(base_ref, eta_ref, cells_ref, k + n, chunk, lanes) for n in range(together)
-            ]
+            filling = Interleave(units, 32)
+            points = [arrival(points_ref, k + n, lanes) for n in range(together)]
             base = pl.multiple_of(k * (5 * STACK), ROWS)
             levels_body(
-                *points_here[2:], base, lanes, k, points, scratch, filling, out_ref
+                *extra, base, lanes, k, points, scratch, keep, filling, *out_refs
             )
             return carry
 
@@ -293,34 +343,31 @@
     lax.fori_loop(0, chunk_total // 2, chunk_pair, 0)
 
 
-def interpolation_call(levels_body, base, fields, nears, points, out_dtype):
-    levels, rows, lon_total = points[0].shape
+def interpolation_call(levels_body, base, fields, points, nears, extra, out_dtype, out_count):
+    _, levels, rows, lon_total = points.shape
     count = levels * rows * lon_total
-    together = 2 if levels % 2 == 0 else 1
+    together = next(n for n in (4, 2, 1) if levels % n == 0)
     scratch = pltpu.VMEM(((levels + 2 * HALO) * 5 * STACK, LANES), jnp.float32)
     in_vmem = pl.BlockSpec(memory_space=pltpu.VMEM)
+    out = jax.ShapeDtypeStruct((2, levels, rows, lon_total), out_dtype)
+    done = jax.ShapeDtypeStruct((ROWS, LANES), jnp.float32)
     return pl.pallas_call(
-        functools.partial(interpolation_kernel, levels_body, together, len(nears)),
-        out_shape=(
-            jax.ShapeDtypeStruct((2, levels, rows, lon_total), out_dtype),
-            jax.ShapeDtypeStruct((ROWS, LANES), jnp.float32),
-        ),
+        functools.partial(interpolation_kernel, levels_body, together, len(nears), out_count),
+        out_shape=(out,) * out_count + (done,),
         in_specs=[pl.BlockSpec(memory_space=pltpu.SMEM)]
-        + [in_vmem] * (1 + len(nears))
-        + [pl.BlockSpec(memory_space=pl.ANY)] * len(points),
-        out_specs=(in_vmem, in_vmem),
+        + [in_vmem] * (2 + len(nears) + len(extra)),
+        out_specs=(in_vmem,) * (out_count + 1),
         scratch_shapes=[
             pltpu.VMEM((levels + 2 * HALO,) + fields.shape[1:], jnp.float32),
             scratch,
             scratch,
-        ]
-        + [pltpu.VMEM(x.shape, x.dtype) for x in points]
-        + [pltpu.SemaphoreType.DMA((len(points),))],
+            pltpu.VMEM((2, together, 16, ROWS, LANES), jnp.float32),
+        ],
         compiler_params=pltpu.CompilerParams(vmem_limit_bytes=32 * 1024 * 1024),
         cost_estimate=pl.CostEstimate(
             flops=count * 500, bytes_accessed=count * 40, transcendentals=0
         ),
-    )(base, fields, *nears, *points)
+    )(base, fields, points, *nears, *extra)
 
 
 def swap_levels(send):
@@ -341,9 +388,10 @@
 
 
 def legendre_kernel(numbers_ref, codes_ref, order_ref, spectra_ref, *others):
-    tables, others = others[:-6], others[-6:]
-    wind_ref, tracer_ref, wind_sums, tracer_sums, table_tail, column_tail = others
-    _, group, level_fields, degrees = spectra_ref.shape
+    tables, others = others[:-7], others[-7:]
+    wind_ref, tracer_ref, done_ref, wind_sums, tracer_sums, table_tail, column_tail = others
+    _, pairs, level_fields, degrees = spectra_ref.shape
+    group = table_tail.shape[0]
     bands, block, _ = wind_ref.shape
     full = degrees // LANES * LANES
     at_top = numbers_ref[0] == 0
@@ -353,6 +401,7 @@
     def _():
         wind_sums[...] = jnp.zeros(wind_sums.shape, jnp.float32)
         tracer_sums[...] = jnp.zeros(tracer_sums.shape, jnp.float32)
+        done_ref[...] = jnp.zeros(done_ref.shape, jnp.float32)
         table_tail[...] = jnp.zeros(table_tail.shape, jnp.float32)
         column_tail[...] = jnp.zeros(column_tail.shape, jnp.float32)
         codes = codes_ref[...]
@@ -371,7 +420,7 @@
         left = []
         for number, table_ref in enumerate(tables):
             for row in range(table_ref.shape[0]):
-                piece = table_ref[row, p]
+                piece = table_ref[row, slot]
                 left.append(piece[:, :full])
                 first = (number * table_ref.shape[0] + row) * bands
                 table_tail[p, first : first + bands, : degrees - full] = piece[:, full:].astype(
@@ -381,7 +430,7 @@
         left = jnp.concatenate([left, table_tail[p].astype(jnp.bfloat16)], axis=1)
         halves = ([], [])
         for part in range(2):
-            piece = spectra_ref[part, p]
+            piece = spectra_ref[part, slot]
             whole = piece[:, :full].astype(jnp.float32)
             lane = lax.broadcasted_iota(jnp.int32, whole.shape, 1)
             zero = jnp.zeros_like(whole)
@@ -454,21 +503,19 @@
     codes = jnp.pad(pairing, (0, LANES - pairs))[None, :]
     shape = jax.ShapeDtypeStruct((bands, block, LANES), jnp.bfloat16)
     whole = pl.BlockSpec((bands, block, LANES), lambda i: (0, 0, 0))
-    by_pair = lambda array: pl.BlockSpec(
-        (array.shape[0], group) + array.shape[2:], lambda i: (0, i, 0, 0)
-    )
+    in_vmem = pl.BlockSpec(memory_space=pltpu.VMEM)
     return pl.pallas_call(
         legendre_kernel,
         grid=(pairs // group,),
-        out_shape=(shape, shape),
+        out_shape=(shape, shape, jax.ShapeDtypeStruct((ROWS, LANES), jnp.float32)),
         in_specs=[
             pl.BlockSpec(memory_space=pltpu.SMEM),
             pl.BlockSpec((1, LANES), lambda i: (0, 0)),
             pl.BlockSpec((4 * level_fields, LANES), lambda i: (0, 0)),
-            by_pair(spectra),
+            in_vmem,
         ]
-        + [by_pair(table) for table in tables],
-        out_specs=(whole, whole),
+        + [in_vmem] * len(tables),
+        out_specs=(whole, whole, in_vmem),
         scratch_shapes=[
             pltpu.VMEM((bands * block, LANES), jnp.float32),
             pltpu.VMEM((bands * block, LANES), jnp.float32),
@@ -539,9 +586,7 @@
         owner_ref, lane_ref, field_ref, send_ref, place_ref = others[:5]
     else:
         place_ref, _, field_ref, send_ref = others[:4]
-    codes, flat, gathered, lhs, table, arrival_sem = others[-6:]
-    copy = pltpu.make_async_copy(table_ref, table, arrival_sem)
-    copy.start()
+    codes, flat, gathered, lhs = others[-4:]
     bands, block, width = sums_ref.shape
     pair_total = bands * pairs
     padded = gathered.shape[0]
@@ -582,8 +627,7 @@
                         lhs[parity, part * blocks + t, pl.ds(first, fields, stride=stride), :] = (
                             both[parity][:, t * LANES : (t + 1) * LANES]
                         )
-    copy.wait()
-    half = table.shape[2]
+    half = table_ref.shape[2]
 
     def transform(first, count):
         found = []
@@ -595,7 +639,7 @@
                 ],
                 axis=1,
             )
-            found.append(jnp.dot(left, table[parity], preferred_element_type=jnp.float32))
+            found.append(jnp.dot(left, table_ref[parity], preferred_element_type=jnp.float32))
         pieces = (found[0] + found[1], found[0] - found[1])
         return [piece.astype(jnp.bfloat16).astype(jnp.float32) for piece in pieces]
 
@@ -638,7 +682,7 @@
         in_specs=[
             pl.BlockSpec(memory_space=pltpu.SMEM),
             in_vmem,
-            pl.BlockSpec(memory_space=pl.ANY),
+            in_vmem,
         ]
         + [in_vmem] * 2,
         out_specs=(in_vmem,) * len(out_shape),
@@ -647,8 +691,6 @@
             pltpu.VMEM((bands * block, width), jnp.float32),
             pltpu.VMEM((padded, width), jnp.float32),
             pltpu.VMEM((2, 2 * padded // LANES, 2 * levels * TALL, LANES), jnp.float32),
-            pltpu.VMEM(table.shape, table.dtype),
-            pltpu.SemaphoreType.DMA,
         ],
         compiler_params=pltpu.CompilerParams(vmem_limit_bytes=32 * 1024 * 1024),
         cost_estimate=pl.CostEstimate(
@@ -674,25 +716,20 @@
         tables = (lax.all_gather(table, "lev", axis=0, tiled=True),)
     base = jnp.stack([lax.axis_index("lev") * levels, lax.axis_index("band") * rows])
     base = base.astype(jnp.int32)
-    wind_sums, tracer_sums = legendre_call(pairing, spectra, tables)
+    wind_sums, tracer_sums, done = legendre_call(pairing, spectra, tables)
     wind_sums = exchange(wind_sums)
-    wind_sums, tracer_sums = lax.optimization_barrier((wind_sums, tracer_sums))
     tracer_sums = exchange(tracer_sums)
     pair_total = pairs * lax.axis_size("band")
     twiddles = jnp.asarray(fourier_table(pair_total, up_to(pair_total, LANES), lon_total))
+    points, twiddles = prepare_call(base, done, eta_shift, cells, twiddles)
     size = (pairs, levels, lon_total)
     winds, send, place = fourier_call(base, wind_sums, twiddles, *size)
-    displacement, done = interpolation_call(
-        wind_levels, base, winds, swap_levels(send), (eta_shift, cells), jnp.float32
+    displacement, moved, done = interpolation_call(
+        wind_levels, base, winds, points, swap_levels(send), (), jnp.float32, 2
     )
     tracers, send = fourier_call(base, tracer_sums, twiddles, *size, place, done)
     advected, _ = interpolation_call(
-        tracer_levels,
-        base,
-        tracers,
-        swap_levels(send),
-        (eta_shift, cells, displacement),
-        jnp.bfloat16,
+        tracer_levels, base, tracers, points, swap_levels(send), (moved,), jnp.bfloat16, 1
     )
     return advected, displacement
 

time: 116 us -> 109 us (0.940)
  Pallas kernels: 69.7 us -> 58.1 us
  local copies, waits for them, and re-layouts: 10.8 us -> 14.9 us
    pallas_call x2, Pallas kernels: 53.8 us -> 42.5 us  [interpolation_call(): pl.pallas_call(functools.partial(interpolation_kernel, levels_body, toget...]
    unnamed x22 -> x30, local copies, waits for them, and re-layouts: 10.1 us -> 14.2 us
    pallas_call x0 -> x1, Pallas kernels: none -> 1.83 us  [prepare_call(): pl.pallas_call(prepare_kernel, out_shape=(jax.ShapeDtypeStruct((7,) + eta...]
  transfers between devices with their start and end apart: 4 -> 4, of which waited for: 3 -> 3; matrix products, arithmetic and copies ran while one was open for 1% -> 1% of each run, Pallas kernels for 28% -> 26%
where the time goes in v7:
time: 109 us; the launch traced here: 107 us
  Pallas kernels  58.1 us (53%)
  blocking collectives  20.1 us (18%)
  local copies, waits for them, and re-layouts  14.9 us (14%)
  starting transfers between devices  7.82 us (7%)
  waiting for transfers between devices  4.77 us (4%)
    pallas_call x2, Pallas kernels, interpolation_call(): pl.pallas_call(functools.partial(interpolation_kernel, levels_body, toget...  42.5 us
    all_to_all x1, blocking collectives, exchange(): return lax.all_to_all(sums, 'band', split_axis=0, concat_axis=0, tiled=True)  20.1 us
    unnamed x30, local copies, waits for them, and re-layouts  14.2 us
    pallas_call x2, Pallas kernels, fourier_call(): pl.pallas_call(functools.partial(fourier_kernel, pairs, levels, leads), o...  6.91 us
    pallas_call x1, Pallas kernels, legendre_call(): pl.pallas_call(legendre_kernel, grid=(pairs // group,), out_shape=(shape,...  6.84 us
    all_to_all x1, starting transfers between devices, exchange(): return lax.all_to_all(sums, 'band', split_axis=0, concat_axis=0, tiled=True)  4.64 us
    ppermute x2, starting transfers between devices, swap_levels(): return (lax.ppermute(send[0], 'lev', [(0, 1), (1, 0)]),)  2.44 us
    ppermute x1, waiting for transfers between devices, per_device(): tables = (table, lax.ppermute(table, 'lev', [(0, 1), (1, 0)]))  2.42 us
  transfers between devices with their start and end apart: 4, of which 3 were waited for; matrix products, arithmetic and copies ran while one was open for 1% of the time, Pallas kernels for 26%

profile of v7, /device:TPU:9, one launch (start us, length us, event | category | flops | bytes accessed | tf_op | source)
XLA Modules:
  0.0 107.2 jit_solution(819575264346374556)
XLA Ops:
  0.6 0.7 collective-permute-start
  1.4 0.7 pad_bitcast_fusion.codes_ref
  2.0 0.7 pad_add_fusion.1.numbers_ref
  2.8 2.4 %collective-permute-done.others_1_ = bf16[4,20,16,641]{3,2,1,0:T(8,128)(2,1)S(1)} collective-permute-done((bf16[4,20,16,641]{3,2,1,0:T(8,128)(2,1)}, bf16[4,20,16,641]{3,2,1,0:T(8,128)(2,1)S(1)}, u32[]{:S(2)}, u32[]{:S(2)}) %collective-permute-start) | collective-permute-done | bytes 1640992 | tf_op jit(solution)/shard_map/ppermute | solution.py:714
  5.2 0.0 copy-start.8
  5.2 1.3 %copy-done.8 = bf16[4,20,16,641]{3,2,1,0:T(8,128)(2,1)} copy-done((bf16[4,20,16,641]{3,2,1,0:T(8,128)(2,1)}, bf16[4,20,16,641]{3,2,1,0:T(8,128)(2,1)S(1)}, u32[]{:S(2)}) %copy-start.8) | copy-done | bytes 1640984
  6.5 0.0 copy-start.6
  6.5 1.5 %copy-done.6 = bf16[2,32,20,641]{3,1,2,0:T(8,128)(2,1)S(1)} copy-done((bf16[2,32,20,641]{3,1,2,0:T(8,128)(2,1)S(1)}, bf16[2,32,20,641]{3,1,2,0:T(8,128)(2,1)}, u32[]{:S(2)}) %copy-start.6) | copy-done | bytes 1640984
  8.0 0.0 copy-start.7
  8.0 1.5 %copy-done.7 = bf16[4,16,20,641]{3,1,2,0:T(8,128)(2,1)S(1)} copy-done((bf16[4,16,20,641]{3,1,2,0:T(8,128)(2,1)S(1)}, bf16[4,16,20,641]{3,1,2,0:T(8,128)(2,1)}, u32[]{:S(2)}) %copy-start.7) | copy-done | bytes 1640984
  9.6 0.0 copy-start.9
  9.6 1.5 %copy-done.9 = bf16[4,20,16,641]{3,2,1,0:T(8,128)(2,1)S(1)} copy-done((bf16[4,20,16,641]{3,2,1,0:T(8,128)(2,1)S(1)}, bf16[4,20,16,641]{3,2,1,0:T(8,128)(2,1)}, u32[]{:S(2)}) %copy-start.9) | copy-done | bytes 1640984
  11.1 0.0 copy-start.14
  11.1 0.8 copy-done.14
  11.9 0.0 copy-start.5
  11.9 6.8 %shard_map.104 = (bf16[16,128,128]{2,1,0:T(8,128)(2,1)S(1)}, bf16[16,128,128]{2,1,0:T(8,128)(2,1)S(1)}, f32[8,128]{1,0:T(8,128)S(1)}) custom-call(s32[21]{0:T(128)S(1)} %pad_add_fusion.1.numbers_ref, s32[1,128]{1,0:T(1,128)S(1)} %pad_bitcast_fusion.codes_ref, bf16[128,128]{1,0:T(8,128)(2,1)S(1)} %copy-done.14, bf16[2,20,32,641]{3,2,1,0:T(8,128)(2,1)S(1)} %bitcast.9, ...), custom_call_target="tpu_custom_call" | custom-call | flops 420085760 | bytes 8000000 | tf_op jit(solution)/shard_map/pallas_call | solution.py:507
  18.7 0.0 copy-start.10
  18.7 20.1 %all_to_all.10.sums_ref = bf16[16,128,128]{2,1,0:T(8,128)(2,1)S(1)} all-to-all(bf16[16,128,128]{2,1,0:T(8,128)(2,1)S(1)} %get-tuple-element.19), channel_id=1, replica_groups=mesh['band'=16,'lev'=2] {'band'}, dimensions={0} | all-to-all | bytes 1048576 | tf_op jit(solution)/shard_map/all_to_all | solution.py:705
  38.8 0.0 copy-done.10
  38.8 4.6 %all-to-all-start = ((bf16[16,128,128]{2,1,0:T(8,128)(2,1)}), bf16[16,128,128]{2,1,0:T(8,128)(2,1)S(1)}, u32[]{:S(2)}, u32[]{:S(2)}) async-start(bf16[16,128,128]{2,1,0:T(8,128)(2,1)} %copy-done.10), calls=%async_computation | async-start | bytes 1048576 | tf_op jit(solution)/shard_map/all_to_all | solution.py:705
  43.5 0.1 pad_add_fusion.base_ref
  43.6 0.0 copy-done.5
  43.6 0.0 copy-start.4
  43.6 2.2 %copy-done.4 = bf16[2,768,1408]{2,1,0:T(8,128)(2,1)S(1)} copy-done((bf16[2,768,1408]{2,1,0:T(8,128)(2,1)S(1)}, bf16[2,768,1408]{2,1,0:T(8,128)(2,1)}, u32[]{:S(2)}) %copy-start.4) | copy-done | bytes 4325400
  45.8 0.0 copy-start.11
  45.8 1.0 copy-done.11
  46.8 0.0 copy-start.12
  46.8 0.0 copy-start.13
  46.8 1.8 %shard_map.105 = (f32[7,8,8,2816]{3,2,1,0:T(8,128)S(1)}, bf16[2,768,1408]{2,1,0:T(8,128)(2,1)S(1)}) custom-call(s32[2]{0:T(128)S(1)} %pad_add_fusion.base_ref, f32[8,128]{1,0:T(8,128)S(1)} %get-tuple-element.17.after_ref, bf16[8,8,2816]{2,1,0:T(8,128)(2,1)S(1)} %copy-done.11, s32[3,8,8,2816]{3,2,1,0:T(8,128)S(1)} %copy-done.5, ...), custom_call_target="tpu_custom_call" | custom-call | flops 7208960 | bytes 20000000 | tf_op jit(solution)/shard_map/pallas_call | solution.py:207
  48.6 0.0 copy-start
  48.6 0.0 copy-done.12
  48.6 0.0 copy-done.13
  48.6 3.5 %shard_map.106 = (f32[8,24,2816]{2,1,0:T(8,128)S(1)}, bf16[1,2,24,2816]{3,2,1,0:T(8,128)(2,1)S(1)}, bf16[384,384]{1,0:T(8,128)(2,1)S(1)}) custom-call(s32[2]{0:T(128)S(1)} %pad_add_fusion.base_ref, bf16[16,128,128]{2,1,0:T(8,128)(2,1)S(1)} %all_to_all.10.sums_ref, bf16[2,768,1408]{2,1,0:T(8,128)(2,1)S(1)} %get-tuple-element.18.table_ref, ...), custom_call_target="tpu_custom_call" | custom-call | flops 830472192 | bytes 8000000 | tf_op jit(solution)/shard_map/pallas_call | solution.py:679
  52.2 0.0 copy-start.2
  52.2 2.1 %copy-done.2 = bf16[2,768,1408]{2,1,0:T(8,128)(2,1)} copy-done((bf16[2,768,1408]{2,1,0:T(8,128)(2,1)}, bf16[2,768,1408]{2,1,0:T(8,128)(2,1)S(1)}, u32[]{:S(2)}) %copy-start.2) | copy-done | bytes 4325400
  54.3 2.0 %collective-permute-start.1 = (bf16[2,24,2816]{2,1,0:T(8,128)(2,1)S(1)}, bf16[2,24,2816]{2,1,0:T(8,128)(2,1)S(1)}, u32[]{:S(2)}, u32[]{:S(2)}) collective-permute-start(bf16[2,24,2816]{2,1,0:T(8,128)(2,1)S(1)} %bitcast.12), channel_id=1, source_target_pairs={{0,1},{1,0},{2,3},{3,2},{4,5},{5,4},{6,7},{7,6},{8,9},{9,8},{10,11... | collective-permute-start | bytes 811016 | tf_op jit(solution)/shard_map/ppermute | solution.py:375
  56.3 1.2 %collective-permute-done.1.others_0_ = bf16[2,24,2816]{2,1,0:T(8,128)(2,1)S(1)} collective-permute-done((bf16[2,24,2816]{2,1,0:T(8,128)(2,1)S(1)}, bf16[2,24,2816]{2,1,0:T(8,128)(2,1)S(1)}, u32[]{:S(2)}, u32[]{:S(2)}) %collective-permute-start.1) | collective-permute-done | bytes 270368 | tf_op jit(solution)/shard_map/ppermute | solution.py:375
  57.4 0.0 copy-done
  57.4 22.4 %shard_map.107 = (f32[2,8,8,2816]{3,2,1,0:T(8,128)}, f32[2,8,8,2816]{3,2,1,0:T(8,128)S(1)}, f32[8,128]{1,0:T(8,128)S(1)}) custom-call(s32[2]{0:T(128)S(1)} %pad_add_fusion.base_ref, f32[8,24,2816]{2,1,0:T(8,128)S(1)} %get-tuple-element.21.field_ref, f32[7,8,8,2816]{3,2,1,0:T(8,128)S(1)} %get-tuple-element.22.points_ref, ...), custom_call_target="tpu_custom_call" | custom-call | flops 90112000 | bytes 7208960 | tf_op jit(solution)/shard_map/pallas_call | solution.py:354
  79.9 0.0 all-to-all-done.sums_ref
  79.9 0.0 copy-start.3
  79.9 2.2 %copy-done.3 = bf16[2,768,1408]{2,1,0:T(8,128)(2,1)S(1)} copy-done((bf16[2,768,1408]{2,1,0:T(8,128)(2,1)S(1)}, bf16[2,768,1408]{2,1,0:T(8,128)(2,1)}, u32[]{:S(2)}) %copy-start.3) | copy-done | bytes 4325400
  82.1 0.0 copy-start.1
  82.1 3.4 %shard_map.108 = (f32[8,24,2816]{2,1,0:T(8,128)S(1)}, bf16[1,2,24,2816]{3,2,1,0:T(8,128)(2,1)S(1)}) custom-call(s32[2]{0:T(128)S(1)} %pad_add_fusion.base_ref, bf16[16,128,128]{2,1,0:T(8,128)(2,1)S(1)} %all-to-all-done.sums_ref, bf16[2,768,1408]{2,1,0:T(8,128)(2,1)S(1)} %copy-done.3, bf16[384,384]{1,0:T(8,128)(2,1)S(1)} %get-tuple-element.20.others_0_, ...), custom_call_target="tpu_custom_call" | custom-call | flops 830472192 | bytes 8000000 | tf_op jit(solution)/shard_map/pallas_call | solution.py:679
  85.5 0.4 collective-permute-start.2
  85.9 1.2 %collective-permute-done.2.others_0_ = bf16[2,24,2816]{2,1,0:T(8,128)(2,1)S(1)} collective-permute-done((bf16[2,24,2816]{2,1,0:T(8,128)(2,1)S(1)}, bf16[2,24,2816]{2,1,0:T(8,128)(2,1)S(1)}, u32[]{:S(2)}, u32[]{:S(2)}) %collective-permute-start.2) | collective-permute-done | bytes 270368 | tf_op jit(solution)/shard_map/ppermute | solution.py:375
  87.1 0.0 copy-done.1
  87.1 20.1 %shard_map.109 = (bf16[2,8,8,2816]{3,2,1,0:T(8,128)(2,1)}, f32[8,128]{1,0:T(8,128)}) custom-call(s32[2]{0:T(128)S(1)} %pad_add_fusion.base_ref, f32[8,24,2816]{2,1,0:T(8,128)S(1)} %get-tuple-element.25.field_ref, f32[7,8,8,2816]{3,2,1,0:T(8,128)S(1)} %copy-done.1, bf16[2,24,2816]{2,1,0:T(8,128)(2,1)S(1)} %collective-permute-done.2.others_0_, ...), custom_call_target="tpu_custom_call" | custom-call | flops 90112000 | bytes 7208960 | tf_op jit(solution)/shard_map/pallas_call | solution.py:354
Async XLA Ops:
  0.6 4.6 %collective-permute-start = (bf16[4,20,16,641]{3,2,1,0:T(8,128)(2,1)}, bf16[4,20,16,641]{3,2,1,0:T(8,128)(2,1)S(1)}, u32[]{:S(2)}, u32[]{:S(2)}) collective-permute-start(bf16[4,20,16,641]{3,2,1,0:T(8,128)(2,1)} %bitcast.10), channel_id=1, source_target_pairs={{0,1},{1,0},{2,3},{3,2},{4,5},{5,4},{6,7},{7,6},{8,9},{9,8},{10,11... | collective-permute-start | bytes 4922888 | tf_op jit(solution)/shard_map/ppermute | solution.py:714
  5.2 1.3 %copy-start.8 = (bf16[4,20,16,641]{3,2,1,0:T(8,128)(2,1)}, bf16[4,20,16,641]{3,2,1,0:T(8,128)(2,1)S(1)}, u32[]{:S(2)}) copy-start(bf16[4,20,16,641]{3,2,1,0:T(8,128)(2,1)S(1)} %collective-permute-done.others_1_) | copy-start | bytes 4922884
  6.5 1.5 %copy-start.6 = (bf16[2,32,20,641]{3,1,2,0:T(8,128)(2,1)S(1)}, bf16[2,32,20,641]{3,1,2,0:T(8,128)(2,1)}, u32[]{:S(2)}) copy-start(bf16[2,32,20,641]{3,1,2,0:T(8,128)(2,1)} %param.9) | copy-start | bytes 4922884
  8.0 1.5 %copy-start.7 = (bf16[4,16,20,641]{3,1,2,0:T(8,128)(2,1)S(1)}, bf16[4,16,20,641]{3,1,2,0:T(8,128)(2,1)}, u32[]{:S(2)}) copy-start(bf16[4,16,20,641]{3,1,2,0:T(8,128)(2,1)} %param.10) | copy-start | bytes 4922884
  9.6 1.5 %copy-start.9 = (bf16[4,20,16,641]{3,2,1,0:T(8,128)(2,1)S(1)}, bf16[4,20,16,641]{3,2,1,0:T(8,128)(2,1)}, u32[]{:S(2)}) copy-start(bf16[4,20,16,641]{3,2,1,0:T(8,128)(2,1)} %copy-done.8) | copy-start | bytes 4922884
  11.1 0.8 copy-start.14
  11.9 31.7 %copy-start.5 = (s32[3,8,8,2816]{3,2,1,0:T(8,128)S(1)}, s32[3,8,8,2816]{3,2,1,0:T(8,128)}, u32[]{:S(2)}) copy-start(s32[3,8,8,2816]{3,2,1,0:T(8,128)} %cells_ref.1) | copy-start | bytes 6488068
  18.7 20.1 %copy-start.10 = (bf16[16,128,128]{2,1,0:T(8,128)(2,1)}, bf16[16,128,128]{2,1,0:T(8,128)(2,1)S(1)}, u32[]{:S(2)}) copy-start(bf16[16,128,128]{2,1,0:T(8,128)(2,1)S(1)} %get-tuple-element.16) | copy-start | bytes 1572868
  38.8 41.0 %all-to-all-start = ((bf16[16,128,128]{2,1,0:T(8,128)(2,1)}), bf16[16,128,128]{2,1,0:T(8,128)(2,1)S(1)}, u32[]{:S(2)}, u32[]{:S(2)}) async-start(bf16[16,128,128]{2,1,0:T(8,128)(2,1)} %copy-done.10), calls=%async_computation | async-start | bytes 1048576 | tf_op jit(solution)/shard_map/all_to_all | solution.py:705
  43.6 2.2 %copy-start.4 = (bf16[2,768,1408]{2,1,0:T(8,128)(2,1)S(1)}, bf16[2,768,1408]{2,1,0:T(8,128)(2,1)}, u32[]{:S(2)}) copy-start(bf16[2,768,1408]{2,1,0:T(8,128)(2,1)} %constant.21.clone.table_ref) | copy-start | bytes 12976132
  45.8 1.0 copy-start.11
  46.8 1.8 %copy-start.12 = (f32[320,128]{1,0:T(8,128)S(1)}, f32[320,128]{1,0:T(8,128)}, u32[]{:S(2)}) copy-start(f32[320,128]{1,0:T(8,128)} %constant.23.clone.others_1_) | copy-start | bytes 491524
  46.8 1.9 %copy-start.13 = (bf16[320,128]{1,0:T(8,128)(2,1)S(1)}, bf16[320,128]{1,0:T(8,128)(2,1)}, u32[]{:S(2)}) copy-start(bf16[320,128]{1,0:T(8,128)(2,1)} %constant.22.clone.others_0_) | copy-start | bytes 245764
  48.6 8.8 %copy-start = (f32[7,8,8,2816]{3,2,1,0:T(8,128)}, f32[7,8,8,2816]{3,2,1,0:T(8,128)S(1)}, u32[]{:S(2)}) copy-start(f32[7,8,8,2816]{3,2,1,0:T(8,128)S(1)} %get-tuple-element.22.points_ref) | copy-start | bytes 15138820
  52.2 2.1 %copy-start.2 = (bf16[2,768,1408]{2,1,0:T(8,128)(2,1)}, bf16[2,768,1408]{2,1,0:T(8,128)(2,1)S(1)}, u32[]{:S(2)}) copy-start(bf16[2,768,1408]{2,1,0:T(8,128)(2,1)S(1)} %get-tuple-element.18.table_ref) | copy-start | bytes 12976132
  54.3 3.2 %collective-permute-start.1 = (bf16[2,24,2816]{2,1,0:T(8,128)(2,1)S(1)}, bf16[2,24,2816]{2,1,0:T(8,128)(2,1)S(1)}, u32[]{:S(2)}, u32[]{:S(2)}) collective-permute-start(bf16[2,24,2816]{2,1,0:T(8,128)(2,1)S(1)} %bitcast.12), channel_id=1, source_target_pairs={{0,1},{1,0},{2,3},{3,2},{4,5},{5,4},{6,7},{7,6},{8,9},{9,8},{10,11... | collective-permute-start | bytes 811016 | tf_op jit(solution)/shard_map/ppermute | solution.py:375
  79.9 2.2 %copy-start.3 = (bf16[2,768,1408]{2,1,0:T(8,128)(2,1)S(1)}, bf16[2,768,1408]{2,1,0:T(8,128)(2,1)}, u32[]{:S(2)}) copy-start(bf16[2,768,1408]{2,1,0:T(8,128)(2,1)} %copy-done.2) | copy-start | bytes 12976132
  82.1 5.0 %copy-start.1 = (f32[7,8,8,2816]{3,2,1,0:T(8,128)S(1)}, f32[7,8,8,2816]{3,2,1,0:T(8,128)}, u32[]{:S(2)}) copy-start(f32[7,8,8,2816]{3,2,1,0:T(8,128)} %copy-done) | copy-start | bytes 15138820
  85.5 1.6 %collective-permute-start.2 = (bf16[2,24,2816]{2,1,0:T(8,128)(2,1)S(1)}, bf16[2,24,2816]{2,1,0:T(8,128)(2,1)S(1)}, u32[]{:S(2)}, u32[]{:S(2)}) collective-permute-start(bf16[2,24,2816]{2,1,0:T(8,128)(2,1)S(1)} %bitcast.13), channel_id=1, source_target_pairs={{0,1},{1,0},{2,3},{3,2},{4,5},{5,4},{6,7},{7,6},{8,9},{9,8},{10,11... | collective-permute-start | bytes 811016 | tf_op jit(solution)/shard_map/ppermute | solution.py:375

commit v8 on v7

--- a/solution.py
+++ b/solution.py
@@ -174,9 +174,15 @@
     )
 
 
-def prepare_kernel(base_ref, after_ref, eta_ref, cells_ref, table_ref, points_ref, out_ref, sem):
-    copy = pltpu.make_async_copy(table_ref, out_ref, sem)
-    copy.start()
+def prepare_kernel(
+    base_ref, eta_ref, cells_ref, table_ref, sums_ref, points_ref, table_out, sums_out, sems
+):
+    copies = [
+        pltpu.make_async_copy(table_ref, table_out, sems.at[0]),
+        pltpu.make_async_copy(sums_ref, sums_out, sems.at[1]),
+    ]
+    for copy in copies:
+        copy.start()
     levels, rows, lon_total = eta_ref.shape
     shape = (rows, LANES)
     row_here = base_ref[1] + lax.broadcasted_iota(jnp.int32, shape, 0)
@@ -199,27 +205,29 @@
         return carry
 
     lax.fori_loop(0, lon_total // LANES, chunk_step, 0)
-    copy.wait()
-
-
-def prepare_call(base, after, eta_shift, cells, table):
+    for copy in copies:
+        copy.wait()
+
+
+def prepare_call(base, eta_shift, cells, table, sums):
     in_vmem = pl.BlockSpec(memory_space=pltpu.VMEM)
     return pl.pallas_call(
         prepare_kernel,
         out_shape=(
             jax.ShapeDtypeStruct((7,) + eta_shift.shape, jnp.float32),
             jax.ShapeDtypeStruct(table.shape, table.dtype),
+            jax.ShapeDtypeStruct(sums.shape, sums.dtype),
         ),
         in_specs=[pl.BlockSpec(memory_space=pltpu.SMEM)]
-        + [in_vmem] * 3
-        + [pl.BlockSpec(memory_space=pl.ANY)],
-        out_specs=(in_vmem, in_vmem),
-        scratch_shapes=[pltpu.SemaphoreType.DMA],
-        compiler_params=pltpu.CompilerParams(vmem_limit_bytes=32 * 1024 * 1024),
+        + [in_vmem] * 2
+        + [pl.BlockSpec(memory_space=pl.ANY)] * 2,
+        out_specs=(in_vmem, in_vmem, pl.BlockSpec(memory_space=pl.ANY)),
+        scratch_shapes=[pltpu.SemaphoreType.DMA((2,))],
+        compiler_params=pltpu.CompilerParams(vmem_limit_bytes=16 * 1024 * 1024),
         cost_estimate=pl.CostEstimate(
             flops=40 * eta_shift.size, bytes_accessed=20_000_000, transcendentals=0
         ),
-    )(base, after, eta_shift, cells, table)
+    )(base, eta_shift, cells, table, sums)
 
 
 def arrival(points_ref, k, lanes):
@@ -363,7 +371,7 @@
             scratch,
             pltpu.VMEM((2, together, 16, ROWS, LANES), jnp.float32),
         ],
-        compiler_params=pltpu.CompilerParams(vmem_limit_bytes=32 * 1024 * 1024),
+        compiler_params=pltpu.CompilerParams(vmem_limit_bytes=16 * 1024 * 1024),
         cost_estimate=pl.CostEstimate(
             flops=count * 500, bytes_accessed=count * 40, transcendentals=0
         ),
@@ -387,9 +395,14 @@
 HALF = LANES // 2
 
 
-def legendre_kernel(numbers_ref, codes_ref, order_ref, spectra_ref, *others):
-    tables, others = others[:-7], others[-7:]
-    wind_ref, tracer_ref, done_ref, wind_sums, tracer_sums, table_tail, column_tail = others
+def touch_kernel(numbers_ref, spectra_ref, table_ref, out_ref):
+    out_ref[...] = numbers_ref[...]
+
+
+def legendre_kernel(numbers_ref, codes_ref, spectra_ref, *others):
+    tables, others = others[:-8], others[-8:]
+    wind_ref, tracer_ref, done_ref, wind_sums, tracer_sums = others[:5]
+    table_tail, column_tail, order_ref = others[5:]
     _, pairs, level_fields, degrees = spectra_ref.shape
     group = table_tail.shape[0]
     bands, block, _ = wind_ref.shape
@@ -404,6 +417,7 @@
         done_ref[...] = jnp.zeros(done_ref.shape, jnp.float32)
         table_tail[...] = jnp.zeros(table_tail.shape, jnp.float32)
         column_tail[...] = jnp.zeros(column_tail.shape, jnp.float32)
+        order_ref[...] = column_order(level_fields)
         codes = codes_ref[...]
         code_row = up_to(pl.num_programs(0) * group * PAIRED, ROWS)
         for band in range(bands):
@@ -480,14 +494,15 @@
 
 
 def column_order(level_fields):
-    levels = level_fields // 4
-    order = np.zeros((4 * level_fields, LANES), np.float32)
-    for column in range(4 * level_fields):
-        part, rest = divmod(column, level_fields)
-        level, field = divmod(rest, 4)
-        target = (field // 2) * HALF + part * 2 * levels + 2 * level + field % 2
-        order[column, target] = 1.0
-    return order.astype(jnp.bfloat16)
+    shift = level_fields.bit_length() - 1
+    shape = (4 * level_fields, LANES)
+    column = lax.broadcasted_iota(jnp.int32, shape, 0)
+    part = jnp.right_shift(column, shift)
+    rest = column & (level_fields - 1)
+    target = jnp.right_shift(rest & 3, 1) * HALF + part * (level_fields // 2)
+    target = target + 2 * jnp.right_shift(rest, 2) + (rest & 1)
+    here = lax.broadcasted_iota(jnp.int32, shape, 1) == target
+    return jnp.where(here, 1.0, 0.0).astype(jnp.bfloat16)
 
 
 def block_rows(pairs):
@@ -500,7 +515,13 @@
     block = block_rows(pairs)
     group = next(n for n in (4, 5, 2, 1) if pairs % n == 0)
     numbers = jnp.concatenate([lax.axis_index("lev").astype(jnp.int32)[None], pairing])
-    codes = jnp.pad(pairing, (0, LANES - pairs))[None, :]
+    codes = pl.pallas_call(
+        touch_kernel,
+        out_shape=jax.ShapeDtypeStruct((1, LANES), jnp.int32),
+        in_specs=[pl.BlockSpec(memory_space=pltpu.VMEM)] * 3,
+        out_specs=pl.BlockSpec(memory_space=pltpu.VMEM),
+        cost_estimate=pl.CostEstimate(flops=0, bytes_accessed=4_000_000, transcendentals=0),
+    )(jnp.pad(pairing, (0, LANES - pairs))[None, :], spectra, tables[0])
     shape = jax.ShapeDtypeStruct((bands, block, LANES), jnp.bfloat16)
     whole = pl.BlockSpec((bands, block, LANES), lambda i: (0, 0, 0))
     in_vmem = pl.BlockSpec(memory_space=pltpu.VMEM)
@@ -511,7 +532,6 @@
         in_specs=[
             pl.BlockSpec(memory_space=pltpu.SMEM),
             pl.BlockSpec((1, LANES), lambda i: (0, 0)),
-            pl.BlockSpec((4 * level_fields, LANES), lambda i: (0, 0)),
             in_vmem,
         ]
         + [in_vmem] * len(tables),
@@ -521,14 +541,15 @@
             pltpu.VMEM((bands * block, LANES), jnp.float32),
             pltpu.VMEM((group, ROWS * bands, LANES), jnp.float32),
             pltpu.VMEM((group, 2 * level_fields, LANES), jnp.float32),
+            pltpu.VMEM((4 * level_fields, LANES), jnp.bfloat16),
         ],
-        compiler_params=pltpu.CompilerParams(vmem_limit_bytes=32 * 1024 * 1024),
+        compiler_params=pltpu.CompilerParams(vmem_limit_bytes=16 * 1024 * 1024),
         cost_estimate=pl.CostEstimate(
             flops=2 * ROWS * bands * 4 * level_fields * pairs * degrees,
             bytes_accessed=8_000_000,
             transcendentals=0,
         ),
-    )(numbers, codes, jnp.asarray(column_order(level_fields)), spectra, *tables)
+    )(numbers, codes, spectra, *tables)
 
 
 def fourier_table(pair_total, padded, lon_total):
@@ -692,7 +713,7 @@
             pltpu.VMEM((padded, width), jnp.float32),
             pltpu.VMEM((2, 2 * padded // LANES, 2 * levels * TALL, LANES), jnp.float32),
         ],
-        compiler_params=pltpu.CompilerParams(vmem_limit_bytes=32 * 1024 * 1024),
+        compiler_params=pltpu.CompilerParams(vmem_limit_bytes=16 * 1024 * 1024),
         cost_estimate=pl.CostEstimate(
             flops=2 * levels * 4 * TALL * padded * lon_total,
             bytes_accessed=8_000_000,
@@ -716,12 +737,12 @@
         tables = (lax.all_gather(table, "lev", axis=0, tiled=True),)
     base = jnp.stack([lax.axis_index("lev") * levels, lax.axis_index("band") * rows])
     base = base.astype(jnp.int32)
-    wind_sums, tracer_sums, done = legendre_call(pairing, spectra, tables)
+    wind_sums, tracer_sums, _ = legendre_call(pairing, spectra, tables)
     wind_sums = exchange(wind_sums)
-    tracer_sums = exchange(tracer_sums)
     pair_total = pairs * lax.axis_size("band")
     twiddles = jnp.asarray(fourier_table(pair_total, up_to(pair_total, LANES), lon_total))
-    points, twiddles = prepare_call(base, done, eta_shift, cells, twiddles)
+    points, twiddles, tracer_sums = prepare_call(base, eta_shift, cells, twiddles, tracer_sums)
+    tracer_sums = exchange(tracer_sums)
     size = (pairs, levels, lon_total)
     winds, send, place = fourier_call(base, wind_sums, twiddles, *size)
     displacement, moved, done = interpolation_call(

time: 109 us -> 104 us (0.954)
  blocking collectives: 20.1 us -> 0 us
  starting transfers between devices: 7.82 us -> 14.5 us
  Pallas kernels: 58.1 us -> 62.8 us
  local copies, waits for them, and re-layouts: 14.9 us -> 18.4 us
  waiting for transfers between devices: 4.77 us -> 5.96 us
    all_to_all x1 -> x0, blocking collectives: 20.1 us -> none  [exchange(): return lax.all_to_all(sums, 'band', split_axis=0, concat_axis=0, tiled=True)]
    all_to_all x1 -> x2, starting transfers between devices: 4.64 us -> 11.3 us  [exchange(): return lax.all_to_all(sums, 'band', split_axis=0, concat_axis=0, tiled=True)]
    all_to_all x1 -> x2, waiting for transfers between devices: 0.01 us -> 3.58 us  [exchange(): return lax.all_to_all(sums, 'band', split_axis=0, concat_axis=0, tiled=True)]
    unnamed x30, local copies, waits for them, and re-layouts: 14.2 us -> 17.2 us
    pallas_call x0 -> x1, Pallas kernels: none -> 2.66 us  [legendre_call(): pl.pallas_call(touch_kernel, out_shape=jax.ShapeDtypeStruct((1, LANES), j...]
    ppermute x1, waiting for transfers between devices: 2.42 us -> 0.03 us  [per_device(): tables = (table, lax.ppermute(table, 'lev', [(0, 1), (1, 0)]))]
    pallas_call x1, Pallas kernels: 6.84 us -> 8.74 us  [legendre_call(): pl.pallas_call(legendre_kernel, grid=(pairs // group,), out_shape=(shape,...]
  transfers between devices with their start and end apart: 4 -> 5, of which waited for: 3 -> 3; matrix products, arithmetic and copies ran while one was open for 1% -> 1% of each run, Pallas kernels for 26% -> 30%
where the time goes in v8:
time: 104 us; the launch traced here: 103 us
  Pallas kernels  62.8 us (60%)
  local copies, waits for them, and re-layouts  18.4 us (18%)
  starting transfers between devices  14.5 us (14%)
  waiting for transfers between devices  5.96 us (6%)
    pallas_call x2, Pallas kernels, interpolation_call(): pl.pallas_call(functools.partial(interpolation_kernel, levels_body, toget...  42.5 us
    unnamed x30, local copies, waits for them, and re-layouts  17.2 us
    all_to_all x2, starting transfers between devices, exchange(): return lax.all_to_all(sums, 'band', split_axis=0, concat_axis=0, tiled=True)  11.3 us
    pallas_call x1, Pallas kernels, legendre_call(): pl.pallas_call(legendre_kernel, grid=(pairs // group,), out_shape=(shape,...  8.74 us
    pallas_call x2, Pallas kernels, fourier_call(): pl.pallas_call(functools.partial(fourier_kernel, pairs, levels, leads), o...  7.02 us
    all_to_all x2, waiting for transfers between devices, exchange(): return lax.all_to_all(sums, 'band', split_axis=0, concat_axis=0, tiled=True)  3.58 us
    pallas_call x1, Pallas kernels, legendre_call(): pl.pallas_call(touch_kernel, out_shape=jax.ShapeDtypeStruct((1, LANES), j...  2.66 us
    ppermute x2, starting transfers between devices, swap_levels(): return (lax.ppermute(send[0], 'lev', [(0, 1), (1, 0)]),)  2.5 us
  transfers between devices with their start and end apart: 5, of which 3 were waited for; matrix products, arithmetic and copies ran while one was open for 1% of the time, Pallas kernels for 30%

profile of v8, /device:TPU:9, one launch (start us, length us, event | category | flops | bytes accessed | tf_op | source)
XLA Modules:
  0.0 102.5 jit_solution(15549203007695779306)
XLA Ops:
  0.6 0.0 copy-start.14
  0.6 0.0 copy-start.6
  0.7 0.7 collective-permute-start
  1.4 1.2 %pad_bitcast_fusion.numbers_ref = s32[1,128]{1,0:T(1,128)} fusion(s32[20]{0:T(128)} %param.10), kind=kLoop, calls=%fused_computation.2 | loop fusion | bytes 592 | tf_op jit(solution)/shard_map/broadcast_in_dim | solution.py:524
  2.6 2.7 %shard_map.95.codes_ref = s32[1,128]{1,0:T(1,128)} custom-call(s32[1,128]{1,0:T(1,128)} %pad_bitcast_fusion.numbers_ref, bf16[2,20,32,641]{3,2,1,0:T(8,128)(2,1)} %bitcast.9, bf16[4,20,16,641]{3,2,1,0:T(8,128)(2,1)} %bitcast.12), custom_call_target="tpu_custom_call" | custom-call | bytes 4000000 | tf_op jit(solution)/shard_map/pallas_call | solution.py:518
  5.2 0.0 copy-done.14
  5.2 0.1 pad_add_fusion.1.numbers_ref
  5.3 0.0 collective-permute-done.others_1_
  5.3 0.0 copy-done.6
  5.3 0.0 copy-start.7
  5.3 1.5 %copy-done.7 = bf16[4,16,20,641]{3,1,2,0:T(8,128)(2,1)S(1)} copy-done((bf16[4,16,20,641]{3,1,2,0:T(8,128)(2,1)S(1)}, bf16[4,16,20,641]{3,1,2,0:T(8,128)(2,1)}, u32[]{:S(2)}) %copy-start.7) | copy-done | bytes 1640984
  6.9 0.0 copy-start.13
  6.9 0.7 copy-done.13
  7.5 0.0 copy-start.10
  7.5 8.7 %shard_map.96 = (bf16[16,128,128]{2,1,0:T(8,128)(2,1)}, bf16[16,128,128]{2,1,0:T(8,128)(2,1)S(1)}, f32[8,128]{1,0:T(8,128)}) custom-call(s32[21]{0:T(128)S(1)} %pad_add_fusion.1.numbers_ref, s32[1,128]{1,0:T(1,128)S(1)} %copy-done.13, bf16[2,20,32,641]{3,2,1,0:T(8,128)(2,1)S(1)} %bitcast.10, bf16[4,20,16,641]{3,2,1,0:T(8,128)(2,1)S(1)} %bitcast.13, ...), custom_call_target="tpu_custom_call" | custom-call | flops 420085760 | bytes 8000000 | tf_op jit(solution)/shard_map/pallas_call | solution.py:528
  16.3 6.7 %all-to-all-start.1 = ((bf16[16,128,128]{2,1,0:T(8,128)(2,1)}), bf16[16,128,128]{2,1,0:T(8,128)(2,1)S(1)}, u32[]{:S(2)}, u32[]{:S(2)}) async-start(bf16[16,128,128]{2,1,0:T(8,128)(2,1)} %get-tuple-element.19), calls=%async_computation.1 | async-start | bytes 1048576 | tf_op jit(solution)/shard_map/all_to_all | solution.py:726
  22.9 0.1 pad_add_fusion.base_ref
  23.0 0.0 copy-done.10
  23.0 0.0 copy-start.8
  23.0 2.2 %copy-done.8 = bf16[2,768,1408]{2,1,0:T(8,128)(2,1)S(1)} copy-done((bf16[2,768,1408]{2,1,0:T(8,128)(2,1)S(1)}, bf16[2,768,1408]{2,1,0:T(8,128)(2,1)}, u32[]{:S(2)}) %copy-start.8) | copy-done | bytes 4325400
  25.2 0.0 copy-start.9
  25.2 1.6 %copy-done.9 = s32[3,8,8,2816]{3,2,1,0:T(8,128)S(1)} copy-done((s32[3,8,8,2816]{3,2,1,0:T(8,128)S(1)}, s32[3,8,8,2816]{3,2,1,0:T(8,128)}, u32[]{:S(2)}) %copy-start.9) | copy-done | bytes 2162712
  26.9 0.0 copy-start.11
  26.9 0.0 copy-start.12
  26.9 1.8 %shard_map.97 = (f32[7,8,8,2816]{3,2,1,0:T(8,128)S(1)}, bf16[2,768,1408]{2,1,0:T(8,128)(2,1)S(1)}, bf16[16,128,128]{2,1,0:T(8,128)(2,1)}) custom-call(s32[2]{0:T(128)S(1)} %pad_add_fusion.base_ref, bf16[8,8,2816]{2,1,0:T(8,128)(2,1)S(1)} %copy-done.10, s32[3,8,8,2816]{3,2,1,0:T(8,128)S(1)} %copy-done.9, bf16[2,768,1408]{2,1,0:T(8,128)(2,1)S(1)} %copy-done.8, ...), custom_call_target="tpu_custom_call" | custom-call | flops 7208960 | bytes 20000000 | tf_op jit(solution)/shard_map/pallas_call | solution.py:214
  28.7 0.0 copy-start
  28.7 2.2 %copy-done = f32[7,8,8,2816]{3,2,1,0:T(8,128)} copy-done((f32[7,8,8,2816]{3,2,1,0:T(8,128)}, f32[7,8,8,2816]{3,2,1,0:T(8,128)S(1)}, u32[]{:S(2)}) %copy-start) | copy-done | bytes 5046296
  31.0 0.0 copy-start.3
  31.0 2.1 %copy-done.3 = bf16[2,768,1408]{2,1,0:T(8,128)(2,1)} copy-done((bf16[2,768,1408]{2,1,0:T(8,128)(2,1)}, bf16[2,768,1408]{2,1,0:T(8,128)(2,1)S(1)}, u32[]{:S(2)}) %copy-start.3) | copy-done | bytes 4325400
  33.0 3.6 %all-to-all-done.1.sums_ref = bf16[16,128,128]{2,1,0:T(8,128)(2,1)S(1)} async-done(((bf16[16,128,128]{2,1,0:T(8,128)(2,1)}), bf16[16,128,128]{2,1,0:T(8,128)(2,1)S(1)}, u32[]{:S(2)}, u32[]{:S(2)}) %all-to-all-start.1) | async-done | bytes 524320 | tf_op jit(solution)/shard_map/all_to_all | solution.py:726
  36.6 4.6 %all-to-all-start = ((bf16[16,128,128]{2,1,0:T(8,128)(2,1)}), bf16[16,128,128]{2,1,0:T(8,128)(2,1)S(1)}, u32[]{:S(2)}, u32[]{:S(2)}) async-start(bf16[16,128,128]{2,1,0:T(8,128)(2,1)} %get-tuple-element.17), calls=%async_computation | async-start | bytes 1048576 | tf_op jit(solution)/shard_map/all_to_all | solution.py:726
  41.2 0.0 copy-done.11
  41.2 0.0 copy-done.12
  41.2 0.0 copy-start.4
  41.3 2.2 %copy-done.4 = bf16[2,768,1408]{2,1,0:T(8,128)(2,1)S(1)} copy-done((bf16[2,768,1408]{2,1,0:T(8,128)(2,1)S(1)}, bf16[2,768,1408]{2,1,0:T(8,128)(2,1)}, u32[]{:S(2)}) %copy-start.4) | copy-done | bytes 4325400
  43.5 0.0 copy-start.1
  43.5 3.6 %shard_map.98 = (f32[8,24,2816]{2,1,0:T(8,128)S(1)}, bf16[1,2,24,2816]{3,2,1,0:T(8,128)(2,1)S(1)}, bf16[384,384]{1,0:T(8,128)(2,1)S(1)}) custom-call(s32[2]{0:T(128)S(1)} %pad_add_fusion.base_ref, bf16[16,128,128]{2,1,0:T(8,128)(2,1)S(1)} %all-to-all-done.1.sums_ref, bf16[2,768,1408]{2,1,0:T(8,128)(2,1)S(1)} %copy-done.4, bf16[320,128]{1,0:T(8,128)(2,1)S(1)} %copy-done.12, ...), custom_call_target="tpu_custom_call" | custom-call | flops 830472192 | bytes 8000000 | tf_op jit(solution)/shard_map/pallas_call | solution.py:700
  47.1 2.1 %collective-permute-start.1 = (bf16[2,24,2816]{2,1,0:T(8,128)(2,1)S(1)}, bf16[2,24,2816]{2,1,0:T(8,128)(2,1)S(1)}, u32[]{:S(2)}, u32[]{:S(2)}) collective-permute-start(bf16[2,24,2816]{2,1,0:T(8,128)(2,1)S(1)} %bitcast.14), channel_id=1, source_target_pairs={{0,1},{1,0},{2,3},{3,2},{4,5},{5,4},{6,7},{7,6},{8,9},{9,8},{10,11... | collective-permute-start | bytes 811016 | tf_op jit(solution)/shard_map/ppermute | solution.py:383
  49.1 1.2 %collective-permute-done.1.others_0_ = bf16[2,24,2816]{2,1,0:T(8,128)(2,1)S(1)} collective-permute-done((bf16[2,24,2816]{2,1,0:T(8,128)(2,1)S(1)}, bf16[2,24,2816]{2,1,0:T(8,128)(2,1)S(1)}, u32[]{:S(2)}, u32[]{:S(2)}) %collective-permute-start.1) | collective-permute-done | bytes 270368 | tf_op jit(solution)/shard_map/ppermute | solution.py:383
  50.3 0.0 copy-done.1
  50.3 22.4 %shard_map.99 = (f32[2,8,8,2816]{3,2,1,0:T(8,128)}, f32[2,8,8,2816]{3,2,1,0:T(8,128)S(1)}, f32[8,128]{1,0:T(8,128)S(1)}) custom-call(s32[2]{0:T(128)S(1)} %pad_add_fusion.base_ref, f32[8,24,2816]{2,1,0:T(8,128)S(1)} %get-tuple-element.21.field_ref, f32[7,8,8,2816]{3,2,1,0:T(8,128)S(1)} %copy-done.1, bf16[2,24,2816]{2,1,0:T(8,128)(2,1)S(1)} %collective-permute-done.1.others_0_), custom_call_target="tpu_custom_call" | custom-call | flops 90112000 | bytes 7208960 | tf_op jit(solution)/shard_map/pallas_call | solution.py:362
  72.7 0.0 all-to-all-done.sums_ref
  72.7 0.0 copy-start.5
  72.7 2.2 %copy-done.5 = bf16[2,768,1408]{2,1,0:T(8,128)(2,1)S(1)} copy-done((bf16[2,768,1408]{2,1,0:T(8,128)(2,1)S(1)}, bf16[2,768,1408]{2,1,0:T(8,128)(2,1)}, u32[]{:S(2)}) %copy-start.5) | copy-done | bytes 4325400
  75.0 3.4 %shard_map.100 = (f32[8,24,2816]{2,1,0:T(8,128)S(1)}, bf16[1,2,24,2816]{3,2,1,0:T(8,128)(2,1)S(1)}) custom-call(s32[2]{0:T(128)S(1)} %pad_add_fusion.base_ref, bf16[16,128,128]{2,1,0:T(8,128)(2,1)S(1)} %all-to-all-done.sums_ref, bf16[2,768,1408]{2,1,0:T(8,128)(2,1)S(1)} %copy-done.5, bf16[384,384]{1,0:T(8,128)(2,1)S(1)} %get-tuple-element.20.others_0_, ...), custom_call_target="tpu_custom_call" | custom-call | flops 830472192 | bytes 8000000 | tf_op jit(solution)/shard_map/pallas_call | solution.py:700
  78.4 0.4 collective-permute-start.2
  78.8 1.2 %collective-permute-done.2.others_0_ = bf16[2,24,2816]{2,1,0:T(8,128)(2,1)S(1)} collective-permute-done((bf16[2,24,2816]{2,1,0:T(8,128)(2,1)S(1)}, bf16[2,24,2816]{2,1,0:T(8,128)(2,1)S(1)}, u32[]{:S(2)}, u32[]{:S(2)}) %collective-permute-start.2) | collective-permute-done | bytes 270368 | tf_op jit(solution)/shard_map/ppermute | solution.py:383
  80.0 0.0 copy-start.2
  80.0 2.4 %copy-done.2 = f32[7,8,8,2816]{3,2,1,0:T(8,128)S(1)} copy-done((f32[7,8,8,2816]{3,2,1,0:T(8,128)S(1)}, f32[7,8,8,2816]{3,2,1,0:T(8,128)}, u32[]{:S(2)}) %copy-start.2) | copy-done | bytes 5046296
  82.4 20.1 %shard_map.101 = (bf16[2,8,8,2816]{3,2,1,0:T(8,128)(2,1)}, f32[8,128]{1,0:T(8,128)}) custom-call(s32[2]{0:T(128)S(1)} %pad_add_fusion.base_ref, f32[8,24,2816]{2,1,0:T(8,128)S(1)} %get-tuple-element.25.field_ref, f32[7,8,8,2816]{3,2,1,0:T(8,128)S(1)} %copy-done.2, bf16[2,24,2816]{2,1,0:T(8,128)(2,1)S(1)} %collective-permute-done.2.others_0_, ...), custom_call_target="tpu_custom_call" | custom-call | flops 90112000 | bytes 7208960 | tf_op jit(solution)/shard_map/pallas_call | solution.py:362
Async XLA Ops:
  0.6 4.6 %copy-start.14 = (s32[20]{0:T(128)S(1)}, s32[20]{0:T(128)}, u32[]{:S(2)}) copy-start(s32[20]{0:T(128)} %param.10) | copy-start | bytes 244
  0.6 4.7 %copy-start.6 = (bf16[2,32,20,641]{3,1,2,0:T(8,128)(2,1)S(1)}, bf16[2,32,20,641]{3,1,2,0:T(8,128)(2,1)}, u32[]{:S(2)}) copy-start(bf16[2,32,20,641]{3,1,2,0:T(8,128)(2,1)} %param.8) | copy-start | bytes 4922884
  0.7 4.7 %collective-permute-start = (bf16[4,20,16,641]{3,2,1,0:T(8,128)(2,1)}, bf16[4,20,16,641]{3,2,1,0:T(8,128)(2,1)}, u32[]{:S(2)}, u32[]{:S(2)}) collective-permute-start(bf16[4,20,16,641]{3,2,1,0:T(8,128)(2,1)} %bitcast.11), channel_id=1, source_target_pairs={{0,1},{1,0},{2,3},{3,2},{4,5},{5,4},{6,7},{7,6},{8,9},{9,8},{10,11... | collective-permute-start | bytes 4922888 | tf_op jit(solution)/shard_map/ppermute | solution.py:735
  5.3 1.5 %copy-start.7 = (bf16[4,16,20,641]{3,1,2,0:T(8,128)(2,1)S(1)}, bf16[4,16,20,641]{3,1,2,0:T(8,128)(2,1)}, u32[]{:S(2)}) copy-start(bf16[4,16,20,641]{3,1,2,0:T(8,128)(2,1)} %param.9) | copy-start | bytes 4922884
  6.9 0.7 copy-start.13
  7.5 15.5 %copy-start.10 = (bf16[8,8,2816]{2,1,0:T(8,128)(2,1)S(1)}, bf16[8,8,2816]{2,1,0:T(8,128)(2,1)}, u32[]{:S(2)}) copy-start(bf16[8,8,2816]{2,1,0:T(8,128)(2,1)} %eta_ref.1) | copy-start | bytes 1081348
  16.3 20.3 %all-to-all-start.1 = ((bf16[16,128,128]{2,1,0:T(8,128)(2,1)}), bf16[16,128,128]{2,1,0:T(8,128)(2,1)S(1)}, u32[]{:S(2)}, u32[]{:S(2)}) async-start(bf16[16,128,128]{2,1,0:T(8,128)(2,1)} %get-tuple-element.19), calls=%async_computation.1 | async-start | bytes 1048576 | tf_op jit(solution)/shard_map/all_to_all | solution.py:726
  23.0 2.2 %copy-start.8 = (bf16[2,768,1408]{2,1,0:T(8,128)(2,1)S(1)}, bf16[2,768,1408]{2,1,0:T(8,128)(2,1)}, u32[]{:S(2)}) copy-start(bf16[2,768,1408]{2,1,0:T(8,128)(2,1)} %constant.18.clone.table_ref) | copy-start | bytes 12976132
  25.2 1.6 %copy-start.9 = (s32[3,8,8,2816]{3,2,1,0:T(8,128)S(1)}, s32[3,8,8,2816]{3,2,1,0:T(8,128)}, u32[]{:S(2)}) copy-start(s32[3,8,8,2816]{3,2,1,0:T(8,128)} %cells_ref.1) | copy-start | bytes 6488068
  26.9 14.4 %copy-start.11 = (f32[320,128]{1,0:T(8,128)S(1)}, f32[320,128]{1,0:T(8,128)}, u32[]{:S(2)}) copy-start(f32[320,128]{1,0:T(8,128)} %constant.20.clone.others_1_) | copy-start | bytes 491524
  26.9 14.4 %copy-start.12 = (bf16[320,128]{1,0:T(8,128)(2,1)S(1)}, bf16[320,128]{1,0:T(8,128)(2,1)}, u32[]{:S(2)}) copy-start(bf16[320,128]{1,0:T(8,128)(2,1)} %constant.19.clone.others_0_) | copy-start | bytes 245764
  28.7 2.2 %copy-start = (f32[7,8,8,2816]{3,2,1,0:T(8,128)}, f32[7,8,8,2816]{3,2,1,0:T(8,128)S(1)}, u32[]{:S(2)}) copy-start(f32[7,8,8,2816]{3,2,1,0:T(8,128)S(1)} %get-tuple-element.22.points_ref) | copy-start | bytes 15138820
  31.0 2.1 %copy-start.3 = (bf16[2,768,1408]{2,1,0:T(8,128)(2,1)}, bf16[2,768,1408]{2,1,0:T(8,128)(2,1)S(1)}, u32[]{:S(2)}) copy-start(bf16[2,768,1408]{2,1,0:T(8,128)(2,1)S(1)} %get-tuple-element.18.table_ref) | copy-start | bytes 12976132
  36.6 36.1 %all-to-all-start = ((bf16[16,128,128]{2,1,0:T(8,128)(2,1)}), bf16[16,128,128]{2,1,0:T(8,128)(2,1)S(1)}, u32[]{:S(2)}, u32[]{:S(2)}) async-start(bf16[16,128,128]{2,1,0:T(8,128)(2,1)} %get-tuple-element.17), calls=%async_computation | async-start | bytes 1048576 | tf_op jit(solution)/shard_map/all_to_all | solution.py:726
  41.2 2.2 %copy-start.4 = (bf16[2,768,1408]{2,1,0:T(8,128)(2,1)S(1)}, bf16[2,768,1408]{2,1,0:T(8,128)(2,1)}, u32[]{:S(2)}) copy-start(bf16[2,768,1408]{2,1,0:T(8,128)(2,1)} %copy-done.3) | copy-start | bytes 12976132
  43.5 6.8 %copy-start.1 = (f32[7,8,8,2816]{3,2,1,0:T(8,128)S(1)}, f32[7,8,8,2816]{3,2,1,0:T(8,128)}, u32[]{:S(2)}) copy-start(f32[7,8,8,2816]{3,2,1,0:T(8,128)} %copy-done) | copy-start | bytes 15138820
  47.1 3.2 %collective-permute-start.1 = (bf16[2,24,2816]{2,1,0:T(8,128)(2,1)S(1)}, bf16[2,24,2816]{2,1,0:T(8,128)(2,1)S(1)}, u32[]{:S(2)}, u32[]{:S(2)}) collective-permute-start(bf16[2,24,2816]{2,1,0:T(8,128)(2,1)S(1)} %bitcast.14), channel_id=1, source_target_pairs={{0,1},{1,0},{2,3},{3,2},{4,5},{5,4},{6,7},{7,6},{8,9},{9,8},{10,11... | collective-permute-start | bytes 811016 | tf_op jit(solution)/shard_map/ppermute | solution.py:383
  72.7 2.2 %copy-start.5 = (bf16[2,768,1408]{2,1,0:T(8,128)(2,1)S(1)}, bf16[2,768,1408]{2,1,0:T(8,128)(2,1)}, u32[]{:S(2)}) copy-start(bf16[2,768,1408]{2,1,0:T(8,128)(2,1)} %copy-done.3) | copy-start | bytes 12976132
  78.4 1.6 %collective-permute-start.2 = (bf16[2,24,2816]{2,1,0:T(8,128)(2,1)S(1)}, bf16[2,24,2816]{2,1,0:T(8,128)(2,1)S(1)}, u32[]{:S(2)}, u32[]{:S(2)}) collective-permute-start(bf16[2,24,2816]{2,1,0:T(8,128)(2,1)S(1)} %bitcast.15), channel_id=1, source_target_pairs={{0,1},{1,0},{2,3},{3,2},{4,5},{5,4},{6,7},{7,6},{8,9},{9,8},{10,11... | collective-permute-start | bytes 811016 | tf_op jit(solution)/shard_map/ppermute | solution.py:383
  80.0 2.4 %copy-start.2 = (f32[7,8,8,2816]{3,2,1,0:T(8,128)S(1)}, f32[7,8,8,2816]{3,2,1,0:T(8,128)}, u32[]{:S(2)}) copy-start(f32[7,8,8,2816]{3,2,1,0:T(8,128)} %copy-done) | copy-start | bytes 15138820

commit v9 on v8

--- a/solution.py
+++ b/solution.py
@@ -174,15 +174,8 @@
     )
 
 
-def prepare_kernel(
-    base_ref, eta_ref, cells_ref, table_ref, sums_ref, points_ref, table_out, sums_out, sems
-):
-    copies = [
-        pltpu.make_async_copy(table_ref, table_out, sems.at[0]),
-        pltpu.make_async_copy(sums_ref, sums_out, sems.at[1]),
-    ]
-    for copy in copies:
-        copy.start()
+def prepare_kernel(base_ref, after_ref, eta_ref, cells_ref, points_ref, done_ref):
+    done_ref[...] = after_ref[...]
     levels, rows, lon_total = eta_ref.shape
     shape = (rows, LANES)
     row_here = base_ref[1] + lax.broadcasted_iota(jnp.int32, shape, 0)
@@ -205,29 +198,23 @@
         return carry
 
     lax.fori_loop(0, lon_total // LANES, chunk_step, 0)
-    for copy in copies:
-        copy.wait()
-
-
-def prepare_call(base, eta_shift, cells, table, sums):
+
+
+def prepare_call(base, after, eta_shift, cells):
     in_vmem = pl.BlockSpec(memory_space=pltpu.VMEM)
     return pl.pallas_call(
         prepare_kernel,
         out_shape=(
             jax.ShapeDtypeStruct((7,) + eta_shift.shape, jnp.float32),
-            jax.ShapeDtypeStruct(table.shape, table.dtype),
-            jax.ShapeDtypeStruct(sums.shape, sums.dtype),
+            jax.ShapeDtypeStruct(after.shape, after.dtype),
         ),
-        in_specs=[pl.BlockSpec(memory_space=pltpu.SMEM)]
-        + [in_vmem] * 2
-        + [pl.BlockSpec(memory_space=pl.ANY)] * 2,
-        out_specs=(in_vmem, in_vmem, pl.BlockSpec(memory_space=pl.ANY)),
-        scratch_shapes=[pltpu.SemaphoreType.DMA((2,))],
+        in_specs=[pl.BlockSpec(memory_space=pltpu.SMEM)] + [in_vmem] * 3,
+        out_specs=(in_vmem, in_vmem),
         compiler_params=pltpu.CompilerParams(vmem_limit_bytes=16 * 1024 * 1024),
         cost_estimate=pl.CostEstimate(
             flops=40 * eta_shift.size, bytes_accessed=20_000_000, transcendentals=0
         ),
-    )(base, eta_shift, cells, table, sums)
+    )(base, after, eta_shift, cells)
 
 
 def arrival(points_ref, k, lanes):
@@ -400,20 +387,19 @@
 
 
 def legendre_kernel(numbers_ref, codes_ref, spectra_ref, *others):
-    tables, others = others[:-8], others[-8:]
-    wind_ref, tracer_ref, done_ref, wind_sums, tracer_sums = others[:5]
-    table_tail, column_tail, order_ref = others[5:]
+    tables, others = others[:-6], others[-6:]
+    out_ref, done_ref, sums = others[:3]
+    table_tail, column_tail, order_ref = others[3:]
     _, pairs, level_fields, degrees = spectra_ref.shape
     group = table_tail.shape[0]
-    bands, block, _ = wind_ref.shape
+    bands, block, _ = out_ref.shape
     full = degrees // LANES * LANES
     at_top = numbers_ref[0] == 0
     step = pl.program_id(0)
 
     @pl.when(step == 0)
     def _():
-        wind_sums[...] = jnp.zeros(wind_sums.shape, jnp.float32)
-        tracer_sums[...] = jnp.zeros(tracer_sums.shape, jnp.float32)
+        sums[...] = jnp.zeros(sums.shape, jnp.float32)
         done_ref[...] = jnp.zeros(done_ref.shape, jnp.float32)
         table_tail[...] = jnp.zeros(table_tail.shape, jnp.float32)
         column_tail[...] = jnp.zeros(column_tail.shape, jnp.float32)
@@ -422,8 +408,8 @@
         code_row = up_to(pl.num_programs(0) * group * PAIRED, ROWS)
         for band in range(bands):
             first = band * block + code_row
-            wind_sums[pl.ds(first, 1), :] = jnp.right_shift(codes, 4).astype(jnp.float32)
-            wind_sums[pl.ds(first + 1, 1), :] = (codes & 15).astype(jnp.float32)
+            sums[pl.ds(first, 1), :] = jnp.right_shift(codes, 4).astype(jnp.float32)
+            sums[pl.ds(first + 1, 1), :] = (codes & 15).astype(jnp.float32)
 
     band_row = lax.broadcasted_iota(jnp.int32, (bands, LANES), 0)
     first_half = lax.broadcasted_iota(jnp.int32, (bands, LANES), 1) < HALF
@@ -483,14 +469,17 @@
         rows = above + found + below
         for i in range(PAIRED):
             low, high = rows[i], rows[PAIRED + i]
-            place = pl.ds(slot * PAIRED + i, bands, stride=block)
-            wind_sums[place, :] = jnp.where(first_half, low, pltpu.roll(high, HALF, 1))
-            tracer_sums[place, :] = jnp.where(first_half, pltpu.roll(low, HALF, 1), high)
+            place = slot * PAIRED + i
+            pairs_of = (
+                jnp.where(first_half, low, pltpu.roll(high, HALF, 1)),
+                jnp.where(first_half, pltpu.roll(low, HALF, 1), high),
+            )
+            for number, value in enumerate(pairs_of):
+                sums[pl.ds(number * (block // 2) + place, bands, stride=block), :] = value
 
     @pl.when(step == pl.num_programs(0) - 1)
     def _():
-        wind_ref[...] = wind_sums[...].astype(jnp.bfloat16).reshape(wind_ref.shape)
-        tracer_ref[...] = tracer_sums[...].astype(jnp.bfloat16).reshape(tracer_ref.shape)
+        out_ref[...] = sums[...].astype(jnp.bfloat16).reshape(out_ref.shape)
 
 
 def column_order(level_fields):
@@ -512,7 +501,7 @@
 def legendre_call(pairing, spectra, tables):
     _, pairs, level_fields, degrees = spectra.shape
     bands = tables[0].shape[2]
-    block = block_rows(pairs)
+    block = 2 * block_rows(pairs)
     group = next(n for n in (4, 5, 2, 1) if pairs % n == 0)
     numbers = jnp.concatenate([lax.axis_index("lev").astype(jnp.int32)[None], pairing])
     codes = pl.pallas_call(
@@ -520,6 +509,7 @@
         out_shape=jax.ShapeDtypeStruct((1, LANES), jnp.int32),
         in_specs=[pl.BlockSpec(memory_space=pltpu.VMEM)] * 3,
         out_specs=pl.BlockSpec(memory_space=pltpu.VMEM),
+        compiler_params=pltpu.CompilerParams(vmem_limit_bytes=4 * 1024 * 1024),
         cost_estimate=pl.CostEstimate(flops=0, bytes_accessed=4_000_000, transcendentals=0),
     )(jnp.pad(pairing, (0, LANES - pairs))[None, :], spectra, tables[0])
     shape = jax.ShapeDtypeStruct((bands, block, LANES), jnp.bfloat16)
@@ -528,16 +518,15 @@
     return pl.pallas_call(
         legendre_kernel,
         grid=(pairs // group,),
-        out_shape=(shape, shape, jax.ShapeDtypeStruct((ROWS, LANES), jnp.float32)),
+        out_shape=(shape, jax.ShapeDtypeStruct((ROWS, LANES), jnp.float32)),
         in_specs=[
             pl.BlockSpec(memory_space=pltpu.SMEM),
             pl.BlockSpec((1, LANES), lambda i: (0, 0)),
             in_vmem,
         ]
         + [in_vmem] * len(tables),
-        out_specs=(whole, whole, in_vmem),
+        out_specs=(whole, in_vmem),
         scratch_shapes=[
-            pltpu.VMEM((bands * block, LANES), jnp.float32),
             pltpu.VMEM((bands * block, LANES), jnp.float32),
             pltpu.VMEM((group, ROWS * bands, LANES), jnp.float32),
             pltpu.VMEM((group, 2 * level_fields, LANES), jnp.float32),
@@ -602,12 +591,8 @@
     return place.astype(jnp.bfloat16)
 
 
-def fourier_kernel(pairs, levels, leads, base_ref, sums_ref, table_ref, *others):
-    if leads:
-        owner_ref, lane_ref, field_ref, send_ref, place_ref = others[:5]
-    else:
-        place_ref, _, field_ref, send_ref = others[:4]
-    codes, flat, gathered, lhs = others[-4:]
+def order_kernel(pairs, levels, after_ref, sums_ref, owner_ref, lane_ref, *others):
+    out_refs, (codes, flat, gathered, lhs) = others[:2], others[2:]
     bands, block, width = sums_ref.shape
     pair_total = bands * pairs
     padded = gathered.shape[0]
@@ -615,52 +600,81 @@
     fields = 2 * levels
     flat[...] = sums_ref[...].astype(jnp.float32).reshape(bands * block, width)
     gathered[pair_total:, :] = jnp.zeros((padded - pair_total, width), jnp.float32)
-    if leads:
-        code_row = up_to(pairs * PAIRED, ROWS)
-        place_ref[...] = pair_places(
-            flat, owner_ref, lane_ref, codes, bands, block, code_row, padded
-        )
-    place = place_ref[...]
+    code_row = up_to(pairs * PAIRED, ROWS)
+    place = pair_places(flat, owner_ref, lane_ref, codes, bands, block, code_row, padded)
     low = lax.broadcasted_iota(jnp.int32, (fields, padded), 1) < pair_total // 2
     middle = fields * ROWS
-    for i in range(PAIRED):
-        for band in range(bands):
-            gathered[band * pairs : (band + 1) * pairs, :] = flat[
-                pl.ds(band * block + i, pairs, stride=PAIRED), :
-            ]
-        ordered = jnp.dot(
-            gathered[...].T.astype(jnp.bfloat16), place, preferred_element_type=jnp.float32
-        )
-        for side in range(2):
-            row = side * PAIRED + i
-            if HALO <= row < HALO + ROWS:
-                first, stride = row - HALO, ROWS
-            else:
-                first, stride = middle + (row - HALO - ROWS) % TALL, 2 * HALO
-            for part in range(2):
-                start = side * HALF + part * fields
-                straight = ordered[start : start + fields]
-                start = start + 2 * fields
-                crossed = ordered[start : start + fields]
-                both = (jnp.where(low, straight, crossed), jnp.where(low, crossed, straight))
-                for parity in range(2):
-                    for t in range(blocks):
-                        lhs[parity, part * blocks + t, pl.ds(first, fields, stride=stride), :] = (
-                            both[parity][:, t * LANES : (t + 1) * LANES]
-                        )
+    for number, out_ref in enumerate(out_refs):
+        for i in range(PAIRED):
+            for band in range(bands):
+                first = band * block + number * (block // 2) + i
+                gathered[band * pairs : (band + 1) * pairs, :] = flat[
+                    pl.ds(first, pairs, stride=PAIRED), :
+                ]
+            ordered = jnp.dot(
+                gathered[...].T.astype(jnp.bfloat16), place, preferred_element_type=jnp.float32
+            )
+            for side in range(2):
+                row = side * PAIRED + i
+                if HALO <= row < HALO + ROWS:
+                    first, stride = row - HALO, ROWS
+                else:
+                    first, stride = middle + (row - HALO - ROWS) % TALL, 2 * HALO
+                for part in range(2):
+                    start = side * HALF + part * fields
+                    straight = ordered[start : start + fields]
+                    start = start + 2 * fields
+                    crossed = ordered[start : start + fields]
+                    both = (jnp.where(low, straight, crossed), jnp.where(low, crossed, straight))
+                    for parity in range(2):
+                        for t in range(blocks):
+                            lhs[
+                                parity, part * blocks + t, pl.ds(first, fields, stride=stride), :
+                            ] = both[parity][:, t * LANES : (t + 1) * LANES]
+        for parity in range(2):
+            for t in range(2 * blocks):
+                out_ref[parity, :, t * LANES : (t + 1) * LANES] = lhs[parity, t].astype(
+                    jnp.bfloat16
+                )
+
+
+def order_call(after, sums, pairs, levels):
+    bands, block, width = sums.shape
+    padded = up_to(bands * pairs, LANES)
+    extra = [jnp.asarray(x) for x in owner_tables(bands, pairs)]
+    shape = jax.ShapeDtypeStruct((2, 2 * levels * TALL, 2 * padded), jnp.bfloat16)
+    in_vmem = pl.BlockSpec(memory_space=pltpu.VMEM)
+    return pl.pallas_call(
+        functools.partial(order_kernel, pairs, levels),
+        out_shape=(shape, shape),
+        in_specs=[in_vmem] * 4,
+        out_specs=(in_vmem, in_vmem),
+        scratch_shapes=[
+            pltpu.VMEM((2, LANES, LANES), jnp.float32),
+            pltpu.VMEM((bands * block, width), jnp.float32),
+            pltpu.VMEM((padded, width), jnp.float32),
+            pltpu.VMEM((2, 2 * padded // LANES, 2 * levels * TALL, LANES), jnp.float32),
+        ],
+        compiler_params=pltpu.CompilerParams(vmem_limit_bytes=16 * 1024 * 1024),
+        cost_estimate=pl.CostEstimate(
+            flops=4_000_000_000, bytes_accessed=8_000_000, transcendentals=0
+        ),
+    )(after, sums, *extra)
+
+
+def transform_kernel(levels, base_ref, lhs_ref, table_ref, field_ref, send_ref):
     half = table_ref.shape[2]
+    middle = 2 * levels * ROWS
 
     def transform(first, count):
-        found = []
-        for parity in range(2):
-            left = jnp.concatenate(
-                [
-                    lhs[parity, t, first : first + count, :].astype(jnp.bfloat16)
-                    for t in range(2 * blocks)
-                ],
-                axis=1,
+        found = [
+            jnp.dot(
+                lhs_ref[parity, first : first + count, :],
+                table_ref[parity],
+                preferred_element_type=jnp.float32,
             )
-            found.append(jnp.dot(left, table_ref[parity], preferred_element_type=jnp.float32))
+            for parity in range(2)
+        ]
         pieces = (found[0] + found[1], found[0] - found[1])
         return [piece.astype(jnp.bfloat16).astype(jnp.float32) for piece in pieces]
 
@@ -670,7 +684,7 @@
         for part, value in enumerate(pieces):
             value = value.reshape(group, 2 * ROWS, half)
             field_ref[level : level + group, : 2 * ROWS, part * half : (part + 1) * half] = value
-    for part, value in enumerate(transform(middle, fields * 2 * HALO)):
+    for part, value in enumerate(transform(middle, 2 * levels * 2 * HALO)):
         value = value.reshape(levels, 4 * HALO, half)
         field_ref[:, 2 * ROWS :, part * half : (part + 1) * half] = value
     if send_ref.shape[0] == 1:
@@ -681,45 +695,23 @@
         send_ref[1] = field_ref[levels - HALO :].astype(jnp.bfloat16)
 
 
-def fourier_call(base, sums, table, pairs, levels, lon_total, place=None, after=None):
-    bands, block, width = sums.shape
-    pair_total = bands * pairs
-    padded = up_to(pair_total, LANES)
-    leads = place is None
+def transform_call(base, lhs, table, levels, lon_total):
     sends = 1 if lax.axis_size("lev") == 2 else 2
     field_shape = (levels, 3 * ROWS, lon_total)
-    out_shape = [
-        jax.ShapeDtypeStruct(field_shape, jnp.float32),
-        jax.ShapeDtypeStruct((sends, HALO) + field_shape[1:], jnp.bfloat16),
-    ]
-    extra = [place, after]
-    if leads:
-        out_shape.append(jax.ShapeDtypeStruct((padded, padded), jnp.bfloat16))
-        extra = [jnp.asarray(x) for x in owner_tables(bands, pairs)]
     in_vmem = pl.BlockSpec(memory_space=pltpu.VMEM)
     return pl.pallas_call(
-        functools.partial(fourier_kernel, pairs, levels, leads),
-        out_shape=tuple(out_shape),
-        in_specs=[
-            pl.BlockSpec(memory_space=pltpu.SMEM),
-            in_vmem,
-            in_vmem,
-        ]
-        + [in_vmem] * 2,
-        out_specs=(in_vmem,) * len(out_shape),
-        scratch_shapes=[
-            pltpu.VMEM((2, LANES, LANES), jnp.float32),
-            pltpu.VMEM((bands * block, width), jnp.float32),
-            pltpu.VMEM((padded, width), jnp.float32),
-            pltpu.VMEM((2, 2 * padded // LANES, 2 * levels * TALL, LANES), jnp.float32),
-        ],
+        functools.partial(transform_kernel, levels),
+        out_shape=(
+            jax.ShapeDtypeStruct(field_shape, jnp.float32),
+            jax.ShapeDtypeStruct((sends, HALO) + field_shape[1:], jnp.bfloat16),
+        ),
+        in_specs=[pl.BlockSpec(memory_space=pltpu.SMEM), in_vmem, in_vmem],
+        out_specs=(in_vmem, in_vmem),
         compiler_params=pltpu.CompilerParams(vmem_limit_bytes=16 * 1024 * 1024),
         cost_estimate=pl.CostEstimate(
-            flops=2 * levels * 4 * TALL * padded * lon_total,
-            bytes_accessed=8_000_000,
-            transcendentals=0,
+            flops=3_000_000_000, bytes_accessed=8_000_000, transcendentals=0
         ),
-    )(base, sums, table, *extra)
+    )(base, lhs, table)
 
 
 def exchange(sums):
@@ -737,20 +729,19 @@
         tables = (lax.all_gather(table, "lev", axis=0, tiled=True),)
     base = jnp.stack([lax.axis_index("lev") * levels, lax.axis_index("band") * rows])
     base = base.astype(jnp.int32)
-    wind_sums, tracer_sums, _ = legendre_call(pairing, spectra, tables)
-    wind_sums = exchange(wind_sums)
+    sums, done = legendre_call(pairing, spectra, tables)
+    sums = exchange(sums)
+    points, done = prepare_call(base, done, eta_shift, cells)
     pair_total = pairs * lax.axis_size("band")
     twiddles = jnp.asarray(fourier_table(pair_total, up_to(pair_total, LANES), lon_total))
-    points, twiddles, tracer_sums = prepare_call(base, eta_shift, cells, twiddles, tracer_sums)
-    tracer_sums = exchange(tracer_sums)
-    size = (pairs, levels, lon_total)
-    winds, send, place = fourier_call(base, wind_sums, twiddles, *size)
-    displacement, moved, done = interpolation_call(
-        wind_levels, base, winds, points, swap_levels(send), (), jnp.float32, 2
-    )
-    tracers, send = fourier_call(base, tracer_sums, twiddles, *size, place, done)
+    ordered = order_call(done, sums, pairs, levels)
+    winds, wind_send = transform_call(base, ordered[0], twiddles, levels, lon_total)
+    tracers, tracer_send = transform_call(base, ordered[1], twiddles, levels, lon_total)
+    displacement, moved, _ = interpolation_call(
+        wind_levels, base, winds, points, swap_levels(wind_send), (), jnp.float32, 2
+    )
     advected, _ = interpolation_call(
-        tracer_levels, base, tracers, points, swap_levels(send), (moved,), jnp.bfloat16, 1
+        tracer_levels, base, tracers, points, swap_levels(tracer_send), (moved,), jnp.bfloat16, 1
     )
     return advected, displacement
 

time: 104 us -> 106 us (1.019)
  waiting for transfers between devices: 5.96 us -> 20 us
  Pallas kernels: 62.8 us -> 57.7 us
  starting transfers between devices: 14.5 us -> 9.81 us
  local copies, waits for them, and re-layouts: 18.4 us -> 16.9 us
    all_to_all x2 -> x1, waiting for transfers between devices: 3.58 us -> 20 us  [exchange(): return lax.all_to_all(sums, 'band', split_axis=0, concat_axis=0, tiled=True)]
    all_to_all x2 -> x1, starting transfers between devices: 11.3 us -> 6.79 us  [exchange(): return lax.all_to_all(sums, 'band', split_axis=0, concat_axis=0, tiled=True)]
    pallas_call x1, Pallas kernels: 2.66 us -> 0.01 us  [legendre_call(): pl.pallas_call(touch_kernel, out_shape=jax.ShapeDtypeStruct((1, LANES), j...]
    ppermute x2, waiting for transfers between devices: 2.35 us -> 0.01 us  [swap_levels(): return (lax.ppermute(send[0], 'lev', [(0, 1), (1, 0)]),)]
    pallas_call x1, Pallas kernels: 8.74 us -> 6.86 us  [legendre_call(): pl.pallas_call(legendre_kernel, grid=(pairs // group,), out_shape=(shape,...]
    unnamed x30 -> x34, local copies, waits for them, and re-layouts: 17.2 us -> 16.2 us
    pallas_call x2 -> x3, Pallas kernels: 7.02 us -> 6.89 us  [the longest x2 5.22 us: transform_call(): pl.pallas_call(functools.partial(transform_kernel, levels), out_shape=(ja...]
  transfers between devices with their start and end apart: 5 -> 4, of which waited for: 3 -> 1; matrix products, arithmetic and copies ran while one was open for 1% -> 1% of each run, Pallas kernels for 30% -> 25%
where the time goes in v9:
time: 106 us; the launch traced here: 105 us
  Pallas kernels  57.7 us (54%)
  waiting for transfers between devices  20 us (19%)
  local copies, waits for them, and re-layouts  16.9 us (16%)
  starting transfers between devices  9.81 us (9%)
    pallas_call x2, Pallas kernels, interpolation_call(): pl.pallas_call(functools.partial(interpolation_kernel, levels_body, toget...  42.5 us
    all_to_all x1, waiting for transfers between devices, exchange(): return lax.all_to_all(sums, 'band', split_axis=0, concat_axis=0, tiled=True)  20 us
    unnamed x34, local copies, waits for them, and re-layouts  16.2 us
    pallas_call x1, Pallas kernels, legendre_call(): pl.pallas_call(legendre_kernel, grid=(pairs // group,), out_shape=(shape,...  6.86 us
    all_to_all x1, starting transfers between devices, exchange(): return lax.all_to_all(sums, 'band', split_axis=0, concat_axis=0, tiled=True)  6.79 us
    pallas_call x2, Pallas kernels, transform_call(): pl.pallas_call(functools.partial(transform_kernel, levels), out_shape=(ja...  5.22 us
    ppermute x2, starting transfers between devices, swap_levels(): return (lax.ppermute(send[0], 'lev', [(0, 1), (1, 0)]),)  2.28 us
  transfers between devices with their start and end apart: 4, of which 1 were waited for; matrix products, arithmetic and copies ran while one was open for 1% of the time, Pallas kernels for 25%

profile of v9, /device:TPU:9, one launch (start us, length us, event | category | flops | bytes accessed | tf_op | source)
XLA Modules:
  0.0 105.3 jit_solution(4266347207301750947)
XLA Ops:
  0.6 0.0 copy-start.14
  0.6 0.7 collective-permute-start
  1.4 0.7 pad_bitcast_fusion.numbers_ref
  2.0 0.0 copy-start.1
  2.0 1.5 %copy-done.1 = bf16[2,32,20,641]{3,1,2,0:T(8,128)(2,1)S(1)} copy-done((bf16[2,32,20,641]{3,1,2,0:T(8,128)(2,1)S(1)}, bf16[2,32,20,641]{3,1,2,0:T(8,128)(2,1)}, u32[]{:S(2)}) %copy-start.1) | copy-done | bytes 1640984
  3.6 0.0 copy-start.3
  3.6 1.5 %copy-done.3 = bf16[4,16,20,641]{3,1,2,0:T(8,128)(2,1)S(1)} copy-done((bf16[4,16,20,641]{3,1,2,0:T(8,128)(2,1)S(1)}, bf16[4,16,20,641]{3,1,2,0:T(8,128)(2,1)}, u32[]{:S(2)}) %copy-start.3) | copy-done | bytes 1640984
  5.1 0.0 copy-start.2
  5.1 0.0 copy-start.4
  5.1 0.0 copy-done.14
  5.1 0.1 pad_add_fusion.1.numbers_ref
  5.2 0.0 collective-permute-done.others_1_
  5.2 0.0 copy-start.6
  5.2 1.3 %copy-done.6 = bf16[4,20,16,641]{3,2,1,0:T(8,128)(2,1)} copy-done((bf16[4,20,16,641]{3,2,1,0:T(8,128)(2,1)}, bf16[4,20,16,641]{3,2,1,0:T(8,128)(2,1)S(1)}, u32[]{:S(2)}) %copy-start.6) | copy-done | bytes 1640984
  6.5 0.9 copy-done.2
  7.4 0.6 copy-done.4
  8.0 0.0 copy-start.7
  8.0 1.5 %copy-done.7 = bf16[4,20,16,641]{3,2,1,0:T(8,128)(2,1)S(1)} copy-done((bf16[4,20,16,641]{3,2,1,0:T(8,128)(2,1)S(1)}, bf16[4,20,16,641]{3,2,1,0:T(8,128)(2,1)}, u32[]{:S(2)}) %copy-start.7) | copy-done | bytes 1640984
  9.5 0.0 copy-start.5
  9.5 6.9 %shard_map.96 = (bf16[16,256,128]{2,1,0:T(8,128)(2,1)S(1)}, f32[8,128]{1,0:T(8,128)S(1)}) custom-call(s32[21]{0:T(128)S(1)} %pad_add_fusion.1.numbers_ref, s32[1,128]{1,0:T(1,128)S(1)} %shard_map.95.codes_ref, bf16[2,20,32,641]{3,2,1,0:T(8,128)(2,1)S(1)} %bitcast.12, bf16[4,20,16,641]{3,2,1,0:T(8,128)(2,1)S(1)} %bitcast.15, ...), custom_call_target="tpu_custom_call" | custom-call | flops 420085760 | bytes 8000000 | tf_op jit(solution)/shard_map/pallas_call | solution.py:518
  16.4 0.0 copy-start.8
  16.4 1.0 copy-done.8
  17.4 0.0 copy-start.12
  17.4 0.0 copy-start.13
  17.4 6.8 %all-to-all-start = ((bf16[16,256,128]{2,1,0:T(8,128)(2,1)}), bf16[16,256,128]{2,1,0:T(8,128)(2,1)S(1)}, u32[]{:S(2)}, u32[]{:S(2)}) async-start(bf16[16,256,128]{2,1,0:T(8,128)(2,1)} %copy-done.8), calls=%async_computation | async-start | bytes 2097152 | tf_op jit(solution)/shard_map/all_to_all | solution.py:718
  24.2 0.1 pad_add_fusion.base_ref
  24.2 0.0 copy-done.5
  24.2 0.0 copy-start.9
  24.2 1.0 copy-done.9
  25.2 1.4 %shard_map.97 = (f32[7,8,8,2816]{3,2,1,0:T(8,128)S(1)}, f32[8,128]{1,0:T(8,128)S(1)}) custom-call(s32[2]{0:T(128)S(1)} %pad_add_fusion.base_ref, f32[8,128]{1,0:T(8,128)S(1)} %get-tuple-element.15.after_ref, bf16[8,8,2816]{2,1,0:T(8,128)(2,1)S(1)} %copy-done.9, s32[3,8,8,2816]{3,2,1,0:T(8,128)S(1)} %copy-done.5), custom_call_target="tpu_custom_call" | custom-call | flops 7208960 | bytes 20000000 | tf_op jit(solution)/shard_map/pallas_call | solution.py:205
  26.6 0.0 copy-start
  26.6 2.2 %copy-done = f32[7,8,8,2816]{3,2,1,0:T(8,128)} copy-done((f32[7,8,8,2816]{3,2,1,0:T(8,128)}, f32[7,8,8,2816]{3,2,1,0:T(8,128)S(1)}, u32[]{:S(2)}) %copy-start) | copy-done | bytes 5046296
  28.8 20.0 %all-to-all-done.sums_ref = bf16[16,256,128]{2,1,0:T(8,128)(2,1)S(1)} async-done(((bf16[16,256,128]{2,1,0:T(8,128)(2,1)}), bf16[16,256,128]{2,1,0:T(8,128)(2,1)S(1)}, u32[]{:S(2)}, u32[]{:S(2)}) %all-to-all-start) | async-done | bytes 1048608 | tf_op jit(solution)/shard_map/all_to_all | solution.py:718
  48.9 0.0 copy-done.12
  48.9 0.0 copy-done.13
  48.9 1.7 %shard_map.98 = (bf16[2,192,768]{2,1,0:T(8,128)(2,1)S(1)}, bf16[2,192,768]{2,1,0:T(8,128)(2,1)S(1)}) custom-call(f32[8,128]{1,0:T(8,128)S(1)} %get-tuple-element.16.after_ref, bf16[16,256,128]{2,1,0:T(8,128)(2,1)S(1)} %all-to-all-done.sums_ref, bf16[320,128]{1,0:T(8,128)(2,1)S(1)} %copy-done.13, f32[320,128]{1,0:T(8,128)S(1)} %copy-done.12), custom_call_target="tpu_custom_call" | custom-call | flops 4000000000 | bytes 8000000 | tf_op jit(solution)/shard_map/pallas_call | solution.py:647
  50.6 0.0 copy-start.10
  50.6 2.2 %copy-done.10 = bf16[2,768,1408]{2,1,0:T(8,128)(2,1)S(1)} copy-done((bf16[2,768,1408]{2,1,0:T(8,128)(2,1)S(1)}, bf16[2,768,1408]{2,1,0:T(8,128)(2,1)}, u32[]{:S(2)}) %copy-start.10) | copy-done | bytes 4325400
  52.8 2.6 %shard_map.100 = (f32[8,24,2816]{2,1,0:T(8,128)S(1)}, bf16[1,2,24,2816]{3,2,1,0:T(8,128)(2,1)S(1)}) custom-call(s32[2]{0:T(128)S(1)} %pad_add_fusion.base_ref, bf16[2,192,768]{2,1,0:T(8,128)(2,1)S(1)} %get-tuple-element.22.lhs_ref, bf16[2,768,1408]{2,1,0:T(8,128)(2,1)S(1)} %copy-done.10), custom_call_target="tpu_custom_call" | custom-call | flops 3000000000 | bytes 8000000 | tf_op jit(solution)/shard_map/pallas_call | solution.py:702
  55.4 2.2 %collective-permute-start.2 = (bf16[2,24,2816]{2,1,0:T(8,128)(2,1)S(1)}, bf16[2,24,2816]{2,1,0:T(8,128)(2,1)S(1)}, u32[]{:S(2)}, u32[]{:S(2)}) collective-permute-start(bf16[2,24,2816]{2,1,0:T(8,128)(2,1)S(1)} %bitcast.17), channel_id=1, source_target_pairs={{0,1},{1,0},{2,3},{3,2},{4,5},{5,4},{6,7},{7,6},{8,9},{9,8},{10,11... | collective-permute-start | bytes 811016 | tf_op jit(solution)/shard_map/ppermute | solution.py:370
  57.6 0.0 slice-start
  57.6 0.0 copy-start.11
  57.6 2.4 %copy-done.11 = bf16[2,768,1408]{2,1,0:T(8,128)(2,1)S(1)} copy-done((bf16[2,768,1408]{2,1,0:T(8,128)(2,1)S(1)}, bf16[2,768,1408]{2,1,0:T(8,128)(2,1)}, u32[]{:S(2)}) %copy-start.11) | copy-done | bytes 4325400
  60.0 0.0 slice-start.1
  60.0 2.6 %shard_map.99 = (f32[8,24,2816]{2,1,0:T(8,128)S(1)}, bf16[1,2,24,2816]{3,2,1,0:T(8,128)(2,1)S(1)}) custom-call(s32[2]{0:T(128)S(1)} %pad_add_fusion.base_ref, bf16[2,192,768]{2,1,0:T(8,128)(2,1)S(1)} %get-tuple-element.18.lhs_ref, bf16[2,768,1408]{2,1,0:T(8,128)(2,1)S(1)} %copy-done.11), custom_call_target="tpu_custom_call" | custom-call | flops 3000000000 | bytes 8000000 | tf_op jit(solution)/shard_map/pallas_call | solution.py:702
  62.6 0.1 collective-permute-start.1
  62.7 0.0 collective-permute-done.2.others_0_
  62.7 0.0 slice-done
  62.7 0.0 slice-done.1
  62.7 22.5 %shard_map.101 = (f32[2,8,8,2816]{3,2,1,0:T(8,128)}, f32[2,8,8,2816]{3,2,1,0:T(8,128)S(1)}, f32[8,128]{1,0:T(8,128)}) custom-call(s32[2]{0:T(128)S(1)} %pad_add_fusion.base_ref, f32[8,24,2816]{2,1,0:T(8,128)S(1)} %get-tuple-element.23.field_ref, f32[7,8,8,2816]{3,2,1,0:T(8,128)S(1)} %bitcast.10, bf16[2,24,2816]{2,1,0:T(8,128)(2,1)S(1)} %collective-permute-done.2.others_0_), custom_call_target="tpu_custom_call" | custom-call | flops 90112000 | bytes 7208960 | tf_op jit(solution)/shard_map/pallas_call | solution.py:349
  85.2 0.0 collective-permute-done.1.others_0_
  85.2 20.1 %shard_map.102 = (bf16[2,8,8,2816]{3,2,1,0:T(8,128)(2,1)}, f32[8,128]{1,0:T(8,128)}) custom-call(s32[2]{0:T(128)S(1)} %pad_add_fusion.base_ref, f32[8,24,2816]{2,1,0:T(8,128)S(1)} %get-tuple-element.19.field_ref, f32[7,8,8,2816]{3,2,1,0:T(8,128)S(1)} %bitcast.10, bf16[2,24,2816]{2,1,0:T(8,128)(2,1)S(1)} %collective-permute-done.1.others_0_, ...), custom_call_target="tpu_custom_call" | custom-call | flops 90112000 | bytes 7208960 | tf_op jit(solution)/shard_map/pallas_call | solution.py:349
  (2 shorter events, 0.0 us)
Async XLA Ops:
  0.6 4.5 %copy-start.14 = (s32[20]{0:T(128)S(1)}, s32[20]{0:T(128)}, u32[]{:S(2)}) copy-start(s32[20]{0:T(128)} %param.10) | copy-start | bytes 244
  0.6 4.6 %collective-permute-start = (bf16[4,20,16,641]{3,2,1,0:T(8,128)(2,1)}, bf16[4,20,16,641]{3,2,1,0:T(8,128)(2,1)S(1)}, u32[]{:S(2)}, u32[]{:S(2)}) collective-permute-start(bf16[4,20,16,641]{3,2,1,0:T(8,128)(2,1)} %bitcast.13), channel_id=1, source_target_pairs={{0,1},{1,0},{2,3},{3,2},{4,5},{5,4},{6,7},{7,6},{8,9},{9,8},{10,11... | collective-permute-start | bytes 4922888 | tf_op jit(solution)/shard_map/ppermute | solution.py:727
  2.0 1.5 %copy-start.1 = (bf16[2,32,20,641]{3,1,2,0:T(8,128)(2,1)S(1)}, bf16[2,32,20,641]{3,1,2,0:T(8,128)(2,1)}, u32[]{:S(2)}) copy-start(bf16[2,32,20,641]{3,1,2,0:T(8,128)(2,1)} %param.8) | copy-start | bytes 4922884
  3.6 1.5 %copy-start.3 = (bf16[4,16,20,641]{3,1,2,0:T(8,128)(2,1)S(1)}, bf16[4,16,20,641]{3,1,2,0:T(8,128)(2,1)}, u32[]{:S(2)}) copy-start(bf16[4,16,20,641]{3,1,2,0:T(8,128)(2,1)} %param.9) | copy-start | bytes 4922884
  5.1 2.3 %copy-start.2 = (bf16[2,32,20,641]{3,1,2,0:T(8,128)(2,1)S(1)}, bf16[2,32,20,641]{3,1,2,0:T(8,128)(2,1)}, u32[]{:S(2)}) copy-start(bf16[2,32,20,641]{3,1,2,0:T(8,128)(2,1)} %param.8) | copy-start | bytes 4922884
  5.1 2.8 %copy-start.4 = (bf16[4,16,20,641]{3,1,2,0:T(8,128)(2,1)S(1)}, bf16[4,16,20,641]{3,1,2,0:T(8,128)(2,1)}, u32[]{:S(2)}) copy-start(bf16[4,16,20,641]{3,1,2,0:T(8,128)(2,1)} %param.9) | copy-start | bytes 4922884
  5.2 1.3 %copy-start.6 = (bf16[4,20,16,641]{3,2,1,0:T(8,128)(2,1)}, bf16[4,20,16,641]{3,2,1,0:T(8,128)(2,1)S(1)}, u32[]{:S(2)}) copy-start(bf16[4,20,16,641]{3,2,1,0:T(8,128)(2,1)S(1)} %collective-permute-done.others_1_) | copy-start | bytes 4922884
  8.0 1.5 %copy-start.7 = (bf16[4,20,16,641]{3,2,1,0:T(8,128)(2,1)S(1)}, bf16[4,20,16,641]{3,2,1,0:T(8,128)(2,1)}, u32[]{:S(2)}) copy-start(bf16[4,20,16,641]{3,2,1,0:T(8,128)(2,1)} %copy-done.6) | copy-start | bytes 4922884
  9.5 14.7 %copy-start.5 = (s32[3,8,8,2816]{3,2,1,0:T(8,128)S(1)}, s32[3,8,8,2816]{3,2,1,0:T(8,128)}, u32[]{:S(2)}) copy-start(s32[3,8,8,2816]{3,2,1,0:T(8,128)} %cells_ref.1) | copy-start | bytes 6488068
  16.4 1.0 copy-start.8
  17.4 31.5 %copy-start.12 = (f32[320,128]{1,0:T(8,128)S(1)}, f32[320,128]{1,0:T(8,128)}, u32[]{:S(2)}) copy-start(f32[320,128]{1,0:T(8,128)} %constant.20.clone.lane_ref) | copy-start | bytes 491524
  17.4 31.5 %copy-start.13 = (bf16[320,128]{1,0:T(8,128)(2,1)S(1)}, bf16[320,128]{1,0:T(8,128)(2,1)}, u32[]{:S(2)}) copy-start(bf16[320,128]{1,0:T(8,128)(2,1)} %constant.19.clone.owner_ref) | copy-start | bytes 245764
  17.4 31.5 %all-to-all-start = ((bf16[16,256,128]{2,1,0:T(8,128)(2,1)}), bf16[16,256,128]{2,1,0:T(8,128)(2,1)S(1)}, u32[]{:S(2)}, u32[]{:S(2)}) async-start(bf16[16,256,128]{2,1,0:T(8,128)(2,1)} %copy-done.8), calls=%async_computation | async-start | bytes 2097152 | tf_op jit(solution)/shard_map/all_to_all | solution.py:718
  24.2 1.0 copy-start.9
  26.6 2.3 %copy-start = (f32[7,8,8,2816]{3,2,1,0:T(8,128)}, f32[7,8,8,2816]{3,2,1,0:T(8,128)S(1)}, u32[]{:S(2)}) copy-start(f32[7,8,8,2816]{3,2,1,0:T(8,128)S(1)} %get-tuple-element.20.points_ref) | copy-start | bytes 15138820
  50.6 2.2 %copy-start.10 = (bf16[2,768,1408]{2,1,0:T(8,128)(2,1)S(1)}, bf16[2,768,1408]{2,1,0:T(8,128)(2,1)}, u32[]{:S(2)}) copy-start(bf16[2,768,1408]{2,1,0:T(8,128)(2,1)} %constant.18.clone.table_ref) | copy-start | bytes 12976132
  55.4 7.3 %collective-permute-start.2 = (bf16[2,24,2816]{2,1,0:T(8,128)(2,1)S(1)}, bf16[2,24,2816]{2,1,0:T(8,128)(2,1)S(1)}, u32[]{:S(2)}, u32[]{:S(2)}) collective-permute-start(bf16[2,24,2816]{2,1,0:T(8,128)(2,1)S(1)} %bitcast.17), channel_id=1, source_target_pairs={{0,1},{1,0},{2,3},{3,2},{4,5},{5,4},{6,7},{7,6},{8,9},{9,8},{10,11... | collective-permute-start | bytes 811016 | tf_op jit(solution)/shard_map/ppermute | solution.py:370
  57.6 5.1 %slice-start = ((s8[5046272]{0:T(1024)(128)(4,1)}), s8[4194304]{0:T(1024)(128)(4,1)S(1)}, s32[]{:S(2)}) async-start(s8[5046272]{0:T(1024)(128)(4,1)} %bitcast.9), calls=%async_computation.1 | async-start | bytes 8388608
  57.6 2.4 %copy-start.11 = (bf16[2,768,1408]{2,1,0:T(8,128)(2,1)S(1)}, bf16[2,768,1408]{2,1,0:T(8,128)(2,1)}, u32[]{:S(2)}) copy-start(bf16[2,768,1408]{2,1,0:T(8,128)(2,1)} %constant.18.clone.table_ref) | copy-start | bytes 12976132
  60.0 2.7 %slice-start.1 = ((s8[5046272]{0:T(1024)(128)(4,1)}), s8[851968]{0:T(1024)(128)(4,1)S(1)}, s32[]{:S(2)}) async-start(s8[5046272]{0:T(1024)(128)(4,1)} %bitcast.9), calls=%async_computation.2 | async-start | bytes 1703936
  62.6 22.6 %collective-permute-start.1 = (bf16[2,24,2816]{2,1,0:T(8,128)(2,1)S(1)}, bf16[2,24,2816]{2,1,0:T(8,128)(2,1)S(1)}, u32[]{:S(2)}, u32[]{:S(2)}) collective-permute-start(bf16[2,24,2816]{2,1,0:T(8,128)(2,1)S(1)} %bitcast.16), channel_id=1, source_target_pairs={{0,1},{1,0},{2,3},{3,2},{4,5},{5,4},{6,7},{7,6},{8,9},{9,8},{10,11... | collective-permute-start | bytes 811016 | tf_op jit(solution)/shard_map/ppermute | solution.py:370

commit v10 on v9

--- a/solution.py
+++ b/solution.py
@@ -282,7 +282,7 @@
 
 
 def interpolation_kernel(
-    levels_body, together, near_count, out_count, base_ref, field_ref, points_ref, *others
+    levels_body, together, number, near_count, out_count, base_ref, field_ref, points_ref, *others
 ):
     nears, others = others[:near_count], others[near_count:]
     full, even_scratch, odd_scratch, keep = others[-4:]
@@ -296,12 +296,12 @@
     full[HALO : HALO + levels] = field_ref[...]
     if near_count == 1:
         found = jnp.where(base_ref[0] == 0, levels + HALO, 0)
-        full[pl.ds(found, HALO)] = nears[0][...].astype(jnp.float32)
+        full[pl.ds(found, HALO)] = nears[0][number].astype(jnp.float32)
         empty = levels + HALO - found
         full[pl.ds(empty, HALO)] = jnp.zeros((HALO,) + full.shape[1:], jnp.float32)
     else:
-        full[:HALO] = nears[0][...].astype(jnp.float32)
-        full[HALO + levels :] = nears[1][...].astype(jnp.float32)
+        full[:HALO] = nears[0][number].astype(jnp.float32)
+        full[HALO + levels :] = nears[1][number].astype(jnp.float32)
 
     def first_fill(slab, carry):
         for start, finish in fill_units(slab, 0, chunk_total, full, even_scratch):
@@ -338,16 +338,20 @@
     lax.fori_loop(0, chunk_total // 2, chunk_pair, 0)
 
 
-def interpolation_call(levels_body, base, fields, points, nears, extra, out_dtype, out_count):
+def interpolation_call(
+    levels_body, base, number, fields, points, nears, extra, out_dtype, out_count
+):
     _, levels, rows, lon_total = points.shape
     count = levels * rows * lon_total
-    together = next(n for n in (4, 2, 1) if levels % n == 0)
+    together = 2 if levels % 2 == 0 else 1
     scratch = pltpu.VMEM(((levels + 2 * HALO) * 5 * STACK, LANES), jnp.float32)
     in_vmem = pl.BlockSpec(memory_space=pltpu.VMEM)
     out = jax.ShapeDtypeStruct((2, levels, rows, lon_total), out_dtype)
     done = jax.ShapeDtypeStruct((ROWS, LANES), jnp.float32)
     return pl.pallas_call(
-        functools.partial(interpolation_kernel, levels_body, together, len(nears), out_count),
+        functools.partial(
+            interpolation_kernel, levels_body, together, number, len(nears), out_count
+        ),
         out_shape=(out,) * out_count + (done,),
         in_specs=[pl.BlockSpec(memory_space=pltpu.SMEM)]
         + [in_vmem] * (2 + len(nears) + len(extra)),
@@ -382,14 +386,16 @@
 HALF = LANES // 2
 
 
-def touch_kernel(numbers_ref, spectra_ref, table_ref, out_ref):
+def codes_kernel(numbers_ref, out_ref):
     out_ref[...] = numbers_ref[...]
 
 
 def legendre_kernel(numbers_ref, codes_ref, spectra_ref, *others):
-    tables, others = others[:-6], others[-6:]
-    out_ref, done_ref, sums = others[:3]
-    table_tail, column_tail, order_ref = others[3:]
+    table_count = (len(others) - 8) // 2
+    sources, others = (spectra_ref,) + others[:table_count], others[table_count:]
+    out_ref, done_ref, sums, table_tail, column_tail, order_ref = others[:6]
+    targets, arrivals = others[6:-1], others[-1]
+    spectra_here, tables = targets[0], targets[1:]
     _, pairs, level_fields, degrees = spectra_ref.shape
     group = table_tail.shape[0]
     bands, block, _ = out_ref.shape
@@ -397,8 +403,18 @@
     at_top = numbers_ref[0] == 0
     step = pl.program_id(0)
 
+    def copies(number):
+        here = pl.ds(number * group, group)
+        return [
+            pltpu.make_async_copy(source.at[:, here], target.at[:, here], arrivals.at[n, number])
+            for n, (source, target) in enumerate(zip(sources, targets))
+        ]
+
     @pl.when(step == 0)
     def _():
+        for number in range(pairs // group):
+            for copy in copies(number):
+                copy.start()
         sums[...] = jnp.zeros(sums.shape, jnp.float32)
         done_ref[...] = jnp.zeros(done_ref.shape, jnp.float32)
         table_tail[...] = jnp.zeros(table_tail.shape, jnp.float32)
@@ -411,6 +427,8 @@
             sums[pl.ds(first, 1), :] = jnp.right_shift(codes, 4).astype(jnp.float32)
             sums[pl.ds(first + 1, 1), :] = (codes & 15).astype(jnp.float32)
 
+    for copy in copies(step):
+        copy.wait()
     band_row = lax.broadcasted_iota(jnp.int32, (bands, LANES), 0)
     first_half = lax.broadcasted_iota(jnp.int32, (bands, LANES), 1) < HALF
     nothing = jnp.zeros((bands, LANES), jnp.float32)
@@ -430,7 +448,7 @@
         left = jnp.concatenate([left, table_tail[p].astype(jnp.bfloat16)], axis=1)
         halves = ([], [])
         for part in range(2):
-            piece = spectra_ref[part, slot]
+            piece = spectra_here[part, slot]
             whole = piece[:, :full].astype(jnp.float32)
             lane = lax.broadcasted_iota(jnp.int32, whole.shape, 1)
             zero = jnp.zeros_like(whole)
@@ -505,16 +523,17 @@
     group = next(n for n in (4, 5, 2, 1) if pairs % n == 0)
     numbers = jnp.concatenate([lax.axis_index("lev").astype(jnp.int32)[None], pairing])
     codes = pl.pallas_call(
-        touch_kernel,
+        codes_kernel,
         out_shape=jax.ShapeDtypeStruct((1, LANES), jnp.int32),
-        in_specs=[pl.BlockSpec(memory_space=pltpu.VMEM)] * 3,
+        in_specs=[pl.BlockSpec(memory_space=pltpu.VMEM)],
         out_specs=pl.BlockSpec(memory_space=pltpu.VMEM),
-        compiler_params=pltpu.CompilerParams(vmem_limit_bytes=4 * 1024 * 1024),
+        compiler_params=pltpu.CompilerParams(vmem_limit_bytes=60 * 1024 * 1024),
         cost_estimate=pl.CostEstimate(flops=0, bytes_accessed=4_000_000, transcendentals=0),
-    )(jnp.pad(pairing, (0, LANES - pairs))[None, :], spectra, tables[0])
+    )(jnp.pad(pairing, (0, LANES - pairs))[None, :])
     shape = jax.ShapeDtypeStruct((bands, block, LANES), jnp.bfloat16)
     whole = pl.BlockSpec((bands, block, LANES), lambda i: (0, 0, 0))
     in_vmem = pl.BlockSpec(memory_space=pltpu.VMEM)
+    in_hbm = pl.BlockSpec(memory_space=pl.ANY)
     return pl.pallas_call(
         legendre_kernel,
         grid=(pairs // group,),
@@ -522,17 +541,19 @@
         in_specs=[
             pl.BlockSpec(memory_space=pltpu.SMEM),
             pl.BlockSpec((1, LANES), lambda i: (0, 0)),
-            in_vmem,
+            in_hbm,
         ]
-        + [in_vmem] * len(tables),
+        + [in_hbm] * len(tables),
         out_specs=(whole, in_vmem),
         scratch_shapes=[
             pltpu.VMEM((bands * block, LANES), jnp.float32),
             pltpu.VMEM((group, ROWS * bands, LANES), jnp.float32),
             pltpu.VMEM((group, 2 * level_fields, LANES), jnp.float32),
             pltpu.VMEM((4 * level_fields, LANES), jnp.bfloat16),
-        ],
-        compiler_params=pltpu.CompilerParams(vmem_limit_bytes=16 * 1024 * 1024),
+        ]
+        + [pltpu.VMEM(x.shape, x.dtype) for x in (spectra,) + tables]
+        + [pltpu.SemaphoreType.DMA((1 + len(tables), pairs // group))],
+        compiler_params=pltpu.CompilerParams(vmem_limit_bytes=60 * 1024 * 1024),
         cost_estimate=pl.CostEstimate(
             flops=2 * ROWS * bands * 4 * level_fields * pairs * degrees,
             bytes_accessed=8_000_000,
@@ -549,13 +570,13 @@
     even = np.concatenate([low, order_total - 1 - high])
     odd = np.concatenate([order_total - 1 - low, high])
     lon = np.arange(lon_total // 2)
-    table = np.zeros((2, 2, padded, lon_total // 2), np.float32)
+    table = np.zeros((4, 2, padded, lon_total // 2), np.float32)
     for parity, orders in enumerate((even, odd)):
         phase = (orders[:, None] * lon[None, :]) % lon_total * (2.0 * math.pi / lon_total)
         weight = np.where(orders == 0, 1.0, 2.0)[:, None]
         table[parity, 0, :pair_total] = weight * np.cos(phase)
         table[parity, 1, :pair_total] = -weight * np.sin(phase)
-    return table.reshape(2, 2 * padded, lon_total // 2).astype(jnp.bfloat16)
+    return table.reshape(4, 2 * padded, lon_total // 2).astype(jnp.bfloat16)
 
 
 def owner_tables(bands, pairs):
@@ -591,8 +612,13 @@
     return place.astype(jnp.bfloat16)
 
 
-def order_kernel(pairs, levels, after_ref, sums_ref, owner_ref, lane_ref, *others):
-    out_refs, (codes, flat, gathered, lhs) = others[:2], others[2:]
+def fourier_kernel(
+    pairs, levels, base_ref, after_ref, sums_ref, owner_ref, lane_ref, table_source, *others
+):
+    field_refs, send_ref, others = others[:2], others[2], others[3:]
+    codes, flat, gathered, lhs, table_ref, arrival_sem = others
+    copy = pltpu.make_async_copy(table_source.at[:2], table_ref, arrival_sem)
+    copy.start()
     bands, block, width = sums_ref.shape
     pair_total = bands * pairs
     padded = gathered.shape[0]
@@ -604,7 +630,7 @@
     place = pair_places(flat, owner_ref, lane_ref, codes, bands, block, code_row, padded)
     low = lax.broadcasted_iota(jnp.int32, (fields, padded), 1) < pair_total // 2
     middle = fields * ROWS
-    for number, out_ref in enumerate(out_refs):
+    for number in range(2):
         for i in range(PAIRED):
             for band in range(bands):
                 first = band * block + number * (block // 2) + i
@@ -629,89 +655,77 @@
                     for parity in range(2):
                         for t in range(blocks):
                             lhs[
-                                parity, part * blocks + t, pl.ds(first, fields, stride=stride), :
+                                number,
+                                parity,
+                                part * blocks + t,
+                                pl.ds(first, fields, stride=stride),
+                                :,
                             ] = both[parity][:, t * LANES : (t + 1) * LANES]
+    copy.wait()
+    half = table_ref.shape[2]
+
+    def transform(number, first, count):
+        found = []
         for parity in range(2):
-            for t in range(2 * blocks):
-                out_ref[parity, :, t * LANES : (t + 1) * LANES] = lhs[parity, t].astype(
-                    jnp.bfloat16
-                )
-
-
-def order_call(after, sums, pairs, levels):
+            left = jnp.concatenate(
+                [
+                    lhs[number, parity, t, first : first + count, :].astype(jnp.bfloat16)
+                    for t in range(2 * blocks)
+                ],
+                axis=1,
+            )
+            found.append(jnp.dot(left, table_ref[parity], preferred_element_type=jnp.float32))
+        pieces = (found[0] + found[1], found[0] - found[1])
+        return [piece.astype(jnp.bfloat16).astype(jnp.float32) for piece in pieces]
+
+    group = next(n for n in (4, 2, 1) if levels % n == 0)
+    for number, field_ref in enumerate(field_refs):
+        for level in range(0, levels, group):
+            pieces = transform(number, level * 2 * ROWS, group * 2 * ROWS)
+            for part, value in enumerate(pieces):
+                value = value.reshape(group, 2 * ROWS, half)
+                lanes = slice(part * half, (part + 1) * half)
+                field_ref[level : level + group, : 2 * ROWS, lanes] = value
+        for part, value in enumerate(transform(number, middle, fields * 2 * HALO)):
+            value = value.reshape(levels, 4 * HALO, half)
+            field_ref[:, 2 * ROWS :, part * half : (part + 1) * half] = value
+        if send_ref.shape[0] == 1:
+            start = jnp.where(base_ref[0] == 0, levels - HALO, 0)
+            send_ref[0, number] = field_ref[pl.ds(start, HALO)].astype(jnp.bfloat16)
+        else:
+            send_ref[0, number] = field_ref[:HALO].astype(jnp.bfloat16)
+            send_ref[1, number] = field_ref[levels - HALO :].astype(jnp.bfloat16)
+
+
+def fourier_call(base, after, sums, table, pairs, levels, lon_total):
     bands, block, width = sums.shape
     padded = up_to(bands * pairs, LANES)
     extra = [jnp.asarray(x) for x in owner_tables(bands, pairs)]
-    shape = jax.ShapeDtypeStruct((2, 2 * levels * TALL, 2 * padded), jnp.bfloat16)
+    sends = 1 if lax.axis_size("lev") == 2 else 2
+    field_shape = (levels, 3 * ROWS, lon_total)
+    field = jax.ShapeDtypeStruct(field_shape, jnp.float32)
+    send = jax.ShapeDtypeStruct((sends, 2, HALO) + field_shape[1:], jnp.bfloat16)
     in_vmem = pl.BlockSpec(memory_space=pltpu.VMEM)
     return pl.pallas_call(
-        functools.partial(order_kernel, pairs, levels),
-        out_shape=(shape, shape),
-        in_specs=[in_vmem] * 4,
-        out_specs=(in_vmem, in_vmem),
+        functools.partial(fourier_kernel, pairs, levels),
+        out_shape=(field, field, send),
+        in_specs=[pl.BlockSpec(memory_space=pltpu.SMEM)]
+        + [in_vmem] * 4
+        + [pl.BlockSpec(memory_space=pl.ANY)],
+        out_specs=(in_vmem,) * 3,
         scratch_shapes=[
             pltpu.VMEM((2, LANES, LANES), jnp.float32),
             pltpu.VMEM((bands * block, width), jnp.float32),
             pltpu.VMEM((padded, width), jnp.float32),
-            pltpu.VMEM((2, 2 * padded // LANES, 2 * levels * TALL, LANES), jnp.float32),
+            pltpu.VMEM((2, 2, 2 * padded // LANES, 2 * levels * TALL, LANES), jnp.float32),
+            pltpu.VMEM((2,) + table.shape[1:], table.dtype),
+            pltpu.SemaphoreType.DMA,
         ],
-        compiler_params=pltpu.CompilerParams(vmem_limit_bytes=16 * 1024 * 1024),
+        compiler_params=pltpu.CompilerParams(vmem_limit_bytes=44 * 1024 * 1024),
         cost_estimate=pl.CostEstimate(
-            flops=4_000_000_000, bytes_accessed=8_000_000, transcendentals=0
+            flops=8_000_000_000, bytes_accessed=8_000_000, transcendentals=0
         ),
-    )(after, sums, *extra)
-
-
-def transform_kernel(levels, base_ref, lhs_ref, table_ref, field_ref, send_ref):
-    half = table_ref.shape[2]
-    middle = 2 * levels * ROWS
-
-    def transform(first, count):
-        found = [
-            jnp.dot(
-                lhs_ref[parity, first : first + count, :],
-                table_ref[parity],
-                preferred_element_type=jnp.float32,
-            )
-            for parity in range(2)
-        ]
-        pieces = (found[0] + found[1], found[0] - found[1])
-        return [piece.astype(jnp.bfloat16).astype(jnp.float32) for piece in pieces]
-
-    group = next(n for n in (4, 2, 1) if levels % n == 0)
-    for level in range(0, levels, group):
-        pieces = transform(level * 2 * ROWS, group * 2 * ROWS)
-        for part, value in enumerate(pieces):
-            value = value.reshape(group, 2 * ROWS, half)
-            field_ref[level : level + group, : 2 * ROWS, part * half : (part + 1) * half] = value
-    for part, value in enumerate(transform(middle, 2 * levels * 2 * HALO)):
-        value = value.reshape(levels, 4 * HALO, half)
-        field_ref[:, 2 * ROWS :, part * half : (part + 1) * half] = value
-    if send_ref.shape[0] == 1:
-        start = jnp.where(base_ref[0] == 0, levels - HALO, 0)
-        send_ref[0] = field_ref[pl.ds(start, HALO)].astype(jnp.bfloat16)
-    else:
-        send_ref[0] = field_ref[:HALO].astype(jnp.bfloat16)
-        send_ref[1] = field_ref[levels - HALO :].astype(jnp.bfloat16)
-
-
-def transform_call(base, lhs, table, levels, lon_total):
-    sends = 1 if lax.axis_size("lev") == 2 else 2
-    field_shape = (levels, 3 * ROWS, lon_total)
-    in_vmem = pl.BlockSpec(memory_space=pltpu.VMEM)
-    return pl.pallas_call(
-        functools.partial(transform_kernel, levels),
-        out_shape=(
-            jax.ShapeDtypeStruct(field_shape, jnp.float32),
-            jax.ShapeDtypeStruct((sends, HALO) + field_shape[1:], jnp.bfloat16),
-        ),
-        in_specs=[pl.BlockSpec(memory_space=pltpu.SMEM), in_vmem, in_vmem],
-        out_specs=(in_vmem, in_vmem),
-        compiler_params=pltpu.CompilerParams(vmem_limit_bytes=16 * 1024 * 1024),
-        cost_estimate=pl.CostEstimate(
-            flops=3_000_000_000, bytes_accessed=8_000_000, transcendentals=0
-        ),
-    )(base, lhs, table)
+    )(base, after, sums, *extra, table)
 
 
 def exchange(sums):
@@ -734,14 +748,13 @@
     points, done = prepare_call(base, done, eta_shift, cells)
     pair_total = pairs * lax.axis_size("band")
     twiddles = jnp.asarray(fourier_table(pair_total, up_to(pair_total, LANES), lon_total))
-    ordered = order_call(done, sums, pairs, levels)
-    winds, wind_send = transform_call(base, ordered[0], twiddles, levels, lon_total)
-    tracers, tracer_send = transform_call(base, ordered[1], twiddles, levels, lon_total)
+    winds, tracers, send = fourier_call(base, done, sums, twiddles, pairs, levels, lon_total)
+    nears = swap_levels(send)
     displacement, moved, _ = interpolation_call(
-        wind_levels, base, winds, points, swap_levels(wind_send), (), jnp.float32, 2
+        wind_levels, base, 0, winds, points, nears, (), jnp.float32, 2
     )
     advected, _ = interpolation_call(
-        tracer_levels, base, tracers, points, swap_levels(tracer_send), (moved,), jnp.bfloat16, 1
+        tracer_levels, base, 1, tracers, points, nears, (moved,), jnp.bfloat16, 1
     )
     return advected, displacement
 

time: 106 us -> 106 us (level)
  local copies, waits for them, and re-layouts: 16.9 us -> 6.39 us
  Pallas kernels: 57.7 us -> 66.3 us
  other arithmetic: 0.15 us -> 1.28 us
    unnamed x34 -> x18, local copies, waits for them, and re-layouts: 16.2 us -> 5.22 us
    pallas_call x2, Pallas kernels: 42.5 us -> 46.8 us  [interpolation_call(): pl.pallas_call(functools.partial(interpolation_kernel, levels_body, toget...]
    pallas_call x1, Pallas kernels: 6.86 us -> 9.26 us  [legendre_call(): pl.pallas_call(legendre_kernel, grid=(pairs // group,), out_shape=(shape,...]
    pallas_call x4 -> x2, Pallas kernels: 6.89 us -> 8.96 us  [the longest x1 7.77 us: fourier_call(): pl.pallas_call(functools.partial(fourier_kernel, pairs, levels), out_shap...]
    ppermute x2 -> x1, waiting for transfers between devices: 0.01 us -> 1.56 us  [swap_levels(): return (lax.ppermute(send[0], 'lev', [(0, 1), (1, 0)]),)]
    concatenate x1, other arithmetic: 0.08 us -> 1.21 us  [legendre_call(): jnp.concatenate([lax.axis_index('lev').astype(jnp.int32)[None], pairing])]
    all_to_all x1, waiting for transfers between devices: 20 us -> 18.9 us  [exchange(): return lax.all_to_all(sums, 'band', split_axis=0, concat_axis=0, tiled=True)]
    ppermute x2 -> x1, starting transfers between devices: 2.28 us -> 2.47 us  [swap_levels(): return (lax.ppermute(send[0], 'lev', [(0, 1), (1, 0)]),)]
  transfers between devices with their start and end apart: 4 -> 3, of which waited for: 1 -> 3; matrix products, arithmetic and copies ran while one was open for 1% -> 2% of each run, Pallas kernels for 25% -> 2%
where the time goes in v10:
time: 106 us; the launch traced here: 105 us
  Pallas kernels  66.3 us (63%)
  waiting for transfers between devices  20.7 us (20%)
  starting transfers between devices  10 us (9%)
  local copies, waits for them, and re-layouts  6.39 us (6%)
  other arithmetic  1.28 us (1%)
    pallas_call x2, Pallas kernels, interpolation_call(): pl.pallas_call(functools.partial(interpolation_kernel, levels_body, toget...  46.8 us
    all_to_all x1, waiting for transfers between devices, exchange(): return lax.all_to_all(sums, 'band', split_axis=0, concat_axis=0, tiled=True)  18.9 us
    pallas_call x1, Pallas kernels, legendre_call(): pl.pallas_call(legendre_kernel, grid=(pairs // group,), out_shape=(shape,...  9.26 us
    pallas_call x1, Pallas kernels, fourier_call(): pl.pallas_call(functools.partial(fourier_kernel, pairs, levels), out_shap...  7.77 us
    all_to_all x1, starting transfers between devices, exchange(): return lax.all_to_all(sums, 'band', split_axis=0, concat_axis=0, tiled=True)  6.81 us
    unnamed x18, local copies, waits for them, and re-layouts  5.22 us
    ppermute x1, starting transfers between devices, swap_levels(): return (lax.ppermute(send[0], 'lev', [(0, 1), (1, 0)]),)  2.47 us
  transfers between devices with their start and end apart: 3, of which 3 were waited for; matrix products, arithmetic and copies ran while one was open for 2% of the time, Pallas kernels for 2%

profile of v10, /device:TPU:9, one launch (start us, length us, event | category | flops | bytes accessed | tf_op | source)
XLA Modules:
  0.0 105.4 jit_solution(7119589542738553620)
XLA Ops:
  0.6 0.7 collective-permute-start
  1.4 1.2 %pad_bitcast_fusion.numbers_ref = s32[1,128]{1,0:T(1,128)} fusion(s32[20]{0:T(128)} %param.10), kind=kLoop, calls=%fused_computation.2 | loop fusion | bytes 592 | tf_op jit(solution)/shard_map/broadcast_in_dim | solution.py:532
  2.5 1.2 %shard_map.95.codes_ref = s32[1,128]{1,0:T(1,128)} custom-call(s32[1,128]{1,0:T(1,128)} %pad_bitcast_fusion.numbers_ref), custom_call_target="tpu_custom_call" | custom-call | bytes 4000000 | tf_op jit(solution)/shard_map/pallas_call | solution.py:525
  3.7 1.2 %pad_add_fusion.1.numbers_ref = s32[21]{0:T(128)} fusion(s32[20]{0:T(128)} %param.10, s32[1]{0:T(128)} %bitcast.2), kind=kLoop, calls=%fused_computation.1 | loop fusion | flops 21 | bytes 168 | tf_op jit(solution)/shard_map/concatenate | solution.py:524
  4.9 0.2 collective-permute-done.others_1_
  5.2 0.0 copy-start.6
  5.2 1.3 %copy-done.6 = bf16[4,20,16,641]{3,2,1,0:T(8,128)(2,1)} copy-done((bf16[4,20,16,641]{3,2,1,0:T(8,128)(2,1)}, bf16[4,20,16,641]{3,2,1,0:T(8,128)(2,1)S(1)}, u32[]{:S(2)}) %copy-start.6) | copy-done | bytes 1640984
  6.5 0.0 copy-start.1
  6.5 9.3 %shard_map.96 = (bf16[16,256,128]{2,1,0:T(8,128)(2,1)}, f32[8,128]{1,0:T(8,128)}) custom-call(s32[21]{0:T(128)} %pad_add_fusion.1.numbers_ref, s32[1,128]{1,0:T(1,128)} %shard_map.95.codes_ref, bf16[2,20,32,641]{3,2,1,0:T(8,128)(2,1)} %bitcast.11, bf16[4,20,16,641]{3,2,1,0:T(8,128)(2,1)} %bitcast.13, bf16[4,20,16,641]{3,2,1,0:T(8,128)(2,1)} %copy-done.6), custom_call_target="tpu_custom_call" | custom-call | flops 420085760 | bytes 8000000 | tf_op jit(solution)/shard_map/pallas_call | solution.py:537
  15.7 0.0 copy-start.4
  15.7 0.0 copy-start.5
  15.8 6.8 %all-to-all-start = ((bf16[16,256,128]{2,1,0:T(8,128)(2,1)}), bf16[16,256,128]{2,1,0:T(8,128)(2,1)S(1)}, u32[]{:S(2)}, u32[]{:S(2)}) async-start(bf16[16,256,128]{2,1,0:T(8,128)(2,1)} %get-tuple-element.14), calls=%async_computation | async-start | bytes 2097152 | tf_op jit(solution)/shard_map/all_to_all | solution.py:732
  22.6 0.1 pad_add_fusion.base_ref
  22.6 0.0 copy-done.1
  22.6 0.0 copy-start.2
  22.6 1.0 copy-done.2
  23.6 0.0 copy-start.3
  23.6 0.7 copy-done.3
  24.3 1.4 %shard_map.97 = (f32[7,8,8,2816]{3,2,1,0:T(8,128)S(1)}, f32[8,128]{1,0:T(8,128)S(1)}) custom-call(s32[2]{0:T(128)S(1)} %pad_add_fusion.base_ref, f32[8,128]{1,0:T(8,128)S(1)} %copy-done.3, bf16[8,8,2816]{2,1,0:T(8,128)(2,1)S(1)} %copy-done.2, s32[3,8,8,2816]{3,2,1,0:T(8,128)S(1)} %copy-done.1), custom_call_target="tpu_custom_call" | custom-call | flops 7208960 | bytes 20000000 | tf_op jit(solution)/shard_map/pallas_call | solution.py:205
  25.7 0.0 copy-start
  25.7 2.2 %copy-done = f32[7,8,8,2816]{3,2,1,0:T(8,128)} copy-done((f32[7,8,8,2816]{3,2,1,0:T(8,128)}, f32[7,8,8,2816]{3,2,1,0:T(8,128)S(1)}, u32[]{:S(2)}) %copy-start) | copy-done | bytes 5046296
  27.9 18.9 %all-to-all-done.sums_ref = bf16[16,256,128]{2,1,0:T(8,128)(2,1)S(1)} async-done(((bf16[16,256,128]{2,1,0:T(8,128)(2,1)}), bf16[16,256,128]{2,1,0:T(8,128)(2,1)S(1)}, u32[]{:S(2)}, u32[]{:S(2)}) %all-to-all-start) | async-done | bytes 1048608 | tf_op jit(solution)/shard_map/all_to_all | solution.py:732
  46.8 0.0 slice-start
  46.8 0.0 copy-done.4
  46.9 0.0 copy-done.5
  46.9 0.0 slice-start.1
  46.9 7.8 %shard_map.98 = (f32[8,24,2816]{2,1,0:T(8,128)S(1)}, f32[8,24,2816]{2,1,0:T(8,128)S(1)}, bf16[1,2,2,24,2816]{4,3,2,1,0:T(8,128)(2,1)S(1)}) custom-call(s32[2]{0:T(128)S(1)} %pad_add_fusion.base_ref, f32[8,128]{1,0:T(8,128)S(1)} %get-tuple-element.13.after_ref, bf16[16,256,128]{2,1,0:T(8,128)(2,1)S(1)} %all-to-all-done.sums_ref, ...), custom_call_target="tpu_custom_call" | custom-call | flops 8000000000 | bytes 8000000 | tf_op jit(solution)/shard_map/pallas_call | solution.py:709
  54.6 2.5 %collective-permute-start.1 = (bf16[2,2,24,2816]{3,2,1,0:T(8,128)(2,1)S(1)}, bf16[2,2,24,2816]{3,2,1,0:T(8,128)(2,1)S(1)}, u32[]{:S(2)}, u32[]{:S(2)}) collective-permute-start(bf16[2,2,24,2816]{3,2,1,0:T(8,128)(2,1)S(1)} %bitcast.10), channel_id=1, source_target_pairs={{0,1},{1,0},{2,3},{3,2},{4,5},{5,4},{6,7},{7,6},{8,9},{9,8},{10,11... | collective-permute-start | bytes 1622024 | tf_op jit(solution)/shard_map/ppermute | solution.py:374
  57.1 1.6 %collective-permute-done.1.others_0_ = bf16[2,2,24,2816]{3,2,1,0:T(8,128)(2,1)S(1)} collective-permute-done((bf16[2,2,24,2816]{3,2,1,0:T(8,128)(2,1)S(1)}, bf16[2,2,24,2816]{3,2,1,0:T(8,128)(2,1)S(1)}, u32[]{:S(2)}, u32[]{:S(2)}) %collective-permute-start.1) | collective-permute-done | bytes 540704 | tf_op jit(solution)/shard_map/ppermute | solution.py:374
  58.7 0.0 slice-done
  58.7 0.0 slice-done.1
  58.7 23.9 %shard_map.99 = (f32[2,8,8,2816]{3,2,1,0:T(8,128)}, f32[2,8,8,2816]{3,2,1,0:T(8,128)S(1)}, f32[8,128]{1,0:T(8,128)}) custom-call(s32[2]{0:T(128)S(1)} %pad_add_fusion.base_ref, f32[8,24,2816]{2,1,0:T(8,128)S(1)} %get-tuple-element.18.field_ref, f32[7,8,8,2816]{3,2,1,0:T(8,128)S(1)} %bitcast.9, bf16[2,2,24,2816]{3,2,1,0:T(8,128)(2,1)S(1)} %collective-permute-done.1.others_0_), custom_call_target="tpu_custom_call" | custom-call | flops 90112000 | bytes 7208960 | tf_op jit(solution)/shard_map/pallas_call | solution.py:351
  82.6 22.9 %shard_map.100 = (bf16[2,8,8,2816]{3,2,1,0:T(8,128)(2,1)}, f32[8,128]{1,0:T(8,128)}) custom-call(s32[2]{0:T(128)S(1)} %pad_add_fusion.base_ref, f32[8,24,2816]{2,1,0:T(8,128)S(1)} %get-tuple-element.15.field_ref, f32[7,8,8,2816]{3,2,1,0:T(8,128)S(1)} %bitcast.9, bf16[2,2,24,2816]{3,2,1,0:T(8,128)(2,1)S(1)} %collective-permute-done.1.others_0_, ...), custom_call_target="tpu_custom_call" | custom-call | flops 90112000 | bytes 7208960 | tf_op jit(solution)/shard_map/pallas_call | solution.py:351
  (1 shorter events, 0.0 us)
Async XLA Ops:
  0.6 4.6 %collective-permute-start = (bf16[4,20,16,641]{3,2,1,0:T(8,128)(2,1)}, bf16[4,20,16,641]{3,2,1,0:T(8,128)(2,1)S(1)}, u32[]{:S(2)}, u32[]{:S(2)}) collective-permute-start(bf16[4,20,16,641]{3,2,1,0:T(8,128)(2,1)} %bitcast.12), channel_id=1, source_target_pairs={{0,1},{1,0},{2,3},{3,2},{4,5},{5,4},{6,7},{7,6},{8,9},{9,8},{10,11... | collective-permute-start | bytes 4922888 | tf_op jit(solution)/shard_map/ppermute | solution.py:741
  5.2 1.3 %copy-start.6 = (bf16[4,20,16,641]{3,2,1,0:T(8,128)(2,1)}, bf16[4,20,16,641]{3,2,1,0:T(8,128)(2,1)S(1)}, u32[]{:S(2)}) copy-start(bf16[4,20,16,641]{3,2,1,0:T(8,128)(2,1)S(1)} %collective-permute-done.others_1_) | copy-start | bytes 4922884
  6.5 16.2 %copy-start.1 = (s32[3,8,8,2816]{3,2,1,0:T(8,128)S(1)}, s32[3,8,8,2816]{3,2,1,0:T(8,128)}, u32[]{:S(2)}) copy-start(s32[3,8,8,2816]{3,2,1,0:T(8,128)} %cells_ref.1) | copy-start | bytes 6488068
  15.7 31.1 %copy-start.4 = (f32[320,128]{1,0:T(8,128)S(1)}, f32[320,128]{1,0:T(8,128)}, u32[]{:S(2)}) copy-start(f32[320,128]{1,0:T(8,128)} %constant.20.clone.lane_ref) | copy-start | bytes 491524
  15.7 31.1 %copy-start.5 = (bf16[320,128]{1,0:T(8,128)(2,1)S(1)}, bf16[320,128]{1,0:T(8,128)(2,1)}, u32[]{:S(2)}) copy-start(bf16[320,128]{1,0:T(8,128)(2,1)} %constant.19.clone.owner_ref) | copy-start | bytes 245764
  15.8 31.1 %all-to-all-start = ((bf16[16,256,128]{2,1,0:T(8,128)(2,1)}), bf16[16,256,128]{2,1,0:T(8,128)(2,1)S(1)}, u32[]{:S(2)}, u32[]{:S(2)}) async-start(bf16[16,256,128]{2,1,0:T(8,128)(2,1)} %get-tuple-element.14), calls=%async_computation | async-start | bytes 2097152 | tf_op jit(solution)/shard_map/all_to_all | solution.py:732
  22.6 1.0 copy-start.2
  23.6 0.7 copy-start.3
  25.7 2.2 %copy-start = (f32[7,8,8,2816]{3,2,1,0:T(8,128)}, f32[7,8,8,2816]{3,2,1,0:T(8,128)S(1)}, u32[]{:S(2)}) copy-start(f32[7,8,8,2816]{3,2,1,0:T(8,128)S(1)} %get-tuple-element.16.points_ref) | copy-start | bytes 15138820
  46.8 11.8 %slice-start = ((s8[5046272]{0:T(1024)(128)(4,1)}), s8[4194304]{0:T(1024)(128)(4,1)S(1)}, s32[]{:S(2)}) async-start(s8[5046272]{0:T(1024)(128)(4,1)} %bitcast.8), calls=%async_computation.1 | async-start | bytes 8388608
  46.9 11.8 %slice-start.1 = ((s8[5046272]{0:T(1024)(128)(4,1)}), s8[851968]{0:T(1024)(128)(4,1)S(1)}, s32[]{:S(2)}) async-start(s8[5046272]{0:T(1024)(128)(4,1)} %bitcast.8), calls=%async_computation.2 | async-start | bytes 1703936
  54.6 4.0 %collective-permute-start.1 = (bf16[2,2,24,2816]{3,2,1,0:T(8,128)(2,1)S(1)}, bf16[2,2,24,2816]{3,2,1,0:T(8,128)(2,1)S(1)}, u32[]{:S(2)}, u32[]{:S(2)}) collective-permute-start(bf16[2,2,24,2816]{3,2,1,0:T(8,128)(2,1)S(1)} %bitcast.10), channel_id=1, source_target_pairs={{0,1},{1,0},{2,3},{3,2},{4,5},{5,4},{6,7},{7,6},{8,9},{9,8},{10,11... | collective-permute-start | bytes 1622024 | tf_op jit(solution)/shard_map/ppermute | solution.py:374

commit v11 on v10

--- a/solution.py
+++ b/solution.py
@@ -63,33 +63,34 @@
 FIELD_ROW = (ROWS, 3 * ROWS)
 
 
-def fill_units(slab, chunk, chunk_total, field_ref, scratch):
+def fill_units(slab, chunk, chunk_total, source, scratch):
+    field_ref, row = source
     before = jnp.where(chunk == 0, chunk_total - 1, chunk - 1)
     after = jnp.where(chunk == chunk_total - 1, 0, chunk + 1)
     starts = [pl.multiple_of(c * LANES, LANES) for c in (before, chunk, after)]
     lane = lax.broadcasted_iota(jnp.int32, (ROWS, LANES), 1)
-    first = pl.multiple_of(slab * (5 * STACK), ROWS)
+    first = slab * (5 * STACK)
 
     def edge_start():
         moved = shifted_lanes(
-            *[field_ref[slab, 2 * ROWS : 3 * ROWS, pl.ds(s, LANES)] for s in starts], lane
+            *[field_ref[row, 2 * ROWS : 3 * ROWS, pl.ds(s, LANES)] for s in starts], lane
         )
         return [(value, pltpu.roll(value, ROWS // 2, 0)) for value in moved]
 
     def edge_finish(values):
         for step, (between, outside) in enumerate(values):
             for offset, value in ((0, outside), (2 * ROWS, between), (4 * ROWS, outside)):
-                scratch[pl.ds(first + (step * STACK + offset), ROWS), :] = value
+                scratch[pl.ds(first + step * STACK + offset, ROWS), :] = value
 
     def center_unit(field):
         def start():
             rows = slice(field * ROWS, (field + 1) * ROWS)
-            blocks = [field_ref[slab, rows, pl.ds(s, LANES)] for s in starts]
+            blocks = [field_ref[row, rows, pl.ds(s, LANES)] for s in starts]
             return shifted_lanes(*blocks, lane)
 
         def finish(values):
             for step, moved in enumerate(values):
-                scratch[pl.ds(first + (step * STACK + FIELD_ROW[field]), ROWS), :] = moved
+                scratch[pl.ds(first + step * STACK + FIELD_ROW[field], ROWS), :] = moved
 
         return start, finish
 
@@ -247,7 +248,6 @@
         across(scratch, field, base, points, row_weights, lon_weights, filling, keep)
         for field in range(2)
     ]
-    filling.flush()
     for step in count:
         east, north = arrival_wind(0, step), arrival_wind(1, step)
         east_found, north_found = found[0][step], found[1][step]
@@ -275,7 +275,6 @@
         across(scratch, field, base, points, row_weights, lon_weights, filling)
         for field in range(2)
     ]
-    filling.flush()
     for field in range(2):
         for step, total in enumerate(found[field]):
             out_ref[field, k + step, :, lanes] = total.astype(out_ref.dtype)
@@ -285,50 +284,40 @@
     levels_body, together, number, near_count, out_count, base_ref, field_ref, points_ref, *others
 ):
     nears, others = others[:near_count], others[near_count:]
-    full, even_scratch, odd_scratch, keep = others[-4:]
+    around, even_scratch, odd_scratch, keep = others[-4:]
     extra, out_refs, done_ref = others[: -5 - out_count], others[-5 - out_count : -5], others[-5]
     done_ref[...] = jnp.zeros(done_ref.shape, done_ref.dtype)
     _, levels, rows, lon_total = points_ref.shape
     chunk_total = lon_total // LANES
-    slabs = levels + 2 * HALO
-    steps = levels // together
-    per_step = -(-slabs // steps)
-    full[HALO : HALO + levels] = field_ref[...]
     if near_count == 1:
-        found = jnp.where(base_ref[0] == 0, levels + HALO, 0)
-        full[pl.ds(found, HALO)] = nears[0][number].astype(jnp.float32)
-        empty = levels + HALO - found
-        full[pl.ds(empty, HALO)] = jnp.zeros((HALO,) + full.shape[1:], jnp.float32)
+        found = jnp.where(base_ref[0] == 0, HALO, 0)
+        around[pl.ds(found, HALO)] = nears[0][number].astype(jnp.float32)
+        around[pl.ds(HALO - found, HALO)] = jnp.zeros((HALO,) + around.shape[1:], jnp.float32)
     else:
-        full[:HALO] = nears[0][number].astype(jnp.float32)
-        full[HALO + levels :] = nears[1][number].astype(jnp.float32)
-
-    def first_fill(slab, carry):
-        for start, finish in fill_units(slab, 0, chunk_total, full, even_scratch):
-            finish(start())
-        return carry
-
-    lax.fori_loop(0, slabs, first_fill, 0)
+        around[:HALO] = nears[0][number].astype(jnp.float32)
+        around[HALO:] = nears[1][number].astype(jnp.float32)
+    sources = [(around, n) for n in range(HALO)]
+    sources += [(field_ref, n) for n in range(levels)]
+    sources += [(around, HALO + n) for n in range(HALO)]
+
+    def all_units(chunk, scratch):
+        units = []
+        for slab, source in enumerate(sources):
+            units += fill_units(slab, chunk, chunk_total, source, scratch)
+        return units
+
+    for start, finish in all_units(0, even_scratch):
+        finish(start())
 
     def one_chunk(chunk, scratch, other):
         lanes = pl.ds(pl.multiple_of(chunk * LANES, LANES), LANES)
         following = jnp.where(chunk == chunk_total - 1, 0, chunk + 1)
-
-        def level_step(step, carry):
-            k = step * together
-            units = []
-            for n in range(per_step):
-                slab = jnp.minimum(step * per_step + n, slabs - 1)
-                units += fill_units(slab, following, chunk_total, full, other)
-            filling = Interleave(units, 32)
+        filling = Interleave(all_units(following, other), 32 * (levels // together))
+        for k in range(0, levels, together):
             points = [arrival(points_ref, k + n, lanes) for n in range(together)]
-            base = pl.multiple_of(k * (5 * STACK), ROWS)
-            levels_body(
-                *extra, base, lanes, k, points, scratch, keep, filling, *out_refs
-            )
-            return carry
-
-        lax.fori_loop(0, steps, level_step, 0)
+            base = k * (5 * STACK)
+            levels_body(*extra, base, lanes, k, points, scratch, keep, filling, *out_refs)
+        filling.flush()
 
     def chunk_pair(pair, carry):
         one_chunk(2 * pair, even_scratch, odd_scratch)
@@ -343,7 +332,7 @@
 ):
     _, levels, rows, lon_total = points.shape
     count = levels * rows * lon_total
-    together = 2 if levels % 2 == 0 else 1
+    together = next(n for n in (4, 2, 1) if levels % n == 0)
     scratch = pltpu.VMEM(((levels + 2 * HALO) * 5 * STACK, LANES), jnp.float32)
     in_vmem = pl.BlockSpec(memory_space=pltpu.VMEM)
     out = jax.ShapeDtypeStruct((2, levels, rows, lon_total), out_dtype)
@@ -357,7 +346,7 @@
         + [in_vmem] * (2 + len(nears) + len(extra)),
         out_specs=(in_vmem,) * (out_count + 1),
         scratch_shapes=[
-            pltpu.VMEM((levels + 2 * HALO,) + fields.shape[1:], jnp.float32),
+            pltpu.VMEM((2 * HALO,) + fields.shape[1:], jnp.float32),
             scratch,
             scratch,
             pltpu.VMEM((2, together, 16, ROWS, LANES), jnp.float32),
@@ -412,9 +401,8 @@
 
     @pl.when(step == 0)
     def _():
-        for number in range(pairs // group):
-            for copy in copies(number):
-                copy.start()
+        for copy in copies(0):
+            copy.start()
         sums[...] = jnp.zeros(sums.shape, jnp.float32)
         done_ref[...] = jnp.zeros(done_ref.shape, jnp.float32)
         table_tail[...] = jnp.zeros(table_tail.shape, jnp.float32)
@@ -426,6 +414,11 @@
             first = band * block + code_row
             sums[pl.ds(first, 1), :] = jnp.right_shift(codes, 4).astype(jnp.float32)
             sums[pl.ds(first + 1, 1), :] = (codes & 15).astype(jnp.float32)
+
+    @pl.when(step + 1 < pairs // group)
+    def _():
+        for copy in copies(step + 1):
+            copy.start()
 
     for copy in copies(step):
         copy.wait()

time: 106 us -> 95.5 us (0.901)
  Pallas kernels: 66.3 us -> 56 us
    pallas_call x2, Pallas kernels: 46.8 us -> 36.4 us  [interpolation_call(): pl.pallas_call(functools.partial(interpolation_kernel, levels_body, toget...]
  transfers between devices with their start and end apart: 3 -> 3, of which waited for: 3 -> 3; matrix products, arithmetic and copies ran while one was open for 2% -> 3% of each run, Pallas kernels for 2% -> 3%
where the time goes in v11:
time: 95.5 us; the launch traced here: 95.1 us
  Pallas kernels  56 us (59%)
  waiting for transfers between devices  20.7 us (22%)
  starting transfers between devices  10 us (10%)
  local copies, waits for them, and re-layouts  6.39 us (7%)
  other arithmetic  1.28 us (1%)
    pallas_call x2, Pallas kernels, interpolation_call(): pl.pallas_call(functools.partial(interpolation_kernel, levels_body, toget...  36.4 us
    all_to_all x1, waiting for transfers between devices, exchange(): return lax.all_to_all(sums, 'band', split_axis=0, concat_axis=0, tiled=True)  18.9 us
    pallas_call x1, Pallas kernels, legendre_call(): pl.pallas_call(legendre_kernel, grid=(pairs // group,), out_shape=(shape,...  9.3 us
    pallas_call x1, Pallas kernels, fourier_call(): pl.pallas_call(functools.partial(fourier_kernel, pairs, levels), out_shap...  7.76 us
    all_to_all x1, starting transfers between devices, exchange(): return lax.all_to_all(sums, 'band', split_axis=0, concat_axis=0, tiled=True)  6.81 us
    unnamed x18, local copies, waits for them, and re-layouts  5.22 us
    ppermute x1, starting transfers between devices, swap_levels(): return (lax.ppermute(send[0], 'lev', [(0, 1), (1, 0)]),)  2.49 us
  transfers between devices with their start and end apart: 3, of which 3 were waited for; matrix products, arithmetic and copies ran while one was open for 3% of the time, Pallas kernels for 3%

profile of v11, /device:TPU:9, one launch (start us, length us, event | category | flops | bytes accessed | tf_op | source)
XLA Modules:
  0.0 95.1 jit_solution(1762370568634680238)
XLA Ops:
  0.6 0.7 collective-permute-start
  1.4 1.2 %pad_bitcast_fusion.numbers_ref = s32[1,128]{1,0:T(1,128)} fusion(s32[20]{0:T(128)} %param.10), kind=kLoop, calls=%fused_computation.2 | loop fusion | bytes 592 | tf_op jit(solution)/shard_map/broadcast_in_dim | solution.py:525
  2.5 1.2 %shard_map.95.codes_ref = s32[1,128]{1,0:T(1,128)} custom-call(s32[1,128]{1,0:T(1,128)} %pad_bitcast_fusion.numbers_ref), custom_call_target="tpu_custom_call" | custom-call | bytes 4000000 | tf_op jit(solution)/shard_map/pallas_call | solution.py:518
  3.7 1.2 %pad_add_fusion.1.numbers_ref = s32[21]{0:T(128)} fusion(s32[20]{0:T(128)} %param.10, s32[1]{0:T(128)} %bitcast.2), kind=kLoop, calls=%fused_computation.1 | loop fusion | flops 21 | bytes 168 | tf_op jit(solution)/shard_map/concatenate | solution.py:517
  4.9 0.2 collective-permute-done.others_1_
  5.2 0.0 copy-start.6
  5.2 1.3 %copy-done.6 = bf16[4,20,16,641]{3,2,1,0:T(8,128)(2,1)} copy-done((bf16[4,20,16,641]{3,2,1,0:T(8,128)(2,1)}, bf16[4,20,16,641]{3,2,1,0:T(8,128)(2,1)S(1)}, u32[]{:S(2)}) %copy-start.6) | copy-done | bytes 1640984
  6.5 0.0 copy-start.1
  6.5 9.3 %shard_map.96 = (bf16[16,256,128]{2,1,0:T(8,128)(2,1)}, f32[8,128]{1,0:T(8,128)}) custom-call(s32[21]{0:T(128)} %pad_add_fusion.1.numbers_ref, s32[1,128]{1,0:T(1,128)} %shard_map.95.codes_ref, bf16[2,20,32,641]{3,2,1,0:T(8,128)(2,1)} %bitcast.11, bf16[4,20,16,641]{3,2,1,0:T(8,128)(2,1)} %bitcast.13, bf16[4,20,16,641]{3,2,1,0:T(8,128)(2,1)} %copy-done.6), custom_call_target="tpu_custom_call" | custom-call | flops 420085760 | bytes 8000000 | tf_op jit(solution)/shard_map/pallas_call | solution.py:530
  15.8 0.0 copy-start.4
  15.8 0.0 copy-start.5
  15.8 6.8 %all-to-all-start = ((bf16[16,256,128]{2,1,0:T(8,128)(2,1)}), bf16[16,256,128]{2,1,0:T(8,128)(2,1)S(1)}, u32[]{:S(2)}, u32[]{:S(2)}) async-start(bf16[16,256,128]{2,1,0:T(8,128)(2,1)} %get-tuple-element.14), calls=%async_computation | async-start | bytes 2097152 | tf_op jit(solution)/shard_map/all_to_all | solution.py:725
  22.6 0.1 pad_add_fusion.base_ref
  22.7 0.0 copy-done.1
  22.7 0.0 copy-start.2
  22.7 1.0 %copy-done.2 = bf16[8,8,2816]{2,1,0:T(8,128)(2,1)S(1)} copy-done((bf16[8,8,2816]{2,1,0:T(8,128)(2,1)S(1)}, bf16[8,8,2816]{2,1,0:T(8,128)(2,1)}, u32[]{:S(2)}) %copy-start.2) | copy-done | bytes 360472
  23.7 0.0 copy-start.3
  23.7 0.7 copy-done.3
  24.4 1.4 %shard_map.97 = (f32[7,8,8,2816]{3,2,1,0:T(8,128)S(1)}, f32[8,128]{1,0:T(8,128)S(1)}) custom-call(s32[2]{0:T(128)S(1)} %pad_add_fusion.base_ref, f32[8,128]{1,0:T(8,128)S(1)} %copy-done.3, bf16[8,8,2816]{2,1,0:T(8,128)(2,1)S(1)} %copy-done.2, s32[3,8,8,2816]{3,2,1,0:T(8,128)S(1)} %copy-done.1), custom_call_target="tpu_custom_call" | custom-call | flops 7208960 | bytes 20000000 | tf_op jit(solution)/shard_map/pallas_call | solution.py:206
  25.7 0.0 copy-start
  25.7 2.2 %copy-done = f32[7,8,8,2816]{3,2,1,0:T(8,128)} copy-done((f32[7,8,8,2816]{3,2,1,0:T(8,128)}, f32[7,8,8,2816]{3,2,1,0:T(8,128)S(1)}, u32[]{:S(2)}) %copy-start) | copy-done | bytes 5046296
  28.0 18.9 %all-to-all-done.sums_ref = bf16[16,256,128]{2,1,0:T(8,128)(2,1)S(1)} async-done(((bf16[16,256,128]{2,1,0:T(8,128)(2,1)}), bf16[16,256,128]{2,1,0:T(8,128)(2,1)S(1)}, u32[]{:S(2)}, u32[]{:S(2)}) %all-to-all-start) | async-done | bytes 1048608 | tf_op jit(solution)/shard_map/all_to_all | solution.py:725
  46.9 0.0 slice-start
  46.9 0.0 copy-done.4
  46.9 0.0 copy-done.5
  46.9 0.0 slice-start.1
  46.9 7.8 %shard_map.98 = (f32[8,24,2816]{2,1,0:T(8,128)S(1)}, f32[8,24,2816]{2,1,0:T(8,128)S(1)}, bf16[1,2,2,24,2816]{4,3,2,1,0:T(8,128)(2,1)S(1)}) custom-call(s32[2]{0:T(128)S(1)} %pad_add_fusion.base_ref, f32[8,128]{1,0:T(8,128)S(1)} %get-tuple-element.13.after_ref, bf16[16,256,128]{2,1,0:T(8,128)(2,1)S(1)} %all-to-all-done.sums_ref, ...), custom_call_target="tpu_custom_call" | custom-call | flops 8000000000 | bytes 8000000 | tf_op jit(solution)/shard_map/pallas_call | solution.py:702
  54.7 2.5 %collective-permute-start.1 = (bf16[2,2,24,2816]{3,2,1,0:T(8,128)(2,1)S(1)}, bf16[2,2,24,2816]{3,2,1,0:T(8,128)(2,1)S(1)}, u32[]{:S(2)}, u32[]{:S(2)}) collective-permute-start(bf16[2,2,24,2816]{3,2,1,0:T(8,128)(2,1)S(1)} %bitcast.10), channel_id=1, source_target_pairs={{0,1},{1,0},{2,3},{3,2},{4,5},{5,4},{6,7},{7,6},{8,9},{9,8},{10,11... | collective-permute-start | bytes 1622024 | tf_op jit(solution)/shard_map/ppermute | solution.py:363
  57.2 1.6 %collective-permute-done.1.others_0_ = bf16[2,2,24,2816]{3,2,1,0:T(8,128)(2,1)S(1)} collective-permute-done((bf16[2,2,24,2816]{3,2,1,0:T(8,128)(2,1)S(1)}, bf16[2,2,24,2816]{3,2,1,0:T(8,128)(2,1)S(1)}, u32[]{:S(2)}, u32[]{:S(2)}) %collective-permute-start.1) | collective-permute-done | bytes 540704 | tf_op jit(solution)/shard_map/ppermute | solution.py:363
  58.7 0.0 slice-done
  58.7 0.0 slice-done.1
  58.7 19.8 %shard_map.99 = (f32[2,8,8,2816]{3,2,1,0:T(8,128)}, f32[2,8,8,2816]{3,2,1,0:T(8,128)S(1)}, f32[8,128]{1,0:T(8,128)}) custom-call(s32[2]{0:T(128)S(1)} %pad_add_fusion.base_ref, f32[8,24,2816]{2,1,0:T(8,128)S(1)} %get-tuple-element.18.field_ref, f32[7,8,8,2816]{3,2,1,0:T(8,128)S(1)} %bitcast.9, bf16[2,2,24,2816]{3,2,1,0:T(8,128)(2,1)S(1)} %collective-permute-done.1.others_0_), custom_call_target="tpu_custom_call" | custom-call | flops 90112000 | bytes 7208960 | tf_op jit(solution)/shard_map/pallas_call | solution.py:340
  78.6 16.5 %shard_map.100 = (bf16[2,8,8,2816]{3,2,1,0:T(8,128)(2,1)}, f32[8,128]{1,0:T(8,128)}) custom-call(s32[2]{0:T(128)S(1)} %pad_add_fusion.base_ref, f32[8,24,2816]{2,1,0:T(8,128)S(1)} %get-tuple-element.15.field_ref, f32[7,8,8,2816]{3,2,1,0:T(8,128)S(1)} %bitcast.9, bf16[2,2,24,2816]{3,2,1,0:T(8,128)(2,1)S(1)} %collective-permute-done.1.others_0_, ...), custom_call_target="tpu_custom_call" | custom-call | flops 90112000 | bytes 7208960 | tf_op jit(solution)/shard_map/pallas_call | solution.py:340
  (1 shorter events, 0.0 us)
Async XLA Ops:
  0.6 4.6 %collective-permute-start = (bf16[4,20,16,641]{3,2,1,0:T(8,128)(2,1)}, bf16[4,20,16,641]{3,2,1,0:T(8,128)(2,1)S(1)}, u32[]{:S(2)}, u32[]{:S(2)}) collective-permute-start(bf16[4,20,16,641]{3,2,1,0:T(8,128)(2,1)} %bitcast.12), channel_id=1, source_target_pairs={{0,1},{1,0},{2,3},{3,2},{4,5},{5,4},{6,7},{7,6},{8,9},{9,8},{10,11... | collective-permute-start | bytes 4922888 | tf_op jit(solution)/shard_map/ppermute | solution.py:734
  5.2 1.3 %copy-start.6 = (bf16[4,20,16,641]{3,2,1,0:T(8,128)(2,1)}, bf16[4,20,16,641]{3,2,1,0:T(8,128)(2,1)S(1)}, u32[]{:S(2)}) copy-start(bf16[4,20,16,641]{3,2,1,0:T(8,128)(2,1)S(1)} %collective-permute-done.others_1_) | copy-start | bytes 4922884
  6.5 16.2 %copy-start.1 = (s32[3,8,8,2816]{3,2,1,0:T(8,128)S(1)}, s32[3,8,8,2816]{3,2,1,0:T(8,128)}, u32[]{:S(2)}) copy-start(s32[3,8,8,2816]{3,2,1,0:T(8,128)} %cells_ref.1) | copy-start | bytes 6488068
  15.8 31.1 %copy-start.4 = (f32[320,128]{1,0:T(8,128)S(1)}, f32[320,128]{1,0:T(8,128)}, u32[]{:S(2)}) copy-start(f32[320,128]{1,0:T(8,128)} %constant.20.clone.lane_ref) | copy-start | bytes 491524
  15.8 31.1 %copy-start.5 = (bf16[320,128]{1,0:T(8,128)(2,1)S(1)}, bf16[320,128]{1,0:T(8,128)(2,1)}, u32[]{:S(2)}) copy-start(bf16[320,128]{1,0:T(8,128)(2,1)} %constant.19.clone.owner_ref) | copy-start | bytes 245764
  15.8 31.1 %all-to-all-start = ((bf16[16,256,128]{2,1,0:T(8,128)(2,1)}), bf16[16,256,128]{2,1,0:T(8,128)(2,1)S(1)}, u32[]{:S(2)}, u32[]{:S(2)}) async-start(bf16[16,256,128]{2,1,0:T(8,128)(2,1)} %get-tuple-element.14), calls=%async_computation | async-start | bytes 2097152 | tf_op jit(solution)/shard_map/all_to_all | solution.py:725
  22.7 1.0 %copy-start.2 = (bf16[8,8,2816]{2,1,0:T(8,128)(2,1)S(1)}, bf16[8,8,2816]{2,1,0:T(8,128)(2,1)}, u32[]{:S(2)}) copy-start(bf16[8,8,2816]{2,1,0:T(8,128)(2,1)} %eta_ref.1) | copy-start | bytes 1081348
  23.7 0.7 copy-start.3
  25.7 2.2 %copy-start = (f32[7,8,8,2816]{3,2,1,0:T(8,128)}, f32[7,8,8,2816]{3,2,1,0:T(8,128)S(1)}, u32[]{:S(2)}) copy-start(f32[7,8,8,2816]{3,2,1,0:T(8,128)S(1)} %get-tuple-element.16.points_ref) | copy-start | bytes 15138820
  46.9 11.8 %slice-start = ((s8[5046272]{0:T(1024)(128)(4,1)}), s8[4194304]{0:T(1024)(128)(4,1)S(1)}, s32[]{:S(2)}) async-start(s8[5046272]{0:T(1024)(128)(4,1)} %bitcast.8), calls=%async_computation.1 | async-start | bytes 8388608
  46.9 11.8 %slice-start.1 = ((s8[5046272]{0:T(1024)(128)(4,1)}), s8[851968]{0:T(1024)(128)(4,1)S(1)}, s32[]{:S(2)}) async-start(s8[5046272]{0:T(1024)(128)(4,1)} %bitcast.8), calls=%async_computation.2 | async-start | bytes 1703936
  54.7 4.0 %collective-permute-start.1 = (bf16[2,2,24,2816]{3,2,1,0:T(8,128)(2,1)S(1)}, bf16[2,2,24,2816]{3,2,1,0:T(8,128)(2,1)S(1)}, u32[]{:S(2)}, u32[]{:S(2)}) collective-permute-start(bf16[2,2,24,2816]{3,2,1,0:T(8,128)(2,1)S(1)} %bitcast.10), channel_id=1, source_target_pairs={{0,1},{1,0},{2,3},{3,2},{4,5},{5,4},{6,7},{7,6},{8,9},{9,8},{10,11... | collective-permute-start | bytes 1622024 | tf_op jit(solution)/shard_map/ppermute | solution.py:363

commit v12 on v11

--- a/solution.py
+++ b/solution.py
@@ -98,11 +98,12 @@
 
 
 class Interleave:
-    def __init__(self, units, ticks):
+    def __init__(self, units, ticks, later):
         self.units = list(units)
         self.every = max(1, ticks // max(1, len(self.units)))
         self.count = 0
         self.pending = None
+        self.later = later
 
     def advance(self):
         if self.pending is not None:
@@ -116,10 +117,16 @@
         if self.count % self.every == 0:
             self.advance()
         self.count += 1
+        if self.later and self.count % 3 == 0:
+            self.later.pop(0)()
 
     def flush(self):
         while self.units or self.pending is not None:
             self.advance()
+
+    def finish_later(self):
+        while self.later:
+            self.later.pop(0)()
 
 
 def level_sums(scratch, field, base, slot, points):
@@ -236,31 +243,35 @@
         middle = (HALO * 5 + HALO) * STACK + step * (5 * STACK) + FIELD_ROW[field]
         return scratch[pl.ds(base + middle, ROWS), :]
 
-    count = range(len(points))
-    weights = [
-        both_weights(
-            COURANT * arrival_wind(1, step), COURANT * arrival_wind(0, step), points[step]
-        )
-        for step in count
-    ]
+    weights = []
+    for step, point in enumerate(points):
+        east, north = arrival_wind(0, step), arrival_wind(1, step)
+        keep[0, step, 16], keep[1, step, 16] = east, north
+        weights.append(both_weights(COURANT * north, COURANT * east, point))
     row_weights, lon_weights = zip(*weights)
     found = [
         across(scratch, field, base, points, row_weights, lon_weights, filling, keep)
         for field in range(2)
     ]
-    for step in count:
-        east, north = arrival_wind(0, step), arrival_wind(1, step)
-        east_found, north_found = found[0][step], found[1][step]
-        for sweep in range(ITERS):
-            shift_row = 0.5 * COURANT * (north + north_found)
-            shift_lon = 0.5 * COURANT * (east + east_found)
-            if sweep < ITERS - 1:
-                weights = both_weights(shift_row, shift_lon, points[step])
-                east_found = across_kept(keep, 0, step, *weights)
-                north_found = across_kept(keep, 1, step, *weights)
-        for out_ref in out_refs:
-            out_ref[0, k + step, :, lanes] = shift_row
-            out_ref[1, k + step, :, lanes] = shift_lon
+    filling.finish_later()
+
+    def tail(step, east_found, north_found):
+        def finish():
+            east, north = keep[0, step, 16], keep[1, step, 16]
+            here = (east_found, north_found)
+            for sweep in range(ITERS):
+                shift_row = 0.5 * COURANT * (north + here[1])
+                shift_lon = 0.5 * COURANT * (east + here[0])
+                if sweep < ITERS - 1:
+                    weights = both_weights(shift_row, shift_lon, points[step])
+                    here = [across_kept(keep, field, step, *weights) for field in range(2)]
+            for out_ref in out_refs:
+                out_ref[0, k + step, :, lanes] = shift_row
+                out_ref[1, k + step, :, lanes] = shift_lon
+
+        return finish
+
+    filling.later += [tail(step, found[0][step], found[1][step]) for step in range(len(points))]
 
 
 def tracer_levels(shift_ref, base, lanes, k, points, scratch, keep, filling, out_ref):
@@ -309,19 +320,25 @@
     for start, finish in all_units(0, even_scratch):
         finish(start())
 
-    def one_chunk(chunk, scratch, other):
+    def one_chunk(chunk, scratch, other, later):
         lanes = pl.ds(pl.multiple_of(chunk * LANES, LANES), LANES)
         following = jnp.where(chunk == chunk_total - 1, 0, chunk + 1)
-        filling = Interleave(all_units(following, other), 32 * (levels // together))
+        filling = Interleave(all_units(following, other), 32 * (levels // together), later)
         for k in range(0, levels, together):
             points = [arrival(points_ref, k + n, lanes) for n in range(together)]
             base = k * (5 * STACK)
-            levels_body(*extra, base, lanes, k, points, scratch, keep, filling, *out_refs)
+            keep_here = keep.at[k // together % 2]
+            levels_body(*extra, base, lanes, k, points, scratch, keep_here, filling, *out_refs)
         filling.flush()
+        if levels // together % 2:
+            filling.finish_later()
 
     def chunk_pair(pair, carry):
-        one_chunk(2 * pair, even_scratch, odd_scratch)
-        one_chunk(2 * pair + 1, odd_scratch, even_scratch)
+        later = []
+        one_chunk(2 * pair, even_scratch, odd_scratch, later)
+        one_chunk(2 * pair + 1, odd_scratch, even_scratch, later)
+        for finish in later:
+            finish()
         return carry
 
     lax.fori_loop(0, chunk_total // 2, chunk_pair, 0)
@@ -349,7 +366,7 @@
             pltpu.VMEM((2 * HALO,) + fields.shape[1:], jnp.float32),
             scratch,
             scratch,
-            pltpu.VMEM((2, together, 16, ROWS, LANES), jnp.float32),
+            pltpu.VMEM((2, 2, together, 17, ROWS, LANES), jnp.float32),
         ],
         compiler_params=pltpu.CompilerParams(vmem_limit_bytes=16 * 1024 * 1024),
         cost_estimate=pl.CostEstimate(
@@ -371,8 +388,6 @@
 
 
 TALL = ROWS + 2 * HALO
-PAIRED = TALL // 2
-HALF = LANES // 2
 
 
 def codes_kernel(numbers_ref, out_ref):
@@ -380,10 +395,10 @@
 
 
 def legendre_kernel(numbers_ref, codes_ref, spectra_ref, *others):
-    table_count = (len(others) - 8) // 2
+    table_count = (len(others) - 7) // 2
     sources, others = (spectra_ref,) + others[:table_count], others[table_count:]
-    out_ref, done_ref, sums, table_tail, column_tail, order_ref = others[:6]
-    targets, arrivals = others[6:-1], others[-1]
+    out_ref, done_ref, sums, table_tail, column_tail = others[:5]
+    targets, arrivals = others[5:-1], others[-1]
     spectra_here, tables = targets[0], targets[1:]
     _, pairs, level_fields, degrees = spectra_ref.shape
     group = table_tail.shape[0]
@@ -407,9 +422,8 @@
         done_ref[...] = jnp.zeros(done_ref.shape, jnp.float32)
         table_tail[...] = jnp.zeros(table_tail.shape, jnp.float32)
         column_tail[...] = jnp.zeros(column_tail.shape, jnp.float32)
-        order_ref[...] = column_order(level_fields)
         codes = codes_ref[...]
-        code_row = up_to(pl.num_programs(0) * group * PAIRED, ROWS)
+        code_row = up_to(pl.num_programs(0) * group * TALL, ROWS)
         for band in range(bands):
             first = band * block + code_row
             sums[pl.ds(first, 1), :] = jnp.right_shift(codes, 4).astype(jnp.float32)
@@ -422,9 +436,9 @@
 
     for copy in copies(step):
         copy.wait()
-    band_row = lax.broadcasted_iota(jnp.int32, (bands, LANES), 0)
-    first_half = lax.broadcasted_iota(jnp.int32, (bands, LANES), 1) < HALF
-    nothing = jnp.zeros((bands, LANES), jnp.float32)
+    band_row = lax.broadcasted_iota(jnp.int32, (bands, 4 * level_fields), 0)
+    count = 2 * level_fields
+    nothing = jnp.zeros((bands, 2 * count), jnp.float32)
     for p in range(group):
         slot = step * group + p
         edge = degrees - 1 - numbers_ref[1 + slot]
@@ -462,9 +476,6 @@
         found = lax.dot_general(
             left, right, (((1,), (1,)), ((), ())), preferred_element_type=jnp.float32
         )
-        found = jnp.dot(
-            found.astype(jnp.bfloat16), order_ref[...], preferred_element_type=jnp.float32
-        )
         found = [found[i * bands : (i + 1) * bands] for i in range(ROWS)]
         if len(tables) == 2:
             low, high = found[: ROWS // 2], found[ROWS // 2 :]
@@ -478,41 +489,23 @@
             for x in found[:HALO]
         ]
         rows = above + found + below
-        for i in range(PAIRED):
-            low, high = rows[i], rows[PAIRED + i]
-            place = slot * PAIRED + i
-            pairs_of = (
-                jnp.where(first_half, low, pltpu.roll(high, HALF, 1)),
-                jnp.where(first_half, pltpu.roll(low, HALF, 1), high),
-            )
-            for number, value in enumerate(pairs_of):
-                sums[pl.ds(number * (block // 2) + place, bands, stride=block), :] = value
+        for i, value in enumerate(rows):
+            place = pl.ds(slot * TALL + i, bands, stride=block)
+            sums[place, : 2 * count] = value
 
     @pl.when(step == pl.num_programs(0) - 1)
     def _():
         out_ref[...] = sums[...].astype(jnp.bfloat16).reshape(out_ref.shape)
 
 
-def column_order(level_fields):
-    shift = level_fields.bit_length() - 1
-    shape = (4 * level_fields, LANES)
-    column = lax.broadcasted_iota(jnp.int32, shape, 0)
-    part = jnp.right_shift(column, shift)
-    rest = column & (level_fields - 1)
-    target = jnp.right_shift(rest & 3, 1) * HALF + part * (level_fields // 2)
-    target = target + 2 * jnp.right_shift(rest, 2) + (rest & 1)
-    here = lax.broadcasted_iota(jnp.int32, shape, 1) == target
-    return jnp.where(here, 1.0, 0.0).astype(jnp.bfloat16)
-
-
 def block_rows(pairs):
-    return up_to(up_to(pairs * PAIRED, ROWS) + 2, 16)
+    return up_to(up_to(pairs * TALL, ROWS) + 2, 16)
 
 
 def legendre_call(pairing, spectra, tables):
     _, pairs, level_fields, degrees = spectra.shape
     bands = tables[0].shape[2]
-    block = 2 * block_rows(pairs)
+    block = block_rows(pairs)
     group = next(n for n in (4, 5, 2, 1) if pairs % n == 0)
     numbers = jnp.concatenate([lax.axis_index("lev").astype(jnp.int32)[None], pairing])
     codes = pl.pallas_call(
@@ -542,7 +535,6 @@
             pltpu.VMEM((bands * block, LANES), jnp.float32),
             pltpu.VMEM((group, ROWS * bands, LANES), jnp.float32),
             pltpu.VMEM((group, 2 * level_fields, LANES), jnp.float32),
-            pltpu.VMEM((4 * level_fields, LANES), jnp.bfloat16),
         ]
         + [pltpu.VMEM(x.shape, x.dtype) for x in (spectra,) + tables]
         + [pltpu.SemaphoreType.DMA((1 + len(tables), pairs // group))],
@@ -573,14 +565,14 @@
 
 
 def owner_tables(bands, pairs):
-    slots = np.arange(bands * pairs)
-    owner = slots[:, None] // pairs == np.arange(LANES)[None, :]
-    lane = slots[:, None] % pairs == np.arange(LANES)[None, :]
+    room = up_to(pairs, ROWS)
+    slots = np.arange(up_to(bands * room, LANES))
+    owner = slots[:, None] // room == np.arange(LANES)[None, :]
+    lane = slots[:, None] % room == np.arange(LANES)[None, :]
     return owner.astype(jnp.bfloat16), lane.astype(np.float32)
 
 
-def pair_places(flat, owner_ref, lane_ref, codes, bands, block, code_row, padded):
-    pair_total = owner_ref.shape[0]
+def pair_places(flat, owner_ref, lane_ref, codes, bands, block, code_row, pair_total, padded):
     codes[...] = jnp.zeros(codes.shape, jnp.float32)
     numbers = []
     for part in range(2):
@@ -596,13 +588,8 @@
         (16.0 * numbers[0] + numbers[1]) * lane_ref[...], axis=1, keepdims=True
     ).astype(jnp.int32)
     place = jnp.right_shift(pair_id, 1) + (pair_id & 1) * (pair_total // 2)
-    columns = lax.broadcasted_iota(jnp.int32, (pair_total, padded), 1)
-    place = jnp.where(columns == place, 1.0, 0.0)
-    if padded > pair_total:
-        place = jnp.concatenate(
-            [place, jnp.zeros((padded - pair_total, padded), jnp.float32)], axis=0
-        )
-    return place.astype(jnp.bfloat16)
+    columns = lax.broadcasted_iota(jnp.int32, (owner_ref.shape[0], padded), 1)
+    return jnp.where(columns == place, 1.0, 0.0).astype(jnp.bfloat16)
 
 
 def fourier_kernel(
@@ -614,55 +601,51 @@
     copy.start()
     bands, block, width = sums_ref.shape
     pair_total = bands * pairs
-    padded = gathered.shape[0]
+    padded = up_to(pair_total, LANES)
     blocks = padded // LANES
-    fields = 2 * levels
+    fields = 4 * levels
+    room = up_to(pairs, ROWS)
     flat[...] = sums_ref[...].astype(jnp.float32).reshape(bands * block, width)
-    gathered[pair_total:, :] = jnp.zeros((padded - pair_total, width), jnp.float32)
-    code_row = up_to(pairs * PAIRED, ROWS)
-    place = pair_places(flat, owner_ref, lane_ref, codes, bands, block, code_row, padded)
+    gathered[...] = jnp.zeros(gathered.shape, jnp.float32)
+    code_row = up_to(pairs * TALL, ROWS)
+    place = pair_places(
+        flat, owner_ref, lane_ref, codes, bands, block, code_row, pair_total, padded
+    )
     low = lax.broadcasted_iota(jnp.int32, (fields, padded), 1) < pair_total // 2
     middle = fields * ROWS
-    for number in range(2):
-        for i in range(PAIRED):
-            for band in range(bands):
-                first = band * block + number * (block // 2) + i
-                gathered[band * pairs : (band + 1) * pairs, :] = flat[
-                    pl.ds(first, pairs, stride=PAIRED), :
-                ]
-            ordered = jnp.dot(
-                gathered[...].T.astype(jnp.bfloat16), place, preferred_element_type=jnp.float32
-            )
-            for side in range(2):
-                row = side * PAIRED + i
-                if HALO <= row < HALO + ROWS:
-                    first, stride = row - HALO, ROWS
-                else:
-                    first, stride = middle + (row - HALO - ROWS) % TALL, 2 * HALO
-                for part in range(2):
-                    start = side * HALF + part * fields
-                    straight = ordered[start : start + fields]
-                    start = start + 2 * fields
-                    crossed = ordered[start : start + fields]
-                    both = (jnp.where(low, straight, crossed), jnp.where(low, crossed, straight))
-                    for parity in range(2):
-                        for t in range(blocks):
-                            lhs[
-                                number,
-                                parity,
-                                part * blocks + t,
-                                pl.ds(first, fields, stride=stride),
-                                :,
-                            ] = both[parity][:, t * LANES : (t + 1) * LANES]
+    for row in range(TALL):
+        here = gathered.at[row % 2]
+        for band in range(bands):
+            here[band * room : band * room + pairs, :] = flat[
+                pl.ds(band * block + row, pairs, stride=TALL), :
+            ]
+        ordered = jnp.dot(
+            here[...].T.astype(jnp.bfloat16), place, preferred_element_type=jnp.float32
+        )
+        if HALO <= row < HALO + ROWS:
+            first, stride = row - HALO, ROWS
+        else:
+            first, stride = middle + (row - HALO - ROWS) % TALL, 2 * HALO
+        for part in range(2):
+            start = part * fields
+            straight = ordered[start : start + fields]
+            start = start + 2 * fields
+            crossed = ordered[start : start + fields]
+            both = (jnp.where(low, straight, crossed), jnp.where(low, crossed, straight))
+            for parity in range(2):
+                for t in range(blocks):
+                    lhs[parity, part * blocks + t, pl.ds(first, fields, stride=stride), :] = both[
+                        parity
+                    ][:, t * LANES : (t + 1) * LANES]
     copy.wait()
     half = table_ref.shape[2]
 
-    def transform(number, first, count):
+    def transform(first, count):
         found = []
         for parity in range(2):
             left = jnp.concatenate(
                 [
-                    lhs[number, parity, t, first : first + count, :].astype(jnp.bfloat16)
+                    lhs[parity, t, first : first + count, :].astype(jnp.bfloat16)
                     for t in range(2 * blocks)
                 ],
                 axis=1,
@@ -672,16 +655,20 @@
         return [piece.astype(jnp.bfloat16).astype(jnp.float32) for piece in pieces]
 
     group = next(n for n in (4, 2, 1) if levels % n == 0)
+    for level in range(0, levels, group):
+        for part, value in enumerate(transform(level * 4 * ROWS, group * 4 * ROWS)):
+            value = value.reshape(group, 4 * ROWS, half)
+            lanes = slice(part * half, (part + 1) * half)
+            for number, field_ref in enumerate(field_refs):
+                field_ref[level : level + group, : 2 * ROWS, lanes] = value[
+                    :, 2 * ROWS * number : 2 * ROWS * (number + 1)
+                ]
+    for part, value in enumerate(transform(middle, fields * 2 * HALO)):
+        value = value.reshape(levels, 8 * HALO, half)
+        lanes = slice(part * half, (part + 1) * half)
+        for number, field_ref in enumerate(field_refs):
+            field_ref[:, 2 * ROWS :, lanes] = value[:, 4 * HALO * number : 4 * HALO * (number + 1)]
     for number, field_ref in enumerate(field_refs):
-        for level in range(0, levels, group):
-            pieces = transform(number, level * 2 * ROWS, group * 2 * ROWS)
-            for part, value in enumerate(pieces):
-                value = value.reshape(group, 2 * ROWS, half)
-                lanes = slice(part * half, (part + 1) * half)
-                field_ref[level : level + group, : 2 * ROWS, lanes] = value
-        for part, value in enumerate(transform(number, middle, fields * 2 * HALO)):
-            value = value.reshape(levels, 4 * HALO, half)
-            field_ref[:, 2 * ROWS :, part * half : (part + 1) * half] = value
         if send_ref.shape[0] == 1:
             start = jnp.where(base_ref[0] == 0, levels - HALO, 0)
             send_ref[0, number] = field_ref[pl.ds(start, HALO)].astype(jnp.bfloat16)
@@ -709,8 +696,8 @@
         scratch_shapes=[
             pltpu.VMEM((2, LANES, LANES), jnp.float32),
             pltpu.VMEM((bands * block, width), jnp.float32),
-            pltpu.VMEM((padded, width), jnp.float32),
-            pltpu.VMEM((2, 2, 2 * padded // LANES, 2 * levels * TALL, LANES), jnp.float32),
+            pltpu.VMEM((2, extra[0].shape[0], width), jnp.float32),
+            pltpu.VMEM((2, 2 * padded // LANES, 4 * levels * TALL, LANES), jnp.float32),
             pltpu.VMEM((2,) + table.shape[1:], table.dtype),
             pltpu.SemaphoreType.DMA,
         ],

time: 95.5 us -> 91.6 us (0.959)
  Pallas kernels: 56 us -> 52 us
    pallas_call x1, Pallas kernels: 9.3 us -> 7.37 us  [legendre_call(): pl.pallas_call(legendre_kernel, grid=(pairs // group,), out_shape=(shape,...]
    pallas_call x1, Pallas kernels: 7.76 us -> 5.87 us  [fourier_call(): pl.pallas_call(functools.partial(fourier_kernel, pairs, levels), out_shap...]
where the time goes in v12:
time: 91.6 us; the launch traced here: 91.2 us
  Pallas kernels  52 us (57%)
  waiting for transfers between devices  20.7 us (23%)
  starting transfers between devices  10 us (11%)
  local copies, waits for them, and re-layouts  6.39 us (7%)
  other arithmetic  1.28 us (1%)
    pallas_call x2, Pallas kernels, interpolation_call(): pl.pallas_call(functools.partial(interpolation_kernel, levels_body, toget...  36.3 us
    all_to_all x1, waiting for transfers between devices, exchange(): return lax.all_to_all(sums, 'band', split_axis=0, concat_axis=0, tiled=True)  18.9 us
    pallas_call x1, Pallas kernels, legendre_call(): pl.pallas_call(legendre_kernel, grid=(pairs // group,), out_shape=(shape,...  7.37 us
    all_to_all x1, starting transfers between devices, exchange(): return lax.all_to_all(sums, 'band', split_axis=0, concat_axis=0, tiled=True)  6.82 us
    pallas_call x1, Pallas kernels, fourier_call(): pl.pallas_call(functools.partial(fourier_kernel, pairs, levels), out_shap...  5.87 us
    unnamed x18, local copies, waits for them, and re-layouts  5.22 us
    ppermute x1, starting transfers between devices, swap_levels(): return (lax.ppermute(send[0], 'lev', [(0, 1), (1, 0)]),)  2.48 us
  transfers between devices with their start and end apart: 3, of which 3 were waited for; matrix products, arithmetic and copies ran while one was open for 3% of the time, Pallas kernels for 3%

profile of v12, /device:TPU:9, one launch (start us, length us, event | category | flops | bytes accessed | tf_op | source)
XLA Modules:
  0.0 91.2 jit_solution(15802653990528251347)
XLA Ops:
  0.6 0.7 collective-permute-start
  1.4 1.2 %pad_bitcast_fusion.numbers_ref = s32[1,128]{1,0:T(1,128)} fusion(s32[20]{0:T(128)} %param.10), kind=kLoop, calls=%fused_computation.2 | loop fusion | bytes 592 | tf_op jit(solution)/shard_map/broadcast_in_dim | solution.py:518
  2.5 1.2 %shard_map.95.codes_ref = s32[1,128]{1,0:T(1,128)} custom-call(s32[1,128]{1,0:T(1,128)} %pad_bitcast_fusion.numbers_ref), custom_call_target="tpu_custom_call" | custom-call | bytes 4000000 | tf_op jit(solution)/shard_map/pallas_call | solution.py:511
  3.7 1.2 %pad_add_fusion.1.numbers_ref = s32[21]{0:T(128)} fusion(s32[20]{0:T(128)} %param.10, s32[1]{0:T(128)} %bitcast.2), kind=kLoop, calls=%fused_computation.1 | loop fusion | flops 21 | bytes 168 | tf_op jit(solution)/shard_map/concatenate | solution.py:510
  4.9 0.2 collective-permute-done.others_1_
  5.2 0.0 copy-start.6
  5.2 1.3 %copy-done.6 = bf16[4,20,16,641]{3,2,1,0:T(8,128)(2,1)} copy-done((bf16[4,20,16,641]{3,2,1,0:T(8,128)(2,1)}, bf16[4,20,16,641]{3,2,1,0:T(8,128)(2,1)S(1)}, u32[]{:S(2)}) %copy-start.6) | copy-done | bytes 1640984
  6.5 0.0 copy-start.1
  6.5 7.4 %shard_map.96 = (bf16[16,256,128]{2,1,0:T(8,128)(2,1)}, f32[8,128]{1,0:T(8,128)}) custom-call(s32[21]{0:T(128)} %pad_add_fusion.1.numbers_ref, s32[1,128]{1,0:T(1,128)} %shard_map.95.codes_ref, bf16[2,20,32,641]{3,2,1,0:T(8,128)(2,1)} %bitcast.11, bf16[4,20,16,641]{3,2,1,0:T(8,128)(2,1)} %bitcast.13, bf16[4,20,16,641]{3,2,1,0:T(8,128)(2,1)} %copy-done.6), custom_call_target="tpu_custom_call" | custom-call | flops 420085760 | bytes 8000000 | tf_op jit(solution)/shard_map/pallas_call | solution.py:523
  13.8 0.0 copy-start.4
  13.9 0.0 copy-start.5
  13.9 6.8 %all-to-all-start = ((bf16[16,256,128]{2,1,0:T(8,128)(2,1)}), bf16[16,256,128]{2,1,0:T(8,128)(2,1)S(1)}, u32[]{:S(2)}, u32[]{:S(2)}) async-start(bf16[16,256,128]{2,1,0:T(8,128)(2,1)} %get-tuple-element.14), calls=%async_computation | async-start | bytes 2097152 | tf_op jit(solution)/shard_map/all_to_all | solution.py:712
  20.7 0.1 pad_add_fusion.base_ref
  20.8 0.0 copy-done.1
  20.8 0.0 copy-start.2
  20.8 1.0 %copy-done.2 = bf16[8,8,2816]{2,1,0:T(8,128)(2,1)S(1)} copy-done((bf16[8,8,2816]{2,1,0:T(8,128)(2,1)S(1)}, bf16[8,8,2816]{2,1,0:T(8,128)(2,1)}, u32[]{:S(2)}) %copy-start.2) | copy-done | bytes 360472
  21.8 0.0 copy-start.3
  21.8 0.7 copy-done.3
  22.4 1.4 %shard_map.97 = (f32[7,8,8,2816]{3,2,1,0:T(8,128)S(1)}, f32[8,128]{1,0:T(8,128)S(1)}) custom-call(s32[2]{0:T(128)S(1)} %pad_add_fusion.base_ref, f32[8,128]{1,0:T(8,128)S(1)} %copy-done.3, bf16[8,8,2816]{2,1,0:T(8,128)(2,1)S(1)} %copy-done.2, s32[3,8,8,2816]{3,2,1,0:T(8,128)S(1)} %copy-done.1), custom_call_target="tpu_custom_call" | custom-call | flops 7208960 | bytes 20000000 | tf_op jit(solution)/shard_map/pallas_call | solution.py:213
  23.8 0.0 copy-start
  23.8 2.2 %copy-done = f32[7,8,8,2816]{3,2,1,0:T(8,128)} copy-done((f32[7,8,8,2816]{3,2,1,0:T(8,128)}, f32[7,8,8,2816]{3,2,1,0:T(8,128)S(1)}, u32[]{:S(2)}) %copy-start) | copy-done | bytes 5046296
  26.0 18.9 %all-to-all-done.sums_ref = bf16[16,256,128]{2,1,0:T(8,128)(2,1)S(1)} async-done(((bf16[16,256,128]{2,1,0:T(8,128)(2,1)}), bf16[16,256,128]{2,1,0:T(8,128)(2,1)S(1)}, u32[]{:S(2)}, u32[]{:S(2)}) %all-to-all-start) | async-done | bytes 1048608 | tf_op jit(solution)/shard_map/all_to_all | solution.py:712
  45.0 0.0 slice-start
  45.0 0.0 copy-done.4
  45.0 0.0 copy-done.5
  45.0 0.0 slice-start.1
  45.0 5.9 %shard_map.98 = (f32[8,24,2816]{2,1,0:T(8,128)S(1)}, f32[8,24,2816]{2,1,0:T(8,128)S(1)}, bf16[1,2,2,24,2816]{4,3,2,1,0:T(8,128)(2,1)S(1)}) custom-call(s32[2]{0:T(128)S(1)} %pad_add_fusion.base_ref, f32[8,128]{1,0:T(8,128)S(1)} %get-tuple-element.13.after_ref, bf16[16,256,128]{2,1,0:T(8,128)(2,1)S(1)} %all-to-all-done.sums_ref, ...), custom_call_target="tpu_custom_call" | custom-call | flops 8000000000 | bytes 8000000 | tf_op jit(solution)/shard_map/pallas_call | solution.py:689
  50.9 2.5 %collective-permute-start.1 = (bf16[2,2,24,2816]{3,2,1,0:T(8,128)(2,1)S(1)}, bf16[2,2,24,2816]{3,2,1,0:T(8,128)(2,1)S(1)}, u32[]{:S(2)}, u32[]{:S(2)}) collective-permute-start(bf16[2,2,24,2816]{3,2,1,0:T(8,128)(2,1)S(1)} %bitcast.10), channel_id=1, source_target_pairs={{0,1},{1,0},{2,3},{3,2},{4,5},{5,4},{6,7},{7,6},{8,9},{9,8},{10,11... | collective-permute-start | bytes 1622024 | tf_op jit(solution)/shard_map/ppermute | solution.py:380
  53.3 1.6 %collective-permute-done.1.others_0_ = bf16[2,2,24,2816]{3,2,1,0:T(8,128)(2,1)S(1)} collective-permute-done((bf16[2,2,24,2816]{3,2,1,0:T(8,128)(2,1)S(1)}, bf16[2,2,24,2816]{3,2,1,0:T(8,128)(2,1)S(1)}, u32[]{:S(2)}, u32[]{:S(2)}) %collective-permute-start.1) | collective-permute-done | bytes 540704 | tf_op jit(solution)/shard_map/ppermute | solution.py:380
  54.9 0.0 slice-done
  54.9 0.0 slice-done.1
  54.9 19.7 %shard_map.99 = (f32[2,8,8,2816]{3,2,1,0:T(8,128)}, f32[2,8,8,2816]{3,2,1,0:T(8,128)S(1)}, f32[8,128]{1,0:T(8,128)}) custom-call(s32[2]{0:T(128)S(1)} %pad_add_fusion.base_ref, f32[8,24,2816]{2,1,0:T(8,128)S(1)} %get-tuple-element.18.field_ref, f32[7,8,8,2816]{3,2,1,0:T(8,128)S(1)} %bitcast.9, bf16[2,2,24,2816]{3,2,1,0:T(8,128)(2,1)S(1)} %collective-permute-done.1.others_0_), custom_call_target="tpu_custom_call" | custom-call | flops 90112000 | bytes 7208960 | tf_op jit(solution)/shard_map/pallas_call | solution.py:357
  74.6 16.5 %shard_map.100 = (bf16[2,8,8,2816]{3,2,1,0:T(8,128)(2,1)}, f32[8,128]{1,0:T(8,128)}) custom-call(s32[2]{0:T(128)S(1)} %pad_add_fusion.base_ref, f32[8,24,2816]{2,1,0:T(8,128)S(1)} %get-tuple-element.15.field_ref, f32[7,8,8,2816]{3,2,1,0:T(8,128)S(1)} %bitcast.9, bf16[2,2,24,2816]{3,2,1,0:T(8,128)(2,1)S(1)} %collective-permute-done.1.others_0_, ...), custom_call_target="tpu_custom_call" | custom-call | flops 90112000 | bytes 7208960 | tf_op jit(solution)/shard_map/pallas_call | solution.py:357
  (1 shorter events, 0.0 us)
Async XLA Ops:
  0.6 4.6 %collective-permute-start = (bf16[4,20,16,641]{3,2,1,0:T(8,128)(2,1)}, bf16[4,20,16,641]{3,2,1,0:T(8,128)(2,1)S(1)}, u32[]{:S(2)}, u32[]{:S(2)}) collective-permute-start(bf16[4,20,16,641]{3,2,1,0:T(8,128)(2,1)} %bitcast.12), channel_id=1, source_target_pairs={{0,1},{1,0},{2,3},{3,2},{4,5},{5,4},{6,7},{7,6},{8,9},{9,8},{10,11... | collective-permute-start | bytes 4922888 | tf_op jit(solution)/shard_map/ppermute | solution.py:721
  5.2 1.3 %copy-start.6 = (bf16[4,20,16,641]{3,2,1,0:T(8,128)(2,1)}, bf16[4,20,16,641]{3,2,1,0:T(8,128)(2,1)S(1)}, u32[]{:S(2)}) copy-start(bf16[4,20,16,641]{3,2,1,0:T(8,128)(2,1)S(1)} %collective-permute-done.others_1_) | copy-start | bytes 4922884
  6.5 14.3 %copy-start.1 = (s32[3,8,8,2816]{3,2,1,0:T(8,128)S(1)}, s32[3,8,8,2816]{3,2,1,0:T(8,128)}, u32[]{:S(2)}) copy-start(s32[3,8,8,2816]{3,2,1,0:T(8,128)} %cells_ref.1) | copy-start | bytes 6488068
  13.8 31.1 %copy-start.4 = (f32[384,128]{1,0:T(8,128)S(1)}, f32[384,128]{1,0:T(8,128)}, u32[]{:S(2)}) copy-start(f32[384,128]{1,0:T(8,128)} %constant.20.clone.lane_ref) | copy-start | bytes 589828
  13.9 31.1 %copy-start.5 = (bf16[384,128]{1,0:T(8,128)(2,1)S(1)}, bf16[384,128]{1,0:T(8,128)(2,1)}, u32[]{:S(2)}) copy-start(bf16[384,128]{1,0:T(8,128)(2,1)} %constant.19.clone.owner_ref) | copy-start | bytes 294916
  13.9 31.1 %all-to-all-start = ((bf16[16,256,128]{2,1,0:T(8,128)(2,1)}), bf16[16,256,128]{2,1,0:T(8,128)(2,1)S(1)}, u32[]{:S(2)}, u32[]{:S(2)}) async-start(bf16[16,256,128]{2,1,0:T(8,128)(2,1)} %get-tuple-element.14), calls=%async_computation | async-start | bytes 2097152 | tf_op jit(solution)/shard_map/all_to_all | solution.py:712
  20.8 1.0 %copy-start.2 = (bf16[8,8,2816]{2,1,0:T(8,128)(2,1)S(1)}, bf16[8,8,2816]{2,1,0:T(8,128)(2,1)}, u32[]{:S(2)}) copy-start(bf16[8,8,2816]{2,1,0:T(8,128)(2,1)} %eta_ref.1) | copy-start | bytes 1081348
  21.8 0.7 copy-start.3
  23.8 2.2 %copy-start = (f32[7,8,8,2816]{3,2,1,0:T(8,128)}, f32[7,8,8,2816]{3,2,1,0:T(8,128)S(1)}, u32[]{:S(2)}) copy-start(f32[7,8,8,2816]{3,2,1,0:T(8,128)S(1)} %get-tuple-element.16.points_ref) | copy-start | bytes 15138820
  45.0 9.9 %slice-start = ((s8[5046272]{0:T(1024)(128)(4,1)}), s8[4194304]{0:T(1024)(128)(4,1)S(1)}, s32[]{:S(2)}) async-start(s8[5046272]{0:T(1024)(128)(4,1)} %bitcast.8), calls=%async_computation.1 | async-start | bytes 8388608
  45.0 9.9 %slice-start.1 = ((s8[5046272]{0:T(1024)(128)(4,1)}), s8[851968]{0:T(1024)(128)(4,1)S(1)}, s32[]{:S(2)}) async-start(s8[5046272]{0:T(1024)(128)(4,1)} %bitcast.8), calls=%async_computation.2 | async-start | bytes 1703936
  50.9 4.0 %collective-permute-start.1 = (bf16[2,2,24,2816]{3,2,1,0:T(8,128)(2,1)S(1)}, bf16[2,2,24,2816]{3,2,1,0:T(8,128)(2,1)S(1)}, u32[]{:S(2)}, u32[]{:S(2)}) collective-permute-start(bf16[2,2,24,2816]{3,2,1,0:T(8,128)(2,1)S(1)} %bitcast.10), channel_id=1, source_target_pairs={{0,1},{1,0},{2,3},{3,2},{4,5},{5,4},{6,7},{7,6},{8,9},{9,8},{10,11... | collective-permute-start | bytes 1622024 | tf_op jit(solution)/shard_map/ppermute | solution.py:380

commit v13 on v12

--- a/solution.py
+++ b/solution.py
@@ -134,8 +134,6 @@
 
     def load(a, b, c):
         offset = ((a + HALO) * 5 + c + HALO) * STACK + FIELD_ROW[field] + b
-        if slot == (2, 2):
-            return scratch[pl.ds(base + offset, ROWS), :]
         if (a, b, c) not in loaded:
             loaded[a, b, c] = scratch[pl.ds(base + offset, ROWS), :]
         return loaded[a, b, c]
@@ -238,7 +236,7 @@
     )
 
 
-def wind_levels(base, lanes, k, points, scratch, keep, filling, *out_refs):
+def wind_levels(base, lanes, k, points, scratch, keep, filling, out_ref):
     def arrival_wind(field, step):
         middle = (HALO * 5 + HALO) * STACK + step * (5 * STACK) + FIELD_ROW[field]
         return scratch[pl.ds(base + middle, ROWS), :]
@@ -265,9 +263,8 @@
                 if sweep < ITERS - 1:
                     weights = both_weights(shift_row, shift_lon, points[step])
                     here = [across_kept(keep, field, step, *weights) for field in range(2)]
-            for out_ref in out_refs:
-                out_ref[0, k + step, :, lanes] = shift_row
-                out_ref[1, k + step, :, lanes] = shift_lon
+            out_ref[0, k + step, :, lanes] = shift_row
+            out_ref[1, k + step, :, lanes] = shift_lon
 
         return finish
 
@@ -292,12 +289,17 @@
 
 
 def interpolation_kernel(
-    levels_body, together, number, near_count, out_count, base_ref, field_ref, points_ref, *others
+    levels_body, together, number, near_count, base_ref, field_ref, points_ref, *others
 ):
     nears, others = others[:near_count], others[near_count:]
-    around, even_scratch, odd_scratch, keep = others[-4:]
-    extra, out_refs, done_ref = others[: -5 - out_count], others[-5 - out_count : -5], others[-5]
-    done_ref[...] = jnp.zeros(done_ref.shape, done_ref.dtype)
+    extra = ()
+    if number == 1:
+        shift_ref, out_ref, shift_out, around, even_scratch, odd_scratch, keep, sem = others
+        extra = (shift_ref,)
+        copy = pltpu.make_async_copy(shift_ref, shift_out, sem)
+        copy.start()
+    else:
+        out_ref, around, even_scratch, odd_scratch, keep = others
     _, levels, rows, lon_total = points_ref.shape
     chunk_total = lon_total // LANES
     if near_count == 1:
@@ -328,7 +330,7 @@
             points = [arrival(points_ref, k + n, lanes) for n in range(together)]
             base = k * (5 * STACK)
             keep_here = keep.at[k // together % 2]
-            levels_body(*extra, base, lanes, k, points, scratch, keep_here, filling, *out_refs)
+            levels_body(*extra, base, lanes, k, points, scratch, keep_here, filling, out_ref)
         filling.flush()
         if levels // together % 2:
             filling.finish_later()
@@ -342,32 +344,30 @@
         return carry
 
     lax.fori_loop(0, chunk_total // 2, chunk_pair, 0)
-
-
-def interpolation_call(
-    levels_body, base, number, fields, points, nears, extra, out_dtype, out_count
-):
+    if number == 1:
+        copy.wait()
+
+
+def interpolation_call(levels_body, base, number, fields, points, nears, extra, out_dtype):
     _, levels, rows, lon_total = points.shape
     count = levels * rows * lon_total
     together = next(n for n in (4, 2, 1) if levels % n == 0)
     scratch = pltpu.VMEM(((levels + 2 * HALO) * 5 * STACK, LANES), jnp.float32)
     in_vmem = pl.BlockSpec(memory_space=pltpu.VMEM)
-    out = jax.ShapeDtypeStruct((2, levels, rows, lon_total), out_dtype)
-    done = jax.ShapeDtypeStruct((ROWS, LANES), jnp.float32)
     return pl.pallas_call(
-        functools.partial(
-            interpolation_kernel, levels_body, together, number, len(nears), out_count
-        ),
-        out_shape=(out,) * out_count + (done,),
+        functools.partial(interpolation_kernel, levels_body, together, number, len(nears)),
+        out_shape=(jax.ShapeDtypeStruct((2, levels, rows, lon_total), out_dtype),)
+        + tuple(jax.ShapeDtypeStruct(x.shape, x.dtype) for x in extra),
         in_specs=[pl.BlockSpec(memory_space=pltpu.SMEM)]
         + [in_vmem] * (2 + len(nears) + len(extra)),
-        out_specs=(in_vmem,) * (out_count + 1),
+        out_specs=(in_vmem,) + (pl.BlockSpec(memory_space=pl.ANY),) * len(extra),
         scratch_shapes=[
             pltpu.VMEM((2 * HALO,) + fields.shape[1:], jnp.float32),
             scratch,
             scratch,
             pltpu.VMEM((2, 2, together, 17, ROWS, LANES), jnp.float32),
-        ],
+        ]
+        + [pltpu.SemaphoreType.DMA] * len(extra),
         compiler_params=pltpu.CompilerParams(vmem_limit_bytes=16 * 1024 * 1024),
         cost_estimate=pl.CostEstimate(
             flops=count * 500, bytes_accessed=count * 40, transcendentals=0
@@ -395,10 +395,10 @@
 
 
 def legendre_kernel(numbers_ref, codes_ref, spectra_ref, *others):
-    table_count = (len(others) - 7) // 2
+    table_count = (len(others) - 9) // 2
     sources, others = (spectra_ref,) + others[:table_count], others[table_count:]
-    out_ref, done_ref, sums, table_tail, column_tail = others[:5]
-    targets, arrivals = others[5:-1], others[-1]
+    out_ref, done_ref, sums, table_tail, column_tail, staged = others[:6]
+    targets, arrivals, departures = others[6:-2], others[-2], others[-1]
     spectra_here, tables = targets[0], targets[1:]
     _, pairs, level_fields, degrees = spectra_ref.shape
     group = table_tail.shape[0]
@@ -495,7 +495,15 @@
 
     @pl.when(step == pl.num_programs(0) - 1)
     def _():
-        out_ref[...] = sums[...].astype(jnp.bfloat16).reshape(out_ref.shape)
+        leaving = []
+        for band in range(bands):
+            staged[band] = sums[band * block : (band + 1) * block, :].astype(jnp.bfloat16)
+            leaving.append(
+                pltpu.make_async_copy(staged.at[band], out_ref.at[band], departures.at[band])
+            )
+            leaving[-1].start()
+        for copy in leaving:
+            copy.wait()
 
 
 def block_rows(pairs):
@@ -517,7 +525,6 @@
         cost_estimate=pl.CostEstimate(flops=0, bytes_accessed=4_000_000, transcendentals=0),
     )(jnp.pad(pairing, (0, LANES - pairs))[None, :])
     shape = jax.ShapeDtypeStruct((bands, block, LANES), jnp.bfloat16)
-    whole = pl.BlockSpec((bands, block, LANES), lambda i: (0, 0, 0))
     in_vmem = pl.BlockSpec(memory_space=pltpu.VMEM)
     in_hbm = pl.BlockSpec(memory_space=pl.ANY)
     return pl.pallas_call(
@@ -530,14 +537,16 @@
             in_hbm,
         ]
         + [in_hbm] * len(tables),
-        out_specs=(whole, in_vmem),
+        out_specs=(in_hbm, in_vmem),
         scratch_shapes=[
             pltpu.VMEM((bands * block, LANES), jnp.float32),
             pltpu.VMEM((group, ROWS * bands, LANES), jnp.float32),
             pltpu.VMEM((group, 2 * level_fields, LANES), jnp.float32),
+            pltpu.VMEM(shape.shape, shape.dtype),
         ]
         + [pltpu.VMEM(x.shape, x.dtype) for x in (spectra,) + tables]
-        + [pltpu.SemaphoreType.DMA((1 + len(tables), pairs // group))],
+        + [pltpu.SemaphoreType.DMA((1 + len(tables), pairs // group))]
+        + [pltpu.SemaphoreType.DMA((bands,))],
         compiler_params=pltpu.CompilerParams(vmem_limit_bytes=60 * 1024 * 1024),
         cost_estimate=pl.CostEstimate(
             flops=2 * ROWS * bands * 4 * level_fields * pairs * degrees,
@@ -730,11 +739,11 @@
     twiddles = jnp.asarray(fourier_table(pair_total, up_to(pair_total, LANES), lon_total))
     winds, tracers, send = fourier_call(base, done, sums, twiddles, pairs, levels, lon_total)
     nears = swap_levels(send)
-    displacement, moved, _ = interpolation_call(
-        wind_levels, base, 0, winds, points, nears, (), jnp.float32, 2
-    )
-    advected, _ = interpolation_call(
-        tracer_levels, base, 1, tracers, points, nears, (moved,), jnp.bfloat16, 1
+    (moved,) = interpolation_call(
+        wind_levels, base, 0, winds, points, nears, (), jnp.float32
+    )
+    advected, displacement = interpolation_call(
+        tracer_levels, base, 1, tracers, points, nears, (moved,), jnp.bfloat16
     )
     return advected, displacement
 

time: 91.6 us -> 91.1 us (level)
    pallas_call x2, Pallas kernels: 36.3 us -> 35.1 us  [interpolation_call(): pl.pallas_call(functools.partial(interpolation_kernel, levels_body, toget...]
where the time goes in v13:
time: 91.1 us; the launch traced here: 90.7 us
  Pallas kernels  51.6 us (57%)
  waiting for transfers between devices  20.6 us (23%)
  starting transfers between devices  10 us (11%)
  local copies, waits for them, and re-layouts  6.39 us (7%)
  other arithmetic  1.38 us (2%)
    pallas_call x2, Pallas kernels, interpolation_call(): pl.pallas_call(functools.partial(interpolation_kernel, levels_body, toget...  35.1 us
    all_to_all x1, waiting for transfers between devices, exchange(): return lax.all_to_all(sums, 'band', split_axis=0, concat_axis=0, tiled=True)  18.9 us
    pallas_call x1, Pallas kernels, legendre_call(): pl.pallas_call(legendre_kernel, grid=(pairs // group,), out_shape=(shape,...  8.02 us
    all_to_all x1, starting transfers between devices, exchange(): return lax.all_to_all(sums, 'band', split_axis=0, concat_axis=0, tiled=True)  6.8 us
    pallas_call x1, Pallas kernels, fourier_call(): pl.pallas_call(functools.partial(fourier_kernel, pairs, levels), out_shap...  5.87 us
    unnamed x18, local copies, waits for them, and re-layouts  5.22 us
    ppermute x1, starting transfers between devices, swap_levels(): return (lax.ppermute(send[0], 'lev', [(0, 1), (1, 0)]),)  2.48 us
  transfers between devices with their start and end apart: 3, of which 3 were waited for; matrix products, arithmetic and copies ran while one was open for 3% of the time, Pallas kernels for 3%

profile of v13, /device:TPU:9, one launch (start us, length us, event | category | flops | bytes accessed | tf_op | source)
XLA Modules:
  0.0 90.7 jit_solution(366490012822952623)
XLA Ops:
  0.6 0.7 collective-permute-start
  1.4 1.2 %pad_bitcast_fusion.numbers_ref = s32[1,128]{1,0:T(1,128)} fusion(s32[20]{0:T(128)} %param.10), kind=kLoop, calls=%fused_computation.2 | loop fusion | bytes 592 | tf_op jit(solution)/shard_map/broadcast_in_dim | solution.py:526
  2.5 1.2 %shard_map.95.codes_ref = s32[1,128]{1,0:T(1,128)} custom-call(s32[1,128]{1,0:T(1,128)} %pad_bitcast_fusion.numbers_ref), custom_call_target="tpu_custom_call" | custom-call | bytes 4000000 | tf_op jit(solution)/shard_map/pallas_call | solution.py:519
  3.8 1.3 %pad_add_fusion.1.numbers_ref = s32[21]{0:T(128)} fusion(s32[20]{0:T(128)} %param.10, s32[1]{0:T(128)} %bitcast.2), kind=kLoop, calls=%fused_computation.1 | loop fusion | flops 21 | bytes 168 | tf_op jit(solution)/shard_map/concatenate | solution.py:518
  5.1 0.1 collective-permute-done.others_1_
  5.2 0.0 copy-start.6
  5.2 1.3 %copy-done.6 = bf16[4,20,16,641]{3,2,1,0:T(8,128)(2,1)} copy-done((bf16[4,20,16,641]{3,2,1,0:T(8,128)(2,1)}, bf16[4,20,16,641]{3,2,1,0:T(8,128)(2,1)S(1)}, u32[]{:S(2)}) %copy-start.6) | copy-done | bytes 1640984
  6.5 0.0 copy-start.1
  6.5 8.0 %shard_map.96 = (bf16[16,256,128]{2,1,0:T(8,128)(2,1)}, f32[8,128]{1,0:T(8,128)}) custom-call(s32[21]{0:T(128)} %pad_add_fusion.1.numbers_ref, s32[1,128]{1,0:T(1,128)} %shard_map.95.codes_ref, bf16[2,20,32,641]{3,2,1,0:T(8,128)(2,1)} %bitcast.11, bf16[4,20,16,641]{3,2,1,0:T(8,128)(2,1)} %bitcast.13, bf16[4,20,16,641]{3,2,1,0:T(8,128)(2,1)} %copy-done.6), custom_call_target="tpu_custom_call" | custom-call | flops 420085760 | bytes 8000000 | tf_op jit(solution)/shard_map/pallas_call | solution.py:530
  14.5 0.0 copy-start.4
  14.5 0.0 copy-start.5
  14.5 6.8 %all-to-all-start = ((bf16[16,256,128]{2,1,0:T(8,128)(2,1)}), bf16[16,256,128]{2,1,0:T(8,128)(2,1)S(1)}, u32[]{:S(2)}, u32[]{:S(2)}) async-start(bf16[16,256,128]{2,1,0:T(8,128)(2,1)} %get-tuple-element.11), calls=%async_computation | async-start | bytes 2097152 | tf_op jit(solution)/shard_map/all_to_all | solution.py:721
  21.3 0.1 pad_add_fusion.base_ref
  21.4 0.0 copy-done.1
  21.4 0.0 copy-start.2
  21.4 1.0 %copy-done.2 = bf16[8,8,2816]{2,1,0:T(8,128)(2,1)S(1)} copy-done((bf16[8,8,2816]{2,1,0:T(8,128)(2,1)S(1)}, bf16[8,8,2816]{2,1,0:T(8,128)(2,1)}, u32[]{:S(2)}) %copy-start.2) | copy-done | bytes 360472
  22.4 0.0 copy-start.3
  22.4 0.7 copy-done.3
  23.1 1.4 %shard_map.97 = (f32[7,8,8,2816]{3,2,1,0:T(8,128)S(1)}, f32[8,128]{1,0:T(8,128)S(1)}) custom-call(s32[2]{0:T(128)S(1)} %pad_add_fusion.base_ref, f32[8,128]{1,0:T(8,128)S(1)} %copy-done.3, bf16[8,8,2816]{2,1,0:T(8,128)(2,1)S(1)} %copy-done.2, s32[3,8,8,2816]{3,2,1,0:T(8,128)S(1)} %copy-done.1), custom_call_target="tpu_custom_call" | custom-call | flops 7208960 | bytes 20000000 | tf_op jit(solution)/shard_map/pallas_call | solution.py:211
  24.4 0.0 copy-start
  24.5 2.2 %copy-done = f32[7,8,8,2816]{3,2,1,0:T(8,128)} copy-done((f32[7,8,8,2816]{3,2,1,0:T(8,128)}, f32[7,8,8,2816]{3,2,1,0:T(8,128)S(1)}, u32[]{:S(2)}) %copy-start) | copy-done | bytes 5046296
  26.7 18.9 %all-to-all-done.sums_ref = bf16[16,256,128]{2,1,0:T(8,128)(2,1)S(1)} async-done(((bf16[16,256,128]{2,1,0:T(8,128)(2,1)}), bf16[16,256,128]{2,1,0:T(8,128)(2,1)S(1)}, u32[]{:S(2)}, u32[]{:S(2)}) %all-to-all-start) | async-done | bytes 1048608 | tf_op jit(solution)/shard_map/all_to_all | solution.py:721
  45.6 0.0 slice-start
  45.6 0.0 copy-done.4
  45.6 0.0 copy-done.5
  45.6 0.0 slice-start.1
  45.6 5.9 %shard_map.98 = (f32[8,24,2816]{2,1,0:T(8,128)S(1)}, f32[8,24,2816]{2,1,0:T(8,128)S(1)}, bf16[1,2,2,24,2816]{4,3,2,1,0:T(8,128)(2,1)S(1)}) custom-call(s32[2]{0:T(128)S(1)} %pad_add_fusion.base_ref, f32[8,128]{1,0:T(8,128)S(1)} %get-tuple-element.10.after_ref, bf16[16,256,128]{2,1,0:T(8,128)(2,1)S(1)} %all-to-all-done.sums_ref, ...), custom_call_target="tpu_custom_call" | custom-call | flops 8000000000 | bytes 8000000 | tf_op jit(solution)/shard_map/pallas_call | solution.py:698
  51.5 2.5 %collective-permute-start.1 = (bf16[2,2,24,2816]{3,2,1,0:T(8,128)(2,1)S(1)}, bf16[2,2,24,2816]{3,2,1,0:T(8,128)(2,1)S(1)}, u32[]{:S(2)}, u32[]{:S(2)}) collective-permute-start(bf16[2,2,24,2816]{3,2,1,0:T(8,128)(2,1)S(1)} %bitcast.10), channel_id=1, source_target_pairs={{0,1},{1,0},{2,3},{3,2},{4,5},{5,4},{6,7},{7,6},{8,9},{9,8},{10,11... | collective-permute-start | bytes 1622024 | tf_op jit(solution)/shard_map/ppermute | solution.py:380
  54.0 1.6 %collective-permute-done.1.others_0_ = bf16[2,2,24,2816]{3,2,1,0:T(8,128)(2,1)S(1)} collective-permute-done((bf16[2,2,24,2816]{3,2,1,0:T(8,128)(2,1)S(1)}, bf16[2,2,24,2816]{3,2,1,0:T(8,128)(2,1)S(1)}, u32[]{:S(2)}, u32[]{:S(2)}) %collective-permute-start.1) | collective-permute-done | bytes 540704 | tf_op jit(solution)/shard_map/ppermute | solution.py:380
  55.5 0.0 slice-done
  55.5 0.0 slice-done.1
  55.5 18.6 %shard_map.99.others_1_ = f32[2,8,8,2816]{3,2,1,0:T(8,128)S(1)} custom-call(s32[2]{0:T(128)S(1)} %pad_add_fusion.base_ref, f32[8,24,2816]{2,1,0:T(8,128)S(1)} %get-tuple-element.15.field_ref, f32[7,8,8,2816]{3,2,1,0:T(8,128)S(1)} %bitcast.9, bf16[2,2,24,2816]{3,2,1,0:T(8,128)(2,1)S(1)} %collective-permute-done.1.others_0_), custom_call_target="tpu_custom_call" | custom-call | flops 90112000 | bytes 7208960 | tf_op jit(solution)/shard_map/pallas_call | solution.py:357
  74.1 16.6 %shard_map.100 = (bf16[2,8,8,2816]{3,2,1,0:T(8,128)(2,1)}, f32[2,8,8,2816]{3,2,1,0:T(8,128)}) custom-call(s32[2]{0:T(128)S(1)} %pad_add_fusion.base_ref, f32[8,24,2816]{2,1,0:T(8,128)S(1)} %get-tuple-element.12.field_ref, f32[7,8,8,2816]{3,2,1,0:T(8,128)S(1)} %bitcast.9, bf16[2,2,24,2816]{3,2,1,0:T(8,128)(2,1)S(1)} %collective-permute-done.1.others_0_, ...), custom_call_target="tpu_custom_call" | custom-call | flops 90112000 | bytes 7208960 | tf_op jit(solution)/shard_map/pallas_call | solution.py:357
  (1 shorter events, 0.0 us)
Async XLA Ops:
  0.6 4.6 %collective-permute-start = (bf16[4,20,16,641]{3,2,1,0:T(8,128)(2,1)}, bf16[4,20,16,641]{3,2,1,0:T(8,128)(2,1)S(1)}, u32[]{:S(2)}, u32[]{:S(2)}) collective-permute-start(bf16[4,20,16,641]{3,2,1,0:T(8,128)(2,1)} %bitcast.12), channel_id=1, source_target_pairs={{0,1},{1,0},{2,3},{3,2},{4,5},{5,4},{6,7},{7,6},{8,9},{9,8},{10,11... | collective-permute-start | bytes 4922888 | tf_op jit(solution)/shard_map/ppermute | solution.py:730
  5.2 1.3 %copy-start.6 = (bf16[4,20,16,641]{3,2,1,0:T(8,128)(2,1)}, bf16[4,20,16,641]{3,2,1,0:T(8,128)(2,1)S(1)}, u32[]{:S(2)}) copy-start(bf16[4,20,16,641]{3,2,1,0:T(8,128)(2,1)S(1)} %collective-permute-done.others_1_) | copy-start | bytes 4922884
  6.5 14.9 %copy-start.1 = (s32[3,8,8,2816]{3,2,1,0:T(8,128)S(1)}, s32[3,8,8,2816]{3,2,1,0:T(8,128)}, u32[]{:S(2)}) copy-start(s32[3,8,8,2816]{3,2,1,0:T(8,128)} %cells_ref.1) | copy-start | bytes 6488068
  14.5 31.1 %copy-start.4 = (f32[384,128]{1,0:T(8,128)S(1)}, f32[384,128]{1,0:T(8,128)}, u32[]{:S(2)}) copy-start(f32[384,128]{1,0:T(8,128)} %constant.20.clone.lane_ref) | copy-start | bytes 589828
  14.5 31.1 %copy-start.5 = (bf16[384,128]{1,0:T(8,128)(2,1)S(1)}, bf16[384,128]{1,0:T(8,128)(2,1)}, u32[]{:S(2)}) copy-start(bf16[384,128]{1,0:T(8,128)(2,1)} %constant.19.clone.owner_ref) | copy-start | bytes 294916
  14.5 31.1 %all-to-all-start = ((bf16[16,256,128]{2,1,0:T(8,128)(2,1)}), bf16[16,256,128]{2,1,0:T(8,128)(2,1)S(1)}, u32[]{:S(2)}, u32[]{:S(2)}) async-start(bf16[16,256,128]{2,1,0:T(8,128)(2,1)} %get-tuple-element.11), calls=%async_computation | async-start | bytes 2097152 | tf_op jit(solution)/shard_map/all_to_all | solution.py:721
  21.4 1.0 %copy-start.2 = (bf16[8,8,2816]{2,1,0:T(8,128)(2,1)S(1)}, bf16[8,8,2816]{2,1,0:T(8,128)(2,1)}, u32[]{:S(2)}) copy-start(bf16[8,8,2816]{2,1,0:T(8,128)(2,1)} %eta_ref.1) | copy-start | bytes 1081348
  22.4 0.7 copy-start.3
  24.4 2.2 %copy-start = (f32[7,8,8,2816]{3,2,1,0:T(8,128)}, f32[7,8,8,2816]{3,2,1,0:T(8,128)S(1)}, u32[]{:S(2)}) copy-start(f32[7,8,8,2816]{3,2,1,0:T(8,128)S(1)} %get-tuple-element.13.points_ref) | copy-start | bytes 15138820
  45.6 9.9 %slice-start = ((s8[5046272]{0:T(1024)(128)(4,1)}), s8[4194304]{0:T(1024)(128)(4,1)S(1)}, s32[]{:S(2)}) async-start(s8[5046272]{0:T(1024)(128)(4,1)} %bitcast.8), calls=%async_computation.1 | async-start | bytes 8388608
  45.6 9.9 %slice-start.1 = ((s8[5046272]{0:T(1024)(128)(4,1)}), s8[851968]{0:T(1024)(128)(4,1)S(1)}, s32[]{:S(2)}) async-start(s8[5046272]{0:T(1024)(128)(4,1)} %bitcast.8), calls=%async_computation.2 | async-start | bytes 1703936
  51.5 4.0 %collective-permute-start.1 = (bf16[2,2,24,2816]{3,2,1,0:T(8,128)(2,1)S(1)}, bf16[2,2,24,2816]{3,2,1,0:T(8,128)(2,1)S(1)}, u32[]{:S(2)}, u32[]{:S(2)}) collective-permute-start(bf16[2,2,24,2816]{3,2,1,0:T(8,128)(2,1)S(1)} %bitcast.10), channel_id=1, source_target_pairs={{0,1},{1,0},{2,3},{3,2},{4,5},{5,4},{6,7},{7,6},{8,9},{9,8},{10,11... | collective-permute-start | bytes 1622024 | tf_op jit(solution)/shard_map/ppermute | solution.py:380

commit v14 on v13

--- a/solution.py
+++ b/solution.py
@@ -351,7 +351,7 @@
 def interpolation_call(levels_body, base, number, fields, points, nears, extra, out_dtype):
     _, levels, rows, lon_total = points.shape
     count = levels * rows * lon_total
-    together = next(n for n in (4, 2, 1) if levels % n == 0)
+    together = 2 if levels % 2 == 0 else 1
     scratch = pltpu.VMEM(((levels + 2 * HALO) * 5 * STACK, LANES), jnp.float32)
     in_vmem = pl.BlockSpec(memory_space=pltpu.VMEM)
     return pl.pallas_call(
@@ -395,10 +395,10 @@
 
 
 def legendre_kernel(numbers_ref, codes_ref, spectra_ref, *others):
-    table_count = (len(others) - 9) // 2
+    table_count = (len(others) - 7) // 2
     sources, others = (spectra_ref,) + others[:table_count], others[table_count:]
-    out_ref, done_ref, sums, table_tail, column_tail, staged = others[:6]
-    targets, arrivals, departures = others[6:-2], others[-2], others[-1]
+    out_ref, done_ref, sums, table_tail, column_tail = others[:5]
+    targets, arrivals = others[5:-1], others[-1]
     spectra_here, tables = targets[0], targets[1:]
     _, pairs, level_fields, degrees = spectra_ref.shape
     group = table_tail.shape[0]
@@ -495,15 +495,7 @@
 
     @pl.when(step == pl.num_programs(0) - 1)
     def _():
-        leaving = []
-        for band in range(bands):
-            staged[band] = sums[band * block : (band + 1) * block, :].astype(jnp.bfloat16)
-            leaving.append(
-                pltpu.make_async_copy(staged.at[band], out_ref.at[band], departures.at[band])
-            )
-            leaving[-1].start()
-        for copy in leaving:
-            copy.wait()
+        out_ref[...] = sums[...].astype(jnp.bfloat16).reshape(out_ref.shape)
 
 
 def block_rows(pairs):
@@ -537,16 +529,14 @@
             in_hbm,
         ]
         + [in_hbm] * len(tables),
-        out_specs=(in_hbm, in_vmem),
+        out_specs=(in_vmem, in_vmem),
         scratch_shapes=[
             pltpu.VMEM((bands * block, LANES), jnp.float32),
             pltpu.VMEM((group, ROWS * bands, LANES), jnp.float32),
             pltpu.VMEM((group, 2 * level_fields, LANES), jnp.float32),
-            pltpu.VMEM(shape.shape, shape.dtype),
         ]
         + [pltpu.VMEM(x.shape, x.dtype) for x in (spectra,) + tables]
-        + [pltpu.SemaphoreType.DMA((1 + len(tables), pairs // group))]
-        + [pltpu.SemaphoreType.DMA((bands,))],
+        + [pltpu.SemaphoreType.DMA((1 + len(tables), pairs // group))],
         compiler_params=pltpu.CompilerParams(vmem_limit_bytes=60 * 1024 * 1024),
         cost_estimate=pl.CostEstimate(
             flops=2 * ROWS * bands * 4 * level_fields * pairs * degrees,

time: 91.1 us -> 89.6 us (0.984)
  Pallas kernels: 51.6 us -> 50.1 us
where the time goes in v14:
time: 89.6 us; the launch traced here: 89.2 us
  Pallas kernels  50.1 us (56%)
  waiting for transfers between devices  20.6 us (23%)
  starting transfers between devices  10 us (11%)
  local copies, waits for them, and re-layouts  6.39 us (7%)
  other arithmetic  1.38 us (2%)
    pallas_call x2, Pallas kernels, interpolation_call(): pl.pallas_call(functools.partial(interpolation_kernel, levels_body, toget...  34.2 us
    all_to_all x1, waiting for transfers between devices, exchange(): return lax.all_to_all(sums, 'band', split_axis=0, concat_axis=0, tiled=True)  18.9 us
    pallas_call x1, Pallas kernels, legendre_call(): pl.pallas_call(legendre_kernel, grid=(pairs // group,), out_shape=(shape,...  7.4 us
    all_to_all x1, starting transfers between devices, exchange(): return lax.all_to_all(sums, 'band', split_axis=0, concat_axis=0, tiled=True)  6.81 us
    pallas_call x1, Pallas kernels, fourier_call(): pl.pallas_call(functools.partial(fourier_kernel, pairs, levels), out_shap...  5.87 us
    unnamed x18, local copies, waits for them, and re-layouts  5.22 us
    ppermute x1, starting transfers between devices, swap_levels(): return (lax.ppermute(send[0], 'lev', [(0, 1), (1, 0)]),)  2.48 us
  transfers between devices with their start and end apart: 3, of which 3 were waited for; matrix products, arithmetic and copies ran while one was open for 3% of the time, Pallas kernels for 3%

profile of v14, /device:TPU:9, one launch (start us, length us, event | category | flops | bytes accessed | tf_op | source)
XLA Modules:
  0.0 89.2 jit_solution(1381176357031448321)
XLA Ops:
  0.6 0.7 collective-permute-start
  1.4 1.2 %pad_bitcast_fusion.numbers_ref = s32[1,128]{1,0:T(1,128)} fusion(s32[20]{0:T(128)} %param.10), kind=kLoop, calls=%fused_computation.2 | loop fusion | bytes 592 | tf_op jit(solution)/shard_map/broadcast_in_dim | solution.py:518
  2.5 1.2 %shard_map.95.codes_ref = s32[1,128]{1,0:T(1,128)} custom-call(s32[1,128]{1,0:T(1,128)} %pad_bitcast_fusion.numbers_ref), custom_call_target="tpu_custom_call" | custom-call | bytes 4000000 | tf_op jit(solution)/shard_map/pallas_call | solution.py:511
  3.8 1.3 %pad_add_fusion.1.numbers_ref = s32[21]{0:T(128)} fusion(s32[20]{0:T(128)} %param.10, s32[1]{0:T(128)} %bitcast.2), kind=kLoop, calls=%fused_computation.1 | loop fusion | flops 21 | bytes 168 | tf_op jit(solution)/shard_map/concatenate | solution.py:510
  5.1 0.1 collective-permute-done.others_1_
  5.2 0.0 copy-start.6
  5.2 1.3 %copy-done.6 = bf16[4,20,16,641]{3,2,1,0:T(8,128)(2,1)} copy-done((bf16[4,20,16,641]{3,2,1,0:T(8,128)(2,1)}, bf16[4,20,16,641]{3,2,1,0:T(8,128)(2,1)S(1)}, u32[]{:S(2)}) %copy-start.6) | copy-done | bytes 1640984
  6.5 0.0 copy-start.1
  6.5 7.4 %shard_map.96 = (bf16[16,256,128]{2,1,0:T(8,128)(2,1)}, f32[8,128]{1,0:T(8,128)}) custom-call(s32[21]{0:T(128)} %pad_add_fusion.1.numbers_ref, s32[1,128]{1,0:T(1,128)} %shard_map.95.codes_ref, bf16[2,20,32,641]{3,2,1,0:T(8,128)(2,1)} %bitcast.11, bf16[4,20,16,641]{3,2,1,0:T(8,128)(2,1)} %bitcast.13, bf16[4,20,16,641]{3,2,1,0:T(8,128)(2,1)} %copy-done.6), custom_call_target="tpu_custom_call" | custom-call | flops 420085760 | bytes 8000000 | tf_op jit(solution)/shard_map/pallas_call | solution.py:522
  13.9 0.0 copy-start.4
  13.9 0.0 copy-start.5
  13.9 6.8 %all-to-all-start = ((bf16[16,256,128]{2,1,0:T(8,128)(2,1)}), bf16[16,256,128]{2,1,0:T(8,128)(2,1)S(1)}, u32[]{:S(2)}, u32[]{:S(2)}) async-start(bf16[16,256,128]{2,1,0:T(8,128)(2,1)} %get-tuple-element.11), calls=%async_computation | async-start | bytes 2097152 | tf_op jit(solution)/shard_map/all_to_all | solution.py:711
  20.7 0.1 pad_add_fusion.base_ref
  20.8 0.0 copy-done.1
  20.8 0.0 copy-start.2
  20.8 1.0 %copy-done.2 = bf16[8,8,2816]{2,1,0:T(8,128)(2,1)S(1)} copy-done((bf16[8,8,2816]{2,1,0:T(8,128)(2,1)S(1)}, bf16[8,8,2816]{2,1,0:T(8,128)(2,1)}, u32[]{:S(2)}) %copy-start.2) | copy-done | bytes 360472
  21.8 0.0 copy-start.3
  21.8 0.7 copy-done.3
  22.5 1.4 %shard_map.97 = (f32[7,8,8,2816]{3,2,1,0:T(8,128)S(1)}, f32[8,128]{1,0:T(8,128)S(1)}) custom-call(s32[2]{0:T(128)S(1)} %pad_add_fusion.base_ref, f32[8,128]{1,0:T(8,128)S(1)} %copy-done.3, bf16[8,8,2816]{2,1,0:T(8,128)(2,1)S(1)} %copy-done.2, s32[3,8,8,2816]{3,2,1,0:T(8,128)S(1)} %copy-done.1), custom_call_target="tpu_custom_call" | custom-call | flops 7208960 | bytes 20000000 | tf_op jit(solution)/shard_map/pallas_call | solution.py:211
  23.8 0.0 copy-start
  23.8 2.2 %copy-done = f32[7,8,8,2816]{3,2,1,0:T(8,128)} copy-done((f32[7,8,8,2816]{3,2,1,0:T(8,128)}, f32[7,8,8,2816]{3,2,1,0:T(8,128)S(1)}, u32[]{:S(2)}) %copy-start) | copy-done | bytes 5046296
  26.1 18.9 %all-to-all-done.sums_ref = bf16[16,256,128]{2,1,0:T(8,128)(2,1)S(1)} async-done(((bf16[16,256,128]{2,1,0:T(8,128)(2,1)}), bf16[16,256,128]{2,1,0:T(8,128)(2,1)S(1)}, u32[]{:S(2)}, u32[]{:S(2)}) %all-to-all-start) | async-done | bytes 1048608 | tf_op jit(solution)/shard_map/all_to_all | solution.py:711
  45.0 0.0 slice-start
  45.0 0.0 copy-done.4
  45.0 0.0 copy-done.5
  45.0 0.0 slice-start.1
  45.0 5.9 %shard_map.98 = (f32[8,24,2816]{2,1,0:T(8,128)S(1)}, f32[8,24,2816]{2,1,0:T(8,128)S(1)}, bf16[1,2,2,24,2816]{4,3,2,1,0:T(8,128)(2,1)S(1)}) custom-call(s32[2]{0:T(128)S(1)} %pad_add_fusion.base_ref, f32[8,128]{1,0:T(8,128)S(1)} %get-tuple-element.10.after_ref, bf16[16,256,128]{2,1,0:T(8,128)(2,1)S(1)} %all-to-all-done.sums_ref, ...), custom_call_target="tpu_custom_call" | custom-call | flops 8000000000 | bytes 8000000 | tf_op jit(solution)/shard_map/pallas_call | solution.py:688
  50.9 2.5 %collective-permute-start.1 = (bf16[2,2,24,2816]{3,2,1,0:T(8,128)(2,1)S(1)}, bf16[2,2,24,2816]{3,2,1,0:T(8,128)(2,1)S(1)}, u32[]{:S(2)}, u32[]{:S(2)}) collective-permute-start(bf16[2,2,24,2816]{3,2,1,0:T(8,128)(2,1)S(1)} %bitcast.10), channel_id=1, source_target_pairs={{0,1},{1,0},{2,3},{3,2},{4,5},{5,4},{6,7},{7,6},{8,9},{9,8},{10,11... | collective-permute-start | bytes 1622024 | tf_op jit(solution)/shard_map/ppermute | solution.py:380
  53.4 1.6 %collective-permute-done.1.others_0_ = bf16[2,2,24,2816]{3,2,1,0:T(8,128)(2,1)S(1)} collective-permute-done((bf16[2,2,24,2816]{3,2,1,0:T(8,128)(2,1)S(1)}, bf16[2,2,24,2816]{3,2,1,0:T(8,128)(2,1)S(1)}, u32[]{:S(2)}, u32[]{:S(2)}) %collective-permute-start.1) | collective-permute-done | bytes 540704 | tf_op jit(solution)/shard_map/ppermute | solution.py:380
  54.9 0.0 slice-done
  54.9 0.0 slice-done.1
  54.9 18.0 %shard_map.99.others_1_ = f32[2,8,8,2816]{3,2,1,0:T(8,128)S(1)} custom-call(s32[2]{0:T(128)S(1)} %pad_add_fusion.base_ref, f32[8,24,2816]{2,1,0:T(8,128)S(1)} %get-tuple-element.15.field_ref, f32[7,8,8,2816]{3,2,1,0:T(8,128)S(1)} %bitcast.9, bf16[2,2,24,2816]{3,2,1,0:T(8,128)(2,1)S(1)} %collective-permute-done.1.others_0_), custom_call_target="tpu_custom_call" | custom-call | flops 90112000 | bytes 7208960 | tf_op jit(solution)/shard_map/pallas_call | solution.py:357
  73.0 16.2 %shard_map.100 = (bf16[2,8,8,2816]{3,2,1,0:T(8,128)(2,1)}, f32[2,8,8,2816]{3,2,1,0:T(8,128)}) custom-call(s32[2]{0:T(128)S(1)} %pad_add_fusion.base_ref, f32[8,24,2816]{2,1,0:T(8,128)S(1)} %get-tuple-element.12.field_ref, f32[7,8,8,2816]{3,2,1,0:T(8,128)S(1)} %bitcast.9, bf16[2,2,24,2816]{3,2,1,0:T(8,128)(2,1)S(1)} %collective-permute-done.1.others_0_, ...), custom_call_target="tpu_custom_call" | custom-call | flops 90112000 | bytes 7208960 | tf_op jit(solution)/shard_map/pallas_call | solution.py:357
  (1 shorter events, 0.0 us)
Async XLA Ops:
  0.6 4.6 %collective-permute-start = (bf16[4,20,16,641]{3,2,1,0:T(8,128)(2,1)}, bf16[4,20,16,641]{3,2,1,0:T(8,128)(2,1)S(1)}, u32[]{:S(2)}, u32[]{:S(2)}) collective-permute-start(bf16[4,20,16,641]{3,2,1,0:T(8,128)(2,1)} %bitcast.12), channel_id=1, source_target_pairs={{0,1},{1,0},{2,3},{3,2},{4,5},{5,4},{6,7},{7,6},{8,9},{9,8},{10,11... | collective-permute-start | bytes 4922888 | tf_op jit(solution)/shard_map/ppermute | solution.py:720
  5.2 1.3 %copy-start.6 = (bf16[4,20,16,641]{3,2,1,0:T(8,128)(2,1)}, bf16[4,20,16,641]{3,2,1,0:T(8,128)(2,1)S(1)}, u32[]{:S(2)}) copy-start(bf16[4,20,16,641]{3,2,1,0:T(8,128)(2,1)S(1)} %collective-permute-done.others_1_) | copy-start | bytes 4922884
  6.5 14.3 %copy-start.1 = (s32[3,8,8,2816]{3,2,1,0:T(8,128)S(1)}, s32[3,8,8,2816]{3,2,1,0:T(8,128)}, u32[]{:S(2)}) copy-start(s32[3,8,8,2816]{3,2,1,0:T(8,128)} %cells_ref.1) | copy-start | bytes 6488068
  13.9 31.1 %copy-start.4 = (f32[384,128]{1,0:T(8,128)S(1)}, f32[384,128]{1,0:T(8,128)}, u32[]{:S(2)}) copy-start(f32[384,128]{1,0:T(8,128)} %constant.20.clone.lane_ref) | copy-start | bytes 589828
  13.9 31.1 %copy-start.5 = (bf16[384,128]{1,0:T(8,128)(2,1)S(1)}, bf16[384,128]{1,0:T(8,128)(2,1)}, u32[]{:S(2)}) copy-start(bf16[384,128]{1,0:T(8,128)(2,1)} %constant.19.clone.owner_ref) | copy-start | bytes 294916
  13.9 31.1 %all-to-all-start = ((bf16[16,256,128]{2,1,0:T(8,128)(2,1)}), bf16[16,256,128]{2,1,0:T(8,128)(2,1)S(1)}, u32[]{:S(2)}, u32[]{:S(2)}) async-start(bf16[16,256,128]{2,1,0:T(8,128)(2,1)} %get-tuple-element.11), calls=%async_computation | async-start | bytes 2097152 | tf_op jit(solution)/shard_map/all_to_all | solution.py:711
  20.8 1.0 %copy-start.2 = (bf16[8,8,2816]{2,1,0:T(8,128)(2,1)S(1)}, bf16[8,8,2816]{2,1,0:T(8,128)(2,1)}, u32[]{:S(2)}) copy-start(bf16[8,8,2816]{2,1,0:T(8,128)(2,1)} %eta_ref.1) | copy-start | bytes 1081348
  21.8 0.7 copy-start.3
  23.8 2.2 %copy-start = (f32[7,8,8,2816]{3,2,1,0:T(8,128)}, f32[7,8,8,2816]{3,2,1,0:T(8,128)S(1)}, u32[]{:S(2)}) copy-start(f32[7,8,8,2816]{3,2,1,0:T(8,128)S(1)} %get-tuple-element.13.points_ref) | copy-start | bytes 15138820
  45.0 9.9 %slice-start = ((s8[5046272]{0:T(1024)(128)(4,1)}), s8[4194304]{0:T(1024)(128)(4,1)S(1)}, s32[]{:S(2)}) async-start(s8[5046272]{0:T(1024)(128)(4,1)} %bitcast.8), calls=%async_computation.1 | async-start | bytes 8388608
  45.0 9.9 %slice-start.1 = ((s8[5046272]{0:T(1024)(128)(4,1)}), s8[851968]{0:T(1024)(128)(4,1)S(1)}, s32[]{:S(2)}) async-start(s8[5046272]{0:T(1024)(128)(4,1)} %bitcast.8), calls=%async_computation.2 | async-start | bytes 1703936
  50.9 4.0 %collective-permute-start.1 = (bf16[2,2,24,2816]{3,2,1,0:T(8,128)(2,1)S(1)}, bf16[2,2,24,2816]{3,2,1,0:T(8,128)(2,1)S(1)}, u32[]{:S(2)}, u32[]{:S(2)}) collective-permute-start(bf16[2,2,24,2816]{3,2,1,0:T(8,128)(2,1)S(1)} %bitcast.10), channel_id=1, source_target_pairs={{0,1},{1,0},{2,3},{3,2},{4,5},{5,4},{6,7},{7,6},{8,9},{9,8},{10,11... | collective-permute-start | bytes 1622024 | tf_op jit(solution)/shard_map/ppermute | solution.py:380

commit v15 on v14

--- a/solution.py
+++ b/solution.py
@@ -351,7 +351,7 @@
 def interpolation_call(levels_body, base, number, fields, points, nears, extra, out_dtype):
     _, levels, rows, lon_total = points.shape
     count = levels * rows * lon_total
-    together = 2 if levels % 2 == 0 else 1
+    together = 1
     scratch = pltpu.VMEM(((levels + 2 * HALO) * 5 * STACK, LANES), jnp.float32)
     in_vmem = pl.BlockSpec(memory_space=pltpu.VMEM)
     return pl.pallas_call(
@@ -495,11 +495,12 @@
 
     @pl.when(step == pl.num_programs(0) - 1)
     def _():
-        out_ref[...] = sums[...].astype(jnp.bfloat16).reshape(out_ref.shape)
+        for band in range(bands):
+            out_ref[band] = sums[band * block : (band + 1) * block, :].astype(jnp.bfloat16)
 
 
 def block_rows(pairs):
-    return up_to(up_to(pairs * TALL, ROWS) + 2, 16)
+    return up_to(up_to(pairs * TALL, ROWS) + 2, ROWS)
 
 
 def legendre_call(pairing, spectra, tables):
@@ -604,7 +605,8 @@
     blocks = padded // LANES
     fields = 4 * levels
     room = up_to(pairs, ROWS)
-    flat[...] = sums_ref[...].astype(jnp.float32).reshape(bands * block, width)
+    for band in range(bands):
+        flat[band * block : (band + 1) * block, :] = sums_ref[band].astype(jnp.float32)
     gathered[...] = jnp.zeros(gathered.shape, jnp.float32)
     code_row = up_to(pairs * TALL, ROWS)
     place = pair_places(

time: 89.6 us -> 90.7 us (1.012)
  local copies, waits for them, and re-layouts: 6.39 us -> 7.62 us
    unnamed x18, local copies, waits for them, and re-layouts: 5.22 us -> 6.46 us
where the time goes in v15:
time: 90.7 us; the launch traced here: 90.3 us
  Pallas kernels  49.8 us (55%)
  waiting for transfers between devices  20.9 us (23%)
  starting transfers between devices  10 us (11%)
  local copies, waits for them, and re-layouts  7.62 us (8%)
  other arithmetic  1.38 us (2%)
    pallas_call x2, Pallas kernels, interpolation_call(): pl.pallas_call(functools.partial(interpolation_kernel, levels_body, toget...  34.8 us
    all_to_all x1, waiting for transfers between devices, exchange(): return lax.all_to_all(sums, 'band', split_axis=0, concat_axis=0, tiled=True)  19.2 us
    pallas_call x1, Pallas kernels, legendre_call(): pl.pallas_call(legendre_kernel, grid=(pairs // group,), out_shape=(shape,...  6.98 us
    all_to_all x1, starting transfers between devices, exchange(): return lax.all_to_all(sums, 'band', split_axis=0, concat_axis=0, tiled=True)  6.8 us
    unnamed x18, local copies, waits for them, and re-layouts  6.46 us
    pallas_call x1, Pallas kernels, fourier_call(): pl.pallas_call(functools.partial(fourier_kernel, pairs, levels), out_shap...  5.37 us
    ppermute x1, starting transfers between devices, swap_levels(): return (lax.ppermute(send[0], 'lev', [(0, 1), (1, 0)]),)  2.46 us
  transfers between devices with their start and end apart: 3, of which 3 were waited for; matrix products, arithmetic and copies ran while one was open for 3% of the time, Pallas kernels for 3%

profile of v15, /device:TPU:9, one launch (start us, length us, event | category | flops | bytes accessed | tf_op | source)
XLA Modules:
  0.0 90.3 jit_solution(8244171532053891215)
XLA Ops:
  0.6 0.7 collective-permute-start
  1.4 1.2 %pad_bitcast_fusion.numbers_ref = s32[1,128]{1,0:T(1,128)} fusion(s32[20]{0:T(128)} %param.10), kind=kLoop, calls=%fused_computation.2 | loop fusion | bytes 592 | tf_op jit(solution)/shard_map/broadcast_in_dim | solution.py:519
  2.5 1.2 %shard_map.95.codes_ref = s32[1,128]{1,0:T(1,128)} custom-call(s32[1,128]{1,0:T(1,128)} %pad_bitcast_fusion.numbers_ref), custom_call_target="tpu_custom_call" | custom-call | bytes 4000000 | tf_op jit(solution)/shard_map/pallas_call | solution.py:512
  3.8 1.3 %pad_add_fusion.1.numbers_ref = s32[21]{0:T(128)} fusion(s32[20]{0:T(128)} %param.10, s32[1]{0:T(128)} %bitcast.2), kind=kLoop, calls=%fused_computation.1 | loop fusion | flops 21 | bytes 168 | tf_op jit(solution)/shard_map/concatenate | solution.py:511
  5.1 0.1 collective-permute-done.others_1_
  5.2 0.0 copy-start.6
  5.2 1.3 %copy-done.6 = bf16[4,20,16,641]{3,2,1,0:T(8,128)(2,1)} copy-done((bf16[4,20,16,641]{3,2,1,0:T(8,128)(2,1)}, bf16[4,20,16,641]{3,2,1,0:T(8,128)(2,1)S(1)}, u32[]{:S(2)}) %copy-start.6) | copy-done | bytes 1640984
  6.5 0.0 copy-start.1
  6.5 7.0 %shard_map.96 = (bf16[16,248,128]{2,1,0:T(8,128)(2,1)}, f32[8,128]{1,0:T(8,128)}) custom-call(s32[21]{0:T(128)} %pad_add_fusion.1.numbers_ref, s32[1,128]{1,0:T(1,128)} %shard_map.95.codes_ref, bf16[2,20,32,641]{3,2,1,0:T(8,128)(2,1)} %bitcast.11, bf16[4,20,16,641]{3,2,1,0:T(8,128)(2,1)} %bitcast.13, bf16[4,20,16,641]{3,2,1,0:T(8,128)(2,1)} %copy-done.6), custom_call_target="tpu_custom_call" | custom-call | flops 420085760 | bytes 8000000 | tf_op jit(solution)/shard_map/pallas_call | solution.py:523
  13.5 0.0 copy-start.2
  13.5 6.8 %all-to-all-start = ((bf16[16,248,128]{2,1,0:T(8,128)(2,1)}), bf16[16,248,128]{2,1,0:T(8,128)(2,1)S(1)}, u32[]{:S(2)}, u32[]{:S(2)}) async-start(bf16[16,248,128]{2,1,0:T(8,128)(2,1)} %get-tuple-element.11), calls=%async_computation | async-start | bytes 2031616 | tf_op jit(solution)/shard_map/all_to_all | solution.py:713
  20.3 0.1 pad_add_fusion.base_ref
  20.4 0.0 copy-done.1
  20.4 0.0 copy-done.2
  20.4 0.0 copy-start.3
  20.4 0.7 copy-done.3
  21.0 1.4 %shard_map.97 = (f32[7,8,8,2816]{3,2,1,0:T(8,128)S(1)}, f32[8,128]{1,0:T(8,128)S(1)}) custom-call(s32[2]{0:T(128)S(1)} %pad_add_fusion.base_ref, f32[8,128]{1,0:T(8,128)S(1)} %copy-done.3, bf16[8,8,2816]{2,1,0:T(8,128)(2,1)S(1)} %copy-done.2, s32[3,8,8,2816]{3,2,1,0:T(8,128)S(1)} %copy-done.1), custom_call_target="tpu_custom_call" | custom-call | flops 7208960 | bytes 20000000 | tf_op jit(solution)/shard_map/pallas_call | solution.py:211
  22.4 0.0 copy-start
  22.4 2.2 %copy-done = f32[7,8,8,2816]{3,2,1,0:T(8,128)} copy-done((f32[7,8,8,2816]{3,2,1,0:T(8,128)}, f32[7,8,8,2816]{3,2,1,0:T(8,128)S(1)}, u32[]{:S(2)}) %copy-start) | copy-done | bytes 5046296
  24.6 19.2 %all-to-all-done.sums_ref = bf16[16,248,128]{2,1,0:T(8,128)(2,1)S(1)} async-done(((bf16[16,248,128]{2,1,0:T(8,128)(2,1)}), bf16[16,248,128]{2,1,0:T(8,128)(2,1)S(1)}, u32[]{:S(2)}, u32[]{:S(2)}) %all-to-all-start) | async-done | bytes 1015840 | tf_op jit(solution)/shard_map/all_to_all | solution.py:713
  43.9 0.0 slice-start
  43.9 0.0 copy-start.4
  43.9 1.1 %copy-done.4 = f32[384,128]{1,0:T(8,128)S(1)} copy-done((f32[384,128]{1,0:T(8,128)S(1)}, f32[384,128]{1,0:T(8,128)}, u32[]{:S(2)}) %copy-start.4) | copy-done | bytes 196632
  44.9 0.0 copy-start.5
  44.9 1.1 %copy-done.5 = bf16[384,128]{1,0:T(8,128)(2,1)S(1)} copy-done((bf16[384,128]{1,0:T(8,128)(2,1)S(1)}, bf16[384,128]{1,0:T(8,128)(2,1)}, u32[]{:S(2)}) %copy-start.5) | copy-done | bytes 98328
  46.1 0.0 slice-start.1
  46.1 5.4 %shard_map.98 = (f32[8,24,2816]{2,1,0:T(8,128)S(1)}, f32[8,24,2816]{2,1,0:T(8,128)S(1)}, bf16[1,2,2,24,2816]{4,3,2,1,0:T(8,128)(2,1)S(1)}) custom-call(s32[2]{0:T(128)S(1)} %pad_add_fusion.base_ref, f32[8,128]{1,0:T(8,128)S(1)} %get-tuple-element.10.after_ref, bf16[16,248,128]{2,1,0:T(8,128)(2,1)S(1)} %all-to-all-done.sums_ref, ...), custom_call_target="tpu_custom_call" | custom-call | flops 8000000000 | bytes 8000000 | tf_op jit(solution)/shard_map/pallas_call | solution.py:690
  51.5 2.5 %collective-permute-start.1 = (bf16[2,2,24,2816]{3,2,1,0:T(8,128)(2,1)S(1)}, bf16[2,2,24,2816]{3,2,1,0:T(8,128)(2,1)S(1)}, u32[]{:S(2)}, u32[]{:S(2)}) collective-permute-start(bf16[2,2,24,2816]{3,2,1,0:T(8,128)(2,1)S(1)} %bitcast.10), channel_id=1, source_target_pairs={{0,1},{1,0},{2,3},{3,2},{4,5},{5,4},{6,7},{7,6},{8,9},{9,8},{10,11... | collective-permute-start | bytes 1622024 | tf_op jit(solution)/shard_map/ppermute | solution.py:380
  53.9 1.6 %collective-permute-done.1.others_0_ = bf16[2,2,24,2816]{3,2,1,0:T(8,128)(2,1)S(1)} collective-permute-done((bf16[2,2,24,2816]{3,2,1,0:T(8,128)(2,1)S(1)}, bf16[2,2,24,2816]{3,2,1,0:T(8,128)(2,1)S(1)}, u32[]{:S(2)}, u32[]{:S(2)}) %collective-permute-start.1) | collective-permute-done | bytes 540704 | tf_op jit(solution)/shard_map/ppermute | solution.py:380
  55.5 0.0 slice-done
  55.5 0.0 slice-done.1
  55.5 18.4 %shard_map.99.others_1_ = f32[2,8,8,2816]{3,2,1,0:T(8,128)S(1)} custom-call(s32[2]{0:T(128)S(1)} %pad_add_fusion.base_ref, f32[8,24,2816]{2,1,0:T(8,128)S(1)} %get-tuple-element.15.field_ref, f32[7,8,8,2816]{3,2,1,0:T(8,128)S(1)} %bitcast.9, bf16[2,2,24,2816]{3,2,1,0:T(8,128)(2,1)S(1)} %collective-permute-done.1.others_0_), custom_call_target="tpu_custom_call" | custom-call | flops 90112000 | bytes 7208960 | tf_op jit(solution)/shard_map/pallas_call | solution.py:357
  73.9 16.4 %shard_map.100 = (bf16[2,8,8,2816]{3,2,1,0:T(8,128)(2,1)}, f32[2,8,8,2816]{3,2,1,0:T(8,128)}) custom-call(s32[2]{0:T(128)S(1)} %pad_add_fusion.base_ref, f32[8,24,2816]{2,1,0:T(8,128)S(1)} %get-tuple-element.12.field_ref, f32[7,8,8,2816]{3,2,1,0:T(8,128)S(1)} %bitcast.9, bf16[2,2,24,2816]{3,2,1,0:T(8,128)(2,1)S(1)} %collective-permute-done.1.others_0_, ...), custom_call_target="tpu_custom_call" | custom-call | flops 90112000 | bytes 7208960 | tf_op jit(solution)/shard_map/pallas_call | solution.py:357
  (1 shorter events, 0.0 us)
Async XLA Ops:
  0.6 4.6 %collective-permute-start = (bf16[4,20,16,641]{3,2,1,0:T(8,128)(2,1)}, bf16[4,20,16,641]{3,2,1,0:T(8,128)(2,1)S(1)}, u32[]{:S(2)}, u32[]{:S(2)}) collective-permute-start(bf16[4,20,16,641]{3,2,1,0:T(8,128)(2,1)} %bitcast.12), channel_id=1, source_target_pairs={{0,1},{1,0},{2,3},{3,2},{4,5},{5,4},{6,7},{7,6},{8,9},{9,8},{10,11... | collective-permute-start | bytes 4922888 | tf_op jit(solution)/shard_map/ppermute | solution.py:722
  5.2 1.3 %copy-start.6 = (bf16[4,20,16,641]{3,2,1,0:T(8,128)(2,1)}, bf16[4,20,16,641]{3,2,1,0:T(8,128)(2,1)S(1)}, u32[]{:S(2)}) copy-start(bf16[4,20,16,641]{3,2,1,0:T(8,128)(2,1)S(1)} %collective-permute-done.others_1_) | copy-start | bytes 4922884
  6.5 13.9 %copy-start.1 = (s32[3,8,8,2816]{3,2,1,0:T(8,128)S(1)}, s32[3,8,8,2816]{3,2,1,0:T(8,128)}, u32[]{:S(2)}) copy-start(s32[3,8,8,2816]{3,2,1,0:T(8,128)} %cells_ref.1) | copy-start | bytes 6488068
  13.5 6.9 %copy-start.2 = (bf16[8,8,2816]{2,1,0:T(8,128)(2,1)S(1)}, bf16[8,8,2816]{2,1,0:T(8,128)(2,1)}, u32[]{:S(2)}) copy-start(bf16[8,8,2816]{2,1,0:T(8,128)(2,1)} %eta_ref.1) | copy-start | bytes 1081348
  13.5 30.4 %all-to-all-start = ((bf16[16,248,128]{2,1,0:T(8,128)(2,1)}), bf16[16,248,128]{2,1,0:T(8,128)(2,1)S(1)}, u32[]{:S(2)}, u32[]{:S(2)}) async-start(bf16[16,248,128]{2,1,0:T(8,128)(2,1)} %get-tuple-element.11), calls=%async_computation | async-start | bytes 2031616 | tf_op jit(solution)/shard_map/all_to_all | solution.py:713
  20.4 0.7 copy-start.3
  22.4 2.2 %copy-start = (f32[7,8,8,2816]{3,2,1,0:T(8,128)}, f32[7,8,8,2816]{3,2,1,0:T(8,128)S(1)}, u32[]{:S(2)}) copy-start(f32[7,8,8,2816]{3,2,1,0:T(8,128)S(1)} %get-tuple-element.13.points_ref) | copy-start | bytes 15138820
  43.9 11.6 %slice-start = ((s8[5046272]{0:T(1024)(128)(4,1)}), s8[4194304]{0:T(1024)(128)(4,1)S(1)}, s32[]{:S(2)}) async-start(s8[5046272]{0:T(1024)(128)(4,1)} %bitcast.8), calls=%async_computation.1 | async-start | bytes 8388608
  43.9 1.1 %copy-start.4 = (f32[384,128]{1,0:T(8,128)S(1)}, f32[384,128]{1,0:T(8,128)}, u32[]{:S(2)}) copy-start(f32[384,128]{1,0:T(8,128)} %constant.20.clone.lane_ref) | copy-start | bytes 589828
  44.9 1.1 %copy-start.5 = (bf16[384,128]{1,0:T(8,128)(2,1)S(1)}, bf16[384,128]{1,0:T(8,128)(2,1)}, u32[]{:S(2)}) copy-start(bf16[384,128]{1,0:T(8,128)(2,1)} %constant.19.clone.owner_ref) | copy-start | bytes 294916
  46.1 9.4 %slice-start.1 = ((s8[5046272]{0:T(1024)(128)(4,1)}), s8[851968]{0:T(1024)(128)(4,1)S(1)}, s32[]{:S(2)}) async-start(s8[5046272]{0:T(1024)(128)(4,1)} %bitcast.8), calls=%async_computation.2 | async-start | bytes 1703936
  51.5 4.0 %collective-permute-start.1 = (bf16[2,2,24,2816]{3,2,1,0:T(8,128)(2,1)S(1)}, bf16[2,2,24,2816]{3,2,1,0:T(8,128)(2,1)S(1)}, u32[]{:S(2)}, u32[]{:S(2)}) collective-permute-start(bf16[2,2,24,2816]{3,2,1,0:T(8,128)(2,1)S(1)} %bitcast.10), channel_id=1, source_target_pairs={{0,1},{1,0},{2,3},{3,2},{4,5},{5,4},{6,7},{7,6},{8,9},{9,8},{10,11... | collective-permute-start | bytes 1622024 | tf_op jit(solution)/shard_map/ppermute | solution.py:380

commit v16 on v15

--- a/solution.py
+++ b/solution.py
@@ -351,7 +351,7 @@
 def interpolation_call(levels_body, base, number, fields, points, nears, extra, out_dtype):
     _, levels, rows, lon_total = points.shape
     count = levels * rows * lon_total
-    together = 1
+    together = 2 if levels % 2 == 0 else 1
     scratch = pltpu.VMEM(((levels + 2 * HALO) * 5 * STACK, LANES), jnp.float32)
     in_vmem = pl.BlockSpec(memory_space=pltpu.VMEM)
     return pl.pallas_call(
@@ -564,36 +564,41 @@
     return table.reshape(4, 2 * padded, lon_total // 2).astype(jnp.bfloat16)
 
 
-def owner_tables(bands, pairs):
+def owner_tables(slots, pairs):
     room = up_to(pairs, ROWS)
-    slots = np.arange(up_to(bands * room, LANES))
-    owner = slots[:, None] // room == np.arange(LANES)[None, :]
-    lane = slots[:, None] % room == np.arange(LANES)[None, :]
-    return owner.astype(jnp.bfloat16), lane.astype(np.float32)
-
-
-def pair_places(flat, owner_ref, lane_ref, codes, bands, block, code_row, pair_total, padded):
+    slot = lax.broadcasted_iota(jnp.int32, (slots, LANES), 0)
+    lane = lax.broadcasted_iota(jnp.int32, (slots, LANES), 1)
+    owner = ((slot.astype(jnp.float32) + 0.5) * (1.0 / room)).astype(jnp.int32)
+    return (
+        jnp.where(owner == lane, 1.0, 0.0).astype(jnp.bfloat16),
+        jnp.where(slot - room * owner == lane, 1.0, 0.0),
+    )
+
+
+def pair_places(flat, codes, bands, block, code_row, pairs, slots, padded):
+    pair_total = bands * pairs
+    owner, own_lane = owner_tables(slots, pairs)
     codes[...] = jnp.zeros(codes.shape, jnp.float32)
     numbers = []
     for part in range(2):
         codes[part, :bands, :] = flat[pl.ds(code_row + part, bands, stride=block), :]
         numbers.append(
             jnp.dot(
-                owner_ref[...],
+                owner,
                 codes[part].astype(jnp.bfloat16),
                 preferred_element_type=jnp.float32,
             )
         )
     pair_id = jnp.sum(
-        (16.0 * numbers[0] + numbers[1]) * lane_ref[...], axis=1, keepdims=True
+        (16.0 * numbers[0] + numbers[1]) * own_lane, axis=1, keepdims=True
     ).astype(jnp.int32)
     place = jnp.right_shift(pair_id, 1) + (pair_id & 1) * (pair_total // 2)
-    columns = lax.broadcasted_iota(jnp.int32, (owner_ref.shape[0], padded), 1)
+    columns = lax.broadcasted_iota(jnp.int32, (slots, padded), 1)
     return jnp.where(columns == place, 1.0, 0.0).astype(jnp.bfloat16)
 
 
 def fourier_kernel(
-    pairs, levels, base_ref, after_ref, sums_ref, owner_ref, lane_ref, table_source, *others
+    pairs, levels, base_ref, after_ref, sums_ref, table_source, *others
 ):
     field_refs, send_ref, others = others[:2], others[2], others[3:]
     codes, flat, gathered, lhs, table_ref, arrival_sem = others
@@ -609,9 +614,7 @@
         flat[band * block : (band + 1) * block, :] = sums_ref[band].astype(jnp.float32)
     gathered[...] = jnp.zeros(gathered.shape, jnp.float32)
     code_row = up_to(pairs * TALL, ROWS)
-    place = pair_places(
-        flat, owner_ref, lane_ref, codes, bands, block, code_row, pair_total, padded
-    )
+    place = pair_places(flat, codes, bands, block, code_row, pairs, gathered.shape[1], padded)
     low = lax.broadcasted_iota(jnp.int32, (fields, padded), 1) < pair_total // 2
     middle = fields * ROWS
     for row in range(TALL):
@@ -681,7 +684,7 @@
 def fourier_call(base, after, sums, table, pairs, levels, lon_total):
     bands, block, width = sums.shape
     padded = up_to(bands * pairs, LANES)
-    extra = [jnp.asarray(x) for x in owner_tables(bands, pairs)]
+    slots = up_to(bands * up_to(pairs, ROWS), LANES)
     sends = 1 if lax.axis_size("lev") == 2 else 2
     field_shape = (levels, 3 * ROWS, lon_total)
     field = jax.ShapeDtypeStruct(field_shape, jnp.float32)
@@ -691,13 +694,13 @@
         functools.partial(fourier_kernel, pairs, levels),
         out_shape=(field, field, send),
         in_specs=[pl.BlockSpec(memory_space=pltpu.SMEM)]
-        + [in_vmem] * 4
+        + [in_vmem] * 2
         + [pl.BlockSpec(memory_space=pl.ANY)],
         out_specs=(in_vmem,) * 3,
         scratch_shapes=[
             pltpu.VMEM((2, LANES, LANES), jnp.float32),
             pltpu.VMEM((bands * block, width), jnp.float32),
-            pltpu.VMEM((2, extra[0].shape[0], width), jnp.float32),
+            pltpu.VMEM((2, slots, width), jnp.float32),
             pltpu.VMEM((2, 2 * padded // LANES, 4 * levels * TALL, LANES), jnp.float32),
             pltpu.VMEM((2,) + table.shape[1:], table.dtype),
             pltpu.SemaphoreType.DMA,
@@ -706,7 +709,7 @@
         cost_estimate=pl.CostEstimate(
             flops=8_000_000_000, bytes_accessed=8_000_000, transcendentals=0
         ),
-    )(base, after, sums, *extra, table)
+    )(base, after, sums, table)
 
 
 def exchange(sums):

time: 90.7 us -> 88.3 us (0.974)
  local copies, waits for them, and re-layouts: 7.62 us -> 5.41 us
    unnamed x18 -> x14, local copies, waits for them, and re-layouts: 6.46 us -> 4.24 us
where the time goes in v16:
time: 88.3 us; the launch traced here: 88 us
  Pallas kernels  49.6 us (56%)
  waiting for transfers between devices  20.9 us (24%)
  starting transfers between devices  10 us (11%)
  local copies, waits for them, and re-layouts  5.41 us (6%)
  other arithmetic  1.38 us (2%)
    pallas_call x2, Pallas kernels, interpolation_call(): pl.pallas_call(functools.partial(interpolation_kernel, levels_body, toget...  34.2 us
    all_to_all x1, waiting for transfers between devices, exchange(): return lax.all_to_all(sums, 'band', split_axis=0, concat_axis=0, tiled=True)  19.2 us
    pallas_call x1, Pallas kernels, legendre_call(): pl.pallas_call(legendre_kernel, grid=(pairs // group,), out_shape=(shape,...  6.96 us
    all_to_all x1, starting transfers between devices, exchange(): return lax.all_to_all(sums, 'band', split_axis=0, concat_axis=0, tiled=True)  6.81 us
    pallas_call x1, Pallas kernels, fourier_call(): pl.pallas_call(functools.partial(fourier_kernel, pairs, levels), out_shap...  5.84 us
    unnamed x14, local copies, waits for them, and re-layouts  4.24 us
    ppermute x1, starting transfers between devices, swap_levels(): return (lax.ppermute(send[0], 'lev', [(0, 1), (1, 0)]),)  2.46 us
  transfers between devices with their start and end apart: 3, of which 3 were waited for; matrix products, arithmetic and copies ran while one was open for 3% of the time, Pallas kernels for 3%

profile of v16, /device:TPU:9, one launch (start us, length us, event | category | flops | bytes accessed | tf_op | source)
XLA Modules:
  0.0 88.0 jit_solution(13161566162827995592)
XLA Ops:
  0.6 0.7 collective-permute-start
  1.4 1.2 %pad_bitcast_fusion.numbers_ref = s32[1,128]{1,0:T(1,128)} fusion(s32[20]{0:T(128)} %param.8), kind=kLoop, calls=%fused_computation.2 | loop fusion | bytes 592 | tf_op jit(solution)/shard_map/broadcast_in_dim | solution.py:519
  2.5 1.2 %shard_map.77.codes_ref = s32[1,128]{1,0:T(1,128)} custom-call(s32[1,128]{1,0:T(1,128)} %pad_bitcast_fusion.numbers_ref), custom_call_target="tpu_custom_call" | custom-call | bytes 4000000 | tf_op jit(solution)/shard_map/pallas_call | solution.py:512
  3.8 1.3 %pad_add_fusion.1.numbers_ref = s32[21]{0:T(128)} fusion(s32[20]{0:T(128)} %param.8, s32[1]{0:T(128)} %bitcast.2), kind=kLoop, calls=%fused_computation.1 | loop fusion | flops 21 | bytes 168 | tf_op jit(solution)/shard_map/concatenate | solution.py:511
  5.1 0.1 collective-permute-done.others_1_
  5.2 0.0 copy-start.4
  5.2 1.3 %copy-done.4 = bf16[4,20,16,641]{3,2,1,0:T(8,128)(2,1)} copy-done((bf16[4,20,16,641]{3,2,1,0:T(8,128)(2,1)}, bf16[4,20,16,641]{3,2,1,0:T(8,128)(2,1)S(1)}, u32[]{:S(2)}) %copy-start.4) | copy-done | bytes 1640984
  6.5 0.0 copy-start.1
  6.5 7.0 %shard_map.78 = (bf16[16,248,128]{2,1,0:T(8,128)(2,1)}, f32[8,128]{1,0:T(8,128)}) custom-call(s32[21]{0:T(128)} %pad_add_fusion.1.numbers_ref, s32[1,128]{1,0:T(1,128)} %shard_map.77.codes_ref, bf16[2,20,32,641]{3,2,1,0:T(8,128)(2,1)} %bitcast.11, bf16[4,20,16,641]{3,2,1,0:T(8,128)(2,1)} %bitcast.13, bf16[4,20,16,641]{3,2,1,0:T(8,128)(2,1)} %copy-done.4), custom_call_target="tpu_custom_call" | custom-call | flops 420085760 | bytes 8000000 | tf_op jit(solution)/shard_map/pallas_call | solution.py:523
  13.5 0.0 copy-start.2
  13.5 6.8 %all-to-all-start = ((bf16[16,248,128]{2,1,0:T(8,128)(2,1)}), bf16[16,248,128]{2,1,0:T(8,128)(2,1)S(1)}, u32[]{:S(2)}, u32[]{:S(2)}) async-start(bf16[16,248,128]{2,1,0:T(8,128)(2,1)} %get-tuple-element.11), calls=%async_computation | async-start | bytes 2031616 | tf_op jit(solution)/shard_map/all_to_all | solution.py:716
  20.3 0.1 pad_add_fusion.base_ref
  20.4 0.0 copy-done.1
  20.4 0.0 copy-done.2
  20.4 0.0 copy-start.3
  20.4 0.7 copy-done.3
  21.0 1.4 %shard_map.79 = (f32[7,8,8,2816]{3,2,1,0:T(8,128)S(1)}, f32[8,128]{1,0:T(8,128)S(1)}) custom-call(s32[2]{0:T(128)S(1)} %pad_add_fusion.base_ref, f32[8,128]{1,0:T(8,128)S(1)} %copy-done.3, bf16[8,8,2816]{2,1,0:T(8,128)(2,1)S(1)} %copy-done.2, s32[3,8,8,2816]{3,2,1,0:T(8,128)S(1)} %copy-done.1), custom_call_target="tpu_custom_call" | custom-call | flops 7208960 | bytes 20000000 | tf_op jit(solution)/shard_map/pallas_call | solution.py:211
  22.4 0.0 copy-start
  22.4 2.2 %copy-done = f32[7,8,8,2816]{3,2,1,0:T(8,128)} copy-done((f32[7,8,8,2816]{3,2,1,0:T(8,128)}, f32[7,8,8,2816]{3,2,1,0:T(8,128)S(1)}, u32[]{:S(2)}) %copy-start) | copy-done | bytes 5046296
  24.6 19.2 %all-to-all-done.sums_ref = bf16[16,248,128]{2,1,0:T(8,128)(2,1)S(1)} async-done(((bf16[16,248,128]{2,1,0:T(8,128)(2,1)}), bf16[16,248,128]{2,1,0:T(8,128)(2,1)S(1)}, u32[]{:S(2)}, u32[]{:S(2)}) %all-to-all-start) | async-done | bytes 1015840 | tf_op jit(solution)/shard_map/all_to_all | solution.py:716
  43.9 0.0 slice-start
  43.9 0.0 slice-start.1
  43.9 5.8 %shard_map.80 = (f32[8,24,2816]{2,1,0:T(8,128)S(1)}, f32[8,24,2816]{2,1,0:T(8,128)S(1)}, bf16[1,2,2,24,2816]{4,3,2,1,0:T(8,128)(2,1)S(1)}) custom-call(s32[2]{0:T(128)S(1)} %pad_add_fusion.base_ref, f32[8,128]{1,0:T(8,128)S(1)} %get-tuple-element.10.after_ref, bf16[16,248,128]{2,1,0:T(8,128)(2,1)S(1)} %all-to-all-done.sums_ref, ...), custom_call_target="tpu_custom_call" | custom-call | flops 8000000000 | bytes 8000000 | tf_op jit(solution)/shard_map/pallas_call | solution.py:693
  49.7 2.5 %collective-permute-start.1 = (bf16[2,2,24,2816]{3,2,1,0:T(8,128)(2,1)S(1)}, bf16[2,2,24,2816]{3,2,1,0:T(8,128)(2,1)S(1)}, u32[]{:S(2)}, u32[]{:S(2)}) collective-permute-start(bf16[2,2,24,2816]{3,2,1,0:T(8,128)(2,1)S(1)} %bitcast.10), channel_id=1, source_target_pairs={{0,1},{1,0},{2,3},{3,2},{4,5},{5,4},{6,7},{7,6},{8,9},{9,8},{10,11... | collective-permute-start | bytes 1622024 | tf_op jit(solution)/shard_map/ppermute | solution.py:380
  52.2 1.6 %collective-permute-done.1.others_0_ = bf16[2,2,24,2816]{3,2,1,0:T(8,128)(2,1)S(1)} collective-permute-done((bf16[2,2,24,2816]{3,2,1,0:T(8,128)(2,1)S(1)}, bf16[2,2,24,2816]{3,2,1,0:T(8,128)(2,1)S(1)}, u32[]{:S(2)}, u32[]{:S(2)}) %collective-permute-start.1) | collective-permute-done | bytes 540704 | tf_op jit(solution)/shard_map/ppermute | solution.py:380
  53.7 0.0 slice-done
  53.7 0.0 slice-done.1
  53.7 18.0 %shard_map.81.others_1_ = f32[2,8,8,2816]{3,2,1,0:T(8,128)S(1)} custom-call(s32[2]{0:T(128)S(1)} %pad_add_fusion.base_ref, f32[8,24,2816]{2,1,0:T(8,128)S(1)} %get-tuple-element.15.field_ref, f32[7,8,8,2816]{3,2,1,0:T(8,128)S(1)} %bitcast.9, bf16[2,2,24,2816]{3,2,1,0:T(8,128)(2,1)S(1)} %collective-permute-done.1.others_0_), custom_call_target="tpu_custom_call" | custom-call | flops 90112000 | bytes 7208960 | tf_op jit(solution)/shard_map/pallas_call | solution.py:357
  71.8 16.2 %shard_map.82 = (bf16[2,8,8,2816]{3,2,1,0:T(8,128)(2,1)}, f32[2,8,8,2816]{3,2,1,0:T(8,128)}) custom-call(s32[2]{0:T(128)S(1)} %pad_add_fusion.base_ref, f32[8,24,2816]{2,1,0:T(8,128)S(1)} %get-tuple-element.12.field_ref, f32[7,8,8,2816]{3,2,1,0:T(8,128)S(1)} %bitcast.9, bf16[2,2,24,2816]{3,2,1,0:T(8,128)(2,1)S(1)} %collective-permute-done.1.others_0_, ...), custom_call_target="tpu_custom_call" | custom-call | flops 90112000 | bytes 7208960 | tf_op jit(solution)/shard_map/pallas_call | solution.py:357
  (1 shorter events, 0.0 us)
Async XLA Ops:
  0.6 4.6 %collective-permute-start = (bf16[4,20,16,641]{3,2,1,0:T(8,128)(2,1)}, bf16[4,20,16,641]{3,2,1,0:T(8,128)(2,1)S(1)}, u32[]{:S(2)}, u32[]{:S(2)}) collective-permute-start(bf16[4,20,16,641]{3,2,1,0:T(8,128)(2,1)} %bitcast.12), channel_id=1, source_target_pairs={{0,1},{1,0},{2,3},{3,2},{4,5},{5,4},{6,7},{7,6},{8,9},{9,8},{10,11... | collective-permute-start | bytes 4922888 | tf_op jit(solution)/shard_map/ppermute | solution.py:725
  5.2 1.3 %copy-start.4 = (bf16[4,20,16,641]{3,2,1,0:T(8,128)(2,1)}, bf16[4,20,16,641]{3,2,1,0:T(8,128)(2,1)S(1)}, u32[]{:S(2)}) copy-start(bf16[4,20,16,641]{3,2,1,0:T(8,128)(2,1)S(1)} %collective-permute-done.others_1_) | copy-start | bytes 4922884
  6.5 13.9 %copy-start.1 = (s32[3,8,8,2816]{3,2,1,0:T(8,128)S(1)}, s32[3,8,8,2816]{3,2,1,0:T(8,128)}, u32[]{:S(2)}) copy-start(s32[3,8,8,2816]{3,2,1,0:T(8,128)} %cells_ref.1) | copy-start | bytes 6488068
  13.5 6.9 %copy-start.2 = (bf16[8,8,2816]{2,1,0:T(8,128)(2,1)S(1)}, bf16[8,8,2816]{2,1,0:T(8,128)(2,1)}, u32[]{:S(2)}) copy-start(bf16[8,8,2816]{2,1,0:T(8,128)(2,1)} %eta_ref.1) | copy-start | bytes 1081348
  13.5 30.4 %all-to-all-start = ((bf16[16,248,128]{2,1,0:T(8,128)(2,1)}), bf16[16,248,128]{2,1,0:T(8,128)(2,1)S(1)}, u32[]{:S(2)}, u32[]{:S(2)}) async-start(bf16[16,248,128]{2,1,0:T(8,128)(2,1)} %get-tuple-element.11), calls=%async_computation | async-start | bytes 2031616 | tf_op jit(solution)/shard_map/all_to_all | solution.py:716
  20.4 0.7 copy-start.3
  22.4 2.2 %copy-start = (f32[7,8,8,2816]{3,2,1,0:T(8,128)}, f32[7,8,8,2816]{3,2,1,0:T(8,128)S(1)}, u32[]{:S(2)}) copy-start(f32[7,8,8,2816]{3,2,1,0:T(8,128)S(1)} %get-tuple-element.13.points_ref) | copy-start | bytes 15138820
  43.9 9.9 %slice-start = ((s8[5046272]{0:T(1024)(128)(4,1)}), s8[4194304]{0:T(1024)(128)(4,1)S(1)}, s32[]{:S(2)}) async-start(s8[5046272]{0:T(1024)(128)(4,1)} %bitcast.8), calls=%async_computation.1 | async-start | bytes 8388608
  43.9 9.9 %slice-start.1 = ((s8[5046272]{0:T(1024)(128)(4,1)}), s8[851968]{0:T(1024)(128)(4,1)S(1)}, s32[]{:S(2)}) async-start(s8[5046272]{0:T(1024)(128)(4,1)} %bitcast.8), calls=%async_computation.2 | async-start | bytes 1703936
  49.7 4.0 %collective-permute-start.1 = (bf16[2,2,24,2816]{3,2,1,0:T(8,128)(2,1)S(1)}, bf16[2,2,24,2816]{3,2,1,0:T(8,128)(2,1)S(1)}, u32[]{:S(2)}, u32[]{:S(2)}) collective-permute-start(bf16[2,2,24,2816]{3,2,1,0:T(8,128)(2,1)S(1)} %bitcast.10), channel_id=1, source_target_pairs={{0,1},{1,0},{2,3},{3,2},{4,5},{5,4},{6,7},{7,6},{8,9},{9,8},{10,11... | collective-permute-start | bytes 1622024 | tf_op jit(solution)/shard_map/ppermute | solution.py:380

commit v17 on v16

--- a/solution.py
+++ b/solution.py
@@ -514,7 +514,6 @@
         out_shape=jax.ShapeDtypeStruct((1, LANES), jnp.int32),
         in_specs=[pl.BlockSpec(memory_space=pltpu.VMEM)],
         out_specs=pl.BlockSpec(memory_space=pltpu.VMEM),
-        compiler_params=pltpu.CompilerParams(vmem_limit_bytes=60 * 1024 * 1024),
         cost_estimate=pl.CostEstimate(flops=0, bytes_accessed=4_000_000, transcendentals=0),
     )(jnp.pad(pairing, (0, LANES - pairs))[None, :])
     shape = jax.ShapeDtypeStruct((bands, block, LANES), jnp.bfloat16)

time: 88.3 us -> 88.3 us (level)
  no operation moved by 1% of the time
where the time goes in v17:
time: 88.3 us; the launch traced here: 88 us
  Pallas kernels  49.6 us (56%)
  waiting for transfers between devices  20.9 us (24%)
  starting transfers between devices  10 us (11%)
  local copies, waits for them, and re-layouts  5.41 us (6%)
  other arithmetic  1.38 us (2%)
    pallas_call x2, Pallas kernels, interpolation_call(): pl.pallas_call(functools.partial(interpolation_kernel, levels_body, toget...  34.2 us
    all_to_all x1, waiting for transfers between devices, exchange(): return lax.all_to_all(sums, 'band', split_axis=0, concat_axis=0, tiled=True)  19.2 us
    pallas_call x1, Pallas kernels, legendre_call(): pl.pallas_call(legendre_kernel, grid=(pairs // group,), out_shape=(shape,...  6.96 us
    all_to_all x1, starting transfers between devices, exchange(): return lax.all_to_all(sums, 'band', split_axis=0, concat_axis=0, tiled=True)  6.81 us
    pallas_call x1, Pallas kernels, fourier_call(): pl.pallas_call(functools.partial(fourier_kernel, pairs, levels), out_shap...  5.84 us
    unnamed x14, local copies, waits for them, and re-layouts  4.24 us
    ppermute x1, starting transfers between devices, swap_levels(): return (lax.ppermute(send[0], 'lev', [(0, 1), (1, 0)]),)  2.46 us
  transfers between devices with their start and end apart: 3, of which 3 were waited for; matrix products, arithmetic and copies ran while one was open for 3% of the time, Pallas kernels for 3%

profile of v17, /device:TPU:9, one launch (start us, length us, event | category | flops | bytes accessed | tf_op | source)
XLA Modules:
  0.0 88.0 jit_solution(13161566162827995592)
XLA Ops:
  0.6 0.7 collective-permute-start
  1.4 1.2 %pad_bitcast_fusion.numbers_ref = s32[1,128]{1,0:T(1,128)} fusion(s32[20]{0:T(128)} %param.8), kind=kLoop, calls=%fused_computation.2 | loop fusion | bytes 592 | tf_op jit(solution)/shard_map/broadcast_in_dim | solution.py:518
  2.5 1.2 %shard_map.77.codes_ref = s32[1,128]{1,0:T(1,128)} custom-call(s32[1,128]{1,0:T(1,128)} %pad_bitcast_fusion.numbers_ref), custom_call_target="tpu_custom_call" | custom-call | bytes 4000000 | tf_op jit(solution)/shard_map/pallas_call | solution.py:512
  3.8 1.3 %pad_add_fusion.1.numbers_ref = s32[21]{0:T(128)} fusion(s32[20]{0:T(128)} %param.8, s32[1]{0:T(128)} %bitcast.2), kind=kLoop, calls=%fused_computation.1 | loop fusion | flops 21 | bytes 168 | tf_op jit(solution)/shard_map/concatenate | solution.py:511
  5.1 0.1 collective-permute-done.others_1_
  5.2 0.0 copy-start.4
  5.2 1.3 %copy-done.4 = bf16[4,20,16,641]{3,2,1,0:T(8,128)(2,1)} copy-done((bf16[4,20,16,641]{3,2,1,0:T(8,128)(2,1)}, bf16[4,20,16,641]{3,2,1,0:T(8,128)(2,1)S(1)}, u32[]{:S(2)}) %copy-start.4) | copy-done | bytes 1640984
  6.5 0.0 copy-start.1
  6.5 7.0 %shard_map.78 = (bf16[16,248,128]{2,1,0:T(8,128)(2,1)}, f32[8,128]{1,0:T(8,128)}) custom-call(s32[21]{0:T(128)} %pad_add_fusion.1.numbers_ref, s32[1,128]{1,0:T(1,128)} %shard_map.77.codes_ref, bf16[2,20,32,641]{3,2,1,0:T(8,128)(2,1)} %bitcast.11, bf16[4,20,16,641]{3,2,1,0:T(8,128)(2,1)} %bitcast.13, bf16[4,20,16,641]{3,2,1,0:T(8,128)(2,1)} %copy-done.4), custom_call_target="tpu_custom_call" | custom-call | flops 420085760 | bytes 8000000 | tf_op jit(solution)/shard_map/pallas_call | solution.py:522
  13.5 0.0 copy-start.2
  13.5 6.8 %all-to-all-start = ((bf16[16,248,128]{2,1,0:T(8,128)(2,1)}), bf16[16,248,128]{2,1,0:T(8,128)(2,1)S(1)}, u32[]{:S(2)}, u32[]{:S(2)}) async-start(bf16[16,248,128]{2,1,0:T(8,128)(2,1)} %get-tuple-element.11), calls=%async_computation | async-start | bytes 2031616 | tf_op jit(solution)/shard_map/all_to_all | solution.py:715
  20.3 0.1 pad_add_fusion.base_ref
  20.4 0.0 copy-done.1
  20.4 0.0 copy-done.2
  20.4 0.0 copy-start.3
  20.4 0.7 copy-done.3
  21.0 1.4 %shard_map.79 = (f32[7,8,8,2816]{3,2,1,0:T(8,128)S(1)}, f32[8,128]{1,0:T(8,128)S(1)}) custom-call(s32[2]{0:T(128)S(1)} %pad_add_fusion.base_ref, f32[8,128]{1,0:T(8,128)S(1)} %copy-done.3, bf16[8,8,2816]{2,1,0:T(8,128)(2,1)S(1)} %copy-done.2, s32[3,8,8,2816]{3,2,1,0:T(8,128)S(1)} %copy-done.1), custom_call_target="tpu_custom_call" | custom-call | flops 7208960 | bytes 20000000 | tf_op jit(solution)/shard_map/pallas_call | solution.py:211
  22.4 0.0 copy-start
  22.4 2.2 %copy-done = f32[7,8,8,2816]{3,2,1,0:T(8,128)} copy-done((f32[7,8,8,2816]{3,2,1,0:T(8,128)}, f32[7,8,8,2816]{3,2,1,0:T(8,128)S(1)}, u32[]{:S(2)}) %copy-start) | copy-done | bytes 5046296
  24.6 19.2 %all-to-all-done.sums_ref = bf16[16,248,128]{2,1,0:T(8,128)(2,1)S(1)} async-done(((bf16[16,248,128]{2,1,0:T(8,128)(2,1)}), bf16[16,248,128]{2,1,0:T(8,128)(2,1)S(1)}, u32[]{:S(2)}, u32[]{:S(2)}) %all-to-all-start) | async-done | bytes 1015840 | tf_op jit(solution)/shard_map/all_to_all | solution.py:715
  43.9 0.0 slice-start
  43.9 0.0 slice-start.1
  43.9 5.8 %shard_map.80 = (f32[8,24,2816]{2,1,0:T(8,128)S(1)}, f32[8,24,2816]{2,1,0:T(8,128)S(1)}, bf16[1,2,2,24,2816]{4,3,2,1,0:T(8,128)(2,1)S(1)}) custom-call(s32[2]{0:T(128)S(1)} %pad_add_fusion.base_ref, f32[8,128]{1,0:T(8,128)S(1)} %get-tuple-element.10.after_ref, bf16[16,248,128]{2,1,0:T(8,128)(2,1)S(1)} %all-to-all-done.sums_ref, ...), custom_call_target="tpu_custom_call" | custom-call | flops 8000000000 | bytes 8000000 | tf_op jit(solution)/shard_map/pallas_call | solution.py:692
  49.7 2.5 %collective-permute-start.1 = (bf16[2,2,24,2816]{3,2,1,0:T(8,128)(2,1)S(1)}, bf16[2,2,24,2816]{3,2,1,0:T(8,128)(2,1)S(1)}, u32[]{:S(2)}, u32[]{:S(2)}) collective-permute-start(bf16[2,2,24,2816]{3,2,1,0:T(8,128)(2,1)S(1)} %bitcast.10), channel_id=1, source_target_pairs={{0,1},{1,0},{2,3},{3,2},{4,5},{5,4},{6,7},{7,6},{8,9},{9,8},{10,11... | collective-permute-start | bytes 1622024 | tf_op jit(solution)/shard_map/ppermute | solution.py:380
  52.2 1.6 %collective-permute-done.1.others_0_ = bf16[2,2,24,2816]{3,2,1,0:T(8,128)(2,1)S(1)} collective-permute-done((bf16[2,2,24,2816]{3,2,1,0:T(8,128)(2,1)S(1)}, bf16[2,2,24,2816]{3,2,1,0:T(8,128)(2,1)S(1)}, u32[]{:S(2)}, u32[]{:S(2)}) %collective-permute-start.1) | collective-permute-done | bytes 540704 | tf_op jit(solution)/shard_map/ppermute | solution.py:380
  53.7 0.0 slice-done
  53.7 0.0 slice-done.1
  53.7 18.0 %shard_map.81.others_1_ = f32[2,8,8,2816]{3,2,1,0:T(8,128)S(1)} custom-call(s32[2]{0:T(128)S(1)} %pad_add_fusion.base_ref, f32[8,24,2816]{2,1,0:T(8,128)S(1)} %get-tuple-element.15.field_ref, f32[7,8,8,2816]{3,2,1,0:T(8,128)S(1)} %bitcast.9, bf16[2,2,24,2816]{3,2,1,0:T(8,128)(2,1)S(1)} %collective-permute-done.1.others_0_), custom_call_target="tpu_custom_call" | custom-call | flops 90112000 | bytes 7208960 | tf_op jit(solution)/shard_map/pallas_call | solution.py:357
  71.8 16.2 %shard_map.82 = (bf16[2,8,8,2816]{3,2,1,0:T(8,128)(2,1)}, f32[2,8,8,2816]{3,2,1,0:T(8,128)}) custom-call(s32[2]{0:T(128)S(1)} %pad_add_fusion.base_ref, f32[8,24,2816]{2,1,0:T(8,128)S(1)} %get-tuple-element.12.field_ref, f32[7,8,8,2816]{3,2,1,0:T(8,128)S(1)} %bitcast.9, bf16[2,2,24,2816]{3,2,1,0:T(8,128)(2,1)S(1)} %collective-permute-done.1.others_0_, ...), custom_call_target="tpu_custom_call" | custom-call | flops 90112000 | bytes 7208960 | tf_op jit(solution)/shard_map/pallas_call | solution.py:357
  (1 shorter events, 0.0 us)
Async XLA Ops:
  0.6 4.6 %collective-permute-start = (bf16[4,20,16,641]{3,2,1,0:T(8,128)(2,1)}, bf16[4,20,16,641]{3,2,1,0:T(8,128)(2,1)S(1)}, u32[]{:S(2)}, u32[]{:S(2)}) collective-permute-start(bf16[4,20,16,641]{3,2,1,0:T(8,128)(2,1)} %bitcast.12), channel_id=1, source_target_pairs={{0,1},{1,0},{2,3},{3,2},{4,5},{5,4},{6,7},{7,6},{8,9},{9,8},{10,11... | collective-permute-start | bytes 4922888 | tf_op jit(solution)/shard_map/ppermute | solution.py:724
  5.2 1.3 %copy-start.4 = (bf16[4,20,16,641]{3,2,1,0:T(8,128)(2,1)}, bf16[4,20,16,641]{3,2,1,0:T(8,128)(2,1)S(1)}, u32[]{:S(2)}) copy-start(bf16[4,20,16,641]{3,2,1,0:T(8,128)(2,1)S(1)} %collective-permute-done.others_1_) | copy-start | bytes 4922884
  6.5 13.9 %copy-start.1 = (s32[3,8,8,2816]{3,2,1,0:T(8,128)S(1)}, s32[3,8,8,2816]{3,2,1,0:T(8,128)}, u32[]{:S(2)}) copy-start(s32[3,8,8,2816]{3,2,1,0:T(8,128)} %cells_ref.1) | copy-start | bytes 6488068
  13.5 6.9 %copy-start.2 = (bf16[8,8,2816]{2,1,0:T(8,128)(2,1)S(1)}, bf16[8,8,2816]{2,1,0:T(8,128)(2,1)}, u32[]{:S(2)}) copy-start(bf16[8,8,2816]{2,1,0:T(8,128)(2,1)} %eta_ref.1) | copy-start | bytes 1081348
  13.5 30.4 %all-to-all-start = ((bf16[16,248,128]{2,1,0:T(8,128)(2,1)}), bf16[16,248,128]{2,1,0:T(8,128)(2,1)S(1)}, u32[]{:S(2)}, u32[]{:S(2)}) async-start(bf16[16,248,128]{2,1,0:T(8,128)(2,1)} %get-tuple-element.11), calls=%async_computation | async-start | bytes 2031616 | tf_op jit(solution)/shard_map/all_to_all | solution.py:715
  20.4 0.7 copy-start.3
  22.4 2.2 %copy-start = (f32[7,8,8,2816]{3,2,1,0:T(8,128)}, f32[7,8,8,2816]{3,2,1,0:T(8,128)S(1)}, u32[]{:S(2)}) copy-start(f32[7,8,8,2816]{3,2,1,0:T(8,128)S(1)} %get-tuple-element.13.points_ref) | copy-start | bytes 15138820
  43.9 9.9 %slice-start = ((s8[5046272]{0:T(1024)(128)(4,1)}), s8[4194304]{0:T(1024)(128)(4,1)S(1)}, s32[]{:S(2)}) async-start(s8[5046272]{0:T(1024)(128)(4,1)} %bitcast.8), calls=%async_computation.1 | async-start | bytes 8388608
  43.9 9.9 %slice-start.1 = ((s8[5046272]{0:T(1024)(128)(4,1)}), s8[851968]{0:T(1024)(128)(4,1)S(1)}, s32[]{:S(2)}) async-start(s8[5046272]{0:T(1024)(128)(4,1)} %bitcast.8), calls=%async_computation.2 | async-start | bytes 1703936
  49.7 4.0 %collective-permute-start.1 = (bf16[2,2,24,2816]{3,2,1,0:T(8,128)(2,1)S(1)}, bf16[2,2,24,2816]{3,2,1,0:T(8,128)(2,1)S(1)}, u32[]{:S(2)}, u32[]{:S(2)}) collective-permute-start(bf16[2,2,24,2816]{3,2,1,0:T(8,128)(2,1)S(1)} %bitcast.10), channel_id=1, source_target_pairs={{0,1},{1,0},{2,3},{3,2},{4,5},{5,4},{6,7},{7,6},{8,9},{9,8},{10,11... | collective-permute-start | bytes 1622024 | tf_op jit(solution)/shard_map/ppermute | solution.py:380
